TPU v7x, 512 devices: a whole 4x4x16 slice. The times are simulated.
512 devices in a mesh: band: 16 (over z_lo, y), space: 32 (over z_hi, x, core).
Axes of the slice: x: 4, y: 4, z: 16 (z_hi: 4, z_lo: 4; z = z_hi * 4 + z_lo), core: 2. Of those that a mesh axis runs over, the one named last changes fastest.
Arguments:
- occupied: float32 [2, 256, 64, 1024], P(None, 'band', 'space'), may hold values from -6 to 6
- initial: float32 [128, 64, 1024], P('band', 'space'), may hold values from -6 to 6
- right_side: float32 [128, 64, 1024], P('band', 'space'), may hold values from -6 to 6
- potential: float32 [64, 1024], P('space'), may hold values from 0.5 to 2.5
- energies: float32 [128], P('band'), may hold values from -1.5 to -0.2
Outputs:
- response: float32 [128, 64, 1024], P('band', 'space')
- residual: float32 [128, 64, 1024], P('band', 'space')
All inputs are finite; a program needn't handle non-finite values.
Results may differ from a plain program's by a relative error of at most 0.0001.
Values sent between devices are 32-bit elements; how exact they have to be, the bound alone decides.
No kernel may reach another device: no remote copies, remote signals or barrier semaphores. Data moves between devices by JAX's collectives and lax.ppermute only.
A program may use at most 64 MiB of HBM per device.

v0:
```python
import jax
import jax.numpy as jnp
from jax import lax
from jax.sharding import PartitionSpec as P

BLOCKS = 2
NZ = 32
ITERS = 2


def with_halo(block, sides, width):
    for axis, dim in sides:
        count = lax.axis_size(axis)
        forward = [(i, i + 1) for i in range(count - 1)]
        backward = [(target, source) for source, target in forward]
        low = lax.ppermute(
            lax.slice_in_dim(block, block.shape[dim] - width, None, axis=dim), axis, forward
        )
        high = lax.ppermute(lax.slice_in_dim(block, 0, width, axis=dim), axis, backward)
        block = jnp.concatenate([low, block, high], axis=dim)
    return block


def lateral_terms(vectors, z_cells):
    line_length = vectors.shape[-1]
    leading = [(0, 0)] * (vectors.ndim - 1)
    padded = jnp.pad(vectors, leading + [(2 * z_cells, 2 * z_cells)])
    nearest = (
        padded[..., z_cells : z_cells + line_length]
        + padded[..., 3 * z_cells : 3 * z_cells + line_length]
    )
    second = padded[..., 0:line_length] + padded[..., 4 * z_cells : 4 * z_cells + line_length]
    padded_z = jnp.pad(vectors, leading + [(2, 2)])
    z_index = jnp.arange(line_length) % z_cells
    nearest = nearest + jnp.where(z_index >= 1, padded_z[..., 1 : line_length + 1], 0.0)
    nearest = nearest + jnp.where(z_index <= z_cells - 2, padded_z[..., 3 : line_length + 3], 0.0)
    second = second + jnp.where(z_index >= 2, padded_z[..., 0:line_length], 0.0)
    second = second + jnp.where(z_index <= z_cells - 3, padded_z[..., 4 : line_length + 4], 0.0)
    return (nearest, second)


def state_products(states, flattened):
    return jnp.einsum(
        "jc,vc->jv",
        states,
        flattened,
        precision=lax.Precision.HIGHEST,
        preferred_element_type=jnp.float32,
    )


def state_sums(coefficient, states):
    return jnp.einsum(
        "jv,jc->vc",
        coefficient,
        states,
        precision=lax.Precision.HIGHEST,
        preferred_element_type=jnp.float32,
    )


def project(states, vectors, weight):
    local_count = vectors.shape[0]
    flattened = vectors.reshape(local_count, -1)
    own_states = states.reshape(states.shape[0], -1)
    product = state_products(lax.all_gather(own_states, "band", axis=0, tiled=True), flattened)
    margin = lax.psum(product, "space") * weight
    correction = state_sums(margin, lax.all_gather(own_states, "band", axis=0, tiled=True))
    return (flattened - correction).reshape(vectors.shape)


def on_device(occupied, initial, right_side, potential, energies):
    local_count, plane_count, line_length = initial.shape
    weight = 1.0 / (plane_count * lax.axis_size("space") * line_length)
    diagonal = 3.75 + potential[None, :, :] - energies[:, None, None]
    vectors = initial
    residual = jnp.zeros_like(initial)
    for iteration in range(ITERS):
        for block_index in range(BLOCKS):
            vectors = project(occupied[block_index], vectors, weight)
        padded_x = with_halo(vectors, (("space", 1),), 2)
        nearest = padded_x[:, 1 : plane_count + 1] + padded_x[:, 3 : plane_count + 3]
        second = padded_x[:, 0:plane_count] + padded_x[:, 4 : plane_count + 4]
        inner_near, inner_second = lateral_terms(vectors, NZ)
        applied = (
            diagonal * vectors - 2.0 / 3.0 * (nearest + inner_near) + (second + inner_second) / 24.0
        )
        residual = right_side - applied
        vectors = vectors + residual / diagonal
    return (vectors, residual)


def solution(mesh):
    return jax.shard_map(
        on_device,
        mesh=mesh,
        in_specs=(
            P(None, "band", "space", None),
            P("band", "space", None),
            P("band", "space", None),
            P("space", None),
            P("band"),
        ),
        out_specs=(P("band", "space", None), P("band", "space", None)),
        check_vma=False,
    )
```

profile of v0, /device:TPU:7, one launch (start us, length us, event | category | flops | bytes accessed | tf_op | source)
XLA Modules:
  0.0 838.6 jit_solution(6227800733809984338)
XLA Ops:
  7.2 0.0 all-gather.3.cloned.1.call-start
  7.2 1.0 fusion.45
  8.2 0.7 copy.24
  8.9 0.0 all-gather.3.cloned.1.call-update
  8.9 0.0 all-gather.5.cloned.1.call-start
  9.0 0.7 copy.25
  9.7 0.0 all-gather.5.cloned.1.call-update
  9.7 0.9 copy.23
  10.6 0.7 broadcast_add_fusion
  11.3 81.9 %all-gather.3.cloned.1.call-done = f32[256,2048]{1,0:T(8,128)} async-done(((f32[16,2048]{1,0:T(8,128)}), f32[256,2048]{1,0:T(8,128)}) %all-gather.3.cloned.1.call-update) | async-done | bytes 2097168 | tf_op jit(solution)/shard_map/all_gather | solution.py:66
  93.2 0.0 copy-start
  93.2 3.5 fusion.46
  96.7 175.3 %psum.28 = f32[256,8]{1,0:T(8,128)S(1)} all-reduce(f32[256,8]{1,0:T(8,128)S(1)} %fusion.46), channel_id=1, replica_groups=mesh['band'=16,'space'=32] {'space'}, use_global_device_ids=true, to_apply=%region_0.0 | all-reduce | flops 2048 | bytes 16384 | tf_op jit(solution)/shard_map/psum | solution.py:67
  272.1 0.0 copy-done
  272.1 1.1 convolution_subtract_fusion.3
  273.2 0.0 copy-start.3
  273.2 0.0 copy-start.4
  273.2 0.0 all-gather.5.cloned.1.call-done
  273.2 3.4 convolution_bitcast_fusion.2
  276.6 167.0 %psum.29 = f32[256,8]{1,0:T(8,128)S(1)} all-reduce(f32[256,8]{1,0:T(8,128)S(1)} %convolution_bitcast_fusion.2), channel_id=1, replica_groups=mesh['band'=16,'space'=32] {'space'}, use_global_device_ids=true, to_apply=%region_1.0 | all-reduce | flops 2048 | bytes 16384 | tf_op jit(solution)/shard_map/psum | solution.py:67
  443.6 2.7 convolution_subtract_fusion.2
  446.3 0.1 copy.14
  446.3 10.2 %collective-permute-start = (f32[8,2,1024]{2,1,0:T(2,128)S(1)}, f32[8,2,1024]{2,1,0:T(2,128)S(1)}, u32[]{:S(2)}, u32[]{:S(2)}) collective-permute-start(f32[8,2,1024]{2,1,0:T(2,128)S(1)} %copy.14), channel_id=1, source_target_pairs={{0,1},{1,2},{2,3},{3,4},{4,5},{5,6},{6,7},{7,8},{8,9},{9,10},{10,1... | collective-permute-start | bytes 196616 | tf_op jit(solution)/shard_map/ppermute | solution.py:16
  456.5 1.9 collective-permute-start.1
  458.5 0.0 collective-permute-done
  458.5 9.7 %collective-permute-done.1 = f32[8,2,1024]{2,1,0:T(2,128)S(1)} collective-permute-done((f32[8,2,1024]{2,1,0:T(2,128)S(1)}, f32[8,2,1024]{2,1,0:T(2,128)S(1)}, u32[]{:S(2)}, u32[]{:S(2)}) %collective-permute-start.1) | collective-permute-done | bytes 65568 | tf_op jit(solution)/shard_map/ppermute | solution.py:19
  468.1 0.0 copy-done.3
  468.1 0.0 copy-done.4
  468.1 0.6 fusion.32
  468.8 1.8 convolution_bitcast_fusion.1
  470.6 166.6 %psum.30 = f32[256,8]{1,0:T(8,128)S(1)} all-reduce(f32[256,8]{1,0:T(8,128)S(1)} %convolution_bitcast_fusion.1), channel_id=1, replica_groups=mesh['band'=16,'space'=32] {'space'}, use_global_device_ids=true, to_apply=%region_2.3 | all-reduce | flops 2048 | bytes 16384 | tf_op jit(solution)/shard_map/psum | solution.py:67
  637.2 0.0 copy-start.1
  637.2 1.1 convolution_subtract_fusion.1
  638.3 0.5 copy-done.1
  638.8 0.0 copy-start.2
  638.8 1.8 convolution_bitcast_fusion
  640.5 167.0 %psum.31 = f32[256,8]{1,0:T(8,128)S(1)} all-reduce(f32[256,8]{1,0:T(8,128)S(1)} %convolution_bitcast_fusion), channel_id=1, replica_groups=mesh['band'=16,'space'=32] {'space'}, use_global_device_ids=true, to_apply=%region_3.4 | all-reduce | flops 2048 | bytes 16384 | tf_op jit(solution)/shard_map/psum | solution.py:67
  807.5 0.0 copy-done.2
  807.5 1.1 convolution_subtract_fusion
  808.6 0.1 copy.22
  808.7 10.2 %collective-permute-start.2 = (f32[8,2,1024]{2,1,0:T(2,128)S(1)}, f32[8,2,1024]{2,1,0:T(2,128)S(1)}, u32[]{:S(2)}, u32[]{:S(2)}) collective-permute-start(f32[8,2,1024]{2,1,0:T(2,128)S(1)} %copy.22), channel_id=1, source_target_pairs={{0,1},{1,2},{2,3},{3,4},{4,5},{5,6},{6,7},{7,8},{8,9},{9,10},{10,1... | collective-permute-start | bytes 196616 | tf_op jit(solution)/shard_map/ppermute | solution.py:16
  818.9 1.9 collective-permute-start.3
  820.8 0.0 collective-permute-done.2
  820.8 9.7 %collective-permute-done.3 = f32[8,2,1024]{2,1,0:T(2,128)S(1)} collective-permute-done((f32[8,2,1024]{2,1,0:T(2,128)S(1)}, f32[8,2,1024]{2,1,0:T(2,128)S(1)}, u32[]{:S(2)}, u32[]{:S(2)}) %collective-permute-start.3) | collective-permute-done | bytes 65568 | tf_op jit(solution)/shard_map/ppermute | solution.py:19
  830.5 1.3 fusion.5
  (3 shorter events, 0.0 us)
Async XLA Ops:
  7.2 86.0 %all-gather.3.cloned.1.call-start = ((), (), s32[]{:S(2)}) async-start(), calls=%async_computation | async-start | bytes 2228224 | tf_op jit(solution)/shard_map/all_gather | solution.py:66
  8.9 264.3 %all-gather.5.cloned.1.call-start = ((), (), s32[]{:S(2)}) async-start(), calls=%async_computation.1 | async-start | bytes 2228224 | tf_op jit(solution)/shard_map/all_gather | solution.py:66
  93.2 178.8 %copy-start = (f32[256,2048]{1,0:T(8,128)S(1)}, f32[256,2048]{1,0:T(8,128)}, u32[]{:S(2)}) copy-start(f32[256,2048]{1,0:T(8,128)} %all-gather.3.cloned.1.call-done) | copy-start | bytes 6291460
  273.2 195.0 %copy-start.3 = (f32[8,2,1024]{2,1,0:T(2,128)S(1)}, f32[8,2,1024]{2,1,0:T(2,128)}, u32[]{:S(2)}) copy-start(f32[8,2,1024]{2,1,0:T(2,128)} %param.7) | copy-start | bytes 196612
  273.2 195.0 %copy-start.4 = (f32[8]{0:T(128)S(1)}, f32[8]{0:T(128)}, u32[]{:S(2)}) copy-start(f32[8]{0:T(128)} %param.9) | copy-start | bytes 100
  446.3 12.2 %collective-permute-start = (f32[8,2,1024]{2,1,0:T(2,128)S(1)}, f32[8,2,1024]{2,1,0:T(2,128)S(1)}, u32[]{:S(2)}, u32[]{:S(2)}) collective-permute-start(f32[8,2,1024]{2,1,0:T(2,128)S(1)} %copy.14), channel_id=1, source_target_pairs={{0,1},{1,2},{2,3},{3,4},{4,5},{5,6},{6,7},{7,8},{8,9},{9,10},{10,1... | collective-permute-start | bytes 196616 | tf_op jit(solution)/shard_map/ppermute | solution.py:16
  456.5 11.6 %collective-permute-start.1 = (f32[8,2,1024]{2,1,0:T(2,128)S(1)}, f32[8,2,1024]{2,1,0:T(2,128)S(1)}, u32[]{:S(2)}, u32[]{:S(2)}) collective-permute-start(f32[8,2,1024]{2,1,0:T(2,128)S(1)} %copy.14), channel_id=1, source_target_pairs={{1,0},{2,1},{3,2},{4,3},{5,4},{6,5},{7,6},{8,7},{9,8},{10,9},{11,1... | collective-permute-start | bytes 196616 | tf_op jit(solution)/shard_map/ppermute | solution.py:19
  637.2 1.6 copy-start.1
  638.8 168.7 %copy-start.2 = (f32[256,2048]{1,0:T(8,128)S(1)}, f32[256,2048]{1,0:T(8,128)}, u32[]{:S(2)}) copy-start(f32[256,2048]{1,0:T(8,128)} %all-gather.5.cloned.1.call-done) | copy-start | bytes 6291460
  808.7 12.1 %collective-permute-start.2 = (f32[8,2,1024]{2,1,0:T(2,128)S(1)}, f32[8,2,1024]{2,1,0:T(2,128)S(1)}, u32[]{:S(2)}, u32[]{:S(2)}) collective-permute-start(f32[8,2,1024]{2,1,0:T(2,128)S(1)} %copy.22), channel_id=1, source_target_pairs={{0,1},{1,2},{2,3},{3,4},{4,5},{5,6},{6,7},{7,8},{8,9},{9,10},{10,1... | collective-permute-start | bytes 196616 | tf_op jit(solution)/shard_map/ppermute | solution.py:16
  818.9 11.6 %collective-permute-start.3 = (f32[8,2,1024]{2,1,0:T(2,128)S(1)}, f32[8,2,1024]{2,1,0:T(2,128)S(1)}, u32[]{:S(2)}, u32[]{:S(2)}) collective-permute-start(f32[8,2,1024]{2,1,0:T(2,128)S(1)} %copy.22), channel_id=1, source_target_pairs={{1,0},{2,1},{3,2},{4,3},{5,4},{6,5},{7,6},{8,7},{9,8},{10,9},{11,1... | collective-permute-start | bytes 196616 | tf_op jit(solution)/shard_map/ppermute | solution.py:19
Sparse Core Ops, SparseCore 0:
  10.1 83.0 all-gather.2
  95.3 86.5 all-gather.4
where the time goes:
time: 839 us
  blocking collectives  676 us (81%)
  waiting for transfers between devices  101 us (12%)
  starting transfers between devices  24.3 us (3%)
  matrix products  16.5 us (2%)
  between operations  14.2 us (2%)
    psum x4, blocking collectives, project(): margin = lax.psum(product, 'space') * weight  676 us
    all_gather x2, waiting for transfers between devices, project(): lax.all_gather(own_states, 'band', axis=0, tiled=True)  81.9 us
    ppermute x2, starting transfers between devices, with_halo(): lax.ppermute(lax.slice_in_dim(block, block.shape[dim] - width, None, axis...  20.4 us
    ppermute x2, waiting for transfers between devices, with_halo(): lax.ppermute(lax.slice_in_dim(block, 0, width, axis=dim), axis, backward)  19.3 us
  transfers between devices with their start and end apart: 6, of which 3 were waited for; matrix products, arithmetic and copies ran while one was open for 1% of the time, Pallas kernels for 0%

commit v1 on v0

v1 whole, which is shorter than its diff:
```python
import jax
import jax.numpy as jnp
from jax import lax
from jax.sharding import PartitionSpec as P

NZ = 32
ITERS = 2
BAND_Z = [[z * 4 + y for z in range(4)] for y in range(4)]
BAND_Y = [[z * 4 + y for y in range(4)] for z in range(4)]
SPACE_PLANE = [[z * 8 + r for r in range(8)] for z in range(4)]
SPACE_Z = [[z * 8 + r for z in range(4)] for r in range(8)]


def copies(x, axis, groups):
    count = len(groups[0])
    sent = jnp.broadcast_to(x[None], (count,) + x.shape)
    return lax.all_to_all(sent, axis, 0, 0, axis_index_groups=groups)


def gathered(states):
    columns = copies(states, "band", BAND_Z)
    return copies(columns, "band", BAND_Y).reshape(-1, states.shape[-1])


def space_sum(x):
    near = jnp.sum(copies(x, "space", SPACE_PLANE), axis=0)
    return lax.psum(near, "space", axis_index_groups=SPACE_Z)


def products(vectors, states):
    return jnp.einsum(
        "vc,jc->vj",
        vectors,
        states,
        precision=lax.Precision.HIGH,
        preferred_element_type=jnp.float32,
    )


def combination(margin, states):
    return jnp.einsum(
        "vj,jc->vc",
        margin,
        states,
        precision=lax.Precision.HIGH,
        preferred_element_type=jnp.float32,
    )


def neighbours(vectors):
    count = lax.axis_size("space")
    outer = [(i, i + 1) for i in range(1, count - 1, 2)]
    outer = outer + [(j, i) for i, j in outer]
    across = lax.ppermute(vectors, "space", outer)
    inside = lax.ppermute(vectors, "space", [(i, i ^ 1) for i in range(count)])
    first = lax.axis_index("space") % 2 == 0
    return jnp.where(first, across, inside), jnp.where(first, inside, across)


def shifted(planes, by):
    length = planes.shape[-1]
    pad = [(0, 0)] * (planes.ndim - 1)
    if by > 0:
        return jnp.pad(planes[..., by:], pad + [(0, by)])
    return jnp.pad(planes[..., :length + by], pad + [(-by, 0)])


def coupling(vectors, low, high):
    z = jnp.arange(vectors.shape[-1]) % NZ
    nearest = shifted(vectors, NZ) + shifted(vectors, -NZ)
    second = shifted(vectors, 2 * NZ) + shifted(vectors, -2 * NZ)
    nearest = nearest + jnp.where(z >= 1, shifted(vectors, -1), 0.0)
    nearest = nearest + jnp.where(z <= NZ - 2, shifted(vectors, 1), 0.0)
    second = second + jnp.where(z >= 2, shifted(vectors, -2), 0.0)
    second = second + jnp.where(z <= NZ - 3, shifted(vectors, 2), 0.0)
    x = jnp.concatenate([low, vectors, high], axis=1)
    nearest = nearest + x[:, 1:3] + x[:, 3:5]
    second = second + x[:, 0:2] + x[:, 4:6]
    return second / 24.0 - 2.0 / 3.0 * nearest


def on_device(occupied, initial, right_side, potential, energies):
    count, planes, line = initial.shape
    weight = 1.0 / (planes * lax.axis_size("space") * line)
    states = [occupied[0].reshape(-1, planes * line), occupied[1].reshape(-1, planes * line)]
    later = lax.all_gather(states[1], "band", axis=0, tiled=True)
    blocks = [gathered(states[0]), later]
    diagonal = 3.75 + potential[None, :, :] - energies[:, None, None]
    vectors = initial.reshape(count, planes * line)
    for iteration in range(ITERS):
        for block in blocks:
            margin = space_sum(products(vectors, block)) * weight
            vectors = vectors - combination(margin, block)
        low, high = neighbours(vectors)
        shape = (count, planes, line)
        vectors = vectors.reshape(shape)
        rest = right_side - coupling(vectors, low.reshape(shape), high.reshape(shape))
        residual = rest - diagonal * vectors
        vectors = (rest / diagonal).reshape(count, planes * line)
    return (vectors.reshape(shape), residual)


def solution(mesh):
    return jax.shard_map(
        on_device,
        mesh=mesh,
        in_specs=(
            P(None, "band", "space", None),
            P("band", "space", None),
            P("band", "space", None),
            P("space", None),
            P("band"),
        ),
        out_specs=(P("band", "space", None), P("band", "space", None)),
        check_vma=False,
    )
```

time: 839 us -> 215 us (0.26)
  blocking collectives: 676 us -> 93 us
  waiting for transfers between devices: 101 us -> 42.7 us
  starting transfers between devices: 24.3 us -> 45.2 us
    psum x4, blocking collectives: 676 us -> 56.7 us  [space_sum(): return lax.psum(near, 'space', axis_index_groups=SPACE_Z)]
    all_gather x2 -> x1, waiting for transfers between devices: 81.9 us -> 0.01 us  [on_device(): later = lax.all_gather(states[1], 'band', axis=0, tiled=True)]
    all_to_all x0 -> x3, waiting for transfers between devices: none -> 41.5 us  [copies(): return lax.all_to_all(sent, axis, 0, 0, axis_index_groups=groups)]
    all_to_all x0 -> x3, blocking collectives: none -> 36.3 us  [copies(): return lax.all_to_all(sent, axis, 0, 0, axis_index_groups=groups)]
    all_to_all x0 -> x3, starting transfers between devices: none -> 20.3 us  [copies(): return lax.all_to_all(sent, axis, 0, 0, axis_index_groups=groups)]
    ppermute x4, waiting for transfers between devices: 19.3 us -> 1.2 us  [the longest x2 1.2 us: neighbours(): inside = lax.ppermute(vectors, 'space', [(i, i ^ 1) for i in range(count)])]
  transfers between devices with their start and end apart: 6 -> 8, of which waited for: 3 -> 5; matrix products, arithmetic and copies ran while one was open for 1% -> 2% of each run, Pallas kernels for 0% -> 0%
where the time goes in v1:
time: 215 us; the launch traced here: 214 us
  blocking collectives  93 us (43%)
  starting transfers between devices  45.2 us (21%)
  waiting for transfers between devices  42.7 us (20%)
  between operations  14.3 us (7%)
  matrix products  9.32 us (4%)
  local copies, waits for them, and re-layouts  7.05 us (3%)
  other arithmetic  2.38 us (1%)
    psum x4, blocking collectives, space_sum(): return lax.psum(near, 'space', axis_index_groups=SPACE_Z)  56.7 us
    all_to_all x3, waiting for transfers between devices, copies(): return lax.all_to_all(sent, axis, 0, 0, axis_index_groups=groups)  41.5 us
    all_to_all x3, blocking collectives, copies(): return lax.all_to_all(sent, axis, 0, 0, axis_index_groups=groups)  36.3 us
    ppermute x2, starting transfers between devices, neighbours(): across = lax.ppermute(vectors, 'space', outer)  21 us
    all_to_all x3, starting transfers between devices, copies(): return lax.all_to_all(sent, axis, 0, 0, axis_index_groups=groups)  20.3 us
    dot_general x4, matrix products, products(): jnp.einsum('vc,jc->vj', vectors, states, precision=lax.Precision.HIGH, pr...  5.28 us
  transfers between devices with their start and end apart: 8, of which 5 were waited for; matrix products, arithmetic and copies ran while one was open for 2% of the time, Pallas kernels for 0%

profile of v1, /device:TPU:7, one launch (start us, length us, event | category | flops | bytes accessed | tf_op | source)
XLA Modules:
  0.0 213.9 jit_solution(17693753311654365289)
XLA Ops:
  7.2 0.0 all-gather.2.cloned.1.call-start
  7.2 1.0 fusion.32
  8.2 0.7 copy.67
  8.9 0.0 all-gather.2.cloned.1.call-update
  9.0 19.1 %all_to_all.30 = f32[4,16,2048]{2,1,0:T(8,128)S(1)} all-to-all(f32[4,16,2048]{2,1,0:T(8,128)S(1)} %broadcast_in_dim.76), channel_id=1, replica_groups={{0,128,256,384},{32,160,288,416},{64,192,320,448},{96,224,352,480},{1,1..., dimensions={0} | all-to-all | bytes 1048576 | tf_op jit(solution)/shard_map/all_to_all | solution.py:17
  28.1 1.6 broadcast_in_dim.77
  29.6 0.0 copy-start.3
  29.6 0.0 copy-start.4
  29.6 4.3 %all-to-all-start.1 = ((f32[4,4,16,2048]{3,2,1,0:T(8,128)}), f32[4,4,16,2048]{3,2,1,0:T(8,128)S(1)}, u32[]{:S(2)}, u32[]{:S(2)}) async-start(f32[4,4,16,2048]{3,2,1,0:T(8,128)} %broadcast_in_dim.77), calls=%async_computation.1 | async-start | bytes 4194304 | tf_op jit(solution)/shard_map/all_to_all | solution.py:17
  33.9 0.0 copy-done.3
  34.0 0.0 copy-done.4
  34.0 35.0 %all-to-all-done.1 = f32[4,4,16,2048]{3,2,1,0:T(8,128)S(1)} async-done(((f32[4,4,16,2048]{3,2,1,0:T(8,128)}), f32[4,4,16,2048]{3,2,1,0:T(8,128)S(1)}, u32[]{:S(2)}, u32[]{:S(2)}) %all-to-all-start.1) | async-done | bytes 2097184 | tf_op jit(solution)/shard_map/all_to_all | solution.py:17
  69.0 0.9 fusion.41
  69.9 0.6 broadcast_in_dim.78
  70.6 7.2 %all-to-all-start.2 = ((f32[8,8,256]{2,1,0:T(8,128)}), f32[8,8,256]{2,1,0:T(8,128)S(1)}, u32[]{:S(2)}, u32[]{:S(2)}) async-start(f32[8,8,256]{2,1,0:T(8,128)} %broadcast_in_dim.78), calls=%async_computation.2 | async-start | bytes 131072 | tf_op jit(solution)/shard_map/all_to_all | solution.py:17
  77.8 3.3 %all-to-all-done.2 = f32[8,8,256]{2,1,0:T(8,128)S(1)} async-done(((f32[8,8,256]{2,1,0:T(8,128)}), f32[8,8,256]{2,1,0:T(8,128)S(1)}, u32[]{:S(2)}, u32[]{:S(2)}) %all-to-all-start.2) | async-done | bytes 65568 | tf_op jit(solution)/shard_map/all_to_all | solution.py:17
  81.2 18.4 %psum.28 = f32[8,256]{1,0:T(8,128)S(1)} all-reduce(f32[8,256]{1,0:T(8,128)S(1)} %reduce_sum.36), channel_id=1, replica_groups={{0,8,16,24},{1,9,17,25},{2,10,18,26},{3,11,19,27},{4,12,20,28},{5,13,21..., use_global_device_ids=true, to_apply=%region_1.0 | all-reduce | flops 2048 | bytes 16384 | tf_op jit(solution)/shard_map/psum | solution.py:27
  99.6 0.6 convolution_subtract_fusion.3
  100.2 0.0 all-gather.2.cloned.1.call-done
  100.2 2.5 %fusion.42 = f32[8,256]{1,0:T(8,128)S(1)} fusion(f32[8,2048]{1,0:T(8,128)S(1)} %convolution_subtract_fusion.3, f32[256,2048]{1,0:T(8,128)} %all-gather.2.cloned.1.call-done), kind=kOutput, calls=%fused_computation.59 | convolution fusion | flops 25165824 | bytes 2170880 | tf_op jit(solution)/shard_map/vc,jc->vj/dot_general | solution.py:31
  102.7 0.7 broadcast_in_dim.79
  103.4 0.0 copy-start.2
  103.4 8.7 %all-to-all-start.3 = ((f32[8,8,256]{2,1,0:T(8,128)}), f32[8,8,256]{2,1,0:T(8,128)S(1)}, u32[]{:S(2)}, u32[]{:S(2)}) async-start(f32[8,8,256]{2,1,0:T(8,128)} %broadcast_in_dim.79), calls=%async_computation.3 | async-start | bytes 131072 | tf_op jit(solution)/shard_map/all_to_all | solution.py:17
  112.1 3.1 %all-to-all-done.3 = f32[8,8,256]{2,1,0:T(8,128)S(1)} async-done(((f32[8,8,256]{2,1,0:T(8,128)}), f32[8,8,256]{2,1,0:T(8,128)S(1)}, u32[]{:S(2)}, u32[]{:S(2)}) %all-to-all-start.3) | async-done | bytes 65568 | tf_op jit(solution)/shard_map/all_to_all | solution.py:17
  115.2 14.6 %psum.29 = f32[8,256]{1,0:T(8,128)S(1)} all-reduce(f32[8,256]{1,0:T(8,128)S(1)} %reduce_sum.37), channel_id=1, replica_groups={{0,8,16,24},{1,9,17,25},{2,10,18,26},{3,11,19,27},{4,12,20,28},{5,13,21..., use_global_device_ids=true, to_apply=%region_3.0 | all-reduce | flops 2048 | bytes 16384 | tf_op jit(solution)/shard_map/psum | solution.py:27
  129.9 2.2 %convolution_subtract_fusion.2 = f32[8,2048]{1,0:T(8,128)S(1)} fusion(f32[8,2048]{1,0:T(8,128)S(1)} %convolution_subtract_fusion.3, f32[256,2048]{1,0:T(8,128)} %all-gather.2.cloned.1.call-done, f32[8,256]{1,0:T(8,128)S(1)} %psum.29), kind=kOutput, calls=%fused_computation.2 | convolution fusion | flops 25184256 | bytes 2236416 | tf_op jit(solution)/shard_map/vj,jc->vc/dot_general | solution.py:41
  132.1 10.5 %collective-permute-start = (f32[8,2048]{1,0:T(8,128)S(1)}, f32[8,2048]{1,0:T(8,128)S(1)}, u32[]{:S(2)}, u32[]{:S(2)}) collective-permute-start(f32[8,2048]{1,0:T(8,128)S(1)} %convolution_subtract_fusion.2), channel_id=1, source_target_pairs={{1,2},{3,4},{5,6},{7,8},{9,10},{11,12},{13,14},{15,16},{17,18},{19... | collective-permute-start | bytes 196616 | tf_op jit(solution)/shard_map/ppermute | solution.py:54
  142.5 1.9 collective-permute-start.1
  144.5 0.1 copy.36
  144.5 0.1 fusion.37
  144.7 0.1 fusion.38
  144.8 0.1 fusion.39
  144.9 0.1 fusion.40
  145.1 0.0 collective-permute-done
  145.1 0.6 collective-permute-done.1
  145.7 0.1 copy.40
  145.8 0.1 copy.41
  145.8 0.0 copy-done.2
  145.8 0.0 copy-done.5
  145.8 0.5 fusion
  146.3 0.9 fusion.43
  147.3 7.2 %all_to_all.31 = f32[8,8,256]{2,1,0:T(8,128)S(1)} all-to-all(f32[8,8,256]{2,1,0:T(8,128)S(1)} %broadcast_in_dim.85), channel_id=1, replica_groups={{0,1,2,3,4,5,6,7},{8,9,10,11,12,13,14,15},{16,17,18,19,20,21,22,23},{24..., dimensions={0} | all-to-all | bytes 131072 | tf_op jit(solution)/shard_map/all_to_all | solution.py:17
  154.5 13.9 %psum.30 = f32[8,256]{1,0:T(8,128)S(1)} all-reduce(f32[8,256]{1,0:T(8,128)S(1)} %reduce_sum.38), channel_id=1, replica_groups={{0,8,16,24},{1,9,17,25},{2,10,18,26},{3,11,19,27},{4,12,20,28},{5,13,21..., use_global_device_ids=true, to_apply=%region_5.6 | all-reduce | flops 2048 | bytes 16384 | tf_op jit(solution)/shard_map/psum | solution.py:27
  168.5 0.0 copy-start
  168.5 0.6 convolution_subtract_fusion.1
  169.1 1.0 copy-done
  170.1 0.9 fusion.44
  171.0 10.0 %all_to_all.32 = f32[8,8,256]{2,1,0:T(8,128)S(1)} all-to-all(f32[8,8,256]{2,1,0:T(8,128)S(1)} %broadcast_in_dim.86), channel_id=1, replica_groups={{0,1,2,3,4,5,6,7},{8,9,10,11,12,13,14,15},{16,17,18,19,20,21,22,23},{24..., dimensions={0} | all-to-all | bytes 131072 | tf_op jit(solution)/shard_map/all_to_all | solution.py:17
  181.1 9.7 %psum.31 = f32[8,256]{1,0:T(8,128)S(1)} all-reduce(f32[8,256]{1,0:T(8,128)S(1)} %reduce_sum.39), channel_id=1, replica_groups={{0,8,16,24},{1,9,17,25},{2,10,18,26},{3,11,19,27},{4,12,20,28},{5,13,21..., use_global_device_ids=true, to_apply=%region_7.8 | all-reduce | flops 2048 | bytes 16384 | tf_op jit(solution)/shard_map/psum | solution.py:27
  190.8 0.0 copy-done.1
  190.8 0.6 convolution_subtract_fusion
  191.4 10.6 %collective-permute-start.2 = (f32[8,2048]{1,0:T(8,128)S(1)}, f32[8,2048]{1,0:T(8,128)S(1)}, u32[]{:S(2)}, u32[]{:S(2)}) collective-permute-start(f32[8,2048]{1,0:T(8,128)S(1)} %convolution_subtract_fusion), channel_id=1, source_target_pairs={{1,2},{3,4},{5,6},{7,8},{9,10},{11,12},{13,14},{15,16},{17,18},{19... | collective-permute-start | bytes 196616 | tf_op jit(solution)/shard_map/ppermute | solution.py:54
  202.0 1.9 collective-permute-start.3
  203.9 0.1 copy.50
  204.0 0.1 fusion.33
  204.1 0.1 fusion.34
  204.2 0.1 fusion.35
  204.4 0.1 fusion.36
  204.5 0.0 collective-permute-done.2
  204.5 0.6 collective-permute-done.3
  205.1 0.1 copy.54
  205.2 0.1 copy.55
  205.3 1.1 fusion.1
  206.4 0.7 subtract_divide_fusion
  (17 shorter events, 0.3 us)
Async XLA Ops:
  7.2 93.0 %all-gather.2.cloned.1.call-start = ((), (), s32[]{:S(2)}) async-start(), calls=%async_computation.6 | async-start | bytes 2228224 | tf_op jit(solution)/shard_map/all_gather | solution.py:86
  29.6 4.3 %copy-start.3 = (f32[8,2,1024]{2,1,0:T(2,128)S(1)}, f32[8,2,1024]{2,1,0:T(2,128)}, u32[]{:S(2)}) copy-start(f32[8,2,1024]{2,1,0:T(2,128)} %param.6) | copy-start | bytes 196612
  29.6 4.3 %copy-start.4 = (f32[2,1024]{1,0:T(2,128)S(1)}, f32[2,1024]{1,0:T(2,128)}, u32[]{:S(2)}) copy-start(f32[2,1024]{1,0:T(2,128)} %param.8) | copy-start | bytes 24580
  29.6 39.4 %all-to-all-start.1 = ((f32[4,4,16,2048]{3,2,1,0:T(8,128)}), f32[4,4,16,2048]{3,2,1,0:T(8,128)S(1)}, u32[]{:S(2)}, u32[]{:S(2)}) async-start(f32[4,4,16,2048]{3,2,1,0:T(8,128)} %broadcast_in_dim.77), calls=%async_computation.1 | async-start | bytes 4194304 | tf_op jit(solution)/shard_map/all_to_all | solution.py:17
  70.6 10.6 %all-to-all-start.2 = ((f32[8,8,256]{2,1,0:T(8,128)}), f32[8,8,256]{2,1,0:T(8,128)S(1)}, u32[]{:S(2)}, u32[]{:S(2)}) async-start(f32[8,8,256]{2,1,0:T(8,128)} %broadcast_in_dim.78), calls=%async_computation.2 | async-start | bytes 131072 | tf_op jit(solution)/shard_map/all_to_all | solution.py:17
  103.4 42.5 %copy-start.2 = (f32[8,2,1024]{2,1,0:T(2,128)S(1)}, f32[8,2,1024]{2,1,0:T(2,128)}, u32[]{:S(2)}) copy-start(f32[8,2,1024]{2,1,0:T(2,128)} %param.7) | copy-start | bytes 196612
  103.4 42.5 %copy-start.5 = (f32[8]{0:T(128)S(1)}, f32[8]{0:T(128)}, u32[]{:S(2)}) copy-start(f32[8]{0:T(128)} %param.9) | copy-start | bytes 100
  103.4 11.9 %all-to-all-start.3 = ((f32[8,8,256]{2,1,0:T(8,128)}), f32[8,8,256]{2,1,0:T(8,128)S(1)}, u32[]{:S(2)}, u32[]{:S(2)}) async-start(f32[8,8,256]{2,1,0:T(8,128)} %broadcast_in_dim.79), calls=%async_computation.3 | async-start | bytes 131072 | tf_op jit(solution)/shard_map/all_to_all | solution.py:17
  132.1 13.0 %collective-permute-start = (f32[8,2048]{1,0:T(8,128)S(1)}, f32[8,2048]{1,0:T(8,128)S(1)}, u32[]{:S(2)}, u32[]{:S(2)}) collective-permute-start(f32[8,2048]{1,0:T(8,128)S(1)} %convolution_subtract_fusion.2), channel_id=1, source_target_pairs={{1,2},{3,4},{5,6},{7,8},{9,10},{11,12},{13,14},{15,16},{17,18},{19... | collective-permute-start | bytes 196616 | tf_op jit(solution)/shard_map/ppermute | solution.py:54
  142.5 3.1 %collective-permute-start.1 = (f32[8,2048]{1,0:T(8,128)S(1)}, f32[8,2048]{1,0:T(8,128)S(1)}, u32[]{:S(2)}, u32[]{:S(2)}) collective-permute-start(f32[8,2048]{1,0:T(8,128)S(1)} %convolution_subtract_fusion.2), channel_id=1, source_target_pairs={{0,1},{1,0},{2,3},{3,2},{4,5},{5,4},{6,7},{7,6},{8,9},{9,8},{10,11... | collective-permute-start | bytes 196616 | tf_op jit(solution)/shard_map/ppermute | solution.py:55
  168.5 1.6 copy-start
  170.1 20.7 %copy-start.1 = (f32[256,2048]{1,0:T(8,128)S(1)}, f32[256,2048]{1,0:T(8,128)}, u32[]{:S(2)}) copy-start(f32[256,2048]{1,0:T(8,128)} %all-gather.2.cloned.1.call-done) | copy-start | bytes 6291460
  191.4 13.1 %collective-permute-start.2 = (f32[8,2048]{1,0:T(8,128)S(1)}, f32[8,2048]{1,0:T(8,128)S(1)}, u32[]{:S(2)}, u32[]{:S(2)}) collective-permute-start(f32[8,2048]{1,0:T(8,128)S(1)} %convolution_subtract_fusion), channel_id=1, source_target_pairs={{1,2},{3,4},{5,6},{7,8},{9,10},{11,12},{13,14},{15,16},{17,18},{19... | collective-permute-start | bytes 196616 | tf_op jit(solution)/shard_map/ppermute | solution.py:54
  202.0 3.1 %collective-permute-start.3 = (f32[8,2048]{1,0:T(8,128)S(1)}, f32[8,2048]{1,0:T(8,128)S(1)}, u32[]{:S(2)}, u32[]{:S(2)}) collective-permute-start(f32[8,2048]{1,0:T(8,128)S(1)} %convolution_subtract_fusion), channel_id=1, source_target_pairs={{0,1},{1,0},{2,3},{3,2},{4,5},{5,4},{6,7},{7,6},{8,9},{9,8},{10,11... | collective-permute-start | bytes 196616 | tf_op jit(solution)/shard_map/ppermute | solution.py:55
Sparse Core Ops, SparseCore 0:
  10.1 84.0 all-gather.1

commit v2 on v1

--- a/solution.py
+++ b/solution.py
@@ -7,7 +7,7 @@
 ITERS = 2
 BAND_Z = [[z * 4 + y for z in range(4)] for y in range(4)]
 BAND_Y = [[z * 4 + y for y in range(4)] for z in range(4)]
-SPACE_PLANE = [[z * 8 + r for r in range(8)] for z in range(4)]
+SPACE_X = [[z * 8 + x * 2 + c for x in range(4)] for z in range(4) for c in range(2)]
 SPACE_Z = [[z * 8 + r for z in range(4)] for r in range(8)]
 
 
@@ -18,13 +18,26 @@
 
 
 def gathered(states):
-    columns = copies(states, "band", BAND_Z)
-    return copies(columns, "band", BAND_Y).reshape(-1, states.shape[-1])
+    return copies(copies(states, "band", BAND_Z), "band", BAND_Y)
 
 
 def space_sum(x):
-    near = jnp.sum(copies(x, "space", SPACE_PLANE), axis=0)
-    return lax.psum(near, "space", axis_index_groups=SPACE_Z)
+    half = x.shape[0] // 2
+    flip = [(i, i ^ 1) for i in range(lax.axis_size("space"))]
+    upper = lax.axis_index("space") % 2 == 1
+    lower_half, upper_half = x[:half], x[half:]
+    kept = jnp.where(upper, upper_half, lower_half)
+    kept = kept + lax.ppermute(jnp.where(upper, lower_half, upper_half), "space", flip)
+    if kept.size <= 2048:
+        kept = lax.psum(kept, "space", axis_index_groups=SPACE_X)
+        kept = lax.psum(kept, "space", axis_index_groups=SPACE_Z)
+    else:
+        kept = jnp.sum(copies(kept, "space", SPACE_X), axis=0)
+        kept = jnp.sum(copies(kept, "space", SPACE_Z), axis=0)
+    other = lax.ppermute(kept, "space", flip)
+    return jnp.concatenate(
+        [jnp.where(upper, other, kept), jnp.where(upper, kept, other)], axis=0
+    )
 
 
 def products(vectors, states):
@@ -81,22 +94,53 @@
 
 def on_device(occupied, initial, right_side, potential, energies):
     count, planes, line = initial.shape
-    weight = 1.0 / (planes * lax.axis_size("space") * line)
-    states = [occupied[0].reshape(-1, planes * line), occupied[1].reshape(-1, planes * line)]
-    later = lax.all_gather(states[1], "band", axis=0, tiled=True)
-    blocks = [gathered(states[0]), later]
+    cells = planes * line
+    weight = 1.0 / (lax.axis_size("space") * cells)
+    block = occupied.shape[1]
+    states = occupied.reshape(2 * block, cells)
+    part = block + block // 2
+    last = lax.all_gather(states[part:], "band", axis=0, tiled=True)
+    most = gathered(states[:part]).reshape(16, part, cells)
+    first = most[:, :block].reshape(-1, cells)
+    middle = most[:, block:].reshape(-1, cells)
     diagonal = 3.75 + potential[None, :, :] - energies[:, None, None]
-    vectors = initial.reshape(count, planes * line)
+    vectors = initial.reshape(count, cells)
+    overlap_middle = overlap_last = None
     for iteration in range(ITERS):
-        for block in blocks:
-            margin = space_sum(products(vectors, block)) * weight
-            vectors = vectors - combination(margin, block)
+        raw_second = jnp.concatenate(
+            [products(vectors, middle), products(vectors, last)], axis=1
+        )
+        if iteration == 0:
+            raw = products(jnp.concatenate([vectors, states[block:]], axis=0), first)
+            total = space_sum(
+                weight * jnp.concatenate([raw[:count], raw_second, raw[count:]], axis=0)
+            )
+            rows = lax.all_to_all(
+                jnp.broadcast_to(total[None, 2 * count :], (16, block, total.shape[1])),
+                "band", 0, 0,
+            )
+            overlap_last = rows[:, block // 2 :].reshape(-1, total.shape[1])
+            rows = rows[:, : block // 2].reshape(4, 4, block // 2, total.shape[1])
+            overlap_middle = jnp.swapaxes(rows, 0, 1).reshape(-1, total.shape[1])
+        else:
+            raw = products(vectors, first)
+            total = space_sum(weight * jnp.concatenate([raw, raw_second], axis=0))
+        margin = total[:count]
+        middle_count = middle.shape[0]
+        margin_middle = total[count : 2 * count, :middle_count] - products(margin, overlap_middle)
+        margin_last = total[count : 2 * count, middle_count:] - products(margin, overlap_last)
+        vectors = (
+            vectors
+            - combination(margin, first)
+            - combination(margin_middle, middle)
+            - combination(margin_last, last)
+        )
         low, high = neighbours(vectors)
         shape = (count, planes, line)
         vectors = vectors.reshape(shape)
         rest = right_side - coupling(vectors, low.reshape(shape), high.reshape(shape))
         residual = rest - diagonal * vectors
-        vectors = (rest / diagonal).reshape(count, planes * line)
+        vectors = (rest / diagonal).reshape(count, cells)
     return (vectors.reshape(shape), residual)
 
 

time: 215 us -> 267 us (1.24)
  waiting for transfers between devices: 42.7 us -> 103 us
  blocking collectives: 93 us -> 70.9 us
  starting transfers between devices: 45.2 us -> 50.4 us
  matrix products: 9.32 us -> 14.4 us
    all_gather x1, waiting for transfers between devices: 0.01 us -> 84.1 us  [on_device(): last = lax.all_gather(states[part:], 'band', axis=0, tiled=True)]
    all_to_all x3 -> x1, waiting for transfers between devices: 41.5 us -> 0.01 us  [copies(): return lax.all_to_all(sent, axis, 0, 0, axis_index_groups=groups)]
    psum x4 -> x2, blocking collectives: 56.7 us -> 17.1 us  [the longest x1 11.2 us: space_sum(): kept = lax.psum(kept, 'space', axis_index_groups=SPACE_Z)]
    ppermute x0 -> x4, starting transfers between devices: none -> 24.8 us  [the longest x2 13.4 us: space_sum(): lax.ppermute(jnp.where(upper, lower_half, upper_half), 'space', flip)]
    all_to_all x3, blocking collectives: 36.3 us -> 53.8 us  [copies(): return lax.all_to_all(sent, axis, 0, 0, axis_index_groups=groups)]
    all_to_all x3 -> x1, starting transfers between devices: 20.3 us -> 4.78 us  [copies(): return lax.all_to_all(sent, axis, 0, 0, axis_index_groups=groups)]
    ppermute x2, starting transfers between devices: 21 us -> 12.7 us  [neighbours(): across = lax.ppermute(vectors, 'space', outer)]
    all_to_all x0 -> x1, waiting for transfers between devices: none -> 8.16 us  [on_device(): lax.all_to_all(jnp.broadcast_to(total[None, 2 * count:], (16, block, tota...]
  transfers between devices with their start and end apart: 8 -> 11, of which waited for: 5 -> 8; matrix products, arithmetic and copies ran while one was open for 2% -> 2% of each run, Pallas kernels for 0% -> 0%
where the time goes in v2:
time: 267 us; the launch traced here: 266 us
  waiting for transfers between devices  103 us (39%)
  blocking collectives  70.9 us (27%)
  starting transfers between devices  50.4 us (19%)
  between operations  14.6 us (5%)
  matrix products  14.4 us (5%)
  local copies, waits for them, and re-layouts  8.6 us (3%)
  other arithmetic  4.17 us (2%)
    all_gather x1, waiting for transfers between devices, on_device(): last = lax.all_gather(states[part:], 'band', axis=0, tiled=True)  84.1 us
    all_to_all x3, blocking collectives, copies(): return lax.all_to_all(sent, axis, 0, 0, axis_index_groups=groups)  53.8 us
    ppermute x2, starting transfers between devices, space_sum(): lax.ppermute(jnp.where(upper, lower_half, upper_half), 'space', flip)  13.4 us
    ppermute x2, starting transfers between devices, neighbours(): across = lax.ppermute(vectors, 'space', outer)  12.7 us
    ppermute x2, starting transfers between devices, space_sum(): other = lax.ppermute(kept, 'space', flip)  11.4 us
    psum x1, blocking collectives, space_sum(): kept = lax.psum(kept, 'space', axis_index_groups=SPACE_Z)  11.2 us
    dot_general x10, matrix products, products(): jnp.einsum('vc,jc->vj', vectors, states, precision=lax.Precision.HIGH, pr...  9.07 us
    all_to_all x1, waiting for transfers between devices, on_device(): lax.all_to_all(jnp.broadcast_to(total[None, 2 * count:], (16, block, tota...  8.16 us
  transfers between devices with their start and end apart: 11, of which 8 were waited for; matrix products, arithmetic and copies ran while one was open for 2% of the time, Pallas kernels for 0%

profile of v2, /device:TPU:7, one launch (start us, length us, event | category | flops | bytes accessed | tf_op | source)
XLA Modules:
  0.0 265.8 jit_solution(11841174354635357922)
XLA Ops:
  7.2 1.0 copy.127
  8.2 0.1 broadcast_in_dim.68
  8.3 24.7 %all_to_all.25 = f32[4,24,2048]{2,1,0:T(8,128)S(1)} all-to-all(f32[4,24,2048]{2,1,0:T(8,128)S(1)} %broadcast_in_dim.68), channel_id=1, replica_groups={{0,128,256,384},{32,160,288,416},{64,192,320,448},{96,224,352,480},{1,1..., dimensions={0} | all-to-all | bytes 1572864 | tf_op jit(solution)/shard_map/all_to_all | solution.py:17
  33.0 2.1 broadcast_in_dim.69
  35.0 4.8 %all-to-all-start.1 = ((f32[4,4,24,2048]{3,2,1,0:T(8,128)}), f32[4,4,24,2048]{3,2,1,0:T(8,128)}, u32[]{:S(2)}, u32[]{:S(2)}) async-start(f32[4,4,24,2048]{3,2,1,0:T(8,128)} %broadcast_in_dim.69), calls=%async_computation.1 | async-start | bytes 6291456 | tf_op jit(solution)/shard_map/all_to_all | solution.py:17
  39.9 0.6 slice.164
  40.7 84.1 %all-gather.2.cloned.1.call-done = f32[128,2048]{1,0:T(8,128)} async-done(((f32[8,2048]{1,0:T(8,128)}), f32[128,2048]{1,0:T(8,128)}) %all-gather.2.cloned.1.call-update) | async-done | bytes 1048592 | tf_op jit(solution)/shard_map/all_gather | solution.py:102
  124.8 1.7 fusion.49
  126.5 1.8 slice.161
  128.4 0.9 fusion.8
  129.4 1.8 fusion.7
  131.2 11.5 %collective-permute-start = (f32[16,256]{1,0:T(8,128)S(1)}, f32[16,256]{1,0:T(8,128)S(1)}, u32[]{:S(2)}, u32[]{:S(2)}) collective-permute-start(f32[16,256]{1,0:T(8,128)S(1)} %slice_select_fusion), channel_id=1, source_target_pairs={{0,1},{1,0},{2,3},{3,2},{4,5},{5,4},{6,7},{7,6},{8,9},{9,8},{10,11... | collective-permute-start | bytes 49160 | tf_op jit(solution)/shard_map/ppermute | solution.py:30
  142.7 0.8 collective-permute-done
  143.5 6.7 %all_to_all.26 = f32[4,16,256]{2,1,0:T(8,128)S(1)} all-to-all(f32[4,16,256]{2,1,0:T(8,128)S(1)} %broadcast_in_dim.70), channel_id=1, replica_groups={{0,2,4,6},{1,3,5,7},{8,10,12,14},{9,11,13,15},{16,18,20,22},{17,19,21,2..., dimensions={0} | all-to-all | bytes 131072 | tf_op jit(solution)/shard_map/all_to_all | solution.py:17
  150.3 22.5 %all_to_all.27 = f32[4,16,256]{2,1,0:T(8,128)S(1)} all-to-all(f32[4,16,256]{2,1,0:T(8,128)S(1)} %broadcast_in_dim.71), channel_id=1, replica_groups={{0,8,16,24},{1,9,17,25},{2,10,18,26},{3,11,19,27},{4,12,20,28},{5,13,21..., dimensions={0} | all-to-all | bytes 131072 | tf_op jit(solution)/shard_map/all_to_all | solution.py:17
  172.7 5.1 %collective-permute-start.1 = (f32[16,256]{1,0:T(8,128)S(1)}, f32[16,256]{1,0:T(8,128)S(1)}, u32[]{:S(2)}, u32[]{:S(2)}) collective-permute-start(f32[16,256]{1,0:T(8,128)S(1)} %reduce_sum.19), channel_id=1, source_target_pairs={{0,1},{1,0},{2,3},{3,2},{4,5},{5,4},{6,7},{7,6},{8,9},{9,8},{10,11... | collective-permute-start | bytes 49160 | tf_op jit(solution)/shard_map/ppermute | solution.py:37
  177.8 0.8 collective-permute-done.1
  178.7 0.7 broadcast_in_dim.72
  179.4 4.3 %all-to-all-start.4 = ((f32[16,16,256]{2,1,0:T(8,128)}), f32[16,16,256]{2,1,0:T(8,128)S(1)}, u32[]{:S(2)}, u32[]{:S(2)}) async-start(f32[16,16,256]{2,1,0:T(8,128)} %broadcast_in_dim.72), calls=%async_computation.4 | async-start | bytes 524288 | tf_op jit(solution)/shard_map/all_to_all | solution.py:118
  183.7 0.6 fusion.34
  184.3 0.6 fusion.36
  184.9 0.6 broadcast_add_fusion
  185.5 8.2 %all-to-all-done.4 = f32[16,16,256]{2,1,0:T(8,128)S(1)} async-done(((f32[16,16,256]{2,1,0:T(8,128)}), f32[16,16,256]{2,1,0:T(8,128)S(1)}, u32[]{:S(2)}, u32[]{:S(2)}) %all-to-all-start.4) | async-done | bytes 262176 | tf_op jit(solution)/shard_map/all_to_all | solution.py:118
  193.7 0.6 copy-done.1
  194.3 0.1 fusion.27
  194.4 1.6 fusion.6
  196.1 0.1 fusion.13
  196.2 0.4 fusion.31
  196.7 0.6 fusion.3
  197.3 5.2 %collective-permute-start.2 = (f32[8,2048]{1,0:T(8,128)S(1)}, f32[8,2048]{1,0:T(8,128)S(1)}, u32[]{:S(2)}, u32[]{:S(2)}) collective-permute-start(f32[8,2048]{1,0:T(8,128)S(1)} %fusion.3), channel_id=1, source_target_pairs={{1,2},{3,4},{5,6},{7,8},{9,10},{11,12},{13,14},{15,16},{17,18},{19... | collective-permute-start | bytes 196616 | tf_op jit(solution)/shard_map/ppermute | solution.py:67
  202.5 1.9 collective-permute-start.3
  204.4 0.1 copy.96
  204.5 0.1 fusion.45
  204.6 0.1 fusion.46
  204.7 0.1 fusion.47
  204.9 0.1 fusion.48
  205.0 3.9 %collective-permute-done.2 = f32[8,2048]{1,0:T(8,128)S(1)} collective-permute-done((f32[8,2048]{1,0:T(8,128)S(1)}, f32[8,2048]{1,0:T(8,128)S(1)}, u32[]{:S(2)}, u32[]{:S(2)}) %collective-permute-start.2) | collective-permute-done | bytes 65568 | tf_op jit(solution)/shard_map/ppermute | solution.py:67
  209.0 0.1 copy.101
  209.1 0.4 fusion.14
  209.6 0.9 fusion.50
  210.5 1.7 fusion.5
  212.2 0.5 fusion.51
  212.8 1.9 collective-permute-start.4
  214.7 1.1 collective-permute-done.4
  215.9 5.8 %psum.14 = f32[8,256]{1,0:T(8,128)S(1)} all-reduce(f32[8,256]{1,0:T(8,128)S(1)} %select_add_fusion.1), channel_id=1, replica_groups={{0,2,4,6},{1,3,5,7},{8,10,12,14},{9,11,13,15},{16,18,20,22},{17,19,21,2..., use_global_device_ids=true, to_apply=%region_2.3 | all-reduce | flops 2048 | bytes 16384 | tf_op jit(solution)/shard_map/psum | solution.py:32
  221.7 11.2 %psum.15 = f32[8,256]{1,0:T(8,128)S(1)} all-reduce(f32[8,256]{1,0:T(8,128)S(1)} %psum.14), channel_id=1, replica_groups={{0,8,16,24},{1,9,17,25},{2,10,18,26},{3,11,19,27},{4,12,20,28},{5,13,21..., use_global_device_ids=true, to_apply=%region_3.4 | all-reduce | flops 2048 | bytes 16384 | tf_op jit(solution)/shard_map/psum | solution.py:33
  232.9 6.3 %collective-permute-start.5 = (f32[8,256]{1,0:T(8,128)S(1)}, f32[8,256]{1,0:T(8,128)S(1)}, u32[]{:S(2)}, u32[]{:S(2)}) collective-permute-start(f32[8,256]{1,0:T(8,128)S(1)} %psum.15), channel_id=1, source_target_pairs={{0,1},{1,0},{2,3},{3,2},{4,5},{5,4},{6,7},{7,6},{8,9},{9,8},{10,11... | collective-permute-start | bytes 24584 | tf_op jit(solution)/shard_map/ppermute | solution.py:37
  239.3 0.8 collective-permute-done.5
  240.1 1.0 fusion.52
  241.1 1.6 fusion.4
  242.7 0.1 fusion.12
  242.9 0.4 fusion.30
  243.3 0.6 fusion.1
  243.9 7.5 %collective-permute-start.6 = (f32[8,2048]{1,0:T(8,128)S(1)}, f32[8,2048]{1,0:T(8,128)S(1)}, u32[]{:S(2)}, u32[]{:S(2)}) collective-permute-start(f32[8,2048]{1,0:T(8,128)S(1)} %fusion.1), channel_id=1, source_target_pairs={{1,2},{3,4},{5,6},{7,8},{9,10},{11,12},{13,14},{15,16},{17,18},{19... | collective-permute-start | bytes 196616 | tf_op jit(solution)/shard_map/ppermute | solution.py:67
  251.5 1.9 collective-permute-start.7
  253.4 0.1 copy.110
  253.5 0.1 fusion.42
  253.6 0.1 fusion.43
  253.7 0.1 fusion.44
  253.9 0.1 fusion.41
  254.0 2.9 %collective-permute-done.6 = f32[8,2048]{1,0:T(8,128)S(1)} collective-permute-done((f32[8,2048]{1,0:T(8,128)S(1)}, f32[8,2048]{1,0:T(8,128)S(1)}, u32[]{:S(2)}, u32[]{:S(2)}) %collective-permute-start.6) | collective-permute-done | bytes 65568 | tf_op jit(solution)/shard_map/ppermute | solution.py:67
  257.0 0.1 copy.114
  257.1 1.1 fusion.15
  258.2 0.7 subtract_divide_fusion
  (65 shorter events, 0.5 us)
Async XLA Ops:
  35.0 5.5 %copy-start.2 = (f32[2,16,2,1024]{3,2,1,0:T(2,128)S(1)}, f32[2,16,2,1024]{3,2,1,0:T(2,128)}, u32[]{:S(2)}) copy-start(f32[2,16,2,1024]{3,2,1,0:T(2,128)} %param.5) | copy-start | bytes 786436
  35.0 5.6 %copy-start.6 = (f32[8,2,1024]{2,1,0:T(2,128)S(1)}, f32[8,2,1024]{2,1,0:T(2,128)}, u32[]{:S(2)}) copy-start(f32[8,2,1024]{2,1,0:T(2,128)} %param.6) | copy-start | bytes 196612
  35.0 91.5 %all-to-all-start.1 = ((f32[4,4,24,2048]{3,2,1,0:T(8,128)}), f32[4,4,24,2048]{3,2,1,0:T(8,128)}, u32[]{:S(2)}, u32[]{:S(2)}) async-start(f32[4,4,24,2048]{3,2,1,0:T(8,128)} %broadcast_in_dim.69), calls=%async_computation.1 | async-start | bytes 6291456 | tf_op jit(solution)/shard_map/all_to_all | solution.py:17
  39.8 85.0 %all-gather.2.cloned.1.call-start = ((), (), s32[]{:S(2)}) async-start(), calls=%async_computation.5 | async-start | bytes 1114112 | tf_op jit(solution)/shard_map/all_gather | solution.py:102
  128.4 56.5 %copy-start.15 = (f32[2,1024]{1,0:T(2,128)S(1)}, f32[2,1024]{1,0:T(2,128)}, u32[]{:S(2)}) copy-start(f32[2,1024]{1,0:T(2,128)} %param.8) | copy-start | bytes 24580
  129.4 66.8 %copy-start = (f32[128,2048]{1,0:T(8,128)S(1)}, f32[128,2048]{1,0:T(8,128)}, u32[]{:S(2)}) copy-start(f32[128,2048]{1,0:T(8,128)} %all-gather.2.cloned.1.call-done) | copy-start | bytes 3145732
  131.2 12.3 %collective-permute-start = (f32[16,256]{1,0:T(8,128)S(1)}, f32[16,256]{1,0:T(8,128)S(1)}, u32[]{:S(2)}, u32[]{:S(2)}) collective-permute-start(f32[16,256]{1,0:T(8,128)S(1)} %slice_select_fusion), channel_id=1, source_target_pairs={{0,1},{1,0},{2,3},{3,2},{4,5},{5,4},{6,7},{7,6},{8,9},{9,8},{10,11... | collective-permute-start | bytes 49160 | tf_op jit(solution)/shard_map/ppermute | solution.py:30
  172.7 5.9 %collective-permute-start.1 = (f32[16,256]{1,0:T(8,128)S(1)}, f32[16,256]{1,0:T(8,128)S(1)}, u32[]{:S(2)}, u32[]{:S(2)}) collective-permute-start(f32[16,256]{1,0:T(8,128)S(1)} %reduce_sum.19), channel_id=1, source_target_pairs={{0,1},{1,0},{2,3},{3,2},{4,5},{5,4},{6,7},{7,6},{8,9},{9,8},{10,11... | collective-permute-start | bytes 49160 | tf_op jit(solution)/shard_map/ppermute | solution.py:37
  179.4 14.2 %all-to-all-start.4 = ((f32[16,16,256]{2,1,0:T(8,128)}), f32[16,16,256]{2,1,0:T(8,128)S(1)}, u32[]{:S(2)}, u32[]{:S(2)}) async-start(f32[16,16,256]{2,1,0:T(8,128)} %broadcast_in_dim.72), calls=%async_computation.4 | async-start | bytes 524288 | tf_op jit(solution)/shard_map/all_to_all | solution.py:118
  193.6 0.7 copy-start.1
  196.6 12.4 %copy-start.3 = (f32[8,2,1024]{2,1,0:T(2,128)S(1)}, f32[8,2,1024]{2,1,0:T(2,128)}, u32[]{:S(2)}) copy-start(f32[8,2,1024]{2,1,0:T(2,128)} %param.7) | copy-start | bytes 196612
  196.6 12.4 %copy-start.4 = (f32[2,1024]{1,0:T(2,128)S(1)}, f32[2,1024]{1,0:T(2,128)}, u32[]{:S(2)}) copy-start(f32[2,1024]{1,0:T(2,128)} %broadcast_add_fusion) | copy-start | bytes 24580
  196.6 12.4 %copy-start.7 = (pred[1024]{0:T(1024)(128)(4,1)S(1)}, pred[1024]{0:T(1024)(128)(4,1)}, u32[]{:S(2)}) copy-start(pred[1024]{0:T(1024)(128)(4,1)} %get-tuple-element.28) | copy-start | bytes 3076
  196.6 12.4 %copy-start.9 = (pred[1024]{0:T(1024)(128)(4,1)S(1)}, pred[1024]{0:T(1024)(128)(4,1)}, u32[]{:S(2)}) copy-start(pred[1024]{0:T(1024)(128)(4,1)} %get-tuple-element.29) | copy-start | bytes 3076
  196.6 12.4 %copy-start.11 = (pred[1024]{0:T(1024)(128)(4,1)S(1)}, pred[1024]{0:T(1024)(128)(4,1)}, u32[]{:S(2)}) copy-start(pred[1024]{0:T(1024)(128)(4,1)} %get-tuple-element.30) | copy-start | bytes 3076
  196.6 12.4 %copy-start.13 = (pred[1024]{0:T(1024)(128)(4,1)S(1)}, pred[1024]{0:T(1024)(128)(4,1)}, u32[]{:S(2)}) copy-start(pred[1024]{0:T(1024)(128)(4,1)} %get-tuple-element.31) | copy-start | bytes 3076
  196.7 12.4 %copy-start.16 = (f32[8]{0:T(128)S(1)}, f32[8]{0:T(128)}, u32[]{:S(2)}) copy-start(f32[8]{0:T(128)} %param.9) | copy-start | bytes 100
  197.3 11.6 %collective-permute-start.2 = (f32[8,2048]{1,0:T(8,128)S(1)}, f32[8,2048]{1,0:T(8,128)S(1)}, u32[]{:S(2)}, u32[]{:S(2)}) collective-permute-start(f32[8,2048]{1,0:T(8,128)S(1)} %fusion.3), channel_id=1, source_target_pairs={{1,2},{3,4},{5,6},{7,8},{9,10},{11,12},{13,14},{15,16},{17,18},{19... | collective-permute-start | bytes 196616 | tf_op jit(solution)/shard_map/ppermute | solution.py:67
  202.5 6.4 %collective-permute-start.3 = (f32[8,2048]{1,0:T(8,128)S(1)}, f32[8,2048]{1,0:T(8,128)S(1)}, u32[]{:S(2)}, u32[]{:S(2)}) collective-permute-start(f32[8,2048]{1,0:T(8,128)S(1)} %fusion.3), channel_id=1, source_target_pairs={{0,1},{1,0},{2,3},{3,2},{4,5},{5,4},{6,7},{7,6},{8,9},{9,8},{10,11... | collective-permute-start | bytes 196616 | tf_op jit(solution)/shard_map/ppermute | solution.py:68
  212.8 3.1 %collective-permute-start.4 = (f32[8,256]{1,0:T(8,128)S(1)}, f32[8,256]{1,0:T(8,128)S(1)}, u32[]{:S(2)}, u32[]{:S(2)}) collective-permute-start(f32[8,256]{1,0:T(8,128)S(1)} %slice_select_fusion.1), channel_id=1, source_target_pairs={{0,1},{1,0},{2,3},{3,2},{4,5},{5,4},{6,7},{7,6},{8,9},{9,8},{10,11... | collective-permute-start | bytes 24584 | tf_op jit(solution)/shard_map/ppermute | solution.py:30
  232.9 7.1 %collective-permute-start.5 = (f32[8,256]{1,0:T(8,128)S(1)}, f32[8,256]{1,0:T(8,128)S(1)}, u32[]{:S(2)}, u32[]{:S(2)}) collective-permute-start(f32[8,256]{1,0:T(8,128)S(1)} %psum.15), channel_id=1, source_target_pairs={{0,1},{1,0},{2,3},{3,2},{4,5},{5,4},{6,7},{7,6},{8,9},{9,8},{10,11... | collective-permute-start | bytes 24584 | tf_op jit(solution)/shard_map/ppermute | solution.py:37
  243.3 13.8 %copy-start.5 = (f32[2,1024]{1,0:T(2,128)S(1)}, f32[2,1024]{1,0:T(2,128)}, u32[]{:S(2)}) copy-start(f32[2,1024]{1,0:T(2,128)} %broadcast_add_fusion) | copy-start | bytes 24580
  243.3 13.8 %copy-start.8 = (pred[1024]{0:T(1024)(128)(4,1)S(1)}, pred[1024]{0:T(1024)(128)(4,1)}, u32[]{:S(2)}) copy-start(pred[1024]{0:T(1024)(128)(4,1)} %get-tuple-element.28) | copy-start | bytes 3076
  243.3 13.8 %copy-start.10 = (pred[1024]{0:T(1024)(128)(4,1)S(1)}, pred[1024]{0:T(1024)(128)(4,1)}, u32[]{:S(2)}) copy-start(pred[1024]{0:T(1024)(128)(4,1)} %get-tuple-element.29) | copy-start | bytes 3076
  243.3 13.8 %copy-start.12 = (pred[1024]{0:T(1024)(128)(4,1)S(1)}, pred[1024]{0:T(1024)(128)(4,1)}, u32[]{:S(2)}) copy-start(pred[1024]{0:T(1024)(128)(4,1)} %get-tuple-element.30) | copy-start | bytes 3076
  243.3 13.8 %copy-start.14 = (pred[1024]{0:T(1024)(128)(4,1)S(1)}, pred[1024]{0:T(1024)(128)(4,1)}, u32[]{:S(2)}) copy-start(pred[1024]{0:T(1024)(128)(4,1)} %get-tuple-element.31) | copy-start | bytes 3076
  243.3 13.8 %copy-start.17 = (f32[8]{0:T(128)S(1)}, f32[8]{0:T(128)}, u32[]{:S(2)}) copy-start(f32[8]{0:T(128)} %param.9) | copy-start | bytes 100
  243.9 13.0 %collective-permute-start.6 = (f32[8,2048]{1,0:T(8,128)S(1)}, f32[8,2048]{1,0:T(8,128)S(1)}, u32[]{:S(2)}, u32[]{:S(2)}) collective-permute-start(f32[8,2048]{1,0:T(8,128)S(1)} %fusion.1), channel_id=1, source_target_pairs={{1,2},{3,4},{5,6},{7,8},{9,10},{11,12},{13,14},{15,16},{17,18},{19... | collective-permute-start | bytes 196616 | tf_op jit(solution)/shard_map/ppermute | solution.py:67
  251.5 5.5 %collective-permute-start.7 = (f32[8,2048]{1,0:T(8,128)S(1)}, f32[8,2048]{1,0:T(8,128)S(1)}, u32[]{:S(2)}, u32[]{:S(2)}) collective-permute-start(f32[8,2048]{1,0:T(8,128)S(1)} %fusion.1), channel_id=1, source_target_pairs={{0,1},{1,0},{2,3},{3,2},{4,5},{5,4},{6,7},{7,6},{8,9},{9,8},{10,11... | collective-permute-start | bytes 196616 | tf_op jit(solution)/shard_map/ppermute | solution.py:68
Sparse Core Ops, SparseCore 0:
  43.3 81.4 all-gather.1

commit v3 on v1

--- a/solution.py
+++ b/solution.py
@@ -15,11 +15,6 @@
     count = len(groups[0])
     sent = jnp.broadcast_to(x[None], (count,) + x.shape)
     return lax.all_to_all(sent, axis, 0, 0, axis_index_groups=groups)
-
-
-def gathered(states):
-    columns = copies(states, "band", BAND_Z)
-    return copies(columns, "band", BAND_Y).reshape(-1, states.shape[-1])
 
 
 def space_sum(x):
@@ -79,24 +74,46 @@
     return second / 24.0 - 2.0 / 3.0 * nearest
 
 
+def project_shared(states, vectors, weight):
+    count, cells = vectors.shape
+    run = copies(vectors, "band", BAND_Z).reshape(-1, cells)
+    half = run.shape[0] // 2
+    product = products(run, states)
+    margin = space_sum(jnp.concatenate([product[:half], product[half:]], axis=1)) * weight
+    width = states.shape[0]
+    margin = jnp.concatenate([margin[:, :width], margin[:, width:]], axis=0)
+    partial = combination(margin, states).reshape(-1, count, cells)
+    partial = lax.all_to_all(partial, "band", 0, 0, axis_index_groups=BAND_Z)
+    return vectors - jnp.sum(partial, axis=0)
+
+
+def project_whole(states, vectors, weight):
+    margin = space_sum(products(vectors, states)) * weight
+    return vectors - combination(margin, states)
+
+
 def on_device(occupied, initial, right_side, potential, energies):
     count, planes, line = initial.shape
-    weight = 1.0 / (planes * lax.axis_size("space") * line)
-    states = [occupied[0].reshape(-1, planes * line), occupied[1].reshape(-1, planes * line)]
-    later = lax.all_gather(states[1], "band", axis=0, tiled=True)
-    blocks = [gathered(states[0]), later]
+    cells = planes * line
+    weight = 1.0 / (lax.axis_size("space") * cells)
+    blocks, own = occupied.shape[:2]
+    states = occupied.reshape(blocks, own, cells)
+    whole = lax.all_gather(states, "band", axis=1, tiled=True)
+    ring = copies(states, "band", BAND_Y)
     diagonal = 3.75 + potential[None, :, :] - energies[:, None, None]
-    vectors = initial.reshape(count, planes * line)
+    vectors = initial.reshape(count, cells)
     for iteration in range(ITERS):
-        for block in blocks:
-            margin = space_sum(products(vectors, block)) * weight
-            vectors = vectors - combination(margin, block)
+        for block in range(blocks):
+            if iteration == 0:
+                vectors = project_shared(ring[:, block].reshape(-1, cells), vectors, weight)
+            else:
+                vectors = project_whole(whole[block], vectors, weight)
         low, high = neighbours(vectors)
         shape = (count, planes, line)
         vectors = vectors.reshape(shape)
         rest = right_side - coupling(vectors, low.reshape(shape), high.reshape(shape))
         residual = rest - diagonal * vectors
-        vectors = (rest / diagonal).reshape(count, planes * line)
+        vectors = (rest / diagonal).reshape(count, cells)
     return (vectors.reshape(shape), residual)
 
 

time: 215 us -> 232 us (1.079)
  blocking collectives: 93 us -> 127 us
  waiting for transfers between devices: 42.7 us -> 27 us
  starting transfers between devices: 45.2 us -> 41.8 us
    all_to_all x3 -> x2, waiting for transfers between devices: 41.5 us -> 19 us  [copies(): return lax.all_to_all(sent, axis, 0, 0, axis_index_groups=groups)]
    all_to_all x3 -> x5, blocking collectives: 36.3 us -> 58 us  [copies(): return lax.all_to_all(sent, axis, 0, 0, axis_index_groups=groups)]
    all_to_all x0 -> x1, blocking collectives: none -> 14.8 us  [project_shared(): partial = lax.all_to_all(partial, 'band', 0, 0, axis_index_groups=BAND_Z)]
    all_to_all x3 -> x2, starting transfers between devices: 20.3 us -> 9.8 us  [copies(): return lax.all_to_all(sent, axis, 0, 0, axis_index_groups=groups)]
    all_to_all x0 -> x1, starting transfers between devices: none -> 6.04 us  [project_shared(): partial = lax.all_to_all(partial, 'band', 0, 0, axis_index_groups=BAND_Z)]
    all_to_all x0 -> x1, waiting for transfers between devices: none -> 5.59 us  [project_shared(): partial = lax.all_to_all(partial, 'band', 0, 0, axis_index_groups=BAND_Z)]
where the time goes in v3:
time: 232 us; the launch traced here: 229 us
  blocking collectives  127 us (55%)
  starting transfers between devices  41.8 us (18%)
  waiting for transfers between devices  27 us (12%)
  between operations  14.4 us (6%)
  matrix products  11.4 us (5%)
  local copies, waits for them, and re-layouts  4.73 us (2%)
  other arithmetic  2.69 us (1%)
    all_to_all x5, blocking collectives, copies(): return lax.all_to_all(sent, axis, 0, 0, axis_index_groups=groups)  58 us
    psum x4, blocking collectives, space_sum(): return lax.psum(near, 'space', axis_index_groups=SPACE_Z)  54.5 us
    ppermute x2, starting transfers between devices, neighbours(): across = lax.ppermute(vectors, 'space', outer)  22.1 us
    all_to_all x2, waiting for transfers between devices, copies(): return lax.all_to_all(sent, axis, 0, 0, axis_index_groups=groups)  19 us
    all_to_all x1, blocking collectives, project_shared(): partial = lax.all_to_all(partial, 'band', 0, 0, axis_index_groups=BAND_Z)  14.8 us
    all_to_all x2, starting transfers between devices, copies(): return lax.all_to_all(sent, axis, 0, 0, axis_index_groups=groups)  9.8 us
    all_to_all x1, starting transfers between devices, project_shared(): partial = lax.all_to_all(partial, 'band', 0, 0, axis_index_groups=BAND_Z)  6.04 us
    dot_general x4, matrix products, products(): jnp.einsum('vc,jc->vj', vectors, states, precision=lax.Precision.HIGH, pr...  5.69 us
  transfers between devices with their start and end apart: 8, of which 5 were waited for; matrix products, arithmetic and copies ran while one was open for 2% of the time, Pallas kernels for 0%

profile of v3, /device:TPU:7, one launch (start us, length us, event | category | flops | bytes accessed | tf_op | source)
XLA Modules:
  0.0 229.3 jit_solution(10375746011968338045)
XLA Ops:
  7.2 0.0 copy-start.2
  7.2 1.2 broadcast_in_dim.84
  8.4 1.1 broadcast_in_dim.85
  9.5 4.2 %all-to-all-start.1 = ((f32[4,2,16,2048]{3,2,1,0:T(8,128)}), f32[4,2,16,2048]{3,2,1,0:T(8,128)S(1)}, u32[]{:S(2)}, u32[]{:S(2)}) async-start(f32[4,2,16,2048]{3,2,1,0:T(8,128)} %broadcast_in_dim.85), calls=%async_computation.1 | async-start | bytes 2097152 | tf_op jit(solution)/shard_map/all_to_all | solution.py:17
  13.7 0.0 copy-done
  13.7 0.7 all-gather.2.cloned.1.call-update
  14.4 0.0 copy-done.2
  14.4 13.4 %all-to-all-done.1 = f32[4,2,16,2048]{3,2,1,0:T(8,128)S(1)} async-done(((f32[4,2,16,2048]{3,2,1,0:T(8,128)}), f32[4,2,16,2048]{3,2,1,0:T(8,128)S(1)}, u32[]{:S(2)}, u32[]{:S(2)}) %all-to-all-start.1) | async-done | bytes 1048608 | tf_op jit(solution)/shard_map/all_to_all | solution.py:17
  27.8 0.7 broadcast_in_dim.83
  28.6 5.6 %all-to-all-start = ((f32[4,8,2048]{2,1,0:T(8,128)}), f32[4,8,2048]{2,1,0:T(8,128)S(1)}, u32[]{:S(2)}, u32[]{:S(2)}) async-start(f32[4,8,2048]{2,1,0:T(8,128)} %broadcast_in_dim.83), calls=%async_computation | async-start | bytes 524288 | tf_op jit(solution)/shard_map/all_to_all | solution.py:17
  34.2 0.1 fusion.40
  34.3 5.6 %all-to-all-done = f32[4,8,2048]{2,1,0:T(8,128)S(1)} async-done(((f32[4,8,2048]{2,1,0:T(8,128)}), f32[4,8,2048]{2,1,0:T(8,128)S(1)}, u32[]{:S(2)}, u32[]{:S(2)}) %all-to-all-start) | async-done | bytes 262176 | tf_op jit(solution)/shard_map/all_to_all | solution.py:17
  39.8 0.3 fusion.4
  40.2 0.0 copy-start.1
  40.2 0.0 copy-start.4
  40.2 0.1 pad_maximum_fusion.4
  40.3 14.1 %all_to_all.45 = f32[8,16,128]{2,1,0:T(8,128)S(1)} all-to-all(f32[8,16,128]{2,1,0:T(8,128)S(1)} %broadcast_in_dim.86), channel_id=1, replica_groups={{0,1,2,3,4,5,6,7},{8,9,10,11,12,13,14,15},{16,17,18,19,20,21,22,23},{24..., dimensions={0} | all-to-all | bytes 131072 | tf_op jit(solution)/shard_map/all_to_all | solution.py:17
  54.4 18.4 %psum.28 = f32[16,128]{1,0:T(8,128)S(1)} all-reduce(f32[16,128]{1,0:T(8,128)S(1)} %reduce_sum.58), channel_id=1, replica_groups={{0,8,16,24},{1,9,17,25},{2,10,18,26},{3,11,19,27},{4,12,20,28},{5,13,21..., use_global_device_ids=true, to_apply=%region_1.0 | all-reduce | flops 2048 | bytes 16384 | tf_op jit(solution)/shard_map/psum | solution.py:22
  72.8 0.1 fusion.52
  72.9 0.3 fusion.18
  73.1 14.8 %all_to_all.46 = f32[4,8,2048]{2,1,0:T(8,128)S(1)} all-to-all(f32[4,8,2048]{2,1,0:T(8,128)S(1)} %fusion.18), channel_id=1, replica_groups={{0,128,256,384},{32,160,288,416},{64,192,320,448},{96,224,352,480},{1,1..., dimensions={0} | all-to-all | bytes 524288 | tf_op jit(solution)/shard_map/all_to_all | solution.py:86
  88.0 16.4 %all_to_all.47 = f32[4,8,2048]{2,1,0:T(8,128)S(1)} all-to-all(f32[4,8,2048]{2,1,0:T(8,128)S(1)} %broadcast_in_dim.87), channel_id=1, replica_groups={{0,128,256,384},{32,160,288,416},{64,192,320,448},{96,224,352,480},{1,1..., dimensions={0} | all-to-all | bytes 524288 | tf_op jit(solution)/shard_map/all_to_all | solution.py:17
  104.4 0.3 fusion.2
  104.7 0.1 pad_maximum_fusion.5
  104.8 10.4 %all_to_all.48 = f32[8,16,128]{2,1,0:T(8,128)S(1)} all-to-all(f32[8,16,128]{2,1,0:T(8,128)S(1)} %broadcast_in_dim.88), channel_id=1, replica_groups={{0,1,2,3,4,5,6,7},{8,9,10,11,12,13,14,15},{16,17,18,19,20,21,22,23},{24..., dimensions={0} | all-to-all | bytes 131072 | tf_op jit(solution)/shard_map/all_to_all | solution.py:17
  115.2 12.0 %psum.29 = f32[16,128]{1,0:T(8,128)S(1)} all-reduce(f32[16,128]{1,0:T(8,128)S(1)} %reduce_sum.61), channel_id=1, replica_groups={{0,8,16,24},{1,9,17,25},{2,10,18,26},{3,11,19,27},{4,12,20,28},{5,13,21..., use_global_device_ids=true, to_apply=%region_4.0 | all-reduce | flops 2048 | bytes 16384 | tf_op jit(solution)/shard_map/psum | solution.py:22
  127.2 0.1 fusion.51
  127.3 1.0 fusion.21
  128.3 6.0 %all-to-all-start.6 = ((f32[4,8,2048]{2,1,0:T(8,128)}), f32[4,8,2048]{2,1,0:T(8,128)S(1)}, u32[]{:S(2)}, u32[]{:S(2)}) async-start(f32[4,8,2048]{2,1,0:T(8,128)} %fusion.21), calls=%async_computation.6 | async-start | bytes 524288 | tf_op jit(solution)/shard_map/all_to_all | solution.py:86
  134.3 5.6 %all-to-all-done.6 = f32[4,8,2048]{2,1,0:T(8,128)S(1)} async-done(((f32[4,8,2048]{2,1,0:T(8,128)}), f32[4,8,2048]{2,1,0:T(8,128)S(1)}, u32[]{:S(2)}, u32[]{:S(2)}) %all-to-all-start.6) | async-done | bytes 262176 | tf_op jit(solution)/shard_map/all_to_all | solution.py:86
  140.0 11.2 %collective-permute-start = (f32[8,2048]{1,0:T(8,128)S(1)}, f32[8,2048]{1,0:T(8,128)S(1)}, u32[]{:S(2)}, u32[]{:S(2)}) collective-permute-start(f32[8,2048]{1,0:T(8,128)S(1)} %sub.53), channel_id=1, source_target_pairs={{1,2},{3,4},{5,6},{7,8},{9,10},{11,12},{13,14},{15,16},{17,18},{19... | collective-permute-start | bytes 196616 | tf_op jit(solution)/shard_map/ppermute | solution.py:49
  151.2 1.9 collective-permute-start.1
  153.1 0.1 copy_subtract_fusion
  153.2 0.1 fusion.45
  153.3 0.1 fusion.46
  153.5 0.1 fusion.47
  153.6 0.1 fusion.48
  153.8 1.1 collective-permute-done
  154.9 0.0 collective-permute-done.1
  154.9 0.1 copy.51
  155.0 0.1 copy.52
  155.0 0.4 fusion.6
  155.5 0.0 all-gather.2.cloned.1.call-done
  155.5 2.5 %fusion = f32[8,256]{1,0:T(8,128)S(1)} fusion(f32[8,2048]{1,0:T(8,128)S(1)} %bitcast.52, f32[2,256,2048]{2,1,0:T(8,128)} %all-gather.2.cloned.1.call-done), kind=kOutput, calls=%fused_computation.4 | convolution fusion | flops 25165824 | bytes 2170880 | tf_op jit(solution)/shard_map/vc,jc->vj/dot_general | solution.py:26
  158.1 7.2 %all_to_all.49 = f32[8,8,256]{2,1,0:T(8,128)S(1)} all-to-all(f32[8,8,256]{2,1,0:T(8,128)S(1)} %broadcast_in_dim.94), channel_id=1, replica_groups={{0,1,2,3,4,5,6,7},{8,9,10,11,12,13,14,15},{16,17,18,19,20,21,22,23},{24..., dimensions={0} | all-to-all | bytes 131072 | tf_op jit(solution)/shard_map/all_to_all | solution.py:17
  165.3 14.8 %psum.30 = f32[8,256]{1,0:T(8,128)S(1)} all-reduce(f32[8,256]{1,0:T(8,128)S(1)} %reduce_sum.64), channel_id=1, replica_groups={{0,8,16,24},{1,9,17,25},{2,10,18,26},{3,11,19,27},{4,12,20,28},{5,13,21..., use_global_device_ids=true, to_apply=%region_7.8 | all-reduce | flops 2048 | bytes 16384 | tf_op jit(solution)/shard_map/psum | solution.py:22
  180.1 2.2 convolution_subtract_fusion.1
  182.3 2.5 %fusion.1 = f32[8,256]{1,0:T(8,128)S(1)} fusion(f32[8,2048]{1,0:T(8,128)S(1)} %convolution_subtract_fusion.1, f32[2,256,2048]{2,1,0:T(8,128)} %all-gather.2.cloned.1.call-done), kind=kOutput, calls=%fused_computation.5 | convolution fusion | flops 25165824 | bytes 2170880 | tf_op jit(solution)/shard_map/vc,jc->vj/dot_general | solution.py:26
  184.9 9.9 %all_to_all.50 = f32[8,8,256]{2,1,0:T(8,128)S(1)} all-to-all(f32[8,8,256]{2,1,0:T(8,128)S(1)} %broadcast_in_dim.95), channel_id=1, replica_groups={{0,1,2,3,4,5,6,7},{8,9,10,11,12,13,14,15},{16,17,18,19,20,21,22,23},{24..., dimensions={0} | all-to-all | bytes 131072 | tf_op jit(solution)/shard_map/all_to_all | solution.py:17
  194.8 9.3 %psum.31 = f32[8,256]{1,0:T(8,128)S(1)} all-reduce(f32[8,256]{1,0:T(8,128)S(1)} %reduce_sum.65), channel_id=1, replica_groups={{0,8,16,24},{1,9,17,25},{2,10,18,26},{3,11,19,27},{4,12,20,28},{5,13,21..., use_global_device_ids=true, to_apply=%region_9.10 | all-reduce | flops 2048 | bytes 16384 | tf_op jit(solution)/shard_map/psum | solution.py:22
  204.1 2.2 convolution_subtract_fusion
  206.3 11.0 %collective-permute-start.2 = (f32[8,2048]{1,0:T(8,128)S(1)}, f32[8,2048]{1,0:T(8,128)S(1)}, u32[]{:S(2)}, u32[]{:S(2)}) collective-permute-start(f32[8,2048]{1,0:T(8,128)S(1)} %convolution_subtract_fusion), channel_id=1, source_target_pairs={{1,2},{3,4},{5,6},{7,8},{9,10},{11,12},{13,14},{15,16},{17,18},{19... | collective-permute-start | bytes 196616 | tf_op jit(solution)/shard_map/ppermute | solution.py:49
  217.3 1.9 collective-permute-start.3
  219.2 0.1 copy.55
  219.3 0.1 fusion.41
  219.4 0.1 fusion.42
  219.6 0.1 fusion.43
  219.7 0.1 fusion.44
  219.8 0.0 collective-permute-done.2
  219.8 0.6 collective-permute-done.3
  220.5 0.1 copy.59
  220.5 0.1 copy.60
  220.6 1.1 fusion.7
  221.7 0.7 subtract_divide_fusion
  (30 shorter events, 0.3 us)
Async XLA Ops:
  7.2 7.2 %copy-start.2 = (f32[8,2,1024]{2,1,0:T(2,128)S(1)}, f32[8,2,1024]{2,1,0:T(2,128)}, u32[]{:S(2)}) copy-start(f32[8,2,1024]{2,1,0:T(2,128)} %param.6) | copy-start | bytes 196612
  8.4 5.3 %copy-start = (f32[2,16,2048]{2,1,0:T(8,128)}, f32[2,16,2048]{2,1,0:T(8,128)S(1)}, u32[]{:S(2)}) copy-start(f32[2,16,2048]{2,1,0:T(8,128)S(1)} %broadcast_in_dim.84) | copy-start | bytes 786436
  9.5 18.4 %all-to-all-start.1 = ((f32[4,2,16,2048]{3,2,1,0:T(8,128)}), f32[4,2,16,2048]{3,2,1,0:T(8,128)S(1)}, u32[]{:S(2)}, u32[]{:S(2)}) async-start(f32[4,2,16,2048]{3,2,1,0:T(8,128)} %broadcast_in_dim.85), calls=%async_computation.1 | async-start | bytes 2097152 | tf_op jit(solution)/shard_map/all_to_all | solution.py:17
  13.7 141.9 %all-gather.2.cloned.1.call-start = ((), (), s32[]{:S(2)}) async-start(), calls=%async_computation.9 | async-start | bytes 4456448 | tf_op jit(solution)/shard_map/all_gather | solution.py:101
  28.6 11.3 %all-to-all-start = ((f32[4,8,2048]{2,1,0:T(8,128)}), f32[4,8,2048]{2,1,0:T(8,128)S(1)}, u32[]{:S(2)}, u32[]{:S(2)}) async-start(f32[4,8,2048]{2,1,0:T(8,128)} %broadcast_in_dim.83), calls=%async_computation | async-start | bytes 524288 | tf_op jit(solution)/shard_map/all_to_all | solution.py:17
  34.2 100.1 %copy-start.3 = (f32[2,1024]{1,0:T(2,128)S(1)}, f32[2,1024]{1,0:T(2,128)}, u32[]{:S(2)}) copy-start(f32[2,1024]{1,0:T(2,128)} %param.8) | copy-start | bytes 24580
  40.2 114.8 %copy-start.1 = (f32[8,2,1024]{2,1,0:T(2,128)S(1)}, f32[8,2,1024]{2,1,0:T(2,128)}, u32[]{:S(2)}) copy-start(f32[8,2,1024]{2,1,0:T(2,128)} %param.7) | copy-start | bytes 196612
  40.2 114.8 %copy-start.4 = (f32[8]{0:T(128)S(1)}, f32[8]{0:T(128)}, u32[]{:S(2)}) copy-start(f32[8]{0:T(128)} %param.9) | copy-start | bytes 100
  128.3 11.7 %all-to-all-start.6 = ((f32[4,8,2048]{2,1,0:T(8,128)}), f32[4,8,2048]{2,1,0:T(8,128)S(1)}, u32[]{:S(2)}, u32[]{:S(2)}) async-start(f32[4,8,2048]{2,1,0:T(8,128)} %fusion.21), calls=%async_computation.6 | async-start | bytes 524288 | tf_op jit(solution)/shard_map/all_to_all | solution.py:86
  140.0 14.9 %collective-permute-start = (f32[8,2048]{1,0:T(8,128)S(1)}, f32[8,2048]{1,0:T(8,128)S(1)}, u32[]{:S(2)}, u32[]{:S(2)}) collective-permute-start(f32[8,2048]{1,0:T(8,128)S(1)} %sub.53), channel_id=1, source_target_pairs={{1,2},{3,4},{5,6},{7,8},{9,10},{11,12},{13,14},{15,16},{17,18},{19... | collective-permute-start | bytes 196616 | tf_op jit(solution)/shard_map/ppermute | solution.py:49
  151.2 3.7 %collective-permute-start.1 = (f32[8,2048]{1,0:T(8,128)S(1)}, f32[8,2048]{1,0:T(8,128)S(1)}, u32[]{:S(2)}, u32[]{:S(2)}) collective-permute-start(f32[8,2048]{1,0:T(8,128)S(1)} %sub.53), channel_id=1, source_target_pairs={{0,1},{1,0},{2,3},{3,2},{4,5},{5,4},{6,7},{7,6},{8,9},{9,8},{10,11... | collective-permute-start | bytes 196616 | tf_op jit(solution)/shard_map/ppermute | solution.py:50
  206.3 13.5 %collective-permute-start.2 = (f32[8,2048]{1,0:T(8,128)S(1)}, f32[8,2048]{1,0:T(8,128)S(1)}, u32[]{:S(2)}, u32[]{:S(2)}) collective-permute-start(f32[8,2048]{1,0:T(8,128)S(1)} %convolution_subtract_fusion), channel_id=1, source_target_pairs={{1,2},{3,4},{5,6},{7,8},{9,10},{11,12},{13,14},{15,16},{17,18},{19... | collective-permute-start | bytes 196616 | tf_op jit(solution)/shard_map/ppermute | solution.py:49
  217.3 3.1 %collective-permute-start.3 = (f32[8,2048]{1,0:T(8,128)S(1)}, f32[8,2048]{1,0:T(8,128)S(1)}, u32[]{:S(2)}, u32[]{:S(2)}) collective-permute-start(f32[8,2048]{1,0:T(8,128)S(1)} %convolution_subtract_fusion), channel_id=1, source_target_pairs={{0,1},{1,0},{2,3},{3,2},{4,5},{5,4},{6,7},{7,6},{8,9},{9,8},{10,11... | collective-permute-start | bytes 196616 | tf_op jit(solution)/shard_map/ppermute | solution.py:50
Sparse Core Ops, SparseCore 0:
  16.6 93.4 all-gather.1

commit v4 on v1

--- a/solution.py
+++ b/solution.py
@@ -15,11 +15,6 @@
     count = len(groups[0])
     sent = jnp.broadcast_to(x[None], (count,) + x.shape)
     return lax.all_to_all(sent, axis, 0, 0, axis_index_groups=groups)
-
-
-def gathered(states):
-    columns = copies(states, "band", BAND_Z)
-    return copies(columns, "band", BAND_Y).reshape(-1, states.shape[-1])
 
 
 def space_sum(x):
@@ -82,9 +77,13 @@
 def on_device(occupied, initial, right_side, potential, energies):
     count, planes, line = initial.shape
     weight = 1.0 / (planes * lax.axis_size("space") * line)
-    states = [occupied[0].reshape(-1, planes * line), occupied[1].reshape(-1, planes * line)]
-    later = lax.all_gather(states[1], "band", axis=0, tiled=True)
-    blocks = [gathered(states[0]), later]
+    own = [states.reshape(-1, planes * line) for states in occupied]
+    run = copies(own[0], "band", BAND_Z).reshape(-1, planes * line)
+    run, other = lax.optimization_barrier((run, own[1]))
+    first = copies(run, "band", BAND_Y).reshape(-1, planes * line)
+    run = copies(other, "band", BAND_Z).reshape(-1, planes * line)
+    later = lax.all_gather(run, "band", axis=0, tiled=True, axis_index_groups=BAND_Y)
+    blocks = [first, later]
     diagonal = 3.75 + potential[None, :, :] - energies[:, None, None]
     vectors = initial.reshape(count, planes * line)
     for iteration in range(ITERS):

time: 215 us -> 228 us (1.060)
  starting transfers between devices: 45.2 us -> 54.8 us
  waiting for transfers between devices: 42.7 us -> 50 us
  blocking collectives: 93 us -> 88.6 us
    all_to_all x3 -> x4, starting transfers between devices: 20.3 us -> 30.7 us  [copies(): return lax.all_to_all(sent, axis, 0, 0, axis_index_groups=groups)]
    all_to_all x3 -> x4, waiting for transfers between devices: 41.5 us -> 48.8 us  [copies(): return lax.all_to_all(sent, axis, 0, 0, axis_index_groups=groups)]
    all_to_all x3, blocking collectives: 36.3 us -> 33.9 us  [copies(): return lax.all_to_all(sent, axis, 0, 0, axis_index_groups=groups)]
  transfers between devices with their start and end apart: 8 -> 9, of which waited for: 5 -> 6; matrix products, arithmetic and copies ran while one was open for 2% -> 2% of each run, Pallas kernels for 0% -> 0%
where the time goes in v4:
time: 228 us; the launch traced here: 227 us
  blocking collectives  88.6 us (39%)
  starting transfers between devices  54.8 us (24%)
  waiting for transfers between devices  50 us (22%)
  between operations  14.3 us (6%)
  matrix products  9.3 us (4%)
  local copies, waits for them, and re-layouts  7.25 us (3%)
  other arithmetic  2.38 us (1%)
    psum x4, blocking collectives, space_sum(): return lax.psum(near, 'space', axis_index_groups=SPACE_Z)  54.7 us
    all_to_all x4, waiting for transfers between devices, copies(): return lax.all_to_all(sent, axis, 0, 0, axis_index_groups=groups)  48.8 us
    all_to_all x3, blocking collectives, copies(): return lax.all_to_all(sent, axis, 0, 0, axis_index_groups=groups)  33.9 us
    all_to_all x4, starting transfers between devices, copies(): return lax.all_to_all(sent, axis, 0, 0, axis_index_groups=groups)  30.7 us
    ppermute x2, starting transfers between devices, neighbours(): across = lax.ppermute(vectors, 'space', outer)  20.3 us
    dot_general x4, matrix products, products(): jnp.einsum('vc,jc->vj', vectors, states, precision=lax.Precision.HIGH, pr...  5.26 us
  transfers between devices with their start and end apart: 9, of which 6 were waited for; matrix products, arithmetic and copies ran while one was open for 2% of the time, Pallas kernels for 0%

profile of v4, /device:TPU:7, one launch (start us, length us, event | category | flops | bytes accessed | tf_op | source)
XLA Modules:
  0.0 226.8 jit_solution(9416813079766061636)
XLA Ops:
  7.2 1.0 fusion.32
  8.2 0.8 broadcast_in_dim.82
  9.0 5.6 %all-to-all-start = ((f32[4,16,2048]{2,1,0:T(8,128)}), f32[4,16,2048]{2,1,0:T(8,128)S(1)}, u32[]{:S(2)}, u32[]{:S(2)}) async-start(f32[4,16,2048]{2,1,0:T(8,128)} %broadcast_in_dim.82), calls=%async_computation | async-start | bytes 1048576 | tf_op jit(solution)/shard_map/all_to_all | solution.py:17
  14.6 0.0 all-gather.2.cloned.1.call-start
  14.7 13.9 %all-to-all-done = f32[4,16,2048]{2,1,0:T(8,128)S(1)} async-done(((f32[4,16,2048]{2,1,0:T(8,128)}), f32[4,16,2048]{2,1,0:T(8,128)S(1)}, u32[]{:S(2)}, u32[]{:S(2)}) %all-to-all-start) | async-done | bytes 524320 | tf_op jit(solution)/shard_map/all_to_all | solution.py:17
  28.7 16.6 %all_to_all.35 = f32[4,16,2048]{2,1,0:T(8,128)} all-to-all(f32[4,16,2048]{2,1,0:T(8,128)S(1)} %broadcast_in_dim.85), channel_id=1, replica_groups={{0,128,256,384},{32,160,288,416},{64,192,320,448},{96,224,352,480},{1,1..., dimensions={0} | all-to-all | bytes 1048576 | tf_op jit(solution)/shard_map/all_to_all | solution.py:17
  45.3 0.0 all-gather.2.cloned.1.call-update
  45.4 1.6 broadcast_in_dim.83
  46.9 0.0 copy-start.3
  46.9 0.0 copy-start.4
  46.9 4.3 %all-to-all-start.1 = ((f32[4,64,2048]{2,1,0:T(8,128)}), f32[4,64,2048]{2,1,0:T(8,128)S(1)}, u32[]{:S(2)}, u32[]{:S(2)}) async-start(f32[4,64,2048]{2,1,0:T(8,128)} %broadcast_in_dim.83), calls=%async_computation.1 | async-start | bytes 4194304 | tf_op jit(solution)/shard_map/all_to_all | solution.py:17
  51.2 0.0 copy-done.3
  51.3 0.0 copy-done.4
  51.3 28.6 %all-to-all-done.1 = f32[4,64,2048]{2,1,0:T(8,128)S(1)} async-done(((f32[4,64,2048]{2,1,0:T(8,128)}), f32[4,64,2048]{2,1,0:T(8,128)S(1)}, u32[]{:S(2)}, u32[]{:S(2)}) %all-to-all-start.1) | async-done | bytes 2097184 | tf_op jit(solution)/shard_map/all_to_all | solution.py:17
  79.9 0.9 convolution_bitcast_fusion
  80.8 0.7 broadcast_in_dim.84
  81.5 12.9 %all-to-all-start.2 = ((f32[8,8,256]{2,1,0:T(8,128)}), f32[8,8,256]{2,1,0:T(8,128)S(1)}, u32[]{:S(2)}, u32[]{:S(2)}) async-start(f32[8,8,256]{2,1,0:T(8,128)} %broadcast_in_dim.84), calls=%async_computation.2 | async-start | bytes 131072 | tf_op jit(solution)/shard_map/all_to_all | solution.py:17
  94.4 3.1 %all-to-all-done.2 = f32[8,8,256]{2,1,0:T(8,128)S(1)} async-done(((f32[8,8,256]{2,1,0:T(8,128)}), f32[8,8,256]{2,1,0:T(8,128)S(1)}, u32[]{:S(2)}, u32[]{:S(2)}) %all-to-all-start.2) | async-done | bytes 65568 | tf_op jit(solution)/shard_map/all_to_all | solution.py:17
  97.5 19.4 %psum.28 = f32[8,256]{1,0:T(8,128)S(1)} all-reduce(f32[8,256]{1,0:T(8,128)S(1)} %reduce_sum.36), channel_id=1, replica_groups={{0,8,16,24},{1,9,17,25},{2,10,18,26},{3,11,19,27},{4,12,20,28},{5,13,21..., use_global_device_ids=true, to_apply=%region_1.0 | all-reduce | flops 2048 | bytes 16384 | tf_op jit(solution)/shard_map/psum | solution.py:22
  117.0 0.6 convolution_subtract_fusion.3
  117.6 2.5 %fusion.41 = f32[8,256]{1,0:T(8,128)S(1)} fusion(f32[8,2048]{1,0:T(8,128)S(1)} %convolution_subtract_fusion.3, f32[256,2048]{1,0:T(8,128)} %all-gather.2.cloned.1.call-done), kind=kOutput, calls=%fused_computation.59 | convolution fusion | flops 25165824 | bytes 2170880 | tf_op jit(solution)/shard_map/vc,jc->vj/dot_general | solution.py:26
  120.1 0.7 broadcast_in_dim.86
  120.7 7.9 %all-to-all-start.4 = ((f32[8,8,256]{2,1,0:T(8,128)}), f32[8,8,256]{2,1,0:T(8,128)S(1)}, u32[]{:S(2)}, u32[]{:S(2)}) async-start(f32[8,8,256]{2,1,0:T(8,128)} %broadcast_in_dim.86), calls=%async_computation.4 | async-start | bytes 131072 | tf_op jit(solution)/shard_map/all_to_all | solution.py:17
  128.7 3.1 %all-to-all-done.4 = f32[8,8,256]{2,1,0:T(8,128)S(1)} async-done(((f32[8,8,256]{2,1,0:T(8,128)}), f32[8,8,256]{2,1,0:T(8,128)S(1)}, u32[]{:S(2)}, u32[]{:S(2)}) %all-to-all-start.4) | async-done | bytes 65568 | tf_op jit(solution)/shard_map/all_to_all | solution.py:17
  131.8 10.6 %psum.29 = f32[8,256]{1,0:T(8,128)S(1)} all-reduce(f32[8,256]{1,0:T(8,128)S(1)} %reduce_sum.37), channel_id=1, replica_groups={{0,8,16,24},{1,9,17,25},{2,10,18,26},{3,11,19,27},{4,12,20,28},{5,13,21..., use_global_device_ids=true, to_apply=%region_3.0 | all-reduce | flops 2048 | bytes 16384 | tf_op jit(solution)/shard_map/psum | solution.py:22
  142.4 2.2 convolution_subtract_fusion.2
  144.6 9.7 %collective-permute-start = (f32[8,2048]{1,0:T(8,128)S(1)}, f32[8,2048]{1,0:T(8,128)S(1)}, u32[]{:S(2)}, u32[]{:S(2)}) collective-permute-start(f32[8,2048]{1,0:T(8,128)S(1)} %convolution_subtract_fusion.2), channel_id=1, source_target_pairs={{1,2},{3,4},{5,6},{7,8},{9,10},{11,12},{13,14},{15,16},{17,18},{19... | collective-permute-start | bytes 196616 | tf_op jit(solution)/shard_map/ppermute | solution.py:49
  154.3 1.9 collective-permute-start.1
  156.2 0.1 copy.37
  156.3 0.1 fusion.37
  156.4 0.1 fusion.38
  156.6 0.1 fusion.39
  156.7 0.1 fusion.40
  156.8 0.0 collective-permute-done
  156.9 0.6 collective-permute-done.1
  157.5 0.1 copy.41
  157.5 0.1 copy.42
  157.6 0.0 copy-done.2
  157.6 0.0 copy-done.5
  157.6 0.5 fusion
  158.1 0.9 fusion.42
  159.0 7.2 %all_to_all.36 = f32[8,8,256]{2,1,0:T(8,128)S(1)} all-to-all(f32[8,8,256]{2,1,0:T(8,128)S(1)} %broadcast_in_dim.92), channel_id=1, replica_groups={{0,1,2,3,4,5,6,7},{8,9,10,11,12,13,14,15},{16,17,18,19,20,21,22,23},{24..., dimensions={0} | all-to-all | bytes 131072 | tf_op jit(solution)/shard_map/all_to_all | solution.py:17
  166.3 15.0 %psum.30 = f32[8,256]{1,0:T(8,128)S(1)} all-reduce(f32[8,256]{1,0:T(8,128)S(1)} %reduce_sum.38), channel_id=1, replica_groups={{0,8,16,24},{1,9,17,25},{2,10,18,26},{3,11,19,27},{4,12,20,28},{5,13,21..., use_global_device_ids=true, to_apply=%region_5.6 | all-reduce | flops 2048 | bytes 16384 | tf_op jit(solution)/shard_map/psum | solution.py:22
  181.3 0.0 copy-start
  181.3 0.6 convolution_subtract_fusion.1
  181.9 1.0 copy-done
  182.9 0.9 fusion.43
  183.9 10.0 %all_to_all.37 = f32[8,8,256]{2,1,0:T(8,128)S(1)} all-to-all(f32[8,8,256]{2,1,0:T(8,128)S(1)} %broadcast_in_dim.93), channel_id=1, replica_groups={{0,1,2,3,4,5,6,7},{8,9,10,11,12,13,14,15},{16,17,18,19,20,21,22,23},{24..., dimensions={0} | all-to-all | bytes 131072 | tf_op jit(solution)/shard_map/all_to_all | solution.py:17
  193.9 9.7 %psum.31 = f32[8,256]{1,0:T(8,128)S(1)} all-reduce(f32[8,256]{1,0:T(8,128)S(1)} %reduce_sum.39), channel_id=1, replica_groups={{0,8,16,24},{1,9,17,25},{2,10,18,26},{3,11,19,27},{4,12,20,28},{5,13,21..., use_global_device_ids=true, to_apply=%region_7.8 | all-reduce | flops 2048 | bytes 16384 | tf_op jit(solution)/shard_map/psum | solution.py:22
  203.6 0.0 copy-done.1
  203.6 0.6 convolution_subtract_fusion
  204.2 10.6 %collective-permute-start.2 = (f32[8,2048]{1,0:T(8,128)S(1)}, f32[8,2048]{1,0:T(8,128)S(1)}, u32[]{:S(2)}, u32[]{:S(2)}) collective-permute-start(f32[8,2048]{1,0:T(8,128)S(1)} %convolution_subtract_fusion), channel_id=1, source_target_pairs={{1,2},{3,4},{5,6},{7,8},{9,10},{11,12},{13,14},{15,16},{17,18},{19... | collective-permute-start | bytes 196616 | tf_op jit(solution)/shard_map/ppermute | solution.py:49
  214.8 1.9 collective-permute-start.3
  216.7 0.1 copy.51
  216.8 0.1 fusion.33
  216.9 0.1 fusion.34
  217.1 0.1 fusion.35
  217.2 0.1 fusion.36
  217.3 0.0 collective-permute-done.2
  217.3 0.6 collective-permute-done.3
  218.0 0.1 copy.55
  218.0 0.1 copy.56
  218.1 1.1 fusion.1
  219.2 0.7 subtract_divide_fusion
  (20 shorter events, 0.3 us)
Async XLA Ops:
  9.0 19.6 %all-to-all-start = ((f32[4,16,2048]{2,1,0:T(8,128)}), f32[4,16,2048]{2,1,0:T(8,128)S(1)}, u32[]{:S(2)}, u32[]{:S(2)}) async-start(f32[4,16,2048]{2,1,0:T(8,128)} %broadcast_in_dim.82), calls=%async_computation | async-start | bytes 1048576 | tf_op jit(solution)/shard_map/all_to_all | solution.py:17
  14.6 102.9 %all-gather.2.cloned.1.call-start = ((), (), s32[]{:S(2)}) async-start(), calls=%async_computation.7 | async-start | bytes 2621440 | tf_op jit(solution)/shard_map/all_gather | solution.py:85
  46.9 4.3 %copy-start.3 = (f32[8,2,1024]{2,1,0:T(2,128)S(1)}, f32[8,2,1024]{2,1,0:T(2,128)}, u32[]{:S(2)}) copy-start(f32[8,2,1024]{2,1,0:T(2,128)} %param.6) | copy-start | bytes 196612
  46.9 4.3 %copy-start.4 = (f32[2,1024]{1,0:T(2,128)S(1)}, f32[2,1024]{1,0:T(2,128)}, u32[]{:S(2)}) copy-start(f32[2,1024]{1,0:T(2,128)} %param.8) | copy-start | bytes 24580
  46.9 33.0 %all-to-all-start.1 = ((f32[4,64,2048]{2,1,0:T(8,128)}), f32[4,64,2048]{2,1,0:T(8,128)S(1)}, u32[]{:S(2)}, u32[]{:S(2)}) async-start(f32[4,64,2048]{2,1,0:T(8,128)} %broadcast_in_dim.83), calls=%async_computation.1 | async-start | bytes 4194304 | tf_op jit(solution)/shard_map/all_to_all | solution.py:17
  81.5 16.0 %all-to-all-start.2 = ((f32[8,8,256]{2,1,0:T(8,128)}), f32[8,8,256]{2,1,0:T(8,128)S(1)}, u32[]{:S(2)}, u32[]{:S(2)}) async-start(f32[8,8,256]{2,1,0:T(8,128)} %broadcast_in_dim.84), calls=%async_computation.2 | async-start | bytes 131072 | tf_op jit(solution)/shard_map/all_to_all | solution.py:17
  120.7 36.8 %copy-start.2 = (f32[8,2,1024]{2,1,0:T(2,128)S(1)}, f32[8,2,1024]{2,1,0:T(2,128)}, u32[]{:S(2)}) copy-start(f32[8,2,1024]{2,1,0:T(2,128)} %param.7) | copy-start | bytes 196612
  120.7 36.9 %copy-start.5 = (f32[8]{0:T(128)S(1)}, f32[8]{0:T(128)}, u32[]{:S(2)}) copy-start(f32[8]{0:T(128)} %param.9) | copy-start | bytes 100
  120.7 11.0 %all-to-all-start.4 = ((f32[8,8,256]{2,1,0:T(8,128)}), f32[8,8,256]{2,1,0:T(8,128)S(1)}, u32[]{:S(2)}, u32[]{:S(2)}) async-start(f32[8,8,256]{2,1,0:T(8,128)} %broadcast_in_dim.86), calls=%async_computation.4 | async-start | bytes 131072 | tf_op jit(solution)/shard_map/all_to_all | solution.py:17
  144.6 12.2 %collective-permute-start = (f32[8,2048]{1,0:T(8,128)S(1)}, f32[8,2048]{1,0:T(8,128)S(1)}, u32[]{:S(2)}, u32[]{:S(2)}) collective-permute-start(f32[8,2048]{1,0:T(8,128)S(1)} %convolution_subtract_fusion.2), channel_id=1, source_target_pairs={{1,2},{3,4},{5,6},{7,8},{9,10},{11,12},{13,14},{15,16},{17,18},{19... | collective-permute-start | bytes 196616 | tf_op jit(solution)/shard_map/ppermute | solution.py:49
  154.3 3.1 %collective-permute-start.1 = (f32[8,2048]{1,0:T(8,128)S(1)}, f32[8,2048]{1,0:T(8,128)S(1)}, u32[]{:S(2)}, u32[]{:S(2)}) collective-permute-start(f32[8,2048]{1,0:T(8,128)S(1)} %convolution_subtract_fusion.2), channel_id=1, source_target_pairs={{0,1},{1,0},{2,3},{3,2},{4,5},{5,4},{6,7},{7,6},{8,9},{9,8},{10,11... | collective-permute-start | bytes 196616 | tf_op jit(solution)/shard_map/ppermute | solution.py:50
  181.3 1.6 copy-start
  182.9 20.6 %copy-start.1 = (f32[256,2048]{1,0:T(8,128)S(1)}, f32[256,2048]{1,0:T(8,128)}, u32[]{:S(2)}) copy-start(f32[256,2048]{1,0:T(8,128)} %all-gather.2.cloned.1.call-done) | copy-start | bytes 6291460
  204.2 13.2 %collective-permute-start.2 = (f32[8,2048]{1,0:T(8,128)S(1)}, f32[8,2048]{1,0:T(8,128)S(1)}, u32[]{:S(2)}, u32[]{:S(2)}) collective-permute-start(f32[8,2048]{1,0:T(8,128)S(1)} %convolution_subtract_fusion), channel_id=1, source_target_pairs={{1,2},{3,4},{5,6},{7,8},{9,10},{11,12},{13,14},{15,16},{17,18},{19... | collective-permute-start | bytes 196616 | tf_op jit(solution)/shard_map/ppermute | solution.py:49
  214.8 3.1 %collective-permute-start.3 = (f32[8,2048]{1,0:T(8,128)S(1)}, f32[8,2048]{1,0:T(8,128)S(1)}, u32[]{:S(2)}, u32[]{:S(2)}) collective-permute-start(f32[8,2048]{1,0:T(8,128)S(1)} %convolution_subtract_fusion), channel_id=1, source_target_pairs={{0,1},{1,0},{2,3},{3,2},{4,5},{5,4},{6,7},{7,6},{8,9},{9,8},{10,11... | collective-permute-start | bytes 196616 | tf_op jit(solution)/shard_map/ppermute | solution.py:50
Sparse Core Ops, SparseCore 0:
  45.5 49.8 all-gather.1

commit v5 on v1

--- a/solution.py
+++ b/solution.py
@@ -57,47 +57,63 @@
     return jnp.where(first, across, inside), jnp.where(first, inside, across)
 
 
-def shifted(planes, by):
-    length = planes.shape[-1]
-    pad = [(0, 0)] * (planes.ndim - 1)
-    if by > 0:
-        return jnp.pad(planes[..., by:], pad + [(0, by)])
-    return jnp.pad(planes[..., :length + by], pad + [(-by, 0)])
+def stencil_rows(cells, line):
+    cell = lax.broadcasted_iota(jnp.int32, (1, cells), 1)
+    z = cell % NZ
+    y = (cell % line) // NZ
+    lines = line // NZ
+    rows = []
+    for step, factor in ((1, -2.0 / 3.0), (2, 1.0 / 24.0)):
+        rows.append((step, jnp.where(z >= step, factor, 0.0)))
+        rows.append((-step, jnp.where(z < NZ - step, factor, 0.0)))
+        rows.append((step * NZ, jnp.where(y >= step, factor, 0.0)))
+        rows.append((-step * NZ, jnp.where(y < lines - step, factor, 0.0)))
+    return [shift for shift, _ in rows], [row for _, row in rows]
 
 
-def coupling(vectors, low, high):
-    z = jnp.arange(vectors.shape[-1]) % NZ
-    nearest = shifted(vectors, NZ) + shifted(vectors, -NZ)
-    second = shifted(vectors, 2 * NZ) + shifted(vectors, -2 * NZ)
-    nearest = nearest + jnp.where(z >= 1, shifted(vectors, -1), 0.0)
-    nearest = nearest + jnp.where(z <= NZ - 2, shifted(vectors, 1), 0.0)
-    second = second + jnp.where(z >= 2, shifted(vectors, -2), 0.0)
-    second = second + jnp.where(z <= NZ - 3, shifted(vectors, 2), 0.0)
-    x = jnp.concatenate([low, vectors, high], axis=1)
-    nearest = nearest + x[:, 1:3] + x[:, 3:5]
-    second = second + x[:, 0:2] + x[:, 4:6]
-    return second / 24.0 - 2.0 / 3.0 * nearest
+def across_planes(vectors, low, high, line):
+    low0, low1 = low[:, :line], low[:, line:]
+    own0, own1 = vectors[:, :line], vectors[:, line:]
+    high0, high1 = high[:, :line], high[:, line:]
+    return jnp.concatenate(
+        [
+            (low0 + high0) / 24.0 - 2.0 / 3.0 * (low1 + own1),
+            (low1 + high1) / 24.0 - 2.0 / 3.0 * (own0 + high0),
+        ],
+        axis=1,
+    )
 
 
 def on_device(occupied, initial, right_side, potential, energies):
     count, planes, line = initial.shape
-    weight = 1.0 / (planes * lax.axis_size("space") * line)
-    states = [occupied[0].reshape(-1, planes * line), occupied[1].reshape(-1, planes * line)]
-    later = lax.all_gather(states[1], "band", axis=0, tiled=True)
-    blocks = [gathered(states[0]), later]
-    diagonal = 3.75 + potential[None, :, :] - energies[:, None, None]
-    vectors = initial.reshape(count, planes * line)
+    cells = planes * line
+    scale = (lax.axis_size("space") * cells) ** -0.5
+    own = [states.reshape(-1, cells) for states in occupied]
+    later = lax.all_gather(own[1], "band", axis=0, tiled=True)
+    run = copies(own[0], "band", BAND_Z).reshape(-1, cells)
+    diagonal = 3.75 + potential.reshape(1, cells) - energies[:, None]
+    shifts, rows = stencil_rows(cells, line)
+    ready = (initial.reshape(count, cells), right_side.reshape(count, cells), diagonal, 1.0 / diagonal, rows)
+    run, ready = lax.optimization_barrier((run, ready))
+    vectors, right, diagonal, inverse, rows = ready
+    first = lax.optimization_barrier(scale * copies(run, "band", BAND_Y).reshape(-1, cells))
+    blocks = [first, None]
     for iteration in range(ITERS):
-        for block in blocks:
-            margin = space_sum(products(vectors, block)) * weight
-            vectors = vectors - combination(margin, block)
+        for index in range(2):
+            if blocks[index] is None:
+                vectors, later = lax.optimization_barrier((vectors, later))
+                blocks[index] = lax.optimization_barrier(scale * later)
+            margin = space_sum(products(vectors, blocks[index]))
+            vectors = vectors - combination(margin, blocks[index])
         low, high = neighbours(vectors)
-        shape = (count, planes, line)
-        vectors = vectors.reshape(shape)
-        rest = right_side - coupling(vectors, low.reshape(shape), high.reshape(shape))
+        rest = right
+        for shift, row in zip(shifts, rows):
+            rest = rest - row * jnp.roll(vectors, shift, axis=1)
+        rest = rest - across_planes(vectors, low, high, line)
         residual = rest - diagonal * vectors
-        vectors = (rest / diagonal).reshape(count, planes * line)
-    return (vectors.reshape(shape), residual)
+        vectors = rest * inverse
+    shape = (count, planes, line)
+    return (vectors.reshape(shape), residual.reshape(shape))
 
 
 def solution(mesh):

time: 215 us -> 221 us (1.028)
  blocking collectives: 93 us -> 123 us
  waiting for transfers between devices: 42.7 us -> 19.6 us
    all_to_all x3 -> x4, blocking collectives: 36.3 us -> 66.1 us  [copies(): return lax.all_to_all(sent, axis, 0, 0, axis_index_groups=groups)]
    all_to_all x3 -> x2, waiting for transfers between devices: 41.5 us -> 16.1 us  [copies(): return lax.all_to_all(sent, axis, 0, 0, axis_index_groups=groups)]
    unnamed x16 -> x21, local copies, waits for them, and re-layouts: 1.77 us -> 4.47 us
    all_to_all x3 -> x2, starting transfers between devices: 20.3 us -> 20 us  [copies(): return lax.all_to_all(sent, axis, 0, 0, axis_index_groups=groups)]
  transfers between devices with their start and end apart: 8 -> 7, of which waited for: 5 -> 5; matrix products, arithmetic and copies ran while one was open for 2% -> 2% of each run, Pallas kernels for 0% -> 0%
where the time goes in v5:
time: 221 us
  blocking collectives  123 us (56%)
  starting transfers between devices  44.4 us (20%)
  waiting for transfers between devices  19.6 us (9%)
  between operations  14.4 us (7%)
  local copies, waits for them, and re-layouts  8.55 us (4%)
  matrix products  7.73 us (3%)
  other arithmetic  2.59 us (1%)
    all_to_all x4, blocking collectives, copies(): return lax.all_to_all(sent, axis, 0, 0, axis_index_groups=groups)  66.1 us
    psum x4, blocking collectives, space_sum(): return lax.psum(near, 'space', axis_index_groups=SPACE_Z)  57.4 us
    ppermute x2, starting transfers between devices, neighbours(): across = lax.ppermute(vectors, 'space', outer)  20.5 us
    all_to_all x2, starting transfers between devices, copies(): return lax.all_to_all(sent, axis, 0, 0, axis_index_groups=groups)  20 us
    all_to_all x2, waiting for transfers between devices, copies(): return lax.all_to_all(sent, axis, 0, 0, axis_index_groups=groups)  16.1 us
    unnamed x21, local copies, waits for them, and re-layouts  4.47 us
  transfers between devices with their start and end apart: 7, of which 5 were waited for; matrix products, arithmetic and copies ran while one was open for 2% of the time, Pallas kernels for 0%

profile of v5, /device:TPU:7, one launch (start us, length us, event | category | flops | bytes accessed | tf_op | source)
XLA Modules:
  0.0 220.7 jit_solution(1168852787804077431)
XLA Ops:
  7.2 0.0 copy-start.5
  7.2 0.0 copy-start.3
  7.2 1.0 fusion.32
  8.3 0.8 broadcast_in_dim.63
  9.1 5.6 %all-to-all-start = ((f32[4,16,2048]{2,1,0:T(8,128)}), f32[4,16,2048]{2,1,0:T(8,128)S(1)}, u32[]{:S(2)}, u32[]{:S(2)}) async-start(f32[4,16,2048]{2,1,0:T(8,128)} %broadcast_in_dim.63), calls=%async_computation | async-start | bytes 1048576 | tf_op jit(solution)/shard_map/all_to_all | solution.py:17
  14.7 0.7 copy.15
  15.4 0.0 all-gather.2.cloned.1.call-update
  15.5 0.0 copy-done.5
  15.7 0.1 broadcast_divide_fusion
  15.8 13.0 %all-to-all-done = f32[4,16,2048]{2,1,0:T(8,128)S(1)} async-done(((f32[4,16,2048]{2,1,0:T(8,128)}), f32[4,16,2048]{2,1,0:T(8,128)S(1)}, u32[]{:S(2)}, u32[]{:S(2)}) %all-to-all-start) | async-done | bytes 524320 | tf_op jit(solution)/shard_map/all_to_all | solution.py:17
  28.7 0.2 broadcast_in_dim.67
  29.0 36.9 %all_to_all.30 = f32[4,64,2048]{2,1,0:T(8,128)S(1)} all-to-all(f32[4,64,2048]{2,1,0:T(8,128)S(1)} %broadcast_in_dim.67), channel_id=1, replica_groups={{0,32,64,96},{128,160,192,224},{256,288,320,352},{384,416,448,480},{1,3..., dimensions={0} | all-to-all | bytes 4194304 | tf_op jit(solution)/shard_map/all_to_all | solution.py:17
  65.9 0.2 broadcast_multiply_fusion.1
  66.1 0.9 fusion.49
  67.1 11.9 %all_to_all.31 = f32[8,8,256]{2,1,0:T(8,128)S(1)} all-to-all(f32[8,8,256]{2,1,0:T(8,128)S(1)} %broadcast_in_dim.68), channel_id=1, replica_groups={{0,1,2,3,4,5,6,7},{8,9,10,11,12,13,14,15},{16,17,18,19,20,21,22,23},{24..., dimensions={0} | all-to-all | bytes 131072 | tf_op jit(solution)/shard_map/all_to_all | solution.py:17
  79.0 19.3 %psum.28 = f32[8,256]{1,0:T(8,128)S(1)} all-reduce(f32[8,256]{1,0:T(8,128)S(1)} %reduce_sum.36), channel_id=1, replica_groups={{0,8,16,24},{1,9,17,25},{2,10,18,26},{3,11,19,27},{4,12,20,28},{5,13,21..., use_global_device_ids=true, to_apply=%region_1.2 | all-reduce | flops 2048 | bytes 16384 | tf_op jit(solution)/shard_map/psum | solution.py:27
  98.4 0.6 convolution_subtract_fusion.3
  99.0 1.8 all-gather.2.cloned.1.call-done
  100.8 1.7 broadcast_multiply_fusion
  102.5 0.0 copy-start
  102.5 1.3 copy-done
  103.8 0.9 fusion.50
  104.8 0.7 broadcast_in_dim.69
  105.4 14.4 %all-to-all-start.3 = ((f32[8,8,256]{2,1,0:T(8,128)}), f32[8,8,256]{2,1,0:T(8,128)S(1)}, u32[]{:S(2)}, u32[]{:S(2)}) async-start(f32[8,8,256]{2,1,0:T(8,128)} %broadcast_in_dim.69), calls=%async_computation.3 | async-start | bytes 131072 | tf_op jit(solution)/shard_map/all_to_all | solution.py:17
  119.9 3.1 %all-to-all-done.3 = f32[8,8,256]{2,1,0:T(8,128)S(1)} async-done(((f32[8,8,256]{2,1,0:T(8,128)}), f32[8,8,256]{2,1,0:T(8,128)S(1)}, u32[]{:S(2)}, u32[]{:S(2)}) %all-to-all-start.3) | async-done | bytes 65568 | tf_op jit(solution)/shard_map/all_to_all | solution.py:17
  123.0 14.1 %psum.29 = f32[8,256]{1,0:T(8,128)S(1)} all-reduce(f32[8,256]{1,0:T(8,128)S(1)} %reduce_sum.37), channel_id=1, replica_groups={{0,8,16,24},{1,9,17,25},{2,10,18,26},{3,11,19,27},{4,12,20,28},{5,13,21..., use_global_device_ids=true, to_apply=%region_3.4 | all-reduce | flops 2048 | bytes 16384 | tf_op jit(solution)/shard_map/psum | solution.py:27
  137.1 2.2 convolution_subtract_fusion.2
  139.3 0.1 fusion.47
  139.4 0.1 fusion.48
  139.5 0.1 fusion.45
  139.6 0.1 fusion.46
  139.6 0.1 fusion.43
  139.7 0.1 fusion.44
  139.8 0.1 fusion.41
  139.9 10.3 %collective-permute-start = (f32[8,2048]{1,0:T(8,128)S(1)}, f32[8,2048]{1,0:T(8,128)S(1)}, u32[]{:S(2)}, u32[]{:S(2)}) collective-permute-start(f32[8,2048]{1,0:T(8,128)S(1)} %convolution_subtract_fusion.2), channel_id=1, source_target_pairs={{1,2},{3,4},{5,6},{7,8},{9,10},{11,12},{13,14},{15,16},{17,18},{19... | collective-permute-start | bytes 196616 | tf_op jit(solution)/shard_map/ppermute | solution.py:54
  150.2 1.9 collective-permute-start.1
  152.1 0.1 fusion.42
  152.2 0.0 collective-permute-done
  152.2 1.1 collective-permute-done.1
  153.3 0.2 fusion.9
  153.5 0.9 fusion.51
  154.5 7.2 %all_to_all.32 = f32[8,8,256]{2,1,0:T(8,128)S(1)} all-to-all(f32[8,8,256]{2,1,0:T(8,128)S(1)} %broadcast_in_dim.70), channel_id=1, replica_groups={{0,1,2,3,4,5,6,7},{8,9,10,11,12,13,14,15},{16,17,18,19,20,21,22,23},{24..., dimensions={0} | all-to-all | bytes 131072 | tf_op jit(solution)/shard_map/all_to_all | solution.py:17
  161.7 13.9 %psum.30 = f32[8,256]{1,0:T(8,128)S(1)} all-reduce(f32[8,256]{1,0:T(8,128)S(1)} %reduce_sum.38), channel_id=1, replica_groups={{0,8,16,24},{1,9,17,25},{2,10,18,26},{3,11,19,27},{4,12,20,28},{5,13,21..., use_global_device_ids=true, to_apply=%region_5.6 | all-reduce | flops 2048 | bytes 16384 | tf_op jit(solution)/shard_map/psum | solution.py:27
  175.7 0.6 convolution_subtract_fusion.1
  176.3 1.0 copy-done.1
  177.2 0.9 fusion.52
  178.2 10.0 %all_to_all.33 = f32[8,8,256]{2,1,0:T(8,128)S(1)} all-to-all(f32[8,8,256]{2,1,0:T(8,128)S(1)} %broadcast_in_dim.71), channel_id=1, replica_groups={{0,1,2,3,4,5,6,7},{8,9,10,11,12,13,14,15},{16,17,18,19,20,21,22,23},{24..., dimensions={0} | all-to-all | bytes 131072 | tf_op jit(solution)/shard_map/all_to_all | solution.py:17
  188.2 10.0 %psum.31 = f32[8,256]{1,0:T(8,128)S(1)} all-reduce(f32[8,256]{1,0:T(8,128)S(1)} %reduce_sum.39), channel_id=1, replica_groups={{0,8,16,24},{1,9,17,25},{2,10,18,26},{3,11,19,27},{4,12,20,28},{5,13,21..., use_global_device_ids=true, to_apply=%region_7.8 | all-reduce | flops 2048 | bytes 16384 | tf_op jit(solution)/shard_map/psum | solution.py:27
  198.2 0.6 convolution_subtract_fusion
  198.9 10.3 %collective-permute-start.2 = (f32[8,2048]{1,0:T(8,128)S(1)}, f32[8,2048]{1,0:T(8,128)S(1)}, u32[]{:S(2)}, u32[]{:S(2)}) collective-permute-start(f32[8,2048]{1,0:T(8,128)S(1)} %convolution_subtract_fusion), channel_id=1, source_target_pairs={{1,2},{3,4},{5,6},{7,8},{9,10},{11,12},{13,14},{15,16},{17,18},{19... | collective-permute-start | bytes 196616 | tf_op jit(solution)/shard_map/ppermute | solution.py:54
  209.1 1.9 collective-permute-start.3
  211.1 0.1 fusion.39
  211.1 0.1 fusion.40
  211.2 0.1 fusion.37
  211.3 0.1 fusion.38
  211.4 0.1 fusion.35
  211.4 0.1 fusion.36
  211.5 0.1 fusion.34
  211.6 0.1 fusion.33
  211.7 0.0 collective-permute-done.2
  211.7 0.6 collective-permute-done.3
  212.3 0.2 multiply_subtract_fusion
  212.5 0.7 copy.9
  213.2 0.7 copy.10
  (30 shorter events, 0.4 us)
Async XLA Ops:
  7.2 8.3 %copy-start.5 = (f32[2,1024]{1,0:T(2,128)S(1)}, f32[2,1024]{1,0:T(2,128)}, u32[]{:S(2)}) copy-start(f32[2,1024]{1,0:T(2,128)} %param.8) | copy-start | bytes 24580
  7.2 8.3 %copy-start.3 = (f32[8,2,1024]{2,1,0:T(2,128)S(1)}, f32[8,2,1024]{2,1,0:T(2,128)}, u32[]{:S(2)}) copy-start(f32[8,2,1024]{2,1,0:T(2,128)} %param.6) | copy-start | bytes 196612
  7.2 8.4 %copy-start.4 = (f32[8,2,1024]{2,1,0:T(2,128)S(1)}, f32[8,2,1024]{2,1,0:T(2,128)}, u32[]{:S(2)}) copy-start(f32[8,2,1024]{2,1,0:T(2,128)} %param.7) | copy-start | bytes 196612
  7.2 8.5 %copy-start.6 = (f32[8]{0:T(128)S(1)}, f32[8]{0:T(128)}, u32[]{:S(2)}) copy-start(f32[8]{0:T(128)} %param.9) | copy-start | bytes 100
  9.1 19.6 %all-to-all-start = ((f32[4,16,2048]{2,1,0:T(8,128)}), f32[4,16,2048]{2,1,0:T(8,128)S(1)}, u32[]{:S(2)}, u32[]{:S(2)}) async-start(f32[4,16,2048]{2,1,0:T(8,128)} %broadcast_in_dim.63), calls=%async_computation | async-start | bytes 1048576 | tf_op jit(solution)/shard_map/all_to_all | solution.py:17
  14.7 86.0 %all-gather.2.cloned.1.call-start = ((), (), s32[]{:S(2)}) async-start(), calls=%async_computation.6 | async-start | bytes 2228224 | tf_op jit(solution)/shard_map/all_gather | solution.py:92
  102.5 1.3 copy-start
  105.4 17.6 %all-to-all-start.3 = ((f32[8,8,256]{2,1,0:T(8,128)}), f32[8,8,256]{2,1,0:T(8,128)S(1)}, u32[]{:S(2)}, u32[]{:S(2)}) async-start(f32[8,8,256]{2,1,0:T(8,128)} %broadcast_in_dim.69), calls=%async_computation.3 | async-start | bytes 131072 | tf_op jit(solution)/shard_map/all_to_all | solution.py:17
  139.9 12.3 %collective-permute-start = (f32[8,2048]{1,0:T(8,128)S(1)}, f32[8,2048]{1,0:T(8,128)S(1)}, u32[]{:S(2)}, u32[]{:S(2)}) collective-permute-start(f32[8,2048]{1,0:T(8,128)S(1)} %convolution_subtract_fusion.2), channel_id=1, source_target_pairs={{1,2},{3,4},{5,6},{7,8},{9,10},{11,12},{13,14},{15,16},{17,18},{19... | collective-permute-start | bytes 196616 | tf_op jit(solution)/shard_map/ppermute | solution.py:54
  150.2 3.1 %collective-permute-start.1 = (f32[8,2048]{1,0:T(8,128)S(1)}, f32[8,2048]{1,0:T(8,128)S(1)}, u32[]{:S(2)}, u32[]{:S(2)}) collective-permute-start(f32[8,2048]{1,0:T(8,128)S(1)} %convolution_subtract_fusion.2), channel_id=1, source_target_pairs={{0,1},{1,0},{2,3},{3,2},{4,5},{5,4},{6,7},{7,6},{8,9},{9,8},{10,11... | collective-permute-start | bytes 196616 | tf_op jit(solution)/shard_map/ppermute | solution.py:55
  175.7 1.6 copy-start.1
  177.2 21.0 %copy-start.2 = (f32[256,2048]{1,0:T(8,128)S(1)}, f32[256,2048]{1,0:T(8,128)}, u32[]{:S(2)}) copy-start(f32[256,2048]{1,0:T(8,128)} %copy-done) | copy-start | bytes 6291460
  198.9 12.8 %collective-permute-start.2 = (f32[8,2048]{1,0:T(8,128)S(1)}, f32[8,2048]{1,0:T(8,128)S(1)}, u32[]{:S(2)}, u32[]{:S(2)}) collective-permute-start(f32[8,2048]{1,0:T(8,128)S(1)} %convolution_subtract_fusion), channel_id=1, source_target_pairs={{1,2},{3,4},{5,6},{7,8},{9,10},{11,12},{13,14},{15,16},{17,18},{19... | collective-permute-start | bytes 196616 | tf_op jit(solution)/shard_map/ppermute | solution.py:54
  209.1 3.1 %collective-permute-start.3 = (f32[8,2048]{1,0:T(8,128)S(1)}, f32[8,2048]{1,0:T(8,128)S(1)}, u32[]{:S(2)}, u32[]{:S(2)}) collective-permute-start(f32[8,2048]{1,0:T(8,128)S(1)} %convolution_subtract_fusion), channel_id=1, source_target_pairs={{0,1},{1,0},{2,3},{3,2},{4,5},{5,4},{6,7},{7,6},{8,9},{9,8},{10,11... | collective-permute-start | bytes 196616 | tf_op jit(solution)/shard_map/ppermute | solution.py:55
Sparse Core Ops, SparseCore 0:
  17.6 83.0 all-gather.1

commit v6 on v3

--- a/solution.py
+++ b/solution.py
@@ -98,7 +98,9 @@
     weight = 1.0 / (lax.axis_size("space") * cells)
     blocks, own = occupied.shape[:2]
     states = occupied.reshape(blocks, own, cells)
-    whole = lax.all_gather(states, "band", axis=1, tiled=True)
+    whole = states
+    for groups in (BAND_Z, BAND_Y):
+        whole = lax.all_gather(whole, "band", axis=1, tiled=True, axis_index_groups=groups)
     ring = copies(states, "band", BAND_Y)
     diagonal = 3.75 + potential[None, :, :] - energies[:, None, None]
     vectors = initial.reshape(count, cells)
@@ -108,6 +110,7 @@
                 vectors = project_shared(ring[:, block].reshape(-1, cells), vectors, weight)
             else:
                 vectors = project_whole(whole[block], vectors, weight)
+        vectors, whole = lax.optimization_barrier((vectors, whole))
         low, high = neighbours(vectors)
         shape = (count, planes, line)
         vectors = vectors.reshape(shape)

time: 232 us -> 232 us (level)
  waiting for transfers between devices: 27 us -> 55.5 us
  blocking collectives: 127 us -> 109 us
  starting transfers between devices: 41.8 us -> 30.2 us
    all_gather x1 -> x2, waiting for transfers between devices: 0.02 us -> 37.6 us  [on_device(): lax.all_gather(whole, 'band', axis=1, tiled=True, axis_index_groups=groups)]
    all_to_all x2, waiting for transfers between devices: 19 us -> 7.42 us  [copies(): return lax.all_to_all(sent, axis, 0, 0, axis_index_groups=groups)]
    all_to_all x5, blocking collectives: 58 us -> 47.5 us  [copies(): return lax.all_to_all(sent, axis, 0, 0, axis_index_groups=groups)]
    ppermute x2, starting transfers between devices: 22.1 us -> 15.3 us  [neighbours(): across = lax.ppermute(vectors, 'space', outer)]
    all_to_all x1, blocking collectives: 14.8 us -> 8.76 us  [project_shared(): partial = lax.all_to_all(partial, 'band', 0, 0, axis_index_groups=BAND_Z)]
    ppermute x2, waiting for transfers between devices: 1.11 us -> 4.9 us  [neighbours(): across = lax.ppermute(vectors, 'space', outer)]
    all_to_all x1, starting transfers between devices: 6.04 us -> 3.4 us  [project_shared(): partial = lax.all_to_all(partial, 'band', 0, 0, axis_index_groups=BAND_Z)]
  transfers between devices with their start and end apart: 8 -> 9, of which waited for: 5 -> 5; matrix products, arithmetic and copies ran while one was open for 2% -> 3% of each run, Pallas kernels for 0% -> 0%
where the time goes in v6:
time: 232 us; the launch traced here: 230 us
  blocking collectives  109 us (47%)
  waiting for transfers between devices  55.5 us (24%)
  starting transfers between devices  30.2 us (13%)
  between operations  14.5 us (6%)
  matrix products  11.4 us (5%)
  local copies, waits for them, and re-layouts  6.45 us (3%)
  other arithmetic  2.58 us (1%)
    psum x4, blocking collectives, space_sum(): return lax.psum(near, 'space', axis_index_groups=SPACE_Z)  53.1 us
    all_to_all x5, blocking collectives, copies(): return lax.all_to_all(sent, axis, 0, 0, axis_index_groups=groups)  47.5 us
    all_gather x2, waiting for transfers between devices, on_device(): lax.all_gather(whole, 'band', axis=1, tiled=True, axis_index_groups=groups)  37.6 us
    ppermute x2, starting transfers between devices, neighbours(): across = lax.ppermute(vectors, 'space', outer)  15.3 us
    all_to_all x1, blocking collectives, project_shared(): partial = lax.all_to_all(partial, 'band', 0, 0, axis_index_groups=BAND_Z)  8.76 us
    all_to_all x2, starting transfers between devices, copies(): return lax.all_to_all(sent, axis, 0, 0, axis_index_groups=groups)  7.59 us
    all_to_all x2, waiting for transfers between devices, copies(): return lax.all_to_all(sent, axis, 0, 0, axis_index_groups=groups)  7.42 us
    dot_general x4, matrix products, combination(): jnp.einsum('vj,jc->vc', margin, states, precision=lax.Precision.HIGH, pre...  5.69 us
  transfers between devices with their start and end apart: 9, of which 5 were waited for; matrix products, arithmetic and copies ran while one was open for 3% of the time, Pallas kernels for 0%

profile of v6, /device:TPU:7, one launch (start us, length us, event | category | flops | bytes accessed | tf_op | source)
XLA Modules:
  0.0 229.9 jit_solution(2516210853221343632)
XLA Ops:
  7.2 0.0 copy-start.1
  7.2 0.0 all-gather.3.cloned.1.call-start
  7.2 1.9 broadcast_in_dim.81
  9.1 0.0 all-gather.3.cloned.1.call-update
  9.1 2.1 broadcast_in_dim.82
  11.2 4.2 %all-to-all-start.1 = ((f32[4,2,16,2048]{3,2,1,0:T(8,128)}), f32[4,2,16,2048]{3,2,1,0:T(8,128)S(1)}, u32[]{:S(2)}, u32[]{:S(2)}) async-start(f32[4,2,16,2048]{3,2,1,0:T(8,128)} %broadcast_in_dim.82), calls=%async_computation.1 | async-start | bytes 2097152 | tf_op jit(solution)/shard_map/all_to_all | solution.py:17
  15.4 37.6 %all-gather.3.cloned.1.call-done = f32[2,64,2048]{2,1,0:T(8,128)} async-done(((f32[2,16,2048]{2,1,0:T(8,128)}), f32[2,64,2048]{2,1,0:T(8,128)}) %all-gather.3.cloned.1.call-update) | async-done | bytes 1048592 | tf_op jit(solution)/shard_map/all_gather | solution.py:103
  53.0 0.0 all-gather.5.cloned.1.call-update
  53.0 0.0 all-to-all-done.1
  53.1 0.7 broadcast_in_dim.80
  53.8 3.4 %all-to-all-start = ((f32[4,8,2048]{2,1,0:T(8,128)}), f32[4,8,2048]{2,1,0:T(8,128)S(1)}, u32[]{:S(2)}, u32[]{:S(2)}) async-start(f32[4,8,2048]{2,1,0:T(8,128)} %broadcast_in_dim.80), calls=%async_computation | async-start | bytes 524288 | tf_op jit(solution)/shard_map/all_to_all | solution.py:17
  57.2 0.0 copy-start.2
  57.2 0.1 fusion.48
  57.3 7.4 %all-to-all-done = f32[4,8,2048]{2,1,0:T(8,128)S(1)} async-done(((f32[4,8,2048]{2,1,0:T(8,128)}), f32[4,8,2048]{2,1,0:T(8,128)S(1)}, u32[]{:S(2)}, u32[]{:S(2)}) %all-to-all-start) | async-done | bytes 262176 | tf_op jit(solution)/shard_map/all_to_all | solution.py:17
  64.7 0.3 fusion.12
  65.1 0.1 pad_maximum_fusion.4
  65.2 9.7 %all_to_all.45 = f32[8,16,128]{2,1,0:T(8,128)S(1)} all-to-all(f32[8,16,128]{2,1,0:T(8,128)S(1)} %broadcast_in_dim.83), channel_id=1, replica_groups={{0,1,2,3,4,5,6,7},{8,9,10,11,12,13,14,15},{16,17,18,19,20,21,22,23},{24..., dimensions={0} | all-to-all | bytes 131072 | tf_op jit(solution)/shard_map/all_to_all | solution.py:17
  74.9 14.3 %psum.28 = f32[16,128]{1,0:T(8,128)S(1)} all-reduce(f32[16,128]{1,0:T(8,128)S(1)} %reduce_sum.54), channel_id=1, replica_groups={{0,8,16,24},{1,9,17,25},{2,10,18,26},{3,11,19,27},{4,12,20,28},{5,13,21..., use_global_device_ids=true, to_apply=%region_1.0 | all-reduce | flops 2048 | bytes 16384 | tf_op jit(solution)/shard_map/psum | solution.py:22
  89.2 0.1 fusion.60
  89.2 0.3 fusion.26
  89.5 8.8 %all_to_all.46 = f32[4,8,2048]{2,1,0:T(8,128)S(1)} all-to-all(f32[4,8,2048]{2,1,0:T(8,128)S(1)} %fusion.26), channel_id=1, replica_groups={{0,128,256,384},{32,160,288,416},{64,192,320,448},{96,224,352,480},{1,1..., dimensions={0} | all-to-all | bytes 524288 | tf_op jit(solution)/shard_map/all_to_all | solution.py:86
  98.4 9.0 %all_to_all.47 = f32[4,8,2048]{2,1,0:T(8,128)S(1)} all-to-all(f32[4,8,2048]{2,1,0:T(8,128)S(1)} %broadcast_in_dim.84), channel_id=1, replica_groups={{0,128,256,384},{32,160,288,416},{64,192,320,448},{96,224,352,480},{1,1..., dimensions={0} | all-to-all | bytes 524288 | tf_op jit(solution)/shard_map/all_to_all | solution.py:17
  107.3 0.3 fusion.10
  107.7 0.1 pad_maximum_fusion.5
  107.8 11.7 %all_to_all.48 = f32[8,16,128]{2,1,0:T(8,128)S(1)} all-to-all(f32[8,16,128]{2,1,0:T(8,128)S(1)} %broadcast_in_dim.85), channel_id=1, replica_groups={{0,1,2,3,4,5,6,7},{8,9,10,11,12,13,14,15},{16,17,18,19,20,21,22,23},{24..., dimensions={0} | all-to-all | bytes 131072 | tf_op jit(solution)/shard_map/all_to_all | solution.py:17
  119.4 12.8 %psum.29 = f32[16,128]{1,0:T(8,128)S(1)} all-reduce(f32[16,128]{1,0:T(8,128)S(1)} %reduce_sum.56), channel_id=1, replica_groups={{0,8,16,24},{1,9,17,25},{2,10,18,26},{3,11,19,27},{4,12,20,28},{5,13,21..., use_global_device_ids=true, to_apply=%region_4.0 | all-reduce | flops 2048 | bytes 16384 | tf_op jit(solution)/shard_map/psum | solution.py:22
  132.3 0.1 fusion.59
  132.4 1.0 fusion.29
  133.4 3.4 %all-to-all-start.6 = ((f32[4,8,2048]{2,1,0:T(8,128)}), f32[4,8,2048]{2,1,0:T(8,128)S(1)}, u32[]{:S(2)}, u32[]{:S(2)}) async-start(f32[4,8,2048]{2,1,0:T(8,128)} %fusion.29), calls=%async_computation.6 | async-start | bytes 524288 | tf_op jit(solution)/shard_map/all_to_all | solution.py:86
  136.9 5.5 %all-to-all-done.6 = f32[4,8,2048]{2,1,0:T(8,128)S(1)} async-done(((f32[4,8,2048]{2,1,0:T(8,128)}), f32[4,8,2048]{2,1,0:T(8,128)S(1)}, u32[]{:S(2)}, u32[]{:S(2)}) %all-to-all-start.6) | async-done | bytes 262176 | tf_op jit(solution)/shard_map/all_to_all | solution.py:86
  142.4 0.0 all-gather.5.cloned.1.call-done
  142.5 8.8 %collective-permute-start = (f32[8,2048]{1,0:T(8,128)S(1)}, f32[8,2048]{1,0:T(8,128)S(1)}, u32[]{:S(2)}, u32[]{:S(2)}) collective-permute-start(f32[8,2048]{1,0:T(8,128)S(1)} %sub.45), channel_id=1, source_target_pairs={{1,2},{3,4},{5,6},{7,8},{9,10},{11,12},{13,14},{15,16},{17,18},{19... | collective-permute-start | bytes 196616 | tf_op jit(solution)/shard_map/ppermute | solution.py:49
  151.2 1.9 collective-permute-start.1
  153.2 0.1 copy.65
  153.2 0.1 fusion.53
  153.4 0.1 fusion.54
  153.5 0.1 fusion.55
  153.6 0.1 fusion.56
  153.8 2.4 %collective-permute-done = f32[8,2048]{1,0:T(8,128)S(1)} collective-permute-done((f32[8,2048]{1,0:T(8,128)S(1)}, f32[8,2048]{1,0:T(8,128)S(1)}, u32[]{:S(2)}, u32[]{:S(2)}) %collective-permute-start) | collective-permute-done | bytes 65568 | tf_op jit(solution)/shard_map/ppermute | solution.py:49
  156.2 0.0 collective-permute-done.1
  156.2 0.1 copy.69
  156.3 0.1 copy.70
  156.3 0.4 fusion.14
  156.8 2.5 %fusion.4 = f32[8,256]{1,0:T(8,128)S(1)} fusion(f32[8,2048]{1,0:T(8,128)S(1)} %bitcast.53, f32[2,256,2048]{2,1,0:T(8,128)} %all-gather.5.cloned.1.call-done), kind=kOutput, calls=%fused_computation.6 | convolution fusion | flops 25165824 | bytes 2170880 | tf_op jit(solution)/shard_map/vc,jc->vj/dot_general | solution.py:26
  159.3 7.2 %all_to_all.49 = f32[8,8,256]{2,1,0:T(8,128)S(1)} all-to-all(f32[8,8,256]{2,1,0:T(8,128)S(1)} %broadcast_in_dim.91), channel_id=1, replica_groups={{0,1,2,3,4,5,6,7},{8,9,10,11,12,13,14,15},{16,17,18,19,20,21,22,23},{24..., dimensions={0} | all-to-all | bytes 131072 | tf_op jit(solution)/shard_map/all_to_all | solution.py:17
  166.6 12.3 %psum.30 = f32[8,256]{1,0:T(8,128)S(1)} all-reduce(f32[8,256]{1,0:T(8,128)S(1)} %reduce_sum.58), channel_id=1, replica_groups={{0,8,16,24},{1,9,17,25},{2,10,18,26},{3,11,19,27},{4,12,20,28},{5,13,21..., use_global_device_ids=true, to_apply=%region_7.8 | all-reduce | flops 2048 | bytes 16384 | tf_op jit(solution)/shard_map/psum | solution.py:22
  178.9 2.2 convolution_subtract_fusion.1
  181.1 2.5 %fusion.1 = f32[8,256]{1,0:T(8,128)S(1)} fusion(f32[8,2048]{1,0:T(8,128)S(1)} %convolution_subtract_fusion.1, f32[2,256,2048]{2,1,0:T(8,128)} %all-gather.5.cloned.1.call-done), kind=kOutput, calls=%fused_computation.3 | convolution fusion | flops 25165824 | bytes 2170880 | tf_op jit(solution)/shard_map/vc,jc->vj/dot_general | solution.py:26
  183.6 10.0 %all_to_all.50 = f32[8,8,256]{2,1,0:T(8,128)S(1)} all-to-all(f32[8,8,256]{2,1,0:T(8,128)S(1)} %broadcast_in_dim.92), channel_id=1, replica_groups={{0,1,2,3,4,5,6,7},{8,9,10,11,12,13,14,15},{16,17,18,19,20,21,22,23},{24..., dimensions={0} | all-to-all | bytes 131072 | tf_op jit(solution)/shard_map/all_to_all | solution.py:17
  193.6 13.7 %psum.31 = f32[8,256]{1,0:T(8,128)S(1)} all-reduce(f32[8,256]{1,0:T(8,128)S(1)} %reduce_sum.59), channel_id=1, replica_groups={{0,8,16,24},{1,9,17,25},{2,10,18,26},{3,11,19,27},{4,12,20,28},{5,13,21..., use_global_device_ids=true, to_apply=%region_9.10 | all-reduce | flops 2048 | bytes 16384 | tf_op jit(solution)/shard_map/psum | solution.py:22
  207.3 2.2 convolution_subtract_fusion
  209.5 6.5 %collective-permute-start.2 = (f32[8,2048]{1,0:T(8,128)S(1)}, f32[8,2048]{1,0:T(8,128)S(1)}, u32[]{:S(2)}, u32[]{:S(2)}) collective-permute-start(f32[8,2048]{1,0:T(8,128)S(1)} %convolution_subtract_fusion), channel_id=1, source_target_pairs={{1,2},{3,4},{5,6},{7,8},{9,10},{11,12},{13,14},{15,16},{17,18},{19... | collective-permute-start | bytes 196616 | tf_op jit(solution)/shard_map/ppermute | solution.py:49
  216.1 1.9 collective-permute-start.3
  218.0 0.1 copy.79
  218.1 0.1 fusion.49
  218.2 0.1 fusion.50
  218.3 0.1 fusion.51
  218.5 0.1 fusion.52
  218.6 2.5 %collective-permute-done.2 = f32[8,2048]{1,0:T(8,128)S(1)} collective-permute-done((f32[8,2048]{1,0:T(8,128)S(1)}, f32[8,2048]{1,0:T(8,128)S(1)}, u32[]{:S(2)}, u32[]{:S(2)}) %collective-permute-start.2) | collective-permute-done | bytes 65568 | tf_op jit(solution)/shard_map/ppermute | solution.py:49
  221.1 0.0 collective-permute-done.3
  221.1 0.1 copy.83
  221.2 0.1 copy.84
  221.3 1.1 fusion.15
  222.4 0.7 subtract_divide_fusion
  (31 shorter events, 0.3 us)
Async XLA Ops:
  7.2 45.8 %copy-start.1 = (f32[8,2,1024]{2,1,0:T(2,128)S(1)}, f32[8,2,1024]{2,1,0:T(2,128)}, u32[]{:S(2)}) copy-start(f32[8,2,1024]{2,1,0:T(2,128)} %param.6) | copy-start | bytes 196612
  7.2 45.8 %all-gather.3.cloned.1.call-start = ((), (), s32[]{:S(2)}) async-start(), calls=%async_computation.9 | async-start | bytes 1310720 | tf_op jit(solution)/shard_map/all_gather | solution.py:103
  11.2 41.9 %all-to-all-start.1 = ((f32[4,2,16,2048]{3,2,1,0:T(8,128)}), f32[4,2,16,2048]{3,2,1,0:T(8,128)S(1)}, u32[]{:S(2)}, u32[]{:S(2)}) async-start(f32[4,2,16,2048]{3,2,1,0:T(8,128)} %broadcast_in_dim.82), calls=%async_computation.1 | async-start | bytes 2097152 | tf_op jit(solution)/shard_map/all_to_all | solution.py:17
  15.4 127.1 %all-gather.5.cloned.1.call-start = ((), (), s32[]{:S(2)}) async-start(), calls=%async_computation.10 | async-start | bytes 5242880 | tf_op jit(solution)/shard_map/all_gather | solution.py:103
  53.8 10.9 %all-to-all-start = ((f32[4,8,2048]{2,1,0:T(8,128)}), f32[4,8,2048]{2,1,0:T(8,128)S(1)}, u32[]{:S(2)}, u32[]{:S(2)}) async-start(f32[4,8,2048]{2,1,0:T(8,128)} %broadcast_in_dim.80), calls=%async_computation | async-start | bytes 524288 | tf_op jit(solution)/shard_map/all_to_all | solution.py:17
  57.2 79.6 %copy-start.2 = (f32[2,1024]{1,0:T(2,128)S(1)}, f32[2,1024]{1,0:T(2,128)}, u32[]{:S(2)}) copy-start(f32[2,1024]{1,0:T(2,128)} %param.8) | copy-start | bytes 24580
  64.7 91.6 %copy-start = (f32[8,2,1024]{2,1,0:T(2,128)S(1)}, f32[8,2,1024]{2,1,0:T(2,128)}, u32[]{:S(2)}) copy-start(f32[8,2,1024]{2,1,0:T(2,128)} %param.7) | copy-start | bytes 196612
  64.7 91.6 %copy-start.3 = (f32[8]{0:T(128)S(1)}, f32[8]{0:T(128)}, u32[]{:S(2)}) copy-start(f32[8]{0:T(128)} %param.9) | copy-start | bytes 100
  133.4 9.0 %all-to-all-start.6 = ((f32[4,8,2048]{2,1,0:T(8,128)}), f32[4,8,2048]{2,1,0:T(8,128)S(1)}, u32[]{:S(2)}, u32[]{:S(2)}) async-start(f32[4,8,2048]{2,1,0:T(8,128)} %fusion.29), calls=%async_computation.6 | async-start | bytes 524288 | tf_op jit(solution)/shard_map/all_to_all | solution.py:86
  142.5 13.7 %collective-permute-start = (f32[8,2048]{1,0:T(8,128)S(1)}, f32[8,2048]{1,0:T(8,128)S(1)}, u32[]{:S(2)}, u32[]{:S(2)}) collective-permute-start(f32[8,2048]{1,0:T(8,128)S(1)} %sub.45), channel_id=1, source_target_pairs={{1,2},{3,4},{5,6},{7,8},{9,10},{11,12},{13,14},{15,16},{17,18},{19... | collective-permute-start | bytes 196616 | tf_op jit(solution)/shard_map/ppermute | solution.py:49
  151.2 4.9 %collective-permute-start.1 = (f32[8,2048]{1,0:T(8,128)S(1)}, f32[8,2048]{1,0:T(8,128)S(1)}, u32[]{:S(2)}, u32[]{:S(2)}) collective-permute-start(f32[8,2048]{1,0:T(8,128)S(1)} %sub.45), channel_id=1, source_target_pairs={{0,1},{1,0},{2,3},{3,2},{4,5},{5,4},{6,7},{7,6},{8,9},{9,8},{10,11... | collective-permute-start | bytes 196616 | tf_op jit(solution)/shard_map/ppermute | solution.py:50
  209.5 11.6 %collective-permute-start.2 = (f32[8,2048]{1,0:T(8,128)S(1)}, f32[8,2048]{1,0:T(8,128)S(1)}, u32[]{:S(2)}, u32[]{:S(2)}) collective-permute-start(f32[8,2048]{1,0:T(8,128)S(1)} %convolution_subtract_fusion), channel_id=1, source_target_pairs={{1,2},{3,4},{5,6},{7,8},{9,10},{11,12},{13,14},{15,16},{17,18},{19... | collective-permute-start | bytes 196616 | tf_op jit(solution)/shard_map/ppermute | solution.py:49
  216.1 5.0 %collective-permute-start.3 = (f32[8,2048]{1,0:T(8,128)S(1)}, f32[8,2048]{1,0:T(8,128)S(1)}, u32[]{:S(2)}, u32[]{:S(2)}) collective-permute-start(f32[8,2048]{1,0:T(8,128)S(1)} %convolution_subtract_fusion), channel_id=1, source_target_pairs={{0,1},{1,0},{2,3},{3,2},{4,5},{5,4},{6,7},{7,6},{8,9},{9,8},{10,11... | collective-permute-start | bytes 196616 | tf_op jit(solution)/shard_map/ppermute | solution.py:50
Sparse Core Ops, SparseCore 0:
  10.1 42.8 all-gather.2
  55.1 55.1 all-gather.4

commit v7 on v3

--- a/solution.py
+++ b/solution.py
@@ -17,9 +17,10 @@
     return lax.all_to_all(sent, axis, 0, 0, axis_index_groups=groups)
 
 
-def space_sum(x):
+def space_sum(x, beside=None):
     near = jnp.sum(copies(x, "space", SPACE_PLANE), axis=0)
-    return lax.psum(near, "space", axis_index_groups=SPACE_Z)
+    near, beside = lax.optimization_barrier((near, beside))
+    return lax.psum(near, "space", axis_index_groups=SPACE_Z), beside
 
 
 def products(vectors, states):
@@ -74,21 +75,22 @@
     return second / 24.0 - 2.0 / 3.0 * nearest
 
 
-def project_shared(states, vectors, weight):
+def project_shared(states, vectors, weight, beside):
     count, cells = vectors.shape
     run = copies(vectors, "band", BAND_Z).reshape(-1, cells)
     half = run.shape[0] // 2
     product = products(run, states)
-    margin = space_sum(jnp.concatenate([product[:half], product[half:]], axis=1)) * weight
+    total, beside = space_sum(jnp.concatenate([product[:half], product[half:]], axis=1), beside)
+    margin = total * weight
     width = states.shape[0]
     margin = jnp.concatenate([margin[:, :width], margin[:, width:]], axis=0)
     partial = combination(margin, states).reshape(-1, count, cells)
     partial = lax.all_to_all(partial, "band", 0, 0, axis_index_groups=BAND_Z)
-    return vectors - jnp.sum(partial, axis=0)
+    return vectors - jnp.sum(partial, axis=0), beside
 
 
 def project_whole(states, vectors, weight):
-    margin = space_sum(products(vectors, states)) * weight
+    margin = space_sum(products(vectors, states))[0] * weight
     return vectors - combination(margin, states)
 
 
@@ -98,14 +100,21 @@
     weight = 1.0 / (lax.axis_size("space") * cells)
     blocks, own = occupied.shape[:2]
     states = occupied.reshape(blocks, own, cells)
-    whole = lax.all_gather(states, "band", axis=1, tiled=True)
+    column = lax.all_gather(states, "band", axis=1, tiled=True, axis_index_groups=BAND_Z)
     ring = copies(states, "band", BAND_Y)
     diagonal = 3.75 + potential[None, :, :] - energies[:, None, None]
     vectors = initial.reshape(count, cells)
     for iteration in range(ITERS):
         for block in range(blocks):
             if iteration == 0:
-                vectors = project_shared(ring[:, block].reshape(-1, cells), vectors, weight)
+                vectors, column = project_shared(
+                    ring[:, block].reshape(-1, cells), vectors, weight, column
+                )
+                if block == 0:
+                    whole = lax.all_gather(
+                        column, "band", axis=1, tiled=True, axis_index_groups=BAND_Y
+                    )
+                    column = None
             else:
                 vectors = project_whole(whole[block], vectors, weight)
         low, high = neighbours(vectors)

time: 232 us -> 220 us (0.948)
  blocking collectives: 127 us -> 115 us
  waiting for transfers between devices: 27 us -> 36.8 us
  starting transfers between devices: 41.8 us -> 33 us
    all_to_all x5, blocking collectives: 58 us -> 50.9 us  [copies(): return lax.all_to_all(sent, axis, 0, 0, axis_index_groups=groups)]
    all_gather x1 -> x2, waiting for transfers between devices: 0.02 us -> 6.96 us  [the longest x1 6.94 us: on_device(): lax.all_gather(states, 'band', axis=1, tiled=True, axis_index_groups=BAND_Z)]
    ppermute x2, starting transfers between devices: 22.1 us -> 15.9 us  [neighbours(): across = lax.ppermute(vectors, 'space', outer)]
    all_to_all x1, blocking collectives: 14.8 us -> 9.04 us  [project_shared(): partial = lax.all_to_all(partial, 'band', 0, 0, axis_index_groups=BAND_Z)]
    ppermute x2, waiting for transfers between devices: 1.11 us -> 4.6 us  [neighbours(): across = lax.ppermute(vectors, 'space', outer)]
    all_to_all x1, starting transfers between devices: 6.04 us -> 3.4 us  [project_shared(): partial = lax.all_to_all(partial, 'band', 0, 0, axis_index_groups=BAND_Z)]
  transfers between devices with their start and end apart: 8 -> 9, of which waited for: 5 -> 6; matrix products, arithmetic and copies ran while one was open for 2% -> 2% of each run, Pallas kernels for 0% -> 0%
where the time goes in v7:
time: 220 us; the launch traced here: 218 us
  blocking collectives  115 us (52%)
  waiting for transfers between devices  36.8 us (17%)
  starting transfers between devices  33 us (15%)
  between operations  14.4 us (7%)
  matrix products  11.4 us (5%)
  local copies, waits for them, and re-layouts  4.71 us (2%)
  other arithmetic  2.69 us (1%)
    psum x4, blocking collectives, space_sum(): return (lax.psum(near, 'space', axis_index_groups=SPACE_Z), beside)  55.1 us
    all_to_all x5, blocking collectives, copies(): return lax.all_to_all(sent, axis, 0, 0, axis_index_groups=groups)  50.9 us
    all_to_all x2, waiting for transfers between devices, copies(): return lax.all_to_all(sent, axis, 0, 0, axis_index_groups=groups)  19 us
    ppermute x2, starting transfers between devices, neighbours(): across = lax.ppermute(vectors, 'space', outer)  15.9 us
    all_to_all x2, starting transfers between devices, copies(): return lax.all_to_all(sent, axis, 0, 0, axis_index_groups=groups)  9.8 us
    all_to_all x1, blocking collectives, project_shared(): partial = lax.all_to_all(partial, 'band', 0, 0, axis_index_groups=BAND_Z)  9.04 us
    all_gather x1, waiting for transfers between devices, on_device(): lax.all_gather(states, 'band', axis=1, tiled=True, axis_index_groups=BAND_Z)  6.94 us
    dot_general x4, matrix products, combination(): jnp.einsum('vj,jc->vc', margin, states, precision=lax.Precision.HIGH, pre...  5.69 us
  transfers between devices with their start and end apart: 9, of which 6 were waited for; matrix products, arithmetic and copies ran while one was open for 2% of the time, Pallas kernels for 0%

profile of v7, /device:TPU:7, one launch (start us, length us, event | category | flops | bytes accessed | tf_op | source)
XLA Modules:
  0.0 218.0 jit_solution(2847316919038080307)
XLA Ops:
  7.2 0.0 copy-start.2
  7.2 1.2 broadcast_in_dim.84
  8.4 1.1 broadcast_in_dim.85
  9.5 4.2 %all-to-all-start.1 = ((f32[4,2,16,2048]{3,2,1,0:T(8,128)}), f32[4,2,16,2048]{3,2,1,0:T(8,128)S(1)}, u32[]{:S(2)}, u32[]{:S(2)}) async-start(f32[4,2,16,2048]{3,2,1,0:T(8,128)} %broadcast_in_dim.85), calls=%async_computation.1 | async-start | bytes 2097152 | tf_op jit(solution)/shard_map/all_to_all | solution.py:17
  13.7 0.0 copy-done
  13.7 0.7 all-gather.3.cloned.1.call-update
  14.4 13.4 %all-to-all-done.1 = f32[4,2,16,2048]{3,2,1,0:T(8,128)S(1)} async-done(((f32[4,2,16,2048]{3,2,1,0:T(8,128)}), f32[4,2,16,2048]{3,2,1,0:T(8,128)S(1)}, u32[]{:S(2)}, u32[]{:S(2)}) %all-to-all-start.1) | async-done | bytes 1048608 | tf_op jit(solution)/shard_map/all_to_all | solution.py:17
  27.8 0.7 broadcast_in_dim.83
  28.5 5.6 %all-to-all-start = ((f32[4,8,2048]{2,1,0:T(8,128)}), f32[4,8,2048]{2,1,0:T(8,128)S(1)}, u32[]{:S(2)}, u32[]{:S(2)}) async-start(f32[4,8,2048]{2,1,0:T(8,128)} %broadcast_in_dim.83), calls=%async_computation | async-start | bytes 524288 | tf_op jit(solution)/shard_map/all_to_all | solution.py:17
  34.2 0.1 fusion.40
  34.3 0.0 copy-start.3
  34.3 5.6 %all-to-all-done = f32[4,8,2048]{2,1,0:T(8,128)S(1)} async-done(((f32[4,8,2048]{2,1,0:T(8,128)}), f32[4,8,2048]{2,1,0:T(8,128)S(1)}, u32[]{:S(2)}, u32[]{:S(2)}) %all-to-all-start) | async-done | bytes 262176 | tf_op jit(solution)/shard_map/all_to_all | solution.py:17
  39.8 0.3 fusion.4
  40.2 0.1 pad_maximum_fusion.4
  40.3 12.8 %all_to_all.45 = f32[8,16,128]{2,1,0:T(8,128)S(1)} all-to-all(f32[8,16,128]{2,1,0:T(8,128)S(1)} %broadcast_in_dim.86), channel_id=1, replica_groups={{0,1,2,3,4,5,6,7},{8,9,10,11,12,13,14,15},{16,17,18,19,20,21,22,23},{24..., dimensions={0} | all-to-all | bytes 131072 | tf_op jit(solution)/shard_map/all_to_all | solution.py:17
  53.1 6.9 %all-gather.3.cloned.1.call-done = f32[2,64,2048]{2,1,0:T(8,128)} async-done(((f32[2,16,2048]{2,1,0:T(8,128)}), f32[2,64,2048]{2,1,0:T(8,128)}) %all-gather.3.cloned.1.call-update) | async-done | bytes 1048592 | tf_op jit(solution)/shard_map/all_gather | solution.py:103
  60.1 0.0 all-gather.5.cloned.1.call-update
  60.1 16.6 %psum.28 = f32[16,128]{1,0:T(8,128)S(1)} all-reduce(f32[16,128]{1,0:T(8,128)S(1)} %reduce_sum.58), channel_id=1, replica_groups={{0,8,16,24},{1,9,17,25},{2,10,18,26},{3,11,19,27},{4,12,20,28},{5,13,21..., use_global_device_ids=true, to_apply=%region_1.0 | all-reduce | flops 2048 | bytes 16384 | tf_op jit(solution)/shard_map/psum | solution.py:23
  76.7 0.1 fusion.52
  76.8 0.3 fusion.18
  77.1 9.0 %all_to_all.46 = f32[4,8,2048]{2,1,0:T(8,128)S(1)} all-to-all(f32[4,8,2048]{2,1,0:T(8,128)S(1)} %fusion.18), channel_id=1, replica_groups={{0,128,256,384},{32,160,288,416},{64,192,320,448},{96,224,352,480},{1,1..., dimensions={0} | all-to-all | bytes 524288 | tf_op jit(solution)/shard_map/all_to_all | solution.py:88
  86.2 8.8 %all_to_all.47 = f32[4,8,2048]{2,1,0:T(8,128)S(1)} all-to-all(f32[4,8,2048]{2,1,0:T(8,128)S(1)} %broadcast_in_dim.87), channel_id=1, replica_groups={{0,128,256,384},{32,160,288,416},{64,192,320,448},{96,224,352,480},{1,1..., dimensions={0} | all-to-all | bytes 524288 | tf_op jit(solution)/shard_map/all_to_all | solution.py:17
  95.0 0.3 fusion.2
  95.3 0.1 pad_maximum_fusion.5
  95.4 12.0 %all_to_all.48 = f32[8,16,128]{2,1,0:T(8,128)S(1)} all-to-all(f32[8,16,128]{2,1,0:T(8,128)S(1)} %broadcast_in_dim.88), channel_id=1, replica_groups={{0,1,2,3,4,5,6,7},{8,9,10,11,12,13,14,15},{16,17,18,19,20,21,22,23},{24..., dimensions={0} | all-to-all | bytes 131072 | tf_op jit(solution)/shard_map/all_to_all | solution.py:17
  107.4 12.2 %psum.29 = f32[16,128]{1,0:T(8,128)S(1)} all-reduce(f32[16,128]{1,0:T(8,128)S(1)} %reduce_sum.61), channel_id=1, replica_groups={{0,8,16,24},{1,9,17,25},{2,10,18,26},{3,11,19,27},{4,12,20,28},{5,13,21..., use_global_device_ids=true, to_apply=%region_4.0 | all-reduce | flops 2048 | bytes 16384 | tf_op jit(solution)/shard_map/psum | solution.py:23
  119.6 0.1 fusion.51
  119.7 1.0 fusion.21
  120.7 3.4 %all-to-all-start.6 = ((f32[4,8,2048]{2,1,0:T(8,128)}), f32[4,8,2048]{2,1,0:T(8,128)S(1)}, u32[]{:S(2)}, u32[]{:S(2)}) async-start(f32[4,8,2048]{2,1,0:T(8,128)} %fusion.21), calls=%async_computation.6 | async-start | bytes 524288 | tf_op jit(solution)/shard_map/all_to_all | solution.py:88
  124.2 5.5 %all-to-all-done.6 = f32[4,8,2048]{2,1,0:T(8,128)S(1)} async-done(((f32[4,8,2048]{2,1,0:T(8,128)}), f32[4,8,2048]{2,1,0:T(8,128)S(1)}, u32[]{:S(2)}, u32[]{:S(2)}) %all-to-all-start.6) | async-done | bytes 262176 | tf_op jit(solution)/shard_map/all_to_all | solution.py:88
  129.7 9.2 %collective-permute-start = (f32[8,2048]{1,0:T(8,128)S(1)}, f32[8,2048]{1,0:T(8,128)S(1)}, u32[]{:S(2)}, u32[]{:S(2)}) collective-permute-start(f32[8,2048]{1,0:T(8,128)S(1)} %sub.53), channel_id=1, source_target_pairs={{1,2},{3,4},{5,6},{7,8},{9,10},{11,12},{13,14},{15,16},{17,18},{19... | collective-permute-start | bytes 196616 | tf_op jit(solution)/shard_map/ppermute | solution.py:50
  139.0 1.9 collective-permute-start.1
  140.9 0.1 copy_subtract_fusion
  141.0 0.1 fusion.45
  141.1 0.1 fusion.46
  141.3 0.1 fusion.47
  141.4 0.1 fusion.48
  141.5 1.9 collective-permute-done
  143.5 0.0 collective-permute-done.1
  143.5 0.1 copy.51
  143.5 0.1 copy.52
  143.6 0.4 fusion.6
  144.1 0.0 all-gather.5.cloned.1.call-done
  144.1 2.5 %fusion = f32[8,256]{1,0:T(8,128)S(1)} fusion(f32[8,2048]{1,0:T(8,128)S(1)} %bitcast.52, f32[2,256,2048]{2,1,0:T(8,128)} %all-gather.5.cloned.1.call-done), kind=kOutput, calls=%fused_computation.4 | convolution fusion | flops 25165824 | bytes 2170880 | tf_op jit(solution)/shard_map/vc,jc->vj/dot_general | solution.py:27
  146.7 7.2 %all_to_all.49 = f32[8,8,256]{2,1,0:T(8,128)S(1)} all-to-all(f32[8,8,256]{2,1,0:T(8,128)S(1)} %broadcast_in_dim.94), channel_id=1, replica_groups={{0,1,2,3,4,5,6,7},{8,9,10,11,12,13,14,15},{16,17,18,19,20,21,22,23},{24..., dimensions={0} | all-to-all | bytes 131072 | tf_op jit(solution)/shard_map/all_to_all | solution.py:17
  153.9 12.7 %psum.30 = f32[8,256]{1,0:T(8,128)S(1)} all-reduce(f32[8,256]{1,0:T(8,128)S(1)} %reduce_sum.64), channel_id=1, replica_groups={{0,8,16,24},{1,9,17,25},{2,10,18,26},{3,11,19,27},{4,12,20,28},{5,13,21..., use_global_device_ids=true, to_apply=%region_7.8 | all-reduce | flops 2048 | bytes 16384 | tf_op jit(solution)/shard_map/psum | solution.py:23
  166.6 2.2 %convolution_subtract_fusion.1 = f32[8,2048]{1,0:T(8,128)S(1)} fusion(f32[8,2048]{1,0:T(8,128)S(1)} %bitcast.53, f32[2,256,2048]{2,1,0:T(8,128)} %all-gather.5.cloned.1.call-done, f32[8,256]{1,0:T(8,128)S(1)} %psum.30), kind=kOutput, calls=%fused_computation.1 | convolution fusion | flops 25184256 | bytes 2236416 | tf_op jit(solution)/shard_map/vj,jc->vc/dot_general | solution.py:37
  168.8 2.5 %fusion.1 = f32[8,256]{1,0:T(8,128)S(1)} fusion(f32[8,2048]{1,0:T(8,128)S(1)} %convolution_subtract_fusion.1, f32[2,256,2048]{2,1,0:T(8,128)} %all-gather.5.cloned.1.call-done), kind=kOutput, calls=%fused_computation.5 | convolution fusion | flops 25165824 | bytes 2170880 | tf_op jit(solution)/shard_map/vc,jc->vj/dot_general | solution.py:27
  171.3 10.1 %all_to_all.50 = f32[8,8,256]{2,1,0:T(8,128)S(1)} all-to-all(f32[8,8,256]{2,1,0:T(8,128)S(1)} %broadcast_in_dim.95), channel_id=1, replica_groups={{0,1,2,3,4,5,6,7},{8,9,10,11,12,13,14,15},{16,17,18,19,20,21,22,23},{24..., dimensions={0} | all-to-all | bytes 131072 | tf_op jit(solution)/shard_map/all_to_all | solution.py:17
  181.4 13.6 %psum.31 = f32[8,256]{1,0:T(8,128)S(1)} all-reduce(f32[8,256]{1,0:T(8,128)S(1)} %reduce_sum.65), channel_id=1, replica_groups={{0,8,16,24},{1,9,17,25},{2,10,18,26},{3,11,19,27},{4,12,20,28},{5,13,21..., use_global_device_ids=true, to_apply=%region_9.10 | all-reduce | flops 2048 | bytes 16384 | tf_op jit(solution)/shard_map/psum | solution.py:23
  195.0 2.2 %convolution_subtract_fusion = f32[8,2048]{1,0:T(8,128)S(1)} fusion(f32[8,2048]{1,0:T(8,128)S(1)} %convolution_subtract_fusion.1, f32[2,256,2048]{2,1,0:T(8,128)} %all-gather.5.cloned.1.call-done, f32[8,256]{1,0:T(8,128)S(1)} %psum.31), kind=kOutput, calls=%fused_computation | convolution fusion | flops 25184256 | bytes 2236416 | tf_op jit(solution)/shard_map/vj,jc->vc/dot_general | solution.py:37
  197.2 6.7 %collective-permute-start.2 = (f32[8,2048]{1,0:T(8,128)S(1)}, f32[8,2048]{1,0:T(8,128)S(1)}, u32[]{:S(2)}, u32[]{:S(2)}) collective-permute-start(f32[8,2048]{1,0:T(8,128)S(1)} %convolution_subtract_fusion), channel_id=1, source_target_pairs={{1,2},{3,4},{5,6},{7,8},{9,10},{11,12},{13,14},{15,16},{17,18},{19... | collective-permute-start | bytes 196616 | tf_op jit(solution)/shard_map/ppermute | solution.py:50
  203.9 1.9 collective-permute-start.3
  205.8 0.1 copy.55
  205.9 0.1 fusion.41
  206.0 0.1 fusion.42
  206.2 0.1 fusion.43
  206.3 0.1 fusion.44
  206.4 2.7 %collective-permute-done.2 = f32[8,2048]{1,0:T(8,128)S(1)} collective-permute-done((f32[8,2048]{1,0:T(8,128)S(1)}, f32[8,2048]{1,0:T(8,128)S(1)}, u32[]{:S(2)}, u32[]{:S(2)}) %collective-permute-start.2) | collective-permute-done | bytes 65568 | tf_op jit(solution)/shard_map/ppermute | solution.py:50
  209.1 0.0 collective-permute-done.3
  209.2 0.1 copy.59
  209.2 0.1 copy.60
  209.3 1.1 fusion.7
  210.4 0.7 subtract_divide_fusion
  (33 shorter events, 0.3 us)
Async XLA Ops:
  7.2 7.2 %copy-start.2 = (f32[8,2,1024]{2,1,0:T(2,128)S(1)}, f32[8,2,1024]{2,1,0:T(2,128)}, u32[]{:S(2)}) copy-start(f32[8,2,1024]{2,1,0:T(2,128)} %param.6) | copy-start | bytes 196612
  8.4 5.3 %copy-start = (f32[2,16,2048]{2,1,0:T(8,128)}, f32[2,16,2048]{2,1,0:T(8,128)S(1)}, u32[]{:S(2)}) copy-start(f32[2,16,2048]{2,1,0:T(8,128)S(1)} %broadcast_in_dim.84) | copy-start | bytes 786436
  9.5 18.4 %all-to-all-start.1 = ((f32[4,2,16,2048]{3,2,1,0:T(8,128)}), f32[4,2,16,2048]{3,2,1,0:T(8,128)S(1)}, u32[]{:S(2)}, u32[]{:S(2)}) async-start(f32[4,2,16,2048]{3,2,1,0:T(8,128)} %broadcast_in_dim.85), calls=%async_computation.1 | async-start | bytes 2097152 | tf_op jit(solution)/shard_map/all_to_all | solution.py:17
  13.6 46.4 %all-gather.3.cloned.1.call-start = ((), (), s32[]{:S(2)}) async-start(), calls=%async_computation.9 | async-start | bytes 1310720 | tf_op jit(solution)/shard_map/all_gather | solution.py:103
  28.5 11.3 %all-to-all-start = ((f32[4,8,2048]{2,1,0:T(8,128)}), f32[4,8,2048]{2,1,0:T(8,128)S(1)}, u32[]{:S(2)}, u32[]{:S(2)}) async-start(f32[4,8,2048]{2,1,0:T(8,128)} %broadcast_in_dim.83), calls=%async_computation | async-start | bytes 524288 | tf_op jit(solution)/shard_map/all_to_all | solution.py:17
  34.2 109.9 %all-gather.5.cloned.1.call-start = ((), (), s32[]{:S(2)}) async-start(), calls=%async_computation.10 | async-start | bytes 5242880 | tf_op jit(solution)/shard_map/all_gather | solution.py:114
  34.3 89.9 %copy-start.3 = (f32[2,1024]{1,0:T(2,128)S(1)}, f32[2,1024]{1,0:T(2,128)}, u32[]{:S(2)}) copy-start(f32[2,1024]{1,0:T(2,128)} %param.8) | copy-start | bytes 24580
  60.0 83.6 %copy-start.1 = (f32[8,2,1024]{2,1,0:T(2,128)S(1)}, f32[8,2,1024]{2,1,0:T(2,128)}, u32[]{:S(2)}) copy-start(f32[8,2,1024]{2,1,0:T(2,128)} %param.7) | copy-start | bytes 196612
  60.1 83.6 %copy-start.4 = (f32[8]{0:T(128)S(1)}, f32[8]{0:T(128)}, u32[]{:S(2)}) copy-start(f32[8]{0:T(128)} %param.9) | copy-start | bytes 100
  120.7 9.0 %all-to-all-start.6 = ((f32[4,8,2048]{2,1,0:T(8,128)}), f32[4,8,2048]{2,1,0:T(8,128)S(1)}, u32[]{:S(2)}, u32[]{:S(2)}) async-start(f32[4,8,2048]{2,1,0:T(8,128)} %fusion.21), calls=%async_computation.6 | async-start | bytes 524288 | tf_op jit(solution)/shard_map/all_to_all | solution.py:88
  129.7 13.7 %collective-permute-start = (f32[8,2048]{1,0:T(8,128)S(1)}, f32[8,2048]{1,0:T(8,128)S(1)}, u32[]{:S(2)}, u32[]{:S(2)}) collective-permute-start(f32[8,2048]{1,0:T(8,128)S(1)} %sub.53), channel_id=1, source_target_pairs={{1,2},{3,4},{5,6},{7,8},{9,10},{11,12},{13,14},{15,16},{17,18},{19... | collective-permute-start | bytes 196616 | tf_op jit(solution)/shard_map/ppermute | solution.py:50
  139.0 4.5 %collective-permute-start.1 = (f32[8,2048]{1,0:T(8,128)S(1)}, f32[8,2048]{1,0:T(8,128)S(1)}, u32[]{:S(2)}, u32[]{:S(2)}) collective-permute-start(f32[8,2048]{1,0:T(8,128)S(1)} %sub.53), channel_id=1, source_target_pairs={{0,1},{1,0},{2,3},{3,2},{4,5},{5,4},{6,7},{7,6},{8,9},{9,8},{10,11... | collective-permute-start | bytes 196616 | tf_op jit(solution)/shard_map/ppermute | solution.py:51
  197.2 11.9 %collective-permute-start.2 = (f32[8,2048]{1,0:T(8,128)S(1)}, f32[8,2048]{1,0:T(8,128)S(1)}, u32[]{:S(2)}, u32[]{:S(2)}) collective-permute-start(f32[8,2048]{1,0:T(8,128)S(1)} %convolution_subtract_fusion), channel_id=1, source_target_pairs={{1,2},{3,4},{5,6},{7,8},{9,10},{11,12},{13,14},{15,16},{17,18},{19... | collective-permute-start | bytes 196616 | tf_op jit(solution)/shard_map/ppermute | solution.py:50
  203.9 5.2 %collective-permute-start.3 = (f32[8,2048]{1,0:T(8,128)S(1)}, f32[8,2048]{1,0:T(8,128)S(1)}, u32[]{:S(2)}, u32[]{:S(2)}) collective-permute-start(f32[8,2048]{1,0:T(8,128)S(1)} %convolution_subtract_fusion), channel_id=1, source_target_pairs={{0,1},{1,0},{2,3},{3,2},{4,5},{5,4},{6,7},{7,6},{8,9},{9,8},{10,11... | collective-permute-start | bytes 196616 | tf_op jit(solution)/shard_map/ppermute | solution.py:51
Sparse Core Ops, SparseCore 0:
  16.6 43.4 all-gather.2
  62.1 55.8 all-gather.4

commit v8 on v7

--- a/solution.py
+++ b/solution.py
@@ -75,18 +75,19 @@
     return second / 24.0 - 2.0 / 3.0 * nearest
 
 
-def project_shared(states, vectors, weight, beside):
-    count, cells = vectors.shape
-    run = copies(vectors, "band", BAND_Z).reshape(-1, cells)
-    half = run.shape[0] // 2
-    product = products(run, states)
-    total, beside = space_sum(jnp.concatenate([product[:half], product[half:]], axis=1), beside)
-    margin = total * weight
-    width = states.shape[0]
-    margin = jnp.concatenate([margin[:, :width], margin[:, width:]], axis=0)
-    partial = combination(margin, states).reshape(-1, count, cells)
-    partial = lax.all_to_all(partial, "band", 0, 0, axis_index_groups=BAND_Z)
-    return vectors - jnp.sum(partial, axis=0), beside
+def swapped(x, bit):
+    return lax.ppermute(x, "band", [(i, i ^ bit) for i in range(lax.axis_size("band"))])
+
+
+def shared_margin(halves, pair, weight, beside=None):
+    product = jnp.concatenate([products(pair, half) for half in halves], axis=1)
+    total, beside = space_sum(product, beside)
+    return total * weight, beside
+
+
+def shared_correction(margin, halves):
+    width = halves[0].shape[0]
+    return combination(margin[:, :width], halves[0]) + combination(margin[:, width:], halves[1])
 
 
 def project_whole(states, vectors, weight):
@@ -102,21 +103,28 @@
     states = occupied.reshape(blocks, own, cells)
     column = lax.all_gather(states, "band", axis=1, tiled=True, axis_index_groups=BAND_Z)
     ring = copies(states, "band", BAND_Y)
+    first, second = ring[:, 0].reshape(-1, cells), ring[:, 1].reshape(-1, cells)
     diagonal = 3.75 + potential[None, :, :] - energies[:, None, None]
     vectors = initial.reshape(count, cells)
+    pair = jnp.concatenate([vectors, swapped(vectors, 8)], axis=0)
+    across_first, second = lax.optimization_barrier((swapped(first, 4), second))
+    across_second = swapped(second, 4)
+    halves = (first, across_first)
+    margin, column = shared_margin(halves, pair, weight, column)
+    whole = lax.all_gather(column, "band", axis=1, tiled=True, axis_index_groups=BAND_Y)
+    partial = shared_correction(margin, halves)
+    other = swapped(jnp.concatenate([partial[count:], partial[:count]], axis=0), 8)
+    pair = pair - partial - other
+    halves = (second, across_second)
+    margin, _ = shared_margin(halves, pair, weight)
+    partial = shared_correction(margin, halves)
+    vectors = pair[:count] - partial[:count] - swapped(partial[count:], 8)
+    vectors, whole = lax.optimization_barrier((vectors, whole))
+    blocks = [lax.optimization_barrier(whole[block]) for block in range(2)]
     for iteration in range(ITERS):
-        for block in range(blocks):
-            if iteration == 0:
-                vectors, column = project_shared(
-                    ring[:, block].reshape(-1, cells), vectors, weight, column
-                )
-                if block == 0:
-                    whole = lax.all_gather(
-                        column, "band", axis=1, tiled=True, axis_index_groups=BAND_Y
-                    )
-                    column = None
-            else:
-                vectors = project_whole(whole[block], vectors, weight)
+        if iteration > 0:
+            for block in blocks:
+                vectors = project_whole(block, vectors, weight)
         low, high = neighbours(vectors)
         shape = (count, planes, line)
         vectors = vectors.reshape(shape)

time: 220 us -> 223 us (1.014)
  blocking collectives: 115 us -> 85.4 us
  starting transfers between devices: 33 us -> 57.1 us
  waiting for transfers between devices: 36.8 us -> 46.9 us
  matrix products: 11.4 us -> 6.99 us
  local copies, waits for them, and re-layouts: 4.71 us -> 8.25 us
    ppermute x0 -> x5, waiting for transfers between devices: none -> 26 us  [swapped(): lax.ppermute(x, 'band', [(i, i ^ bit) for i in range(lax.axis_size('band'...]
    all_to_all x5 -> x2, blocking collectives: 50.9 us -> 26.3 us  [copies(): return lax.all_to_all(sent, axis, 0, 0, axis_index_groups=groups)]
    ppermute x0 -> x5, starting transfers between devices: none -> 15.9 us  [swapped(): lax.ppermute(x, 'band', [(i, i ^ bit) for i in range(lax.axis_size('band'...]
    all_to_all x1 -> x0, blocking collectives: 9.04 us -> none  [project_shared(): partial = lax.all_to_all(partial, 'band', 0, 0, axis_index_groups=BAND_Z)]
    all_to_all x2 -> x3, starting transfers between devices: 9.8 us -> 16 us  [copies(): return lax.all_to_all(sent, axis, 0, 0, axis_index_groups=groups)]
    all_to_all x1 -> x0, waiting for transfers between devices: 5.53 us -> none  [project_shared(): partial = lax.all_to_all(partial, 'band', 0, 0, axis_index_groups=BAND_Z)]
    ppermute x2, starting transfers between devices: 15.9 us -> 21.4 us  [neighbours(): across = lax.ppermute(vectors, 'space', outer)]
    ppermute x2, waiting for transfers between devices: 4.6 us -> 0.01 us  [neighbours(): across = lax.ppermute(vectors, 'space', outer)]
  transfers between devices with their start and end apart: 9 -> 14, of which waited for: 6 -> 9; matrix products, arithmetic and copies ran while one was open for 2% -> 3% of each run, Pallas kernels for 0% -> 0%
where the time goes in v8:
time: 223 us; the launch traced here: 222 us
  blocking collectives  85.4 us (38%)
  starting transfers between devices  57.1 us (26%)
  waiting for transfers between devices  46.9 us (21%)
  between operations  14.5 us (7%)
  local copies, waits for them, and re-layouts  8.25 us (4%)
  matrix products  6.99 us (3%)
  other arithmetic  2.6 us (1%)
    psum x4, blocking collectives, space_sum(): return (lax.psum(near, 'space', axis_index_groups=SPACE_Z), beside)  59.1 us
    all_to_all x2, blocking collectives, copies(): return lax.all_to_all(sent, axis, 0, 0, axis_index_groups=groups)  26.3 us
    ppermute x5, waiting for transfers between devices, swapped(): lax.ppermute(x, 'band', [(i, i ^ bit) for i in range(lax.axis_size('band'...  26 us
    ppermute x2, starting transfers between devices, neighbours(): across = lax.ppermute(vectors, 'space', outer)  21.4 us
    all_to_all x3, starting transfers between devices, copies(): return lax.all_to_all(sent, axis, 0, 0, axis_index_groups=groups)  16 us
    ppermute x5, starting transfers between devices, swapped(): lax.ppermute(x, 'band', [(i, i ^ bit) for i in range(lax.axis_size('band'...  15.9 us
    all_to_all x3, waiting for transfers between devices, copies(): return lax.all_to_all(sent, axis, 0, 0, axis_index_groups=groups)  14.8 us
    all_gather x1, waiting for transfers between devices, on_device(): lax.all_gather(states, 'band', axis=1, tiled=True, axis_index_groups=BAND_Z)  4.74 us
  transfers between devices with their start and end apart: 14, of which 9 were waited for; matrix products, arithmetic and copies ran while one was open for 3% of the time, Pallas kernels for 0%

profile of v8, /device:TPU:7, one launch (start us, length us, event | category | flops | bytes accessed | tf_op | source)
XLA Modules:
  0.0 221.8 jit_solution(7501520025671325035)
XLA Ops:
  7.2 1.2 broadcast_in_dim.69
  8.4 1.1 broadcast_in_dim.70
  9.5 4.2 %all-to-all-start = ((f32[4,2,16,2048]{3,2,1,0:T(8,128)}), f32[4,2,16,2048]{3,2,1,0:T(8,128)S(1)}, u32[]{:S(2)}, u32[]{:S(2)}) async-start(f32[4,2,16,2048]{3,2,1,0:T(8,128)} %broadcast_in_dim.70), calls=%async_computation | async-start | bytes 2097152 | tf_op jit(solution)/shard_map/all_to_all | solution.py:17
  13.7 0.7 all-gather.3.cloned.1.call-update
  14.5 4.9 %collective-permute-start = (f32[8,2048]{1,0:T(8,128)S(1)}, f32[8,2048]{1,0:T(8,128)S(1)}, u32[]{:S(2)}, u32[]{:S(2)}) collective-permute-start(f32[8,2048]{1,0:T(8,128)S(1)} %bitcast.45), channel_id=1, source_target_pairs={{0,256},{32,288},{64,320},{96,352},{128,384},{160,416},{192,448},{... | collective-permute-start | bytes 196616 | tf_op jit(solution)/shard_map/ppermute | solution.py:79
  19.4 8.5 %all-to-all-done = f32[4,2,16,2048]{3,2,1,0:T(8,128)S(1)} async-done(((f32[4,2,16,2048]{3,2,1,0:T(8,128)}), f32[4,2,16,2048]{3,2,1,0:T(8,128)S(1)}, u32[]{:S(2)}, u32[]{:S(2)}) %all-to-all-start) | async-done | bytes 1048608 | tf_op jit(solution)/shard_map/all_to_all | solution.py:17
  27.8 0.1 fusion.33
  27.9 3.5 %collective-permute-start.1 = (f32[64,2048]{1,0:T(8,128)S(1)}, f32[64,2048]{1,0:T(8,128)S(1)}, u32[]{:S(2)}, u32[]{:S(2)}) collective-permute-start(f32[64,2048]{1,0:T(8,128)S(1)} %bitcast.38), channel_id=1, source_target_pairs={{0,128},{32,160},{64,192},{96,224},{128,0},{160,32},{192,64},{224,... | collective-permute-start | bytes 1572872 | tf_op jit(solution)/shard_map/ppermute | solution.py:79
  31.5 0.3 fusion.43
  31.9 9.9 %collective-permute-done.1 = f32[64,2048]{1,0:T(8,128)S(1)} collective-permute-done((f32[64,2048]{1,0:T(8,128)S(1)}, f32[64,2048]{1,0:T(8,128)S(1)}, u32[]{:S(2)}, u32[]{:S(2)}) %collective-permute-start.1) | collective-permute-done | bytes 524320 | tf_op jit(solution)/shard_map/ppermute | solution.py:79
  41.8 0.3 fusion.44
  42.1 0.1 pad_maximum_fusion.5
  42.2 16.2 %all_to_all.25 = f32[8,16,128]{2,1,0:T(8,128)S(1)} all-to-all(f32[8,16,128]{2,1,0:T(8,128)S(1)} %broadcast_in_dim.71), channel_id=1, replica_groups={{0,1,2,3,4,5,6,7},{8,9,10,11,12,13,14,15},{16,17,18,19,20,21,22,23},{24..., dimensions={0} | all-to-all | bytes 131072 | tf_op jit(solution)/shard_map/all_to_all | solution.py:17
  58.4 4.7 %all-gather.3.cloned.1.call-done = f32[2,64,2048]{2,1,0:T(8,128)} async-done(((f32[2,16,2048]{2,1,0:T(8,128)}), f32[2,64,2048]{2,1,0:T(8,128)}) %all-gather.3.cloned.1.call-update) | async-done | bytes 1048592 | tf_op jit(solution)/shard_map/all_gather | solution.py:104
  63.2 24.5 %psum.28 = f32[16,128]{1,0:T(8,128)S(1)} all-reduce(f32[16,128]{1,0:T(8,128)S(1)} %reduce_sum.36), channel_id=1, replica_groups={{0,8,16,24},{1,9,17,25},{2,10,18,26},{3,11,19,27},{4,12,20,28},{5,13,21..., use_global_device_ids=true, to_apply=%region_1.0 | all-reduce | flops 2048 | bytes 16384 | tf_op jit(solution)/shard_map/psum | solution.py:23
  87.7 0.3 fusion.17
  88.0 0.3 convolution_add_fusion.1
  88.3 1.9 collective-permute-start.2
  90.3 3.0 %collective-permute-start.3 = (f32[64,2048]{1,0:T(8,128)S(1)}, f32[64,2048]{1,0:T(8,128)S(1)}, u32[]{:S(2)}, u32[]{:S(2)}) collective-permute-start(f32[64,2048]{1,0:T(8,128)S(1)} %bitcast.35), channel_id=1, source_target_pairs={{0,128},{32,160},{64,192},{96,224},{128,0},{160,32},{192,64},{224,... | collective-permute-start | bytes 1572872 | tf_op jit(solution)/shard_map/ppermute | solution.py:79
  93.2 2.4 %collective-permute-done.2 = f32[16,2048]{1,0:T(8,128)S(1)} collective-permute-done((f32[16,2048]{1,0:T(8,128)S(1)}, f32[16,2048]{1,0:T(8,128)S(1)}, u32[]{:S(2)}, u32[]{:S(2)}) %collective-permute-start.2) | collective-permute-done | bytes 131104 | tf_op jit(solution)/shard_map/ppermute | solution.py:79
  95.6 0.3 fusion.45
  96.0 10.4 %collective-permute-done.3 = f32[64,2048]{1,0:T(8,128)S(1)} collective-permute-done((f32[64,2048]{1,0:T(8,128)S(1)}, f32[64,2048]{1,0:T(8,128)S(1)}, u32[]{:S(2)}, u32[]{:S(2)}) %collective-permute-start.3) | collective-permute-done | bytes 524320 | tf_op jit(solution)/shard_map/ppermute | solution.py:79
  106.3 0.3 fusion.46
  106.6 0.1 pad_maximum_fusion.6
  106.7 0.6 broadcast_in_dim.72
  107.4 7.2 %all-to-all-start.2 = ((f32[8,16,128]{2,1,0:T(8,128)}), f32[8,16,128]{2,1,0:T(8,128)S(1)}, u32[]{:S(2)}, u32[]{:S(2)}) async-start(f32[8,16,128]{2,1,0:T(8,128)} %broadcast_in_dim.72), calls=%async_computation.2 | async-start | bytes 131072 | tf_op jit(solution)/shard_map/all_to_all | solution.py:17
  114.6 3.2 %all-to-all-done.2 = f32[8,16,128]{2,1,0:T(8,128)S(1)} async-done(((f32[8,16,128]{2,1,0:T(8,128)}), f32[8,16,128]{2,1,0:T(8,128)S(1)}, u32[]{:S(2)}, u32[]{:S(2)}) %all-to-all-start.2) | async-done | bytes 65568 | tf_op jit(solution)/shard_map/all_to_all | solution.py:17
  117.8 11.6 %psum.29 = f32[16,128]{1,0:T(8,128)S(1)} all-reduce(f32[16,128]{1,0:T(8,128)S(1)} %reduce_sum.37), channel_id=1, replica_groups={{0,8,16,24},{1,9,17,25},{2,10,18,26},{3,11,19,27},{4,12,20,28},{5,13,21..., use_global_device_ids=true, to_apply=%region_3.0 | all-reduce | flops 2048 | bytes 16384 | tf_op jit(solution)/shard_map/psum | solution.py:23
  129.4 0.3 fusion.13
  129.7 0.3 convolution_add_fusion
  130.0 2.5 %collective-permute-start.4 = (f32[8,2048]{1,0:T(8,128)S(1)}, f32[8,2048]{1,0:T(8,128)S(1)}, u32[]{:S(2)}, u32[]{:S(2)}) collective-permute-start(f32[8,2048]{1,0:T(8,128)S(1)} %slice.146), channel_id=1, source_target_pairs={{0,256},{32,288},{64,320},{96,352},{128,384},{160,416},{192,448},{... | collective-permute-start | bytes 196616 | tf_op jit(solution)/shard_map/ppermute | solution.py:79
  132.5 3.4 %collective-permute-done.4 = f32[8,2048]{1,0:T(8,128)S(1)} collective-permute-done((f32[8,2048]{1,0:T(8,128)S(1)}, f32[8,2048]{1,0:T(8,128)S(1)}, u32[]{:S(2)}, u32[]{:S(2)}) %collective-permute-start.4) | collective-permute-done | bytes 65568 | tf_op jit(solution)/shard_map/ppermute | solution.py:79
  136.0 10.5 %collective-permute-start.5 = (f32[8,2048]{1,0:T(8,128)S(1)}, f32[8,2048]{1,0:T(8,128)S(1)}, u32[]{:S(2)}, u32[]{:S(2)}) collective-permute-start(f32[8,2048]{1,0:T(8,128)S(1)} %fusion.12), channel_id=1, source_target_pairs={{1,2},{3,4},{5,6},{7,8},{9,10},{11,12},{13,14},{15,16},{17,18},{19... | collective-permute-start | bytes 196616 | tf_op jit(solution)/shard_map/ppermute | solution.py:50
  146.4 1.9 collective-permute-start.6
  148.3 0.1 copy.36
  148.4 0.1 fusion.39
  148.5 0.1 fusion.40
  148.7 0.1 fusion.41
  148.8 2.5 %slice_bitcast_fusion = (f32[256,2048]{1,0:T(8,128)S(1)}, f32[256,2048]{1,0:T(8,128)S(1)}) fusion(f32[2,256,2048]{2,1,0:T(8,128)} %all-gather.5.cloned.1.call-done), kind=kLoop, calls=%fused_computation.4 | loop fusion | bytes 8388608 | tf_op jit(solution)/shard_map/squeeze | solution.py:123
  151.4 0.1 fusion.42
  151.6 0.1 copy.40
  151.6 0.1 copy.41
  151.7 0.4 fusion
  152.2 0.5 copy-done
  152.7 0.9 fusion.47
  153.6 0.7 broadcast_in_dim.78
  154.3 4.6 %all-to-all-start.3 = ((f32[8,8,256]{2,1,0:T(8,128)}), f32[8,8,256]{2,1,0:T(8,128)S(1)}, u32[]{:S(2)}, u32[]{:S(2)}) async-start(f32[8,8,256]{2,1,0:T(8,128)} %broadcast_in_dim.78), calls=%async_computation.3 | async-start | bytes 131072 | tf_op jit(solution)/shard_map/all_to_all | solution.py:17
  158.9 3.1 %all-to-all-done.3 = f32[8,8,256]{2,1,0:T(8,128)S(1)} async-done(((f32[8,8,256]{2,1,0:T(8,128)}), f32[8,8,256]{2,1,0:T(8,128)S(1)}, u32[]{:S(2)}, u32[]{:S(2)}) %all-to-all-start.3) | async-done | bytes 65568 | tf_op jit(solution)/shard_map/all_to_all | solution.py:17
  162.1 13.6 %psum.30 = f32[8,256]{1,0:T(8,128)S(1)} all-reduce(f32[8,256]{1,0:T(8,128)S(1)} %reduce_sum.38), channel_id=1, replica_groups={{0,8,16,24},{1,9,17,25},{2,10,18,26},{3,11,19,27},{4,12,20,28},{5,13,21..., use_global_device_ids=true, to_apply=%region_5.6 | all-reduce | flops 2048 | bytes 16384 | tf_op jit(solution)/shard_map/psum | solution.py:23
  175.7 2.2 convolution_subtract_fusion.1
  177.9 0.9 fusion.48
  178.8 10.0 %all_to_all.26 = f32[8,8,256]{2,1,0:T(8,128)S(1)} all-to-all(f32[8,8,256]{2,1,0:T(8,128)S(1)} %broadcast_in_dim.79), channel_id=1, replica_groups={{0,1,2,3,4,5,6,7},{8,9,10,11,12,13,14,15},{16,17,18,19,20,21,22,23},{24..., dimensions={0} | all-to-all | bytes 131072 | tf_op jit(solution)/shard_map/all_to_all | solution.py:17
  188.9 9.4 %psum.31 = f32[8,256]{1,0:T(8,128)S(1)} all-reduce(f32[8,256]{1,0:T(8,128)S(1)} %reduce_sum.39), channel_id=1, replica_groups={{0,8,16,24},{1,9,17,25},{2,10,18,26},{3,11,19,27},{4,12,20,28},{5,13,21..., use_global_device_ids=true, to_apply=%region_7.8 | all-reduce | flops 2048 | bytes 16384 | tf_op jit(solution)/shard_map/psum | solution.py:23
  198.3 0.6 convolution_subtract_fusion
  198.9 10.9 %collective-permute-start.7 = (f32[8,2048]{1,0:T(8,128)S(1)}, f32[8,2048]{1,0:T(8,128)S(1)}, u32[]{:S(2)}, u32[]{:S(2)}) collective-permute-start(f32[8,2048]{1,0:T(8,128)S(1)} %convolution_subtract_fusion), channel_id=1, source_target_pairs={{1,2},{3,4},{5,6},{7,8},{9,10},{11,12},{13,14},{15,16},{17,18},{19... | collective-permute-start | bytes 196616 | tf_op jit(solution)/shard_map/ppermute | solution.py:50
  209.8 1.9 collective-permute-start.8
  211.7 0.1 copy.50
  211.8 0.1 fusion.35
  211.9 0.1 fusion.36
  212.1 0.1 fusion.37
  212.2 0.1 fusion.38
  212.4 0.6 collective-permute-done.8
  213.1 1.1 fusion.1
  214.2 0.7 subtract_divide_fusion
  (43 shorter events, 0.5 us)
Async XLA Ops:
  7.2 7.3 %copy-start.3 = (f32[8,2,1024]{2,1,0:T(2,128)S(1)}, f32[8,2,1024]{2,1,0:T(2,128)}, u32[]{:S(2)}) copy-start(f32[8,2,1024]{2,1,0:T(2,128)} %param.6) | copy-start | bytes 196612
  8.4 5.3 %copy-start.1 = (f32[2,16,2048]{2,1,0:T(8,128)}, f32[2,16,2048]{2,1,0:T(8,128)S(1)}, u32[]{:S(2)}) copy-start(f32[2,16,2048]{2,1,0:T(8,128)S(1)} %broadcast_in_dim.69) | copy-start | bytes 786436
  9.5 18.4 %all-to-all-start = ((f32[4,2,16,2048]{3,2,1,0:T(8,128)}), f32[4,2,16,2048]{3,2,1,0:T(8,128)S(1)}, u32[]{:S(2)}, u32[]{:S(2)}) async-start(f32[4,2,16,2048]{3,2,1,0:T(8,128)} %broadcast_in_dim.70), calls=%async_computation | async-start | bytes 2097152 | tf_op jit(solution)/shard_map/all_to_all | solution.py:17
  13.7 49.5 %all-gather.3.cloned.1.call-start = ((), (), s32[]{:S(2)}) async-start(), calls=%async_computation.5 | async-start | bytes 1310720 | tf_op jit(solution)/shard_map/all_gather | solution.py:104
  14.4 121.6 %all-gather.5.cloned.1.call-start = ((), (), s32[]{:S(2)}) async-start(), calls=%async_computation.6 | async-start | bytes 5242880 | tf_op jit(solution)/shard_map/all_gather | solution.py:114
  14.5 17.0 %collective-permute-start = (f32[8,2048]{1,0:T(8,128)S(1)}, f32[8,2048]{1,0:T(8,128)S(1)}, u32[]{:S(2)}, u32[]{:S(2)}) collective-permute-start(f32[8,2048]{1,0:T(8,128)S(1)} %bitcast.45), channel_id=1, source_target_pairs={{0,256},{32,288},{64,320},{96,352},{128,384},{160,416},{192,448},{... | collective-permute-start | bytes 196616 | tf_op jit(solution)/shard_map/ppermute | solution.py:79
  27.9 13.8 %collective-permute-start.1 = (f32[64,2048]{1,0:T(8,128)S(1)}, f32[64,2048]{1,0:T(8,128)S(1)}, u32[]{:S(2)}, u32[]{:S(2)}) collective-permute-start(f32[64,2048]{1,0:T(8,128)S(1)} %bitcast.38), channel_id=1, source_target_pairs={{0,128},{32,160},{64,192},{96,224},{128,0},{160,32},{192,64},{224,... | collective-permute-start | bytes 1572872 | tf_op jit(solution)/shard_map/ppermute | solution.py:79
  31.9 58.4 %copy-start.4 = (f32[2,1024]{1,0:T(2,128)S(1)}, f32[2,1024]{1,0:T(2,128)}, u32[]{:S(2)}) copy-start(f32[2,1024]{1,0:T(2,128)} %param.8) | copy-start | bytes 24580
  88.3 7.3 %collective-permute-start.2 = (f32[16,2048]{1,0:T(8,128)S(1)}, f32[16,2048]{1,0:T(8,128)S(1)}, u32[]{:S(2)}, u32[]{:S(2)}) collective-permute-start(f32[16,2048]{1,0:T(8,128)S(1)} %pad_maximum_fusion), channel_id=1, source_target_pairs={{0,256},{32,288},{64,320},{96,352},{128,384},{160,416},{192,448},{... | collective-permute-start | bytes 393224 | tf_op jit(solution)/shard_map/ppermute | solution.py:79
  90.3 16.1 %collective-permute-start.3 = (f32[64,2048]{1,0:T(8,128)S(1)}, f32[64,2048]{1,0:T(8,128)S(1)}, u32[]{:S(2)}, u32[]{:S(2)}) collective-permute-start(f32[64,2048]{1,0:T(8,128)S(1)} %bitcast.35), channel_id=1, source_target_pairs={{0,128},{32,160},{64,192},{96,224},{128,0},{160,32},{192,64},{224,... | collective-permute-start | bytes 1572872 | tf_op jit(solution)/shard_map/ppermute | solution.py:79
  107.4 10.4 %all-to-all-start.2 = ((f32[8,16,128]{2,1,0:T(8,128)}), f32[8,16,128]{2,1,0:T(8,128)S(1)}, u32[]{:S(2)}, u32[]{:S(2)}) async-start(f32[8,16,128]{2,1,0:T(8,128)} %broadcast_in_dim.72), calls=%async_computation.2 | async-start | bytes 131072 | tf_op jit(solution)/shard_map/all_to_all | solution.py:17
  130.0 5.9 %collective-permute-start.4 = (f32[8,2048]{1,0:T(8,128)S(1)}, f32[8,2048]{1,0:T(8,128)S(1)}, u32[]{:S(2)}, u32[]{:S(2)}) collective-permute-start(f32[8,2048]{1,0:T(8,128)S(1)} %slice.146), channel_id=1, source_target_pairs={{0,256},{32,288},{64,320},{96,352},{128,384},{160,416},{192,448},{... | collective-permute-start | bytes 196616 | tf_op jit(solution)/shard_map/ppermute | solution.py:79
  136.0 15.6 %collective-permute-start.5 = (f32[8,2048]{1,0:T(8,128)S(1)}, f32[8,2048]{1,0:T(8,128)S(1)}, u32[]{:S(2)}, u32[]{:S(2)}) collective-permute-start(f32[8,2048]{1,0:T(8,128)S(1)} %fusion.12), channel_id=1, source_target_pairs={{1,2},{3,4},{5,6},{7,8},{9,10},{11,12},{13,14},{15,16},{17,18},{19... | collective-permute-start | bytes 196616 | tf_op jit(solution)/shard_map/ppermute | solution.py:50
  146.4 5.1 %collective-permute-start.6 = (f32[8,2048]{1,0:T(8,128)S(1)}, f32[8,2048]{1,0:T(8,128)S(1)}, u32[]{:S(2)}, u32[]{:S(2)}) collective-permute-start(f32[8,2048]{1,0:T(8,128)S(1)} %fusion.12), channel_id=1, source_target_pairs={{0,1},{1,0},{2,3},{3,2},{4,5},{5,4},{6,7},{7,6},{8,9},{9,8},{10,11... | collective-permute-start | bytes 196616 | tf_op jit(solution)/shard_map/ppermute | solution.py:51
  148.8 2.9 %copy-start.2 = (f32[8,2,1024]{2,1,0:T(2,128)S(1)}, f32[8,2,1024]{2,1,0:T(2,128)}, u32[]{:S(2)}) copy-start(f32[8,2,1024]{2,1,0:T(2,128)} %param.7) | copy-start | bytes 196612
  148.8 2.9 %copy-start.5 = (f32[8]{0:T(128)S(1)}, f32[8]{0:T(128)}, u32[]{:S(2)}) copy-start(f32[8]{0:T(128)} %param.9) | copy-start | bytes 100
  151.4 1.3 copy-start
  154.3 7.8 %all-to-all-start.3 = ((f32[8,8,256]{2,1,0:T(8,128)}), f32[8,8,256]{2,1,0:T(8,128)S(1)}, u32[]{:S(2)}, u32[]{:S(2)}) async-start(f32[8,8,256]{2,1,0:T(8,128)} %broadcast_in_dim.78), calls=%async_computation.3 | async-start | bytes 131072 | tf_op jit(solution)/shard_map/all_to_all | solution.py:17
  198.9 13.5 %collective-permute-start.7 = (f32[8,2048]{1,0:T(8,128)S(1)}, f32[8,2048]{1,0:T(8,128)S(1)}, u32[]{:S(2)}, u32[]{:S(2)}) collective-permute-start(f32[8,2048]{1,0:T(8,128)S(1)} %convolution_subtract_fusion), channel_id=1, source_target_pairs={{1,2},{3,4},{5,6},{7,8},{9,10},{11,12},{13,14},{15,16},{17,18},{19... | collective-permute-start | bytes 196616 | tf_op jit(solution)/shard_map/ppermute | solution.py:50
  209.8 3.1 %collective-permute-start.8 = (f32[8,2048]{1,0:T(8,128)S(1)}, f32[8,2048]{1,0:T(8,128)S(1)}, u32[]{:S(2)}, u32[]{:S(2)}) collective-permute-start(f32[8,2048]{1,0:T(8,128)S(1)} %convolution_subtract_fusion), channel_id=1, source_target_pairs={{0,1},{1,0},{2,3},{3,2},{4,5},{5,4},{6,7},{7,6},{8,9},{9,8},{10,11... | collective-permute-start | bytes 196616 | tf_op jit(solution)/shard_map/ppermute | solution.py:51
Sparse Core Ops, SparseCore 0:
  16.6 46.5 all-gather.2
  65.3 59.2 all-gather.4

commit v9 on v8

--- a/solution.py
+++ b/solution.py
@@ -90,9 +90,14 @@
     return combination(margin[:, :width], halves[0]) + combination(margin[:, width:], halves[1])
 
 
-def project_whole(states, vectors, weight):
-    margin = space_sum(products(vectors, states))[0] * weight
-    return vectors - combination(margin, states)
+def project_whole(parts, vectors, weight):
+    product = jnp.concatenate([products(vectors, part) for part in parts], axis=1)
+    margin = space_sum(product)[0] * weight
+    at = 0
+    for part in parts:
+        vectors = vectors - combination(margin[:, at : at + part.shape[0]], part)
+        at += part.shape[0]
+    return vectors
 
 
 def on_device(occupied, initial, right_side, potential, energies):
@@ -101,7 +106,7 @@
     weight = 1.0 / (lax.axis_size("space") * cells)
     blocks, own = occupied.shape[:2]
     states = occupied.reshape(blocks, own, cells)
-    column = lax.all_gather(states, "band", axis=1, tiled=True, axis_index_groups=BAND_Z)
+    far = (swapped(states, 8), swapped(states, 12))
     ring = copies(states, "band", BAND_Y)
     first, second = ring[:, 0].reshape(-1, cells), ring[:, 1].reshape(-1, cells)
     diagonal = 3.75 + potential[None, :, :] - energies[:, None, None]
@@ -110,8 +115,11 @@
     across_first, second = lax.optimization_barrier((swapped(first, 4), second))
     across_second = swapped(second, 4)
     halves = (first, across_first)
-    margin, column = shared_margin(halves, pair, weight, column)
-    whole = lax.all_gather(column, "band", axis=1, tiled=True, axis_index_groups=BAND_Y)
+    near = halves
+    margin, (far, across_second) = shared_margin(halves, pair, weight, (far, across_second))
+    far = lax.all_gather(
+        jnp.concatenate(far, axis=1), "band", axis=1, tiled=True, axis_index_groups=BAND_Y
+    )
     partial = shared_correction(margin, halves)
     other = swapped(jnp.concatenate([partial[count:], partial[:count]], axis=0), 8)
     pair = pair - partial - other
@@ -119,8 +127,8 @@
     margin, _ = shared_margin(halves, pair, weight)
     partial = shared_correction(margin, halves)
     vectors = pair[:count] - partial[:count] - swapped(partial[count:], 8)
-    vectors, whole = lax.optimization_barrier((vectors, whole))
-    blocks = [lax.optimization_barrier(whole[block]) for block in range(2)]
+    vectors, far = lax.optimization_barrier((vectors, far))
+    blocks = [near + (lax.optimization_barrier(far[0]),), halves + (lax.optimization_barrier(far[1]),)]
     for iteration in range(ITERS):
         if iteration > 0:
             for block in blocks:

time: 223 us -> 220 us (0.987)
  waiting for transfers between devices: 46.9 us -> 39.8 us
  starting transfers between devices: 57.1 us -> 62.3 us
    ppermute x2, starting transfers between devices: 21.4 us -> 15.5 us  [neighbours(): across = lax.ppermute(vectors, 'space', outer)]
    ppermute x5 -> x7, starting transfers between devices: 15.9 us -> 21.6 us  [swapped(): lax.ppermute(x, 'band', [(i, i ^ bit) for i in range(lax.axis_size('band'...]
    all_to_all x3, waiting for transfers between devices: 14.8 us -> 9.45 us  [copies(): return lax.all_to_all(sent, axis, 0, 0, axis_index_groups=groups)]
    all_to_all x3, starting transfers between devices: 16 us -> 21.3 us  [copies(): return lax.all_to_all(sent, axis, 0, 0, axis_index_groups=groups)]
    all_gather x2 -> x1, waiting for transfers between devices: 4.76 us -> 0.02 us  [on_device(): lax.all_gather(jnp.concatenate(far, axis=1), 'band', axis=1, tiled=True,...]
    ppermute x2, waiting for transfers between devices: 0.01 us -> 3.37 us  [neighbours(): across = lax.ppermute(vectors, 'space', outer)]
    ppermute x5 -> x7, waiting for transfers between devices: 26 us -> 26.9 us  [swapped(): lax.ppermute(x, 'band', [(i, i ^ bit) for i in range(lax.axis_size('band'...]
  transfers between devices with their start and end apart: 14 -> 15, of which waited for: 9 -> 7; matrix products, arithmetic and copies ran while one was open for 3% -> 3% of each run, Pallas kernels for 0% -> 0%
where the time goes in v9:
time: 220 us; the launch traced here: 219 us
  blocking collectives  85.4 us (39%)
  starting transfers between devices  62.3 us (28%)
  waiting for transfers between devices  39.8 us (18%)
  between operations  14.6 us (7%)
  local copies, waits for them, and re-layouts  6.91 us (3%)
  matrix products  6.47 us (3%)
  other arithmetic  3.61 us (2%)
    psum x4, blocking collectives, space_sum(): return (lax.psum(near, 'space', axis_index_groups=SPACE_Z), beside)  57.3 us
    all_to_all x2, blocking collectives, copies(): return lax.all_to_all(sent, axis, 0, 0, axis_index_groups=groups)  28.1 us
    ppermute x7, waiting for transfers between devices, swapped(): lax.ppermute(x, 'band', [(i, i ^ bit) for i in range(lax.axis_size('band'...  26.9 us
    ppermute x7, starting transfers between devices, swapped(): lax.ppermute(x, 'band', [(i, i ^ bit) for i in range(lax.axis_size('band'...  21.6 us
    all_to_all x3, starting transfers between devices, copies(): return lax.all_to_all(sent, axis, 0, 0, axis_index_groups=groups)  21.3 us
    ppermute x2, starting transfers between devices, neighbours(): across = lax.ppermute(vectors, 'space', outer)  15.5 us
    all_to_all x3, waiting for transfers between devices, copies(): return lax.all_to_all(sent, axis, 0, 0, axis_index_groups=groups)  9.45 us
  transfers between devices with their start and end apart: 15, of which 7 were waited for; matrix products, arithmetic and copies ran while one was open for 3% of the time, Pallas kernels for 0%

profile of v9, /device:TPU:7, one launch (start us, length us, event | category | flops | bytes accessed | tf_op | source)
XLA Modules:
  0.0 219.1 jit_solution(6705481841399683267)
XLA Ops:
  7.2 1.2 broadcast_in_dim.69
  8.5 18.3 %all_to_all.25 = f32[4,2,16,2048]{3,2,1,0:T(8,128)S(1)} all-to-all(f32[4,2,16,2048]{3,2,1,0:T(8,128)S(1)} %broadcast_in_dim.70), channel_id=1, replica_groups={{0,32,64,96},{128,160,192,224},{256,288,320,352},{384,416,448,480},{1,3..., dimensions={0} | all-to-all | bytes 2097152 | tf_op jit(solution)/shard_map/all_to_all | solution.py:17
  26.8 3.5 %collective-permute-start.1 = (f32[64,2048]{1,0:T(8,128)S(1)}, f32[64,2048]{1,0:T(8,128)S(1)}, u32[]{:S(2)}, u32[]{:S(2)}) collective-permute-start(f32[64,2048]{1,0:T(8,128)S(1)} %bitcast.52), channel_id=1, source_target_pairs={{0,128},{32,160},{64,192},{96,224},{128,0},{160,32},{192,64},{224,... | collective-permute-start | bytes 1572872 | tf_op jit(solution)/shard_map/ppermute | solution.py:79
  30.4 4.9 %collective-permute-start.2 = (f32[2,16,2048]{2,1,0:T(8,128)S(1)}, f32[2,16,2048]{2,1,0:T(8,128)S(1)}, u32[]{:S(2)}, u32[]{:S(2)}) collective-permute-start(f32[2,16,2048]{2,1,0:T(8,128)S(1)} %broadcast_in_dim.69), channel_id=1, source_target_pairs={{0,256},{32,288},{64,320},{96,352},{128,384},{160,416},{192,448},{... | collective-permute-start | bytes 786440 | tf_op jit(solution)/shard_map/ppermute | solution.py:79
  35.3 1.9 collective-permute-start.3
  37.3 3.1 %collective-permute-start = (f32[8,2048]{1,0:T(8,128)S(1)}, f32[8,2048]{1,0:T(8,128)S(1)}, u32[]{:S(2)}, u32[]{:S(2)}) collective-permute-start(f32[8,2048]{1,0:T(8,128)S(1)} %bitcast.63), channel_id=1, source_target_pairs={{0,256},{32,288},{64,320},{96,352},{128,384},{160,416},{192,448},{... | collective-permute-start | bytes 196616 | tf_op jit(solution)/shard_map/ppermute | solution.py:79
  40.4 18.8 %collective-permute-done = f32[8,2048]{1,0:T(8,128)S(1)} collective-permute-done((f32[8,2048]{1,0:T(8,128)S(1)}, f32[8,2048]{1,0:T(8,128)S(1)}, u32[]{:S(2)}, u32[]{:S(2)}) %collective-permute-start) | collective-permute-done | bytes 65568 | tf_op jit(solution)/shard_map/ppermute | solution.py:79
  59.2 1.9 collective-permute-start.4
  61.2 0.3 fusion.49
  61.5 0.3 fusion.50
  61.9 0.6 broadcast_in_dim.71
  62.5 7.5 %all-to-all-start.1 = ((f32[8,16,128]{2,1,0:T(8,128)}), f32[8,16,128]{2,1,0:T(8,128)S(1)}, u32[]{:S(2)}, u32[]{:S(2)}) async-start(f32[8,16,128]{2,1,0:T(8,128)} %broadcast_in_dim.71), calls=%async_computation.1 | async-start | bytes 131072 | tf_op jit(solution)/shard_map/all_to_all | solution.py:17
  70.0 3.1 %all-to-all-done.1 = f32[8,16,128]{2,1,0:T(8,128)S(1)} async-done(((f32[8,16,128]{2,1,0:T(8,128)}), f32[8,16,128]{2,1,0:T(8,128)S(1)}, u32[]{:S(2)}, u32[]{:S(2)}) %all-to-all-start.1) | async-done | bytes 65568 | tf_op jit(solution)/shard_map/all_to_all | solution.py:17
  73.2 18.0 %psum.28 = f32[16,128]{1,0:T(8,128)S(1)} all-reduce(f32[16,128]{1,0:T(8,128)S(1)} %reduce_sum.36), channel_id=1, replica_groups={{0,8,16,24},{1,9,17,25},{2,10,18,26},{3,11,19,27},{4,12,20,28},{5,13,21..., use_global_device_ids=true, to_apply=%region_1.0 | all-reduce | flops 2048 | bytes 16384 | tf_op jit(solution)/shard_map/psum | solution.py:23
  91.2 0.3 fusion.20
  91.5 0.3 convolution_add_fusion.1
  91.7 0.8 pad_maximum_fusion
  92.6 3.9 %collective-permute-start.5 = (f32[16,2048]{1,0:T(8,128)S(1)}, f32[16,2048]{1,0:T(8,128)S(1)}, u32[]{:S(2)}, u32[]{:S(2)}) collective-permute-start(f32[16,2048]{1,0:T(8,128)S(1)} %pad_maximum_fusion.1), channel_id=1, source_target_pairs={{0,256},{32,288},{64,320},{96,352},{128,384},{160,416},{192,448},{... | collective-permute-start | bytes 393224 | tf_op jit(solution)/shard_map/ppermute | solution.py:79
  96.6 4.0 %collective-permute-done.5 = f32[16,2048]{1,0:T(8,128)S(1)} collective-permute-done((f32[16,2048]{1,0:T(8,128)S(1)}, f32[16,2048]{1,0:T(8,128)S(1)}, u32[]{:S(2)}, u32[]{:S(2)}) %collective-permute-start.5) | collective-permute-done | bytes 131104 | tf_op jit(solution)/shard_map/ppermute | solution.py:79
  100.7 0.3 fusion.51
  101.0 0.3 fusion.52
  101.4 0.6 broadcast_in_dim.72
  102.1 9.2 %all-to-all-start.2 = ((f32[8,16,128]{2,1,0:T(8,128)}), f32[8,16,128]{2,1,0:T(8,128)S(1)}, u32[]{:S(2)}, u32[]{:S(2)}) async-start(f32[8,16,128]{2,1,0:T(8,128)} %broadcast_in_dim.72), calls=%async_computation.2 | async-start | bytes 131072 | tf_op jit(solution)/shard_map/all_to_all | solution.py:17
  111.3 3.2 %all-to-all-done.2 = f32[8,16,128]{2,1,0:T(8,128)S(1)} async-done(((f32[8,16,128]{2,1,0:T(8,128)}), f32[8,16,128]{2,1,0:T(8,128)S(1)}, u32[]{:S(2)}, u32[]{:S(2)}) %all-to-all-start.2) | async-done | bytes 65568 | tf_op jit(solution)/shard_map/all_to_all | solution.py:17
  114.5 12.0 %psum.29 = f32[16,128]{1,0:T(8,128)S(1)} all-reduce(f32[16,128]{1,0:T(8,128)S(1)} %reduce_sum.37), channel_id=1, replica_groups={{0,8,16,24},{1,9,17,25},{2,10,18,26},{3,11,19,27},{4,12,20,28},{5,13,21..., use_global_device_ids=true, to_apply=%region_3.0 | all-reduce | flops 2048 | bytes 16384 | tf_op jit(solution)/shard_map/psum | solution.py:23
  126.5 0.3 fusion.16
  126.8 0.3 convolution_add_fusion
  127.1 2.3 %collective-permute-start.6 = (f32[8,2048]{1,0:T(8,128)S(1)}, f32[8,2048]{1,0:T(8,128)S(1)}, u32[]{:S(2)}, u32[]{:S(2)}) collective-permute-start(f32[8,2048]{1,0:T(8,128)S(1)} %slice.170), channel_id=1, source_target_pairs={{0,256},{32,288},{64,320},{96,352},{128,384},{160,416},{192,448},{... | collective-permute-start | bytes 196616 | tf_op jit(solution)/shard_map/ppermute | solution.py:79
  129.4 4.0 %collective-permute-done.6 = f32[8,2048]{1,0:T(8,128)S(1)} collective-permute-done((f32[8,2048]{1,0:T(8,128)S(1)}, f32[8,2048]{1,0:T(8,128)S(1)}, u32[]{:S(2)}, u32[]{:S(2)}) %collective-permute-start.6) | collective-permute-done | bytes 65568 | tf_op jit(solution)/shard_map/ppermute | solution.py:79
  133.5 9.2 %collective-permute-start.7 = (f32[8,2048]{1,0:T(8,128)S(1)}, f32[8,2048]{1,0:T(8,128)S(1)}, u32[]{:S(2)}, u32[]{:S(2)}) collective-permute-start(f32[8,2048]{1,0:T(8,128)S(1)} %fusion.15), channel_id=1, source_target_pairs={{1,2},{3,4},{5,6},{7,8},{9,10},{11,12},{13,14},{15,16},{17,18},{19... | collective-permute-start | bytes 196616 | tf_op jit(solution)/shard_map/ppermute | solution.py:50
  142.7 1.9 collective-permute-start.8
  144.7 0.1 fusion.48
  144.9 0.1 fusion.47
  145.0 0.1 fusion.46
  145.2 1.7 slice_bitcast_fusion.1
  146.9 0.1 fusion.45
  147.2 0.5 fusion.3
  147.7 0.3 fusion.54
  148.0 0.3 fusion.53
  148.4 0.5 fusion.55
  149.0 0.6 broadcast_in_dim.78
  149.6 4.6 %all-to-all-start.3 = ((f32[8,8,256]{2,1,0:T(8,128)}), f32[8,8,256]{2,1,0:T(8,128)S(1)}, u32[]{:S(2)}, u32[]{:S(2)}) async-start(f32[8,8,256]{2,1,0:T(8,128)} %broadcast_in_dim.78), calls=%async_computation.3 | async-start | bytes 131072 | tf_op jit(solution)/shard_map/all_to_all | solution.py:17
  154.3 3.1 %all-to-all-done.3 = f32[8,8,256]{2,1,0:T(8,128)S(1)} async-done(((f32[8,8,256]{2,1,0:T(8,128)}), f32[8,8,256]{2,1,0:T(8,128)S(1)}, u32[]{:S(2)}, u32[]{:S(2)}) %all-to-all-start.3) | async-done | bytes 65568 | tf_op jit(solution)/shard_map/all_to_all | solution.py:17
  157.4 13.3 %psum.30 = f32[8,256]{1,0:T(8,128)S(1)} all-reduce(f32[8,256]{1,0:T(8,128)S(1)} %reduce_sum.38), channel_id=1, replica_groups={{0,8,16,24},{1,9,17,25},{2,10,18,26},{3,11,19,27},{4,12,20,28},{5,13,21..., use_global_device_ids=true, to_apply=%region_5.6 | all-reduce | flops 2048 | bytes 16384 | tf_op jit(solution)/shard_map/psum | solution.py:23
  170.8 0.4 fusion.27
  171.1 0.3 convolution_subtract_fusion.2
  171.4 0.4 copy-done.2
  171.8 0.3 fusion
  172.1 0.3 fusion.57
  172.4 0.3 fusion.56
  172.7 0.5 fusion.58
  173.3 9.8 %all_to_all.26 = f32[8,8,256]{2,1,0:T(8,128)S(1)} all-to-all(f32[8,8,256]{2,1,0:T(8,128)S(1)} %broadcast_in_dim.79), channel_id=1, replica_groups={{0,1,2,3,4,5,6,7},{8,9,10,11,12,13,14,15},{16,17,18,19,20,21,22,23},{24..., dimensions={0} | all-to-all | bytes 131072 | tf_op jit(solution)/shard_map/all_to_all | solution.py:17
  183.2 14.0 %psum.31 = f32[8,256]{1,0:T(8,128)S(1)} all-reduce(f32[8,256]{1,0:T(8,128)S(1)} %reduce_sum.39), channel_id=1, replica_groups={{0,8,16,24},{1,9,17,25},{2,10,18,26},{3,11,19,27},{4,12,20,28},{5,13,21..., use_global_device_ids=true, to_apply=%region_7.8 | all-reduce | flops 2048 | bytes 16384 | tf_op jit(solution)/shard_map/psum | solution.py:23
  197.2 0.4 fusion.22
  197.5 0.3 fusion.24
  197.8 0.3 fusion.2
  198.1 6.3 %collective-permute-start.9 = (f32[8,2048]{1,0:T(8,128)S(1)}, f32[8,2048]{1,0:T(8,128)S(1)}, u32[]{:S(2)}, u32[]{:S(2)}) collective-permute-start(f32[8,2048]{1,0:T(8,128)S(1)} %fusion.2), channel_id=1, source_target_pairs={{1,2},{3,4},{5,6},{7,8},{9,10},{11,12},{13,14},{15,16},{17,18},{19... | collective-permute-start | bytes 196616 | tf_op jit(solution)/shard_map/ppermute | solution.py:50
  204.4 1.9 collective-permute-start.10
  206.5 0.1 fusion.43
  206.6 0.1 fusion.42
  206.8 0.1 fusion.41
  206.9 3.4 %collective-permute-done.9 = f32[8,2048]{1,0:T(8,128)S(1)} collective-permute-done((f32[8,2048]{1,0:T(8,128)S(1)}, f32[8,2048]{1,0:T(8,128)S(1)}, u32[]{:S(2)}, u32[]{:S(2)}) %collective-permute-start.9) | collective-permute-done | bytes 65568 | tf_op jit(solution)/shard_map/ppermute | solution.py:50
  210.4 1.1 fusion.4
  211.5 0.7 subtract_divide_fusion
  (65 shorter events, 1.3 us)
Async XLA Ops:
  8.4 28.8 %copy-start.7 = (f32[8,2,1024]{2,1,0:T(2,128)S(1)}, f32[8,2,1024]{2,1,0:T(2,128)}, u32[]{:S(2)}) copy-start(f32[8,2,1024]{2,1,0:T(2,128)} %param.6) | copy-start | bytes 196612
  26.8 32.4 %collective-permute-start.1 = (f32[64,2048]{1,0:T(8,128)S(1)}, f32[64,2048]{1,0:T(8,128)S(1)}, u32[]{:S(2)}, u32[]{:S(2)}) collective-permute-start(f32[64,2048]{1,0:T(8,128)S(1)} %bitcast.52), channel_id=1, source_target_pairs={{0,128},{32,160},{64,192},{96,224},{128,0},{160,32},{192,64},{224,... | collective-permute-start | bytes 1572872 | tf_op jit(solution)/shard_map/ppermute | solution.py:79
  30.4 42.8 %collective-permute-start.2 = (f32[2,16,2048]{2,1,0:T(8,128)S(1)}, f32[2,16,2048]{2,1,0:T(8,128)S(1)}, u32[]{:S(2)}, u32[]{:S(2)}) collective-permute-start(f32[2,16,2048]{2,1,0:T(8,128)S(1)} %broadcast_in_dim.69), channel_id=1, source_target_pairs={{0,256},{32,288},{64,320},{96,352},{128,384},{160,416},{192,448},{... | collective-permute-start | bytes 786440 | tf_op jit(solution)/shard_map/ppermute | solution.py:79
  35.3 37.9 %collective-permute-start.3 = (f32[2,16,2048]{2,1,0:T(8,128)S(1)}, f32[2,16,2048]{2,1,0:T(8,128)S(1)}, u32[]{:S(2)}, u32[]{:S(2)}) collective-permute-start(f32[2,16,2048]{2,1,0:T(8,128)S(1)} %broadcast_in_dim.69), channel_id=1, source_target_pairs={{0,384},{32,416},{64,448},{96,480},{128,256},{160,288},{192,320},{... | collective-permute-start | bytes 786440 | tf_op jit(solution)/shard_map/ppermute | solution.py:79
  37.3 21.9 %collective-permute-start = (f32[8,2048]{1,0:T(8,128)S(1)}, f32[8,2048]{1,0:T(8,128)S(1)}, u32[]{:S(2)}, u32[]{:S(2)}) collective-permute-start(f32[8,2048]{1,0:T(8,128)S(1)} %bitcast.63), channel_id=1, source_target_pairs={{0,256},{32,288},{64,320},{96,352},{128,384},{160,416},{192,448},{... | collective-permute-start | bytes 196616 | tf_op jit(solution)/shard_map/ppermute | solution.py:79
  59.2 33.4 %copy-start = (f32[64,2048]{1,0:T(8,128)}, f32[64,2048]{1,0:T(8,128)S(1)}, u32[]{:S(2)}) copy-start(f32[64,2048]{1,0:T(8,128)S(1)} %collective-permute-done.1) | copy-start | bytes 1572868
  59.2 13.9 %collective-permute-start.4 = (f32[64,2048]{1,0:T(8,128)S(1)}, f32[64,2048]{1,0:T(8,128)S(1)}, u32[]{:S(2)}, u32[]{:S(2)}) collective-permute-start(f32[64,2048]{1,0:T(8,128)S(1)} %bitcast.47), channel_id=1, source_target_pairs={{0,128},{32,160},{64,192},{96,224},{128,0},{160,32},{192,64},{224,... | collective-permute-start | bytes 1572872 | tf_op jit(solution)/shard_map/ppermute | solution.py:79
  61.8 34.8 %copy-start.8 = (f32[2,1024]{1,0:T(2,128)S(1)}, f32[2,1024]{1,0:T(2,128)}, u32[]{:S(2)}) copy-start(f32[2,1024]{1,0:T(2,128)} %param.8) | copy-start | bytes 24580
  62.5 10.6 %all-to-all-start.1 = ((f32[8,16,128]{2,1,0:T(8,128)}), f32[8,16,128]{2,1,0:T(8,128)S(1)}, u32[]{:S(2)}, u32[]{:S(2)}) async-start(f32[8,16,128]{2,1,0:T(8,128)} %broadcast_in_dim.71), calls=%async_computation.1 | async-start | bytes 131072 | tf_op jit(solution)/shard_map/all_to_all | solution.py:17
  70.0 63.5 %all-gather.2.cloned.1.call-start = ((), (), s32[]{:S(2)}) async-start(), calls=%async_computation.5 | async-start | bytes 2621440 | tf_op jit(solution)/shard_map/all_gather | solution.py:120
  73.2 53.3 %copy-start.3 = (f32[64,2048]{1,0:T(8,128)}, f32[64,2048]{1,0:T(8,128)S(1)}, u32[]{:S(2)}) copy-start(f32[64,2048]{1,0:T(8,128)S(1)} %collective-permute-done.4) | copy-start | bytes 1572868
  92.6 8.0 %collective-permute-start.5 = (f32[16,2048]{1,0:T(8,128)S(1)}, f32[16,2048]{1,0:T(8,128)S(1)}, u32[]{:S(2)}, u32[]{:S(2)}) collective-permute-start(f32[16,2048]{1,0:T(8,128)S(1)} %pad_maximum_fusion.1), channel_id=1, source_target_pairs={{0,256},{32,288},{64,320},{96,352},{128,384},{160,416},{192,448},{... | collective-permute-start | bytes 393224 | tf_op jit(solution)/shard_map/ppermute | solution.py:79
  102.1 12.4 %all-to-all-start.2 = ((f32[8,16,128]{2,1,0:T(8,128)}), f32[8,16,128]{2,1,0:T(8,128)S(1)}, u32[]{:S(2)}, u32[]{:S(2)}) async-start(f32[8,16,128]{2,1,0:T(8,128)} %broadcast_in_dim.72), calls=%async_computation.2 | async-start | bytes 131072 | tf_op jit(solution)/shard_map/all_to_all | solution.py:17
  127.1 6.3 %collective-permute-start.6 = (f32[8,2048]{1,0:T(8,128)S(1)}, f32[8,2048]{1,0:T(8,128)S(1)}, u32[]{:S(2)}, u32[]{:S(2)}) collective-permute-start(f32[8,2048]{1,0:T(8,128)S(1)} %slice.170), channel_id=1, source_target_pairs={{0,256},{32,288},{64,320},{96,352},{128,384},{160,416},{192,448},{... | collective-permute-start | bytes 196616 | tf_op jit(solution)/shard_map/ppermute | solution.py:79
  133.5 13.6 %collective-permute-start.7 = (f32[8,2048]{1,0:T(8,128)S(1)}, f32[8,2048]{1,0:T(8,128)S(1)}, u32[]{:S(2)}, u32[]{:S(2)}) collective-permute-start(f32[8,2048]{1,0:T(8,128)S(1)} %fusion.15), channel_id=1, source_target_pairs={{1,2},{3,4},{5,6},{7,8},{9,10},{11,12},{13,14},{15,16},{17,18},{19... | collective-permute-start | bytes 196616 | tf_op jit(solution)/shard_map/ppermute | solution.py:50
  142.7 4.3 %collective-permute-start.8 = (f32[8,2048]{1,0:T(8,128)S(1)}, f32[8,2048]{1,0:T(8,128)S(1)}, u32[]{:S(2)}, u32[]{:S(2)}) collective-permute-start(f32[8,2048]{1,0:T(8,128)S(1)} %fusion.15), channel_id=1, source_target_pairs={{0,1},{1,0},{2,3},{3,2},{4,5},{5,4},{6,7},{7,6},{8,9},{9,8},{10,11... | collective-permute-start | bytes 196616 | tf_op jit(solution)/shard_map/ppermute | solution.py:51
  145.1 2.1 copy-start.6
  145.1 2.1 copy-start.9
  145.2 2.6 %copy-start.1 = (f32[64,2048]{1,0:T(8,128)S(1)}, f32[64,2048]{1,0:T(8,128)}, u32[]{:S(2)}) copy-start(f32[64,2048]{1,0:T(8,128)} %copy-done) | copy-start | bytes 1572868
  149.6 7.8 %all-to-all-start.3 = ((f32[8,8,256]{2,1,0:T(8,128)}), f32[8,8,256]{2,1,0:T(8,128)S(1)}, u32[]{:S(2)}, u32[]{:S(2)}) async-start(f32[8,8,256]{2,1,0:T(8,128)} %broadcast_in_dim.78), calls=%async_computation.3 | async-start | bytes 131072 | tf_op jit(solution)/shard_map/all_to_all | solution.py:17
  170.7 1.0 copy-start.2
  170.8 1.3 copy-start.4
  171.8 25.7 %copy-start.5 = (f32[64,2048]{1,0:T(8,128)S(1)}, f32[64,2048]{1,0:T(8,128)}, u32[]{:S(2)}) copy-start(f32[64,2048]{1,0:T(8,128)} %copy-done.3) | copy-start | bytes 1572868
  198.1 12.2 %collective-permute-start.9 = (f32[8,2048]{1,0:T(8,128)S(1)}, f32[8,2048]{1,0:T(8,128)S(1)}, u32[]{:S(2)}, u32[]{:S(2)}) collective-permute-start(f32[8,2048]{1,0:T(8,128)S(1)} %fusion.2), channel_id=1, source_target_pairs={{1,2},{3,4},{5,6},{7,8},{9,10},{11,12},{13,14},{15,16},{17,18},{19... | collective-permute-start | bytes 196616 | tf_op jit(solution)/shard_map/ppermute | solution.py:50
  204.4 5.9 %collective-permute-start.10 = (f32[8,2048]{1,0:T(8,128)S(1)}, f32[8,2048]{1,0:T(8,128)S(1)}, u32[]{:S(2)}, u32[]{:S(2)}) collective-permute-start(f32[8,2048]{1,0:T(8,128)S(1)} %fusion.2), channel_id=1, source_target_pairs={{0,1},{1,0},{2,3},{3,2},{4,5},{5,4},{6,7},{7,6},{8,9},{9,8},{10,11... | collective-permute-start | bytes 196616 | tf_op jit(solution)/shard_map/ppermute | solution.py:51
Sparse Core Ops, SparseCore 0:
  92.7 35.6 all-gather.1

commit v10 on v9

--- a/solution.py
+++ b/solution.py
@@ -17,10 +17,9 @@
     return lax.all_to_all(sent, axis, 0, 0, axis_index_groups=groups)
 
 
-def space_sum(x, beside=None):
+def space_sum(x):
     near = jnp.sum(copies(x, "space", SPACE_PLANE), axis=0)
-    near, beside = lax.optimization_barrier((near, beside))
-    return lax.psum(near, "space", axis_index_groups=SPACE_Z), beside
+    return lax.psum(near, "space", axis_index_groups=SPACE_Z)
 
 
 def products(vectors, states):
@@ -79,10 +78,9 @@
     return lax.ppermute(x, "band", [(i, i ^ bit) for i in range(lax.axis_size("band"))])
 
 
-def shared_margin(halves, pair, weight, beside=None):
+def shared_margin(halves, pair, weight):
     product = jnp.concatenate([products(pair, half) for half in halves], axis=1)
-    total, beside = space_sum(product, beside)
-    return total * weight, beside
+    return space_sum(product) * weight
 
 
 def shared_correction(margin, halves):
@@ -92,7 +90,7 @@
 
 def project_whole(parts, vectors, weight):
     product = jnp.concatenate([products(vectors, part) for part in parts], axis=1)
-    margin = space_sum(product)[0] * weight
+    margin = space_sum(product) * weight
     at = 0
     for part in parts:
         vectors = vectors - combination(margin[:, at : at + part.shape[0]], part)
@@ -106,17 +104,18 @@
     weight = 1.0 / (lax.axis_size("space") * cells)
     blocks, own = occupied.shape[:2]
     states = occupied.reshape(blocks, own, cells)
-    far = (swapped(states, 8), swapped(states, 12))
     ring = copies(states, "band", BAND_Y)
     first, second = ring[:, 0].reshape(-1, cells), ring[:, 1].reshape(-1, cells)
     diagonal = 3.75 + potential[None, :, :] - energies[:, None, None]
     vectors = initial.reshape(count, cells)
     pair = jnp.concatenate([vectors, swapped(vectors, 8)], axis=0)
-    across_first, second = lax.optimization_barrier((swapped(first, 4), second))
+    across_first, second, states = lax.optimization_barrier((swapped(first, 4), second, states))
     across_second = swapped(second, 4)
+    far = (swapped(states, 8), swapped(states, 12))
     halves = (first, across_first)
     near = halves
-    margin, (far, across_second) = shared_margin(halves, pair, weight, (far, across_second))
+    margin = shared_margin(halves, pair, weight)
+    margin, far, across_second = lax.optimization_barrier((margin, far, across_second))
     far = lax.all_gather(
         jnp.concatenate(far, axis=1), "band", axis=1, tiled=True, axis_index_groups=BAND_Y
     )
@@ -124,7 +123,7 @@
     other = swapped(jnp.concatenate([partial[count:], partial[:count]], axis=0), 8)
     pair = pair - partial - other
     halves = (second, across_second)
-    margin, _ = shared_margin(halves, pair, weight)
+    margin = shared_margin(halves, pair, weight)
     partial = shared_correction(margin, halves)
     vectors = pair[:count] - partial[:count] - swapped(partial[count:], 8)
     vectors, far = lax.optimization_barrier((vectors, far))

time: 220 us -> 218 us (level)
  starting transfers between devices: 62.3 us -> 71.7 us
  blocking collectives: 85.4 us -> 76.9 us
  waiting for transfers between devices: 39.8 us -> 36.2 us
    all_to_all x2 -> x1, blocking collectives: 28.1 us -> 10 us  [copies(): return lax.all_to_all(sent, axis, 0, 0, axis_index_groups=groups)]
    ppermute x7, waiting for transfers between devices: 26.9 us -> 16.3 us  [swapped(): lax.ppermute(x, 'band', [(i, i ^ bit) for i in range(lax.axis_size('band'...]
    psum x4, blocking collectives: 57.3 us -> 66.9 us  [space_sum(): return lax.psum(near, 'space', axis_index_groups=SPACE_Z)]
    ppermute x7, starting transfers between devices: 21.6 us -> 30.2 us  [swapped(): lax.ppermute(x, 'band', [(i, i ^ bit) for i in range(lax.axis_size('band'...]
    all_to_all x3 -> x4, waiting for transfers between devices: 9.45 us -> 15.5 us  [copies(): return lax.all_to_all(sent, axis, 0, 0, axis_index_groups=groups)]
    all_to_all x3 -> x4, starting transfers between devices: 21.3 us -> 22.8 us  [copies(): return lax.all_to_all(sent, axis, 0, 0, axis_index_groups=groups)]
  transfers between devices with their start and end apart: 15 -> 16, of which waited for: 7 -> 8; matrix products, arithmetic and copies ran while one was open for 3% -> 3% of each run, Pallas kernels for 0% -> 0%
where the time goes in v10:
time: 218 us; the launch traced here: 217 us
  blocking collectives  76.9 us (35%)
  starting transfers between devices  71.7 us (33%)
  waiting for transfers between devices  36.2 us (17%)
  between operations  14.6 us (7%)
  local copies, waits for them, and re-layouts  7.96 us (4%)
  matrix products  6.45 us (3%)
  other arithmetic  3.61 us (2%)
    psum x4, blocking collectives, space_sum(): return lax.psum(near, 'space', axis_index_groups=SPACE_Z)  66.9 us
    ppermute x7, starting transfers between devices, swapped(): lax.ppermute(x, 'band', [(i, i ^ bit) for i in range(lax.axis_size('band'...  30.2 us
    all_to_all x4, starting transfers between devices, copies(): return lax.all_to_all(sent, axis, 0, 0, axis_index_groups=groups)  22.8 us
    ppermute x7, waiting for transfers between devices, swapped(): lax.ppermute(x, 'band', [(i, i ^ bit) for i in range(lax.axis_size('band'...  16.3 us
    all_to_all x4, waiting for transfers between devices, copies(): return lax.all_to_all(sent, axis, 0, 0, axis_index_groups=groups)  15.5 us
    ppermute x2, starting transfers between devices, neighbours(): across = lax.ppermute(vectors, 'space', outer)  15 us
    all_to_all x1, blocking collectives, copies(): return lax.all_to_all(sent, axis, 0, 0, axis_index_groups=groups)  10 us
  transfers between devices with their start and end apart: 16, of which 8 were waited for; matrix products, arithmetic and copies ran while one was open for 3% of the time, Pallas kernels for 0%

profile of v10, /device:TPU:7, one launch (start us, length us, event | category | flops | bytes accessed | tf_op | source)
XLA Modules:
  0.0 217.5 jit_solution(12338399992453234358)
XLA Ops:
  7.2 1.2 broadcast_in_dim.69
  8.4 1.1 broadcast_in_dim.70
  9.5 4.2 %all-to-all-start = ((f32[4,2,16,2048]{3,2,1,0:T(8,128)}), f32[4,2,16,2048]{3,2,1,0:T(8,128)S(1)}, u32[]{:S(2)}, u32[]{:S(2)}) async-start(f32[4,2,16,2048]{3,2,1,0:T(8,128)} %broadcast_in_dim.70), calls=%async_computation | async-start | bytes 2097152 | tf_op jit(solution)/shard_map/all_to_all | solution.py:17
  13.7 4.9 %collective-permute-start = (f32[8,2048]{1,0:T(8,128)S(1)}, f32[8,2048]{1,0:T(8,128)S(1)}, u32[]{:S(2)}, u32[]{:S(2)}) collective-permute-start(f32[8,2048]{1,0:T(8,128)S(1)} %bitcast.63), channel_id=1, source_target_pairs={{0,256},{32,288},{64,320},{96,352},{128,384},{160,416},{192,448},{... | collective-permute-start | bytes 196616 | tf_op jit(solution)/shard_map/ppermute | solution.py:78
  18.6 9.2 %all-to-all-done = f32[4,2,16,2048]{3,2,1,0:T(8,128)S(1)} async-done(((f32[4,2,16,2048]{3,2,1,0:T(8,128)}), f32[4,2,16,2048]{3,2,1,0:T(8,128)S(1)}, u32[]{:S(2)}, u32[]{:S(2)}) %all-to-all-start) | async-done | bytes 1048608 | tf_op jit(solution)/shard_map/all_to_all | solution.py:17
  27.9 3.5 %collective-permute-start.1 = (f32[64,2048]{1,0:T(8,128)S(1)}, f32[64,2048]{1,0:T(8,128)S(1)}, u32[]{:S(2)}, u32[]{:S(2)}) collective-permute-start(f32[64,2048]{1,0:T(8,128)S(1)} %bitcast.52), channel_id=1, source_target_pairs={{0,128},{32,160},{64,192},{96,224},{128,0},{160,32},{192,64},{224,... | collective-permute-start | bytes 1572872 | tf_op jit(solution)/shard_map/ppermute | solution.py:78
  31.5 0.3 fusion.49
  31.9 9.9 %collective-permute-done.1 = f32[64,2048]{1,0:T(8,128)S(1)} collective-permute-done((f32[64,2048]{1,0:T(8,128)S(1)}, f32[64,2048]{1,0:T(8,128)S(1)}, u32[]{:S(2)}, u32[]{:S(2)}) %collective-permute-start.1) | collective-permute-done | bytes 524320 | tf_op jit(solution)/shard_map/ppermute | solution.py:78
  41.8 3.2 %collective-permute-start.4 = (f32[64,2048]{1,0:T(8,128)S(1)}, f32[64,2048]{1,0:T(8,128)S(1)}, u32[]{:S(2)}, u32[]{:S(2)}) collective-permute-start(f32[64,2048]{1,0:T(8,128)S(1)} %bitcast.47), channel_id=1, source_target_pairs={{0,128},{32,160},{64,192},{96,224},{128,0},{160,32},{192,64},{224,... | collective-permute-start | bytes 1572872 | tf_op jit(solution)/shard_map/ppermute | solution.py:78
  44.9 0.3 fusion.50
  45.3 0.6 broadcast_in_dim.71
  46.0 7.5 %all-to-all-start.1 = ((f32[8,16,128]{2,1,0:T(8,128)}), f32[8,16,128]{2,1,0:T(8,128)S(1)}, u32[]{:S(2)}, u32[]{:S(2)}) async-start(f32[8,16,128]{2,1,0:T(8,128)} %broadcast_in_dim.71), calls=%async_computation.1 | async-start | bytes 131072 | tf_op jit(solution)/shard_map/all_to_all | solution.py:17
  53.5 4.9 %collective-permute-start.2 = (f32[2,16,2048]{2,1,0:T(8,128)S(1)}, f32[2,16,2048]{2,1,0:T(8,128)S(1)}, u32[]{:S(2)}, u32[]{:S(2)}) collective-permute-start(f32[2,16,2048]{2,1,0:T(8,128)S(1)} %broadcast_in_dim.69), channel_id=1, source_target_pairs={{0,256},{32,288},{64,320},{96,352},{128,384},{160,416},{192,448},{... | collective-permute-start | bytes 786440 | tf_op jit(solution)/shard_map/ppermute | solution.py:78
  58.4 1.9 collective-permute-start.3
  60.3 22.3 %psum.28 = f32[16,128]{1,0:T(8,128)S(1)} all-reduce(f32[16,128]{1,0:T(8,128)S(1)} %reduce_sum.36), channel_id=1, replica_groups={{0,8,16,24},{1,9,17,25},{2,10,18,26},{3,11,19,27},{4,12,20,28},{5,13,21..., use_global_device_ids=true, to_apply=%region_1.0 | all-reduce | flops 2048 | bytes 16384 | tf_op jit(solution)/shard_map/psum | solution.py:22
  82.7 0.3 fusion.19
  83.0 0.3 convolution_add_fusion.1
  83.2 0.8 pad_maximum_fusion
  84.1 9.2 %collective-permute-start.5 = (f32[16,2048]{1,0:T(8,128)S(1)}, f32[16,2048]{1,0:T(8,128)S(1)}, u32[]{:S(2)}, u32[]{:S(2)}) collective-permute-start(f32[16,2048]{1,0:T(8,128)S(1)} %pad_maximum_fusion.1), channel_id=1, source_target_pairs={{0,256},{32,288},{64,320},{96,352},{128,384},{160,416},{192,448},{... | collective-permute-start | bytes 393224 | tf_op jit(solution)/shard_map/ppermute | solution.py:78
  93.3 2.3 %collective-permute-done.5 = f32[16,2048]{1,0:T(8,128)S(1)} collective-permute-done((f32[16,2048]{1,0:T(8,128)S(1)}, f32[16,2048]{1,0:T(8,128)S(1)}, u32[]{:S(2)}, u32[]{:S(2)}) %collective-permute-start.5) | collective-permute-done | bytes 131104 | tf_op jit(solution)/shard_map/ppermute | solution.py:78
  95.7 0.3 fusion.51
  96.0 0.3 fusion.52
  96.4 0.6 broadcast_in_dim.72
  97.1 6.8 %all-to-all-start.2 = ((f32[8,16,128]{2,1,0:T(8,128)}), f32[8,16,128]{2,1,0:T(8,128)S(1)}, u32[]{:S(2)}, u32[]{:S(2)}) async-start(f32[8,16,128]{2,1,0:T(8,128)} %broadcast_in_dim.72), calls=%async_computation.2 | async-start | bytes 131072 | tf_op jit(solution)/shard_map/all_to_all | solution.py:17
  103.9 3.1 %all-to-all-done.2 = f32[8,16,128]{2,1,0:T(8,128)S(1)} async-done(((f32[8,16,128]{2,1,0:T(8,128)}), f32[8,16,128]{2,1,0:T(8,128)S(1)}, u32[]{:S(2)}, u32[]{:S(2)}) %all-to-all-start.2) | async-done | bytes 65568 | tf_op jit(solution)/shard_map/all_to_all | solution.py:17
  107.1 18.9 %psum.29 = f32[16,128]{1,0:T(8,128)S(1)} all-reduce(f32[16,128]{1,0:T(8,128)S(1)} %reduce_sum.37), channel_id=1, replica_groups={{0,8,16,24},{1,9,17,25},{2,10,18,26},{3,11,19,27},{4,12,20,28},{5,13,21..., use_global_device_ids=true, to_apply=%region_3.0 | all-reduce | flops 2048 | bytes 16384 | tf_op jit(solution)/shard_map/psum | solution.py:22
  126.0 0.3 fusion.16
  126.2 0.3 convolution_add_fusion
  126.5 2.6 %collective-permute-start.6 = (f32[8,2048]{1,0:T(8,128)S(1)}, f32[8,2048]{1,0:T(8,128)S(1)}, u32[]{:S(2)}, u32[]{:S(2)}) collective-permute-start(f32[8,2048]{1,0:T(8,128)S(1)} %slice.168), channel_id=1, source_target_pairs={{0,256},{32,288},{64,320},{96,352},{128,384},{160,416},{192,448},{... | collective-permute-start | bytes 196616 | tf_op jit(solution)/shard_map/ppermute | solution.py:78
  129.1 4.0 %collective-permute-done.6 = f32[8,2048]{1,0:T(8,128)S(1)} collective-permute-done((f32[8,2048]{1,0:T(8,128)S(1)}, f32[8,2048]{1,0:T(8,128)S(1)}, u32[]{:S(2)}, u32[]{:S(2)}) %collective-permute-start.6) | collective-permute-done | bytes 65568 | tf_op jit(solution)/shard_map/ppermute | solution.py:78
  133.2 8.0 %collective-permute-start.7 = (f32[8,2048]{1,0:T(8,128)S(1)}, f32[8,2048]{1,0:T(8,128)S(1)}, u32[]{:S(2)}, u32[]{:S(2)}) collective-permute-start(f32[8,2048]{1,0:T(8,128)S(1)} %fusion.15), channel_id=1, source_target_pairs={{1,2},{3,4},{5,6},{7,8},{9,10},{11,12},{13,14},{15,16},{17,18},{19... | collective-permute-start | bytes 196616 | tf_op jit(solution)/shard_map/ppermute | solution.py:49
  141.2 1.9 collective-permute-start.8
  143.3 0.1 fusion.47
  143.4 0.1 fusion.46
  143.6 1.7 slice_bitcast_fusion.1
  145.5 1.4 collective-permute-done.7
  147.1 0.5 fusion.3
  147.6 0.3 fusion.54
  147.9 0.3 fusion.53
  148.2 0.5 fusion.55
  148.8 0.6 broadcast_in_dim.78
  149.5 4.3 %all-to-all-start.3 = ((f32[8,8,256]{2,1,0:T(8,128)}), f32[8,8,256]{2,1,0:T(8,128)S(1)}, u32[]{:S(2)}, u32[]{:S(2)}) async-start(f32[8,8,256]{2,1,0:T(8,128)} %broadcast_in_dim.78), calls=%async_computation.3 | async-start | bytes 131072 | tf_op jit(solution)/shard_map/all_to_all | solution.py:17
  153.7 3.1 %all-to-all-done.3 = f32[8,8,256]{2,1,0:T(8,128)S(1)} async-done(((f32[8,8,256]{2,1,0:T(8,128)}), f32[8,8,256]{2,1,0:T(8,128)S(1)}, u32[]{:S(2)}, u32[]{:S(2)}) %all-to-all-start.3) | async-done | bytes 65568 | tf_op jit(solution)/shard_map/all_to_all | solution.py:17
  156.9 12.4 %psum.30 = f32[8,256]{1,0:T(8,128)S(1)} all-reduce(f32[8,256]{1,0:T(8,128)S(1)} %reduce_sum.38), channel_id=1, replica_groups={{0,8,16,24},{1,9,17,25},{2,10,18,26},{3,11,19,27},{4,12,20,28},{5,13,21..., use_global_device_ids=true, to_apply=%region_5.6 | all-reduce | flops 2048 | bytes 16384 | tf_op jit(solution)/shard_map/psum | solution.py:22
  169.4 0.4 fusion.27
  169.7 0.3 convolution_subtract_fusion.2
  170.0 0.4 copy-done.5
  170.4 0.3 fusion
  170.7 0.3 fusion.57
  171.0 0.3 fusion.56
  171.3 0.5 fusion.58
  171.9 10.0 %all_to_all.25 = f32[8,8,256]{2,1,0:T(8,128)S(1)} all-to-all(f32[8,8,256]{2,1,0:T(8,128)S(1)} %broadcast_in_dim.79), channel_id=1, replica_groups={{0,1,2,3,4,5,6,7},{8,9,10,11,12,13,14,15},{16,17,18,19,20,21,22,23},{24..., dimensions={0} | all-to-all | bytes 131072 | tf_op jit(solution)/shard_map/all_to_all | solution.py:17
  182.0 13.3 %psum.31 = f32[8,256]{1,0:T(8,128)S(1)} all-reduce(f32[8,256]{1,0:T(8,128)S(1)} %reduce_sum.39), channel_id=1, replica_groups={{0,8,16,24},{1,9,17,25},{2,10,18,26},{3,11,19,27},{4,12,20,28},{5,13,21..., use_global_device_ids=true, to_apply=%region_7.8 | all-reduce | flops 2048 | bytes 16384 | tf_op jit(solution)/shard_map/psum | solution.py:22
  195.3 0.4 fusion.22
  195.6 0.3 fusion.24
  195.9 0.3 fusion.2
  196.2 7.0 %collective-permute-start.9 = (f32[8,2048]{1,0:T(8,128)S(1)}, f32[8,2048]{1,0:T(8,128)S(1)}, u32[]{:S(2)}, u32[]{:S(2)}) collective-permute-start(f32[8,2048]{1,0:T(8,128)S(1)} %fusion.2), channel_id=1, source_target_pairs={{1,2},{3,4},{5,6},{7,8},{9,10},{11,12},{13,14},{15,16},{17,18},{19... | collective-permute-start | bytes 196616 | tf_op jit(solution)/shard_map/ppermute | solution.py:49
  203.2 1.9 collective-permute-start.10
  205.3 0.1 fusion.43
  205.4 0.1 fusion.42
  205.6 0.1 fusion.41
  205.7 2.9 %collective-permute-done.9 = f32[8,2048]{1,0:T(8,128)S(1)} collective-permute-done((f32[8,2048]{1,0:T(8,128)S(1)}, f32[8,2048]{1,0:T(8,128)S(1)}, u32[]{:S(2)}, u32[]{:S(2)}) %collective-permute-start.9) | collective-permute-done | bytes 65568 | tf_op jit(solution)/shard_map/ppermute | solution.py:49
  208.8 1.1 fusion.4
  209.9 0.7 subtract_divide_fusion
  (66 shorter events, 1.5 us)
Async XLA Ops:
  7.2 6.5 %copy-start.7 = (f32[8,2,1024]{2,1,0:T(2,128)S(1)}, f32[8,2,1024]{2,1,0:T(2,128)}, u32[]{:S(2)}) copy-start(f32[8,2,1024]{2,1,0:T(2,128)} %param.6) | copy-start | bytes 196612
  9.5 18.4 %all-to-all-start = ((f32[4,2,16,2048]{3,2,1,0:T(8,128)}), f32[4,2,16,2048]{3,2,1,0:T(8,128)S(1)}, u32[]{:S(2)}, u32[]{:S(2)}) async-start(f32[4,2,16,2048]{3,2,1,0:T(8,128)} %broadcast_in_dim.70), calls=%async_computation | async-start | bytes 2097152 | tf_op jit(solution)/shard_map/all_to_all | solution.py:17
  13.7 17.8 %collective-permute-start = (f32[8,2048]{1,0:T(8,128)S(1)}, f32[8,2048]{1,0:T(8,128)S(1)}, u32[]{:S(2)}, u32[]{:S(2)}) collective-permute-start(f32[8,2048]{1,0:T(8,128)S(1)} %bitcast.63), channel_id=1, source_target_pairs={{0,256},{32,288},{64,320},{96,352},{128,384},{160,416},{192,448},{... | collective-permute-start | bytes 196616 | tf_op jit(solution)/shard_map/ppermute | solution.py:78
  27.9 13.8 %collective-permute-start.1 = (f32[64,2048]{1,0:T(8,128)S(1)}, f32[64,2048]{1,0:T(8,128)S(1)}, u32[]{:S(2)}, u32[]{:S(2)}) collective-permute-start(f32[64,2048]{1,0:T(8,128)S(1)} %bitcast.52), channel_id=1, source_target_pairs={{0,128},{32,160},{64,192},{96,224},{128,0},{160,32},{192,64},{224,... | collective-permute-start | bytes 1572872 | tf_op jit(solution)/shard_map/ppermute | solution.py:78
  41.8 42.4 %copy-start.3 = (f32[64,2048]{1,0:T(8,128)}, f32[64,2048]{1,0:T(8,128)S(1)}, u32[]{:S(2)}) copy-start(f32[64,2048]{1,0:T(8,128)S(1)} %collective-permute-done.1) | copy-start | bytes 1572868
  41.8 40.9 %collective-permute-start.4 = (f32[64,2048]{1,0:T(8,128)S(1)}, f32[64,2048]{1,0:T(8,128)S(1)}, u32[]{:S(2)}, u32[]{:S(2)}) collective-permute-start(f32[64,2048]{1,0:T(8,128)S(1)} %bitcast.47), channel_id=1, source_target_pairs={{0,128},{32,160},{64,192},{96,224},{128,0},{160,32},{192,64},{224,... | collective-permute-start | bytes 1572872 | tf_op jit(solution)/shard_map/ppermute | solution.py:78
  45.3 48.1 %copy-start.8 = (f32[2,1024]{1,0:T(2,128)S(1)}, f32[2,1024]{1,0:T(2,128)}, u32[]{:S(2)}) copy-start(f32[2,1024]{1,0:T(2,128)} %param.8) | copy-start | bytes 24580
  46.0 14.3 %all-to-all-start.1 = ((f32[8,16,128]{2,1,0:T(8,128)}), f32[8,16,128]{2,1,0:T(8,128)S(1)}, u32[]{:S(2)}, u32[]{:S(2)}) async-start(f32[8,16,128]{2,1,0:T(8,128)} %broadcast_in_dim.71), calls=%async_computation.1 | async-start | bytes 131072 | tf_op jit(solution)/shard_map/all_to_all | solution.py:17
  53.5 79.7 %all-gather.2.cloned.1.call-start = ((), (), s32[]{:S(2)}) async-start(), calls=%async_computation.5 | async-start | bytes 2621440 | tf_op jit(solution)/shard_map/all_gather | solution.py:119
  53.5 29.2 %collective-permute-start.2 = (f32[2,16,2048]{2,1,0:T(8,128)S(1)}, f32[2,16,2048]{2,1,0:T(8,128)S(1)}, u32[]{:S(2)}, u32[]{:S(2)}) collective-permute-start(f32[2,16,2048]{2,1,0:T(8,128)S(1)} %broadcast_in_dim.69), channel_id=1, source_target_pairs={{0,256},{32,288},{64,320},{96,352},{128,384},{160,416},{192,448},{... | collective-permute-start | bytes 786440 | tf_op jit(solution)/shard_map/ppermute | solution.py:78
  58.4 24.3 %collective-permute-start.3 = (f32[2,16,2048]{2,1,0:T(8,128)S(1)}, f32[2,16,2048]{2,1,0:T(8,128)S(1)}, u32[]{:S(2)}, u32[]{:S(2)}) collective-permute-start(f32[2,16,2048]{2,1,0:T(8,128)S(1)} %broadcast_in_dim.69), channel_id=1, source_target_pairs={{0,384},{32,416},{64,448},{96,480},{128,256},{160,288},{192,320},{... | collective-permute-start | bytes 786440 | tf_op jit(solution)/shard_map/ppermute | solution.py:78
  82.7 43.3 %copy-start = (f32[64,2048]{1,0:T(8,128)}, f32[64,2048]{1,0:T(8,128)S(1)}, u32[]{:S(2)}) copy-start(f32[64,2048]{1,0:T(8,128)S(1)} %collective-permute-done.4) | copy-start | bytes 1572868
  84.1 11.5 %collective-permute-start.5 = (f32[16,2048]{1,0:T(8,128)S(1)}, f32[16,2048]{1,0:T(8,128)S(1)}, u32[]{:S(2)}, u32[]{:S(2)}) collective-permute-start(f32[16,2048]{1,0:T(8,128)S(1)} %pad_maximum_fusion.1), channel_id=1, source_target_pairs={{0,256},{32,288},{64,320},{96,352},{128,384},{160,416},{192,448},{... | collective-permute-start | bytes 393224 | tf_op jit(solution)/shard_map/ppermute | solution.py:78
  97.1 10.0 %all-to-all-start.2 = ((f32[8,16,128]{2,1,0:T(8,128)}), f32[8,16,128]{2,1,0:T(8,128)S(1)}, u32[]{:S(2)}, u32[]{:S(2)}) async-start(f32[8,16,128]{2,1,0:T(8,128)} %broadcast_in_dim.72), calls=%async_computation.2 | async-start | bytes 131072 | tf_op jit(solution)/shard_map/all_to_all | solution.py:17
  126.5 6.6 %collective-permute-start.6 = (f32[8,2048]{1,0:T(8,128)S(1)}, f32[8,2048]{1,0:T(8,128)S(1)}, u32[]{:S(2)}, u32[]{:S(2)}) collective-permute-start(f32[8,2048]{1,0:T(8,128)S(1)} %slice.168), channel_id=1, source_target_pairs={{0,256},{32,288},{64,320},{96,352},{128,384},{160,416},{192,448},{... | collective-permute-start | bytes 196616 | tf_op jit(solution)/shard_map/ppermute | solution.py:78
  133.2 13.7 %collective-permute-start.7 = (f32[8,2048]{1,0:T(8,128)S(1)}, f32[8,2048]{1,0:T(8,128)S(1)}, u32[]{:S(2)}, u32[]{:S(2)}) collective-permute-start(f32[8,2048]{1,0:T(8,128)S(1)} %fusion.15), channel_id=1, source_target_pairs={{1,2},{3,4},{5,6},{7,8},{9,10},{11,12},{13,14},{15,16},{17,18},{19... | collective-permute-start | bytes 196616 | tf_op jit(solution)/shard_map/ppermute | solution.py:49
  141.2 5.7 %collective-permute-start.8 = (f32[8,2048]{1,0:T(8,128)S(1)}, f32[8,2048]{1,0:T(8,128)S(1)}, u32[]{:S(2)}, u32[]{:S(2)}) collective-permute-start(f32[8,2048]{1,0:T(8,128)S(1)} %fusion.15), channel_id=1, source_target_pairs={{0,1},{1,0},{2,3},{3,2},{4,5},{5,4},{6,7},{7,6},{8,9},{9,8},{10,11... | collective-permute-start | bytes 196616 | tf_op jit(solution)/shard_map/ppermute | solution.py:50
  143.6 3.5 %copy-start.6 = (f32[8,2,1024]{2,1,0:T(2,128)S(1)}, f32[8,2,1024]{2,1,0:T(2,128)}, u32[]{:S(2)}) copy-start(f32[8,2,1024]{2,1,0:T(2,128)} %param.7) | copy-start | bytes 196612
  143.6 3.5 %copy-start.9 = (f32[8]{0:T(128)S(1)}, f32[8]{0:T(128)}, u32[]{:S(2)}) copy-start(f32[8]{0:T(128)} %param.9) | copy-start | bytes 100
  143.6 4.0 %copy-start.4 = (f32[64,2048]{1,0:T(8,128)S(1)}, f32[64,2048]{1,0:T(8,128)}, u32[]{:S(2)}) copy-start(f32[64,2048]{1,0:T(8,128)} %copy-done.3) | copy-start | bytes 1572868
  149.5 7.4 %all-to-all-start.3 = ((f32[8,8,256]{2,1,0:T(8,128)}), f32[8,8,256]{2,1,0:T(8,128)S(1)}, u32[]{:S(2)}, u32[]{:S(2)}) async-start(f32[8,8,256]{2,1,0:T(8,128)} %broadcast_in_dim.78), calls=%async_computation.3 | async-start | bytes 131072 | tf_op jit(solution)/shard_map/all_to_all | solution.py:17
  169.3 1.0 copy-start.5
  169.3 1.3 copy-start.1
  170.4 25.3 %copy-start.2 = (f32[64,2048]{1,0:T(8,128)S(1)}, f32[64,2048]{1,0:T(8,128)}, u32[]{:S(2)}) copy-start(f32[64,2048]{1,0:T(8,128)} %copy-done) | copy-start | bytes 1572868
  196.2 12.5 %collective-permute-start.9 = (f32[8,2048]{1,0:T(8,128)S(1)}, f32[8,2048]{1,0:T(8,128)S(1)}, u32[]{:S(2)}, u32[]{:S(2)}) collective-permute-start(f32[8,2048]{1,0:T(8,128)S(1)} %fusion.2), channel_id=1, source_target_pairs={{1,2},{3,4},{5,6},{7,8},{9,10},{11,12},{13,14},{15,16},{17,18},{19... | collective-permute-start | bytes 196616 | tf_op jit(solution)/shard_map/ppermute | solution.py:49
  203.2 5.5 %collective-permute-start.10 = (f32[8,2048]{1,0:T(8,128)S(1)}, f32[8,2048]{1,0:T(8,128)S(1)}, u32[]{:S(2)}, u32[]{:S(2)}) collective-permute-start(f32[8,2048]{1,0:T(8,128)S(1)} %fusion.2), channel_id=1, source_target_pairs={{0,1},{1,0},{2,3},{3,2},{4,5},{5,4},{6,7},{7,6},{8,9},{9,8},{10,11... | collective-permute-start | bytes 196616 | tf_op jit(solution)/shard_map/ppermute | solution.py:50
Sparse Core Ops, SparseCore 0:
  84.2 44.6 all-gather.1

commit v11 on v10

--- a/solution.py
+++ b/solution.py
@@ -104,21 +104,21 @@
     weight = 1.0 / (lax.axis_size("space") * cells)
     blocks, own = occupied.shape[:2]
     states = occupied.reshape(blocks, own, cells)
+    column = lax.all_gather(states, "band", axis=1, tiled=True, axis_index_groups=BAND_Z)
     ring = copies(states, "band", BAND_Y)
     first, second = ring[:, 0].reshape(-1, cells), ring[:, 1].reshape(-1, cells)
     diagonal = 3.75 + potential[None, :, :] - energies[:, None, None]
     vectors = initial.reshape(count, cells)
     pair = jnp.concatenate([vectors, swapped(vectors, 8)], axis=0)
-    across_first, second, states = lax.optimization_barrier((swapped(first, 4), second, states))
+    across_first, second = lax.optimization_barrier((swapped(first, 4), second))
     across_second = swapped(second, 4)
-    far = (swapped(states, 8), swapped(states, 12))
     halves = (first, across_first)
     near = halves
     margin = shared_margin(halves, pair, weight)
-    margin, far, across_second = lax.optimization_barrier((margin, far, across_second))
-    far = lax.all_gather(
-        jnp.concatenate(far, axis=1), "band", axis=1, tiled=True, axis_index_groups=BAND_Y
-    )
+    margin, column = lax.optimization_barrier((margin, column))
+    upper = lax.axis_index("band") // 8
+    far = lax.dynamic_slice_in_dim(column, (1 - upper) * 2 * own, 2 * own, axis=1)
+    far = lax.all_gather(far, "band", axis=1, tiled=True, axis_index_groups=BAND_Y)
     partial = shared_correction(margin, halves)
     other = swapped(jnp.concatenate([partial[count:], partial[:count]], axis=0), 8)
     pair = pair - partial - other

time: 218 us -> 225 us (1.032)
  waiting for transfers between devices: 36.2 us -> 45.4 us
    ppermute x7 -> x5, starting transfers between devices: 30.2 us -> 15.9 us  [swapped(): lax.ppermute(x, 'band', [(i, i ^ bit) for i in range(lax.axis_size('band'...]
    ppermute x7 -> x5, waiting for transfers between devices: 16.3 us -> 26 us  [swapped(): lax.ppermute(x, 'band', [(i, i ^ bit) for i in range(lax.axis_size('band'...]
    ppermute x2, starting transfers between devices: 15 us -> 21.4 us  [neighbours(): across = lax.ppermute(vectors, 'space', outer)]
    all_to_all x4, starting transfers between devices: 22.8 us -> 29 us  [copies(): return lax.all_to_all(sent, axis, 0, 0, axis_index_groups=groups)]
    ppermute x2, waiting for transfers between devices: 4.36 us -> 0.01 us  [neighbours(): across = lax.ppermute(vectors, 'space', outer)]
    all_to_all x4, waiting for transfers between devices: 15.5 us -> 17.9 us  [copies(): return lax.all_to_all(sent, axis, 0, 0, axis_index_groups=groups)]
  transfers between devices with their start and end apart: 16 -> 15, of which waited for: 8 -> 9; matrix products, arithmetic and copies ran while one was open for 3% -> 3% of each run, Pallas kernels for 0% -> 0%
where the time goes in v11:
time: 225 us
  blocking collectives  75.4 us (34%)
  starting transfers between devices  70.1 us (31%)
  waiting for transfers between devices  45.4 us (20%)
  between operations  14.6 us (6%)
  local copies, waits for them, and re-layouts  9.82 us (4%)
  matrix products  6.43 us (3%)
  other arithmetic  2.78 us (1%)
    psum x4, blocking collectives, space_sum(): return lax.psum(near, 'space', axis_index_groups=SPACE_Z)  65.4 us
    all_to_all x4, starting transfers between devices, copies(): return lax.all_to_all(sent, axis, 0, 0, axis_index_groups=groups)  29 us
    ppermute x5, waiting for transfers between devices, swapped(): lax.ppermute(x, 'band', [(i, i ^ bit) for i in range(lax.axis_size('band'...  26 us
    ppermute x2, starting transfers between devices, neighbours(): across = lax.ppermute(vectors, 'space', outer)  21.4 us
    all_to_all x4, waiting for transfers between devices, copies(): return lax.all_to_all(sent, axis, 0, 0, axis_index_groups=groups)  17.9 us
    ppermute x5, starting transfers between devices, swapped(): lax.ppermute(x, 'band', [(i, i ^ bit) for i in range(lax.axis_size('band'...  15.9 us
    all_to_all x1, blocking collectives, copies(): return lax.all_to_all(sent, axis, 0, 0, axis_index_groups=groups)  10 us
  transfers between devices with their start and end apart: 15, of which 9 were waited for; matrix products, arithmetic and copies ran while one was open for 3% of the time, Pallas kernels for 0%

profile of v11, /device:TPU:7, one launch (start us, length us, event | category | flops | bytes accessed | tf_op | source)
XLA Modules:
  0.0 224.6 jit_solution(1568324457424848565)
XLA Ops:
  7.2 1.2 broadcast_in_dim.69
  8.4 1.1 broadcast_in_dim.70
  9.5 4.2 %all-to-all-start = ((f32[4,2,16,2048]{3,2,1,0:T(8,128)}), f32[4,2,16,2048]{3,2,1,0:T(8,128)S(1)}, u32[]{:S(2)}, u32[]{:S(2)}) async-start(f32[4,2,16,2048]{3,2,1,0:T(8,128)} %broadcast_in_dim.70), calls=%async_computation | async-start | bytes 2097152 | tf_op jit(solution)/shard_map/all_to_all | solution.py:17
  13.7 0.7 all-gather.3.cloned.1.call-update
  14.4 4.9 %collective-permute-start = (f32[8,2048]{1,0:T(8,128)S(1)}, f32[8,2048]{1,0:T(8,128)S(1)}, u32[]{:S(2)}, u32[]{:S(2)}) collective-permute-start(f32[8,2048]{1,0:T(8,128)S(1)} %bitcast.63), channel_id=1, source_target_pairs={{0,256},{32,288},{64,320},{96,352},{128,384},{160,416},{192,448},{... | collective-permute-start | bytes 196616 | tf_op jit(solution)/shard_map/ppermute | solution.py:78
  19.3 8.5 %all-to-all-done = f32[4,2,16,2048]{3,2,1,0:T(8,128)S(1)} async-done(((f32[4,2,16,2048]{3,2,1,0:T(8,128)}), f32[4,2,16,2048]{3,2,1,0:T(8,128)S(1)}, u32[]{:S(2)}, u32[]{:S(2)}) %all-to-all-start) | async-done | bytes 1048608 | tf_op jit(solution)/shard_map/all_to_all | solution.py:17
  27.9 3.5 %collective-permute-start.1 = (f32[64,2048]{1,0:T(8,128)S(1)}, f32[64,2048]{1,0:T(8,128)S(1)}, u32[]{:S(2)}, u32[]{:S(2)}) collective-permute-start(f32[64,2048]{1,0:T(8,128)S(1)} %bitcast.52), channel_id=1, source_target_pairs={{0,128},{32,160},{64,192},{96,224},{128,0},{160,32},{192,64},{224,... | collective-permute-start | bytes 1572872 | tf_op jit(solution)/shard_map/ppermute | solution.py:78
  31.5 0.3 fusion.49
  31.8 9.9 %collective-permute-done.1 = f32[64,2048]{1,0:T(8,128)S(1)} collective-permute-done((f32[64,2048]{1,0:T(8,128)S(1)}, f32[64,2048]{1,0:T(8,128)S(1)}, u32[]{:S(2)}, u32[]{:S(2)}) %collective-permute-start.1) | collective-permute-done | bytes 524320 | tf_op jit(solution)/shard_map/ppermute | solution.py:78
  41.7 0.3 fusion.50
  42.1 0.6 broadcast_in_dim.71
  42.8 13.0 %all-to-all-start.1 = ((f32[8,16,128]{2,1,0:T(8,128)}), f32[8,16,128]{2,1,0:T(8,128)S(1)}, u32[]{:S(2)}, u32[]{:S(2)}) async-start(f32[8,16,128]{2,1,0:T(8,128)} %broadcast_in_dim.71), calls=%async_computation.1 | async-start | bytes 131072 | tf_op jit(solution)/shard_map/all_to_all | solution.py:17
  55.8 3.1 %all-to-all-done.1 = f32[8,16,128]{2,1,0:T(8,128)S(1)} async-done(((f32[8,16,128]{2,1,0:T(8,128)}), f32[8,16,128]{2,1,0:T(8,128)S(1)}, u32[]{:S(2)}, u32[]{:S(2)}) %all-to-all-start.1) | async-done | bytes 65568 | tf_op jit(solution)/shard_map/all_to_all | solution.py:17
  58.9 29.5 %psum.28 = f32[16,128]{1,0:T(8,128)S(1)} all-reduce(f32[16,128]{1,0:T(8,128)S(1)} %reduce_sum.36), channel_id=1, replica_groups={{0,8,16,24},{1,9,17,25},{2,10,18,26},{3,11,19,27},{4,12,20,28},{5,13,21..., use_global_device_ids=true, to_apply=%region_1.0 | all-reduce | flops 2048 | bytes 16384 | tf_op jit(solution)/shard_map/psum | solution.py:22
  88.5 0.3 fusion.20
  88.8 0.3 convolution_add_fusion.1
  89.1 1.9 constant_dynamic-slice_fusion
  91.0 1.9 collective-permute-start.2
  93.0 3.0 %collective-permute-start.3 = (f32[64,2048]{1,0:T(8,128)S(1)}, f32[64,2048]{1,0:T(8,128)S(1)}, u32[]{:S(2)}, u32[]{:S(2)}) collective-permute-start(f32[64,2048]{1,0:T(8,128)S(1)} %bitcast.47), channel_id=1, source_target_pairs={{0,128},{32,160},{64,192},{96,224},{128,0},{160,32},{192,64},{224,... | collective-permute-start | bytes 1572872 | tf_op jit(solution)/shard_map/ppermute | solution.py:78
  95.9 2.1 collective-permute-done.2
  98.0 0.3 fusion.51
  98.3 10.7 %collective-permute-done.3 = f32[64,2048]{1,0:T(8,128)S(1)} collective-permute-done((f32[64,2048]{1,0:T(8,128)S(1)}, f32[64,2048]{1,0:T(8,128)S(1)}, u32[]{:S(2)}, u32[]{:S(2)}) %collective-permute-start.3) | collective-permute-done | bytes 524320 | tf_op jit(solution)/shard_map/ppermute | solution.py:78
  109.1 0.3 fusion.52
  109.5 0.6 broadcast_in_dim.72
  110.1 7.2 %all-to-all-start.2 = ((f32[8,16,128]{2,1,0:T(8,128)}), f32[8,16,128]{2,1,0:T(8,128)S(1)}, u32[]{:S(2)}, u32[]{:S(2)}) async-start(f32[8,16,128]{2,1,0:T(8,128)} %broadcast_in_dim.72), calls=%async_computation.2 | async-start | bytes 131072 | tf_op jit(solution)/shard_map/all_to_all | solution.py:17
  117.3 3.2 %all-to-all-done.2 = f32[8,16,128]{2,1,0:T(8,128)S(1)} async-done(((f32[8,16,128]{2,1,0:T(8,128)}), f32[8,16,128]{2,1,0:T(8,128)S(1)}, u32[]{:S(2)}, u32[]{:S(2)}) %all-to-all-start.2) | async-done | bytes 65568 | tf_op jit(solution)/shard_map/all_to_all | solution.py:17
  120.5 11.6 %psum.29 = f32[16,128]{1,0:T(8,128)S(1)} all-reduce(f32[16,128]{1,0:T(8,128)S(1)} %reduce_sum.37), channel_id=1, replica_groups={{0,8,16,24},{1,9,17,25},{2,10,18,26},{3,11,19,27},{4,12,20,28},{5,13,21..., use_global_device_ids=true, to_apply=%region_3.4 | all-reduce | flops 2048 | bytes 16384 | tf_op jit(solution)/shard_map/psum | solution.py:22
  132.2 0.3 fusion.16
  132.4 0.3 convolution_add_fusion
  132.7 2.5 %collective-permute-start.4 = (f32[8,2048]{1,0:T(8,128)S(1)}, f32[8,2048]{1,0:T(8,128)S(1)}, u32[]{:S(2)}, u32[]{:S(2)}) collective-permute-start(f32[8,2048]{1,0:T(8,128)S(1)} %slice.168), channel_id=1, source_target_pairs={{0,256},{32,288},{64,320},{96,352},{128,384},{160,416},{192,448},{... | collective-permute-start | bytes 196616 | tf_op jit(solution)/shard_map/ppermute | solution.py:78
  135.3 3.4 %collective-permute-done.4 = f32[8,2048]{1,0:T(8,128)S(1)} collective-permute-done((f32[8,2048]{1,0:T(8,128)S(1)}, f32[8,2048]{1,0:T(8,128)S(1)}, u32[]{:S(2)}, u32[]{:S(2)}) %collective-permute-start.4) | collective-permute-done | bytes 65568 | tf_op jit(solution)/shard_map/ppermute | solution.py:78
  138.7 10.5 %collective-permute-start.5 = (f32[8,2048]{1,0:T(8,128)S(1)}, f32[8,2048]{1,0:T(8,128)S(1)}, u32[]{:S(2)}, u32[]{:S(2)}) collective-permute-start(f32[8,2048]{1,0:T(8,128)S(1)} %fusion.15), channel_id=1, source_target_pairs={{1,2},{3,4},{5,6},{7,8},{9,10},{11,12},{13,14},{15,16},{17,18},{19... | collective-permute-start | bytes 196616 | tf_op jit(solution)/shard_map/ppermute | solution.py:49
  149.1 1.9 collective-permute-start.6
  151.1 0.1 fusion.48
  151.3 0.1 fusion.47
  151.6 1.7 slice_bitcast_fusion.1
  153.6 0.5 fusion.3
  154.1 0.3 fusion.54
  154.5 0.3 fusion.53
  154.8 0.5 fusion.55
  155.4 0.6 broadcast_in_dim.78
  156.0 4.6 %all-to-all-start.3 = ((f32[8,8,256]{2,1,0:T(8,128)}), f32[8,8,256]{2,1,0:T(8,128)S(1)}, u32[]{:S(2)}, u32[]{:S(2)}) async-start(f32[8,8,256]{2,1,0:T(8,128)} %broadcast_in_dim.78), calls=%async_computation.3 | async-start | bytes 131072 | tf_op jit(solution)/shard_map/all_to_all | solution.py:17
  160.7 3.1 %all-to-all-done.3 = f32[8,8,256]{2,1,0:T(8,128)S(1)} async-done(((f32[8,8,256]{2,1,0:T(8,128)}), f32[8,8,256]{2,1,0:T(8,128)S(1)}, u32[]{:S(2)}, u32[]{:S(2)}) %all-to-all-start.3) | async-done | bytes 65568 | tf_op jit(solution)/shard_map/all_to_all | solution.py:17
  163.8 14.9 %psum.30 = f32[8,256]{1,0:T(8,128)S(1)} all-reduce(f32[8,256]{1,0:T(8,128)S(1)} %reduce_sum.38), channel_id=1, replica_groups={{0,8,16,24},{1,9,17,25},{2,10,18,26},{3,11,19,27},{4,12,20,28},{5,13,21..., use_global_device_ids=true, to_apply=%region_5.6 | all-reduce | flops 2048 | bytes 16384 | tf_op jit(solution)/shard_map/psum | solution.py:22
  178.8 0.4 fusion.27
  179.1 0.3 convolution_subtract_fusion.2
  179.4 0.4 copy-done.2
  179.8 0.3 fusion
  180.1 0.3 fusion.56
  180.4 0.5 fusion.58
  180.9 0.3 fusion.57
  181.3 10.0 %all_to_all.25 = f32[8,8,256]{2,1,0:T(8,128)S(1)} all-to-all(f32[8,8,256]{2,1,0:T(8,128)S(1)} %broadcast_in_dim.79), channel_id=1, replica_groups={{0,1,2,3,4,5,6,7},{8,9,10,11,12,13,14,15},{16,17,18,19,20,21,22,23},{24..., dimensions={0} | all-to-all | bytes 131072 | tf_op jit(solution)/shard_map/all_to_all | solution.py:17
  191.4 9.3 %psum.31 = f32[8,256]{1,0:T(8,128)S(1)} all-reduce(f32[8,256]{1,0:T(8,128)S(1)} %reduce_sum.39), channel_id=1, replica_groups={{0,8,16,24},{1,9,17,25},{2,10,18,26},{3,11,19,27},{4,12,20,28},{5,13,21..., use_global_device_ids=true, to_apply=%region_7.8 | all-reduce | flops 2048 | bytes 16384 | tf_op jit(solution)/shard_map/psum | solution.py:22
  200.7 0.4 fusion.22
  201.1 0.3 fusion.24
  201.4 0.3 fusion.2
  201.6 11.0 %collective-permute-start.7 = (f32[8,2048]{1,0:T(8,128)S(1)}, f32[8,2048]{1,0:T(8,128)S(1)}, u32[]{:S(2)}, u32[]{:S(2)}) collective-permute-start(f32[8,2048]{1,0:T(8,128)S(1)} %fusion.2), channel_id=1, source_target_pairs={{1,2},{3,4},{5,6},{7,8},{9,10},{11,12},{13,14},{15,16},{17,18},{19... | collective-permute-start | bytes 196616 | tf_op jit(solution)/shard_map/ppermute | solution.py:49
  212.6 1.9 collective-permute-start.8
  214.8 0.1 fusion.43
  214.9 0.1 fusion.42
  215.0 0.1 fusion.41
  215.2 0.6 collective-permute-done.8
  215.9 1.1 fusion.4
  217.0 0.7 subtract_divide_fusion
  (67 shorter events, 1.5 us)
Async XLA Ops:
  7.2 7.2 %copy-start.8 = (f32[8,2,1024]{2,1,0:T(2,128)S(1)}, f32[8,2,1024]{2,1,0:T(2,128)}, u32[]{:S(2)}) copy-start(f32[8,2,1024]{2,1,0:T(2,128)} %param.6) | copy-start | bytes 196612
  8.4 5.3 %copy-start.6 = (f32[2,16,2048]{2,1,0:T(8,128)}, f32[2,16,2048]{2,1,0:T(8,128)S(1)}, u32[]{:S(2)}) copy-start(f32[2,16,2048]{2,1,0:T(8,128)S(1)} %broadcast_in_dim.69) | copy-start | bytes 786436
  9.5 18.4 %all-to-all-start = ((f32[4,2,16,2048]{3,2,1,0:T(8,128)}), f32[4,2,16,2048]{3,2,1,0:T(8,128)S(1)}, u32[]{:S(2)}, u32[]{:S(2)}) async-start(f32[4,2,16,2048]{3,2,1,0:T(8,128)} %broadcast_in_dim.70), calls=%async_computation | async-start | bytes 2097152 | tf_op jit(solution)/shard_map/all_to_all | solution.py:17
  13.7 74.8 %all-gather.3.cloned.1.call-start = ((), (), s32[]{:S(2)}) async-start(), calls=%async_computation.5 | async-start | bytes 1310720 | tf_op jit(solution)/shard_map/all_gather | solution.py:107
  14.4 17.1 %collective-permute-start = (f32[8,2048]{1,0:T(8,128)S(1)}, f32[8,2048]{1,0:T(8,128)S(1)}, u32[]{:S(2)}, u32[]{:S(2)}) collective-permute-start(f32[8,2048]{1,0:T(8,128)S(1)} %bitcast.63), channel_id=1, source_target_pairs={{0,256},{32,288},{64,320},{96,352},{128,384},{160,416},{192,448},{... | collective-permute-start | bytes 196616 | tf_op jit(solution)/shard_map/ppermute | solution.py:78
  27.9 13.8 %collective-permute-start.1 = (f32[64,2048]{1,0:T(8,128)S(1)}, f32[64,2048]{1,0:T(8,128)S(1)}, u32[]{:S(2)}, u32[]{:S(2)}) collective-permute-start(f32[64,2048]{1,0:T(8,128)S(1)} %bitcast.52), channel_id=1, source_target_pairs={{0,128},{32,160},{64,192},{96,224},{128,0},{160,32},{192,64},{224,... | collective-permute-start | bytes 1572872 | tf_op jit(solution)/shard_map/ppermute | solution.py:78
  41.7 49.3 %copy-start = (f32[64,2048]{1,0:T(8,128)}, f32[64,2048]{1,0:T(8,128)S(1)}, u32[]{:S(2)}) copy-start(f32[64,2048]{1,0:T(8,128)S(1)} %collective-permute-done.1) | copy-start | bytes 1572868
  42.1 50.9 %copy-start.9 = (f32[2,1024]{1,0:T(2,128)S(1)}, f32[2,1024]{1,0:T(2,128)}, u32[]{:S(2)}) copy-start(f32[2,1024]{1,0:T(2,128)} %param.8) | copy-start | bytes 24580
  42.8 16.1 %all-to-all-start.1 = ((f32[8,16,128]{2,1,0:T(8,128)}), f32[8,16,128]{2,1,0:T(8,128)S(1)}, u32[]{:S(2)}, u32[]{:S(2)}) async-start(f32[8,16,128]{2,1,0:T(8,128)} %broadcast_in_dim.71), calls=%async_computation.1 | async-start | bytes 131072 | tf_op jit(solution)/shard_map/all_to_all | solution.py:17
  55.8 82.9 %all-gather.5.cloned.1.call-start = ((), (), s32[]{:S(2)}) async-start(), calls=%async_computation.6 | async-start | bytes 2621440 | tf_op jit(solution)/shard_map/all_gather | solution.py:121
  91.0 7.0 %collective-permute-start.2 = (f32[16,2048]{1,0:T(8,128)S(1)}, f32[16,2048]{1,0:T(8,128)S(1)}, u32[]{:S(2)}, u32[]{:S(2)}) collective-permute-start(f32[16,2048]{1,0:T(8,128)S(1)} %pad_maximum_fusion), channel_id=1, source_target_pairs={{0,256},{32,288},{64,320},{96,352},{128,384},{160,416},{192,448},{... | collective-permute-start | bytes 393224 | tf_op jit(solution)/shard_map/ppermute | solution.py:78
  93.0 16.1 %collective-permute-start.3 = (f32[64,2048]{1,0:T(8,128)S(1)}, f32[64,2048]{1,0:T(8,128)S(1)}, u32[]{:S(2)}, u32[]{:S(2)}) collective-permute-start(f32[64,2048]{1,0:T(8,128)S(1)} %bitcast.47), channel_id=1, source_target_pairs={{0,128},{32,160},{64,192},{96,224},{128,0},{160,32},{192,64},{224,... | collective-permute-start | bytes 1572872 | tf_op jit(solution)/shard_map/ppermute | solution.py:78
  109.1 42.4 %copy-start.3 = (f32[64,2048]{1,0:T(8,128)}, f32[64,2048]{1,0:T(8,128)S(1)}, u32[]{:S(2)}) copy-start(f32[64,2048]{1,0:T(8,128)S(1)} %collective-permute-done.3) | copy-start | bytes 1572868
  110.1 10.4 %all-to-all-start.2 = ((f32[8,16,128]{2,1,0:T(8,128)}), f32[8,16,128]{2,1,0:T(8,128)S(1)}, u32[]{:S(2)}, u32[]{:S(2)}) async-start(f32[8,16,128]{2,1,0:T(8,128)} %broadcast_in_dim.72), calls=%async_computation.2 | async-start | bytes 131072 | tf_op jit(solution)/shard_map/all_to_all | solution.py:17
  132.7 5.9 %collective-permute-start.4 = (f32[8,2048]{1,0:T(8,128)S(1)}, f32[8,2048]{1,0:T(8,128)S(1)}, u32[]{:S(2)}, u32[]{:S(2)}) collective-permute-start(f32[8,2048]{1,0:T(8,128)S(1)} %slice.168), channel_id=1, source_target_pairs={{0,256},{32,288},{64,320},{96,352},{128,384},{160,416},{192,448},{... | collective-permute-start | bytes 196616 | tf_op jit(solution)/shard_map/ppermute | solution.py:78
  138.7 14.8 %collective-permute-start.5 = (f32[8,2048]{1,0:T(8,128)S(1)}, f32[8,2048]{1,0:T(8,128)S(1)}, u32[]{:S(2)}, u32[]{:S(2)}) collective-permute-start(f32[8,2048]{1,0:T(8,128)S(1)} %fusion.15), channel_id=1, source_target_pairs={{1,2},{3,4},{5,6},{7,8},{9,10},{11,12},{13,14},{15,16},{17,18},{19... | collective-permute-start | bytes 196616 | tf_op jit(solution)/shard_map/ppermute | solution.py:49
  149.1 4.3 %collective-permute-start.6 = (f32[8,2048]{1,0:T(8,128)S(1)}, f32[8,2048]{1,0:T(8,128)S(1)}, u32[]{:S(2)}, u32[]{:S(2)}) collective-permute-start(f32[8,2048]{1,0:T(8,128)S(1)} %fusion.15), channel_id=1, source_target_pairs={{0,1},{1,0},{2,3},{3,2},{4,5},{5,4},{6,7},{7,6},{8,9},{9,8},{10,11... | collective-permute-start | bytes 196616 | tf_op jit(solution)/shard_map/ppermute | solution.py:50
  151.5 2.1 copy-start.7
  151.6 2.1 copy-start.10
  151.6 2.6 %copy-start.1 = (f32[64,2048]{1,0:T(8,128)S(1)}, f32[64,2048]{1,0:T(8,128)}, u32[]{:S(2)}) copy-start(f32[64,2048]{1,0:T(8,128)} %copy-done) | copy-start | bytes 1572868
  156.0 7.8 %all-to-all-start.3 = ((f32[8,8,256]{2,1,0:T(8,128)}), f32[8,8,256]{2,1,0:T(8,128)S(1)}, u32[]{:S(2)}, u32[]{:S(2)}) async-start(f32[8,8,256]{2,1,0:T(8,128)} %broadcast_in_dim.78), calls=%async_computation.3 | async-start | bytes 131072 | tf_op jit(solution)/shard_map/all_to_all | solution.py:17
  178.7 1.0 copy-start.2
  178.8 2.1 copy-start.4
  179.8 21.3 %copy-start.5 = (f32[64,2048]{1,0:T(8,128)S(1)}, f32[64,2048]{1,0:T(8,128)}, u32[]{:S(2)}) copy-start(f32[64,2048]{1,0:T(8,128)} %copy-done.3) | copy-start | bytes 1572868
  201.6 13.5 %collective-permute-start.7 = (f32[8,2048]{1,0:T(8,128)S(1)}, f32[8,2048]{1,0:T(8,128)S(1)}, u32[]{:S(2)}, u32[]{:S(2)}) collective-permute-start(f32[8,2048]{1,0:T(8,128)S(1)} %fusion.2), channel_id=1, source_target_pairs={{1,2},{3,4},{5,6},{7,8},{9,10},{11,12},{13,14},{15,16},{17,18},{19... | collective-permute-start | bytes 196616 | tf_op jit(solution)/shard_map/ppermute | solution.py:49
  212.6 3.1 %collective-permute-start.8 = (f32[8,2048]{1,0:T(8,128)S(1)}, f32[8,2048]{1,0:T(8,128)S(1)}, u32[]{:S(2)}, u32[]{:S(2)}) collective-permute-start(f32[8,2048]{1,0:T(8,128)S(1)} %fusion.2), channel_id=1, source_target_pairs={{0,1},{1,0},{2,3},{3,2},{4,5},{5,4},{6,7},{7,6},{8,9},{9,8},{10,11... | collective-permute-start | bytes 196616 | tf_op jit(solution)/shard_map/ppermute | solution.py:50
Sparse Core Ops, SparseCore 0:
  16.6 46.5 all-gather.2
  91.1 33.5 all-gather.4

commit v12 on v1

--- a/solution.py
+++ b/solution.py
@@ -6,7 +6,6 @@
 NZ = 32
 ITERS = 2
 BAND_Z = [[z * 4 + y for z in range(4)] for y in range(4)]
-BAND_Y = [[z * 4 + y for y in range(4)] for z in range(4)]
 SPACE_PLANE = [[z * 8 + r for r in range(8)] for z in range(4)]
 SPACE_Z = [[z * 8 + r for z in range(4)] for r in range(8)]
 
@@ -15,11 +14,6 @@
     count = len(groups[0])
     sent = jnp.broadcast_to(x[None], (count,) + x.shape)
     return lax.all_to_all(sent, axis, 0, 0, axis_index_groups=groups)
-
-
-def gathered(states):
-    columns = copies(states, "band", BAND_Z)
-    return copies(columns, "band", BAND_Y).reshape(-1, states.shape[-1])
 
 
 def space_sum(x):
@@ -79,24 +73,55 @@
     return second / 24.0 - 2.0 / 3.0 * nearest
 
 
+def swapped(x, bits):
+    return lax.ppermute(x, "band", [(i, i ^ bits) for i in range(lax.axis_size("band"))])
+
+
+def project_whole(parts, vectors, weight):
+    product = jnp.concatenate([products(vectors, part) for part in parts], axis=1)
+    margin = space_sum(product) * weight
+    at = 0
+    for part in parts:
+        vectors = vectors - combination(margin[:, at : at + part.shape[0]], part)
+        at += part.shape[0]
+    return vectors
+
+
 def on_device(occupied, initial, right_side, potential, energies):
     count, planes, line = initial.shape
-    weight = 1.0 / (planes * lax.axis_size("space") * line)
-    states = [occupied[0].reshape(-1, planes * line), occupied[1].reshape(-1, planes * line)]
-    later = lax.all_gather(states[1], "band", axis=0, tiled=True)
-    blocks = [gathered(states[0]), later]
+    cells = planes * line
+    weight = 1.0 / (lax.axis_size("space") * cells)
+    tie = lax.optimization_barrier
+    own = [states.reshape(-1, cells) for states in occupied]
     diagonal = 3.75 + potential[None, :, :] - energies[:, None, None]
-    vectors = initial.reshape(count, planes * line)
+    vectors = initial.reshape(count, cells)
+    run, other = tie((copies(own[0], "band", BAND_Z).reshape(-1, cells), own[1]))
+    across = swapped(run, 1)
+    second = copies(other, "band", BAND_Z).reshape(-1, cells)
+    pair = jnp.concatenate([vectors, swapped(vectors, 3)], axis=0)
+    across, second, pair = tie((across, second, pair))
+    near = [jnp.concatenate([run, across], axis=0)]
+    margin = space_sum(products(pair, near[0])) * weight
+    margin, across, far = tie((margin, swapped(second, 1), swapped(near[0], 3)))
+    partial = combination(margin, near[0])
+    other = swapped(jnp.concatenate([partial[count:], partial[:count]], axis=0), 3)
+    pair, second, across = tie((pair - partial - other, second, across))
+    near.append(jnp.concatenate([second, across], axis=0))
+    margin = space_sum(products(pair, near[1])) * weight
+    margin, far_second = tie((margin, swapped(near[1], 3)))
+    partial = combination(margin, near[1])
+    vectors = pair[:count] - partial[:count] - swapped(partial[count:], 3)
+    blocks = [(near[0], far), (near[1], far_second)]
     for iteration in range(ITERS):
-        for block in blocks:
-            margin = space_sum(products(vectors, block)) * weight
-            vectors = vectors - combination(margin, block)
+        if iteration > 0:
+            for block in blocks:
+                vectors = project_whole(block, vectors, weight)
         low, high = neighbours(vectors)
         shape = (count, planes, line)
         vectors = vectors.reshape(shape)
         rest = right_side - coupling(vectors, low.reshape(shape), high.reshape(shape))
         residual = rest - diagonal * vectors
-        vectors = (rest / diagonal).reshape(count, planes * line)
+        vectors = (rest / diagonal).reshape(count, cells)
     return (vectors.reshape(shape), residual)
 
 

time: 215 us -> 210 us (0.977)
  starting transfers between devices: 45.2 us -> 61.4 us
  between operations: 14.3 us -> 1.17 us
  blocking collectives: 93 us -> 80 us
  waiting for transfers between devices: 42.7 us -> 46.3 us
    all_to_all x3, waiting for transfers between devices: 41.5 us -> 17.1 us  [copies(): return lax.all_to_all(sent, axis, 0, 0, axis_index_groups=groups)]
    ppermute x0 -> x7, starting transfers between devices: none -> 21.5 us  [swapped(): lax.ppermute(x, 'band', [(i, i ^ bits) for i in range(lax.axis_size('band...]
    ppermute x0 -> x7, waiting for transfers between devices: none -> 18.2 us  [swapped(): lax.ppermute(x, 'band', [(i, i ^ bits) for i in range(lax.axis_size('band...]
    ppermute x2, waiting for transfers between devices: 0.01 us -> 11.1 us  [neighbours(): across = lax.ppermute(vectors, 'space', outer)]
    ppermute x2, starting transfers between devices: 21 us -> 10.9 us  [neighbours(): across = lax.ppermute(vectors, 'space', outer)]
    all_to_all x3, blocking collectives: 36.3 us -> 27.6 us  [copies(): return lax.all_to_all(sent, axis, 0, 0, axis_index_groups=groups)]
    ppermute x2, starting transfers between devices: 3.84 us -> 10.6 us  [neighbours(): inside = lax.ppermute(vectors, 'space', [(i, i ^ 1) for i in range(count)])]
    psum x4, blocking collectives: 56.7 us -> 52.4 us  [space_sum(): return lax.psum(near, 'space', axis_index_groups=SPACE_Z)]
  transfers between devices with their start and end apart: 8 -> 14, of which waited for: 5 -> 7; matrix products, arithmetic and copies ran while one was open for 2% -> 1% of each run, Pallas kernels for 0% -> 0%
where the time goes in v12:
time: 210 us; the launch traced here: 207 us
  blocking collectives  80 us (38%)
  starting transfers between devices  61.4 us (29%)
  waiting for transfers between devices  46.3 us (22%)
  local copies, waits for them, and re-layouts  7.88 us (4%)
  matrix products  7.68 us (4%)
  other arithmetic  2.46 us (1%)
    psum x4, blocking collectives, space_sum(): return lax.psum(near, 'space', axis_index_groups=SPACE_Z)  52.4 us
    all_to_all x3, blocking collectives, copies(): return lax.all_to_all(sent, axis, 0, 0, axis_index_groups=groups)  27.6 us
    ppermute x7, starting transfers between devices, swapped(): lax.ppermute(x, 'band', [(i, i ^ bits) for i in range(lax.axis_size('band...  21.5 us
    all_to_all x3, starting transfers between devices, copies(): return lax.all_to_all(sent, axis, 0, 0, axis_index_groups=groups)  18.5 us
    ppermute x7, waiting for transfers between devices, swapped(): lax.ppermute(x, 'band', [(i, i ^ bits) for i in range(lax.axis_size('band...  18.2 us
    all_to_all x3, waiting for transfers between devices, copies(): return lax.all_to_all(sent, axis, 0, 0, axis_index_groups=groups)  17.1 us
    ppermute x2, waiting for transfers between devices, neighbours(): across = lax.ppermute(vectors, 'space', outer)  11.1 us
    ppermute x2, starting transfers between devices, neighbours(): across = lax.ppermute(vectors, 'space', outer)  10.9 us
  transfers between devices with their start and end apart: 14, of which 7 were waited for; matrix products, arithmetic and copies ran while one was open for 1% of the time, Pallas kernels for 0%

profile of v12, /device:TPU:7, one launch (start us, length us, event | category | flops | bytes accessed | tf_op | source)
XLA Modules:
  0.0 207.0 jit_solution(18251141806838597877)
XLA Ops:
  0.6 1.0 fusion.25
  1.7 0.8 broadcast_in_dim.76
  2.5 5.6 %all-to-all-start = ((f32[4,16,2048]{2,1,0:T(8,128)}), f32[4,16,2048]{2,1,0:T(8,128)S(1)}, u32[]{:S(2)}, u32[]{:S(2)}) async-start(f32[4,16,2048]{2,1,0:T(8,128)} %broadcast_in_dim.76), calls=%async_computation | async-start | bytes 1048576 | tf_op jit(solution)/shard_map/all_to_all | solution.py:16
  8.2 14.0 %all-to-all-done = f32[4,16,2048]{2,1,0:T(8,128)S(1)} async-done(((f32[4,16,2048]{2,1,0:T(8,128)}), f32[4,16,2048]{2,1,0:T(8,128)S(1)}, u32[]{:S(2)}, u32[]{:S(2)}) %all-to-all-start) | async-done | bytes 524320 | tf_op jit(solution)/shard_map/all_to_all | solution.py:16
  22.1 0.8 broadcast_in_dim.77
  22.9 3.6 %all-to-all-start.1 = ((f32[4,16,2048]{2,1,0:T(8,128)}), f32[4,16,2048]{2,1,0:T(8,128)S(1)}, u32[]{:S(2)}, u32[]{:S(2)}) async-start(f32[4,16,2048]{2,1,0:T(8,128)} %broadcast_in_dim.77), calls=%async_computation.1 | async-start | bytes 1048576 | tf_op jit(solution)/shard_map/all_to_all | solution.py:16
  26.6 4.6 %collective-permute-start.1 = (f32[8,2048]{1,0:T(8,128)S(1)}, f32[8,2048]{1,0:T(8,128)S(1)}, u32[]{:S(2)}, u32[]{:S(2)}) collective-permute-start(f32[8,2048]{1,0:T(8,128)S(1)} %bitcast.53), channel_id=1, source_target_pairs={{0,96},{32,64},{64,32},{96,0},{128,224},{160,192},{192,160},{224,1... | collective-permute-start | bytes 196616 | tf_op jit(solution)/shard_map/ppermute | solution.py:77
  31.2 1.9 collective-permute-start
  33.2 11.6 %collective-permute-done = f32[64,2048]{1,0:T(8,128)S(1)} collective-permute-done((f32[64,2048]{1,0:T(8,128)S(1)}, f32[64,2048]{1,0:T(8,128)S(1)}, u32[]{:S(2)}, u32[]{:S(2)}) %collective-permute-start) | collective-permute-done | bytes 524320 | tf_op jit(solution)/shard_map/ppermute | solution.py:77
  44.9 2.0 collective-permute-start.3
  46.9 2.0 collective-permute-start.2
  48.9 0.5 fusion.35
  49.4 10.4 %all_to_all.30 = f32[8,16,128]{2,1,0:T(8,128)S(1)} all-to-all(f32[8,16,128]{2,1,0:T(8,128)S(1)} %broadcast_in_dim.78), channel_id=1, replica_groups={{0,1,2,3,4,5,6,7},{8,9,10,11,12,13,14,15},{16,17,18,19,20,21,22,23},{24..., dimensions={0} | all-to-all | bytes 131072 | tf_op jit(solution)/shard_map/all_to_all | solution.py:16
  59.9 17.2 %psum.28 = f32[16,128]{1,0:T(8,128)S(1)} all-reduce(f32[16,128]{1,0:T(8,128)S(1)} %reduce_sum.36), channel_id=1, replica_groups={{0,8,16,24},{1,9,17,25},{2,10,18,26},{3,11,19,27},{4,12,20,28},{5,13,21..., use_global_device_ids=true, to_apply=%region_1.0 | all-reduce | flops 2048 | bytes 16384 | tf_op jit(solution)/shard_map/psum | solution.py:21
  77.1 0.4 fusion.36
  77.5 0.4 copy-done.2
  77.9 4.4 %collective-permute-start.4 = (f32[16,2048]{1,0:T(8,128)S(1)}, f32[16,2048]{1,0:T(8,128)S(1)}, u32[]{:S(2)}, u32[]{:S(2)}) collective-permute-start(f32[16,2048]{1,0:T(8,128)S(1)} %pad_maximum_fusion.1), channel_id=1, source_target_pairs={{0,96},{32,64},{64,32},{96,0},{128,224},{160,192},{192,160},{224,1... | collective-permute-start | bytes 393224 | tf_op jit(solution)/shard_map/ppermute | solution.py:77
  82.4 2.6 %collective-permute-done.4 = f32[16,2048]{1,0:T(8,128)S(1)} collective-permute-done((f32[16,2048]{1,0:T(8,128)S(1)}, f32[16,2048]{1,0:T(8,128)S(1)}, u32[]{:S(2)}, u32[]{:S(2)}) %collective-permute-start.4) | collective-permute-done | bytes 131104 | tf_op jit(solution)/shard_map/ppermute | solution.py:77
  85.1 1.0 copy-done.3
  86.1 4.3 %collective-permute-start.5 = (f32[128,2048]{1,0:T(8,128)S(1)}, f32[128,2048]{1,0:T(8,128)}, u32[]{:S(2)}, u32[]{:S(2)}) collective-permute-start(f32[128,2048]{1,0:T(8,128)S(1)} %constant_dynamic-update-slice_fusion.2), channel_id=1, source_target_pairs={{0,96},{32,64},{64,32},{96,0},{128,224},{160,192},{192,160},{224,1... | collective-permute-start | bytes 3145736 | tf_op jit(solution)/shard_map/ppermute | solution.py:77
  90.4 0.7 copy-done.6
  91.1 0.5 fusion.37
  91.6 0.7 broadcast_in_dim.79
  92.3 9.3 %all-to-all-start.3 = ((f32[8,16,128]{2,1,0:T(8,128)}), f32[8,16,128]{2,1,0:T(8,128)S(1)}, u32[]{:S(2)}, u32[]{:S(2)}) async-start(f32[8,16,128]{2,1,0:T(8,128)} %broadcast_in_dim.79), calls=%async_computation.3 | async-start | bytes 131072 | tf_op jit(solution)/shard_map/all_to_all | solution.py:16
  101.6 3.1 %all-to-all-done.3 = f32[8,16,128]{2,1,0:T(8,128)S(1)} async-done(((f32[8,16,128]{2,1,0:T(8,128)}), f32[8,16,128]{2,1,0:T(8,128)S(1)}, u32[]{:S(2)}, u32[]{:S(2)}) %all-to-all-start.3) | async-done | bytes 65568 | tf_op jit(solution)/shard_map/all_to_all | solution.py:16
  104.7 12.0 %psum.29 = f32[16,128]{1,0:T(8,128)S(1)} all-reduce(f32[16,128]{1,0:T(8,128)S(1)} %reduce_sum.37), channel_id=1, replica_groups={{0,8,16,24},{1,9,17,25},{2,10,18,26},{3,11,19,27},{4,12,20,28},{5,13,21..., use_global_device_ids=true, to_apply=%region_3.0 | all-reduce | flops 2048 | bytes 16384 | tf_op jit(solution)/shard_map/psum | solution.py:21
  116.8 0.4 fusion.38
  117.1 2.2 %collective-permute-start.6 = (f32[8,2048]{1,0:T(8,128)S(1)}, f32[8,2048]{1,0:T(8,128)S(1)}, u32[]{:S(2)}, u32[]{:S(2)}) collective-permute-start(f32[8,2048]{1,0:T(8,128)S(1)} %slice.123), channel_id=1, source_target_pairs={{0,96},{32,64},{64,32},{96,0},{128,224},{160,192},{192,160},{224,1... | collective-permute-start | bytes 196616 | tf_op jit(solution)/shard_map/ppermute | solution.py:77
  119.4 4.0 %collective-permute-done.6 = f32[8,2048]{1,0:T(8,128)S(1)} collective-permute-done((f32[8,2048]{1,0:T(8,128)S(1)}, f32[8,2048]{1,0:T(8,128)S(1)}, u32[]{:S(2)}, u32[]{:S(2)}) %collective-permute-start.6) | collective-permute-done | bytes 65568 | tf_op jit(solution)/shard_map/ppermute | solution.py:77
  123.4 5.9 %collective-permute-start.8 = (f32[8,2048]{1,0:T(8,128)S(1)}, f32[8,2048]{1,0:T(8,128)S(1)}, u32[]{:S(2)}, u32[]{:S(2)}) collective-permute-start(f32[8,2048]{1,0:T(8,128)S(1)} %fusion.12), channel_id=1, source_target_pairs={{0,1},{1,0},{2,3},{3,2},{4,5},{5,4},{6,7},{7,6},{8,9},{9,8},{10,11... | collective-permute-start | bytes 196616 | tf_op jit(solution)/shard_map/ppermute | solution.py:49
  129.2 5.4 %collective-permute-start.7 = (f32[8,2048]{1,0:T(8,128)S(1)}, f32[8,2048]{1,0:T(8,128)S(1)}, u32[]{:S(2)}, u32[]{:S(2)}) collective-permute-start(f32[8,2048]{1,0:T(8,128)S(1)} %fusion.12), channel_id=1, source_target_pairs={{1,2},{3,4},{5,6},{7,8},{9,10},{11,12},{13,14},{15,16},{17,18},{19... | collective-permute-start | bytes 196616 | tf_op jit(solution)/shard_map/ppermute | solution.py:48
  134.7 0.1 copy.36
  134.8 0.1 fusion.33
  134.9 0.1 fusion.34
  135.0 0.1 fusion.32
  135.2 0.1 fusion.31
  135.3 5.5 %collective-permute-done.7 = f32[8,2048]{1,0:T(8,128)S(1)} collective-permute-done((f32[8,2048]{1,0:T(8,128)S(1)}, f32[8,2048]{1,0:T(8,128)S(1)}, u32[]{:S(2)}, u32[]{:S(2)}) %collective-permute-start.7) | collective-permute-done | bytes 65568 | tf_op jit(solution)/shard_map/ppermute | solution.py:48
  140.9 0.1 copy.40
  140.9 0.1 copy.41
  141.0 0.8 copy-done.4
  141.8 0.4 fusion
  142.2 0.5 fusion.39
  142.8 0.5 fusion.40
  143.3 7.2 %all_to_all.31 = f32[8,8,256]{2,1,0:T(8,128)S(1)} all-to-all(f32[8,8,256]{2,1,0:T(8,128)S(1)} %broadcast_in_dim.85), channel_id=1, replica_groups={{0,1,2,3,4,5,6,7},{8,9,10,11,12,13,14,15},{16,17,18,19,20,21,22,23},{24..., dimensions={0} | all-to-all | bytes 131072 | tf_op jit(solution)/shard_map/all_to_all | solution.py:16
  150.5 11.1 %psum.30 = f32[8,256]{1,0:T(8,128)S(1)} all-reduce(f32[8,256]{1,0:T(8,128)S(1)} %reduce_sum.38), channel_id=1, replica_groups={{0,8,16,24},{1,9,17,25},{2,10,18,26},{3,11,19,27},{4,12,20,28},{5,13,21..., use_global_device_ids=true, to_apply=%region_5.6 | all-reduce | flops 2048 | bytes 16384 | tf_op jit(solution)/shard_map/psum | solution.py:21
  161.6 0.4 convolution_subtract_fusion.3
  162.0 0.4 convolution_subtract_fusion.2
  162.3 0.5 fusion.41
  162.8 1.7 fusion.42
  164.6 10.0 %all_to_all.32 = f32[8,8,256]{2,1,0:T(8,128)S(1)} all-to-all(f32[8,8,256]{2,1,0:T(8,128)S(1)} %broadcast_in_dim.86), channel_id=1, replica_groups={{0,1,2,3,4,5,6,7},{8,9,10,11,12,13,14,15},{16,17,18,19,20,21,22,23},{24..., dimensions={0} | all-to-all | bytes 131072 | tf_op jit(solution)/shard_map/all_to_all | solution.py:16
  174.6 12.1 %psum.31 = f32[8,256]{1,0:T(8,128)S(1)} all-reduce(f32[8,256]{1,0:T(8,128)S(1)} %reduce_sum.39), channel_id=1, replica_groups={{0,8,16,24},{1,9,17,25},{2,10,18,26},{3,11,19,27},{4,12,20,28},{5,13,21..., use_global_device_ids=true, to_apply=%region_7.8 | all-reduce | flops 2048 | bytes 16384 | tf_op jit(solution)/shard_map/psum | solution.py:21
  186.7 0.4 convolution_subtract_fusion.1
  187.1 1.6 convolution_subtract_fusion
  188.7 4.7 %collective-permute-start.10 = (f32[8,2048]{1,0:T(8,128)S(1)}, f32[8,2048]{1,0:T(8,128)S(1)}, u32[]{:S(2)}, u32[]{:S(2)}) collective-permute-start(f32[8,2048]{1,0:T(8,128)S(1)} %convolution_subtract_fusion), channel_id=1, source_target_pairs={{0,1},{1,0},{2,3},{3,2},{4,5},{5,4},{6,7},{7,6},{8,9},{9,8},{10,11... | collective-permute-start | bytes 196616 | tf_op jit(solution)/shard_map/ppermute | solution.py:49
  193.4 5.4 %collective-permute-start.9 = (f32[8,2048]{1,0:T(8,128)S(1)}, f32[8,2048]{1,0:T(8,128)S(1)}, u32[]{:S(2)}, u32[]{:S(2)}) collective-permute-start(f32[8,2048]{1,0:T(8,128)S(1)} %convolution_subtract_fusion), channel_id=1, source_target_pairs={{1,2},{3,4},{5,6},{7,8},{9,10},{11,12},{13,14},{15,16},{17,18},{19... | collective-permute-start | bytes 196616 | tf_op jit(solution)/shard_map/ppermute | solution.py:48
  198.8 0.1 copy.50
  198.9 0.1 fusion.29
  199.0 0.1 fusion.30
  199.2 0.1 fusion.28
  199.3 0.1 fusion.27
  199.4 5.5 %collective-permute-done.9 = f32[8,2048]{1,0:T(8,128)S(1)} collective-permute-done((f32[8,2048]{1,0:T(8,128)S(1)}, f32[8,2048]{1,0:T(8,128)S(1)}, u32[]{:S(2)}, u32[]{:S(2)}) %collective-permute-start.9) | collective-permute-done | bytes 65568 | tf_op jit(solution)/shard_map/ppermute | solution.py:48
  205.1 0.1 copy.55
  205.1 1.1 fusion.1
  206.2 0.7 subtract_divide_fusion
  (52 shorter events, 0.6 us)
Async XLA Ops:
  2.5 19.6 %all-to-all-start = ((f32[4,16,2048]{2,1,0:T(8,128)}), f32[4,16,2048]{2,1,0:T(8,128)S(1)}, u32[]{:S(2)}, u32[]{:S(2)}) async-start(f32[4,16,2048]{2,1,0:T(8,128)} %broadcast_in_dim.76), calls=%async_computation | async-start | bytes 1048576 | tf_op jit(solution)/shard_map/all_to_all | solution.py:16
  22.9 3.6 %copy-start.5 = (f32[8,2,1024]{2,1,0:T(2,128)S(1)}, f32[8,2,1024]{2,1,0:T(2,128)}, u32[]{:S(2)}) copy-start(f32[8,2,1024]{2,1,0:T(2,128)} %param.6) | copy-start | bytes 196612
  22.9 21.9 %all-to-all-start.1 = ((f32[4,16,2048]{2,1,0:T(8,128)}), f32[4,16,2048]{2,1,0:T(8,128)S(1)}, u32[]{:S(2)}, u32[]{:S(2)}) async-start(f32[4,16,2048]{2,1,0:T(8,128)} %broadcast_in_dim.77), calls=%async_computation.1 | async-start | bytes 1048576 | tf_op jit(solution)/shard_map/all_to_all | solution.py:16
  26.6 6.6 %collective-permute-start.1 = (f32[8,2048]{1,0:T(8,128)S(1)}, f32[8,2048]{1,0:T(8,128)S(1)}, u32[]{:S(2)}, u32[]{:S(2)}) collective-permute-start(f32[8,2048]{1,0:T(8,128)S(1)} %bitcast.53), channel_id=1, source_target_pairs={{0,96},{32,64},{64,32},{96,0},{128,224},{160,192},{192,160},{224,1... | collective-permute-start | bytes 196616 | tf_op jit(solution)/shard_map/ppermute | solution.py:77
  31.2 13.6 %collective-permute-start = (f32[64,2048]{1,0:T(8,128)S(1)}, f32[64,2048]{1,0:T(8,128)S(1)}, u32[]{:S(2)}, u32[]{:S(2)}) collective-permute-start(f32[64,2048]{1,0:T(8,128)S(1)} %bitcast.41), channel_id=1, source_target_pairs={{0,32},{32,0},{64,96},{96,64},{128,160},{160,128},{192,224},{224,1... | collective-permute-start | bytes 1572872 | tf_op jit(solution)/shard_map/ppermute | solution.py:77
  44.8 2.0 copy-start
  44.9 32.2 %collective-permute-start.3 = (f32[128,2048]{1,0:T(8,128)S(1)}, f32[128,2048]{1,0:T(8,128)S(1)}, u32[]{:S(2)}, u32[]{:S(2)}) collective-permute-start(f32[128,2048]{1,0:T(8,128)S(1)} %constant_dynamic-update-slice_fusion), channel_id=1, source_target_pairs={{0,96},{32,64},{64,32},{96,0},{128,224},{160,192},{192,160},{224,1... | collective-permute-start | bytes 3145736 | tf_op jit(solution)/shard_map/ppermute | solution.py:77
  46.9 30.2 %collective-permute-start.2 = (f32[64,2048]{1,0:T(8,128)S(1)}, f32[64,2048]{1,0:T(8,128)S(1)}, u32[]{:S(2)}, u32[]{:S(2)}) collective-permute-start(f32[64,2048]{1,0:T(8,128)S(1)} %bitcast.39), channel_id=1, source_target_pairs={{0,32},{32,0},{64,96},{96,64},{128,160},{160,128},{192,224},{224,1... | collective-permute-start | bytes 1572872 | tf_op jit(solution)/shard_map/ppermute | solution.py:77
  77.1 0.8 copy-start.2
  77.9 7.1 %copy-start.1 = (f32[4,16,2048]{2,1,0:T(8,128)S(1)}, f32[4,16,2048]{2,1,0:T(8,128)}, u32[]{:S(2)}) copy-start(f32[4,16,2048]{2,1,0:T(8,128)} %copy-done) | copy-start | bytes 1572868
  77.9 7.1 %collective-permute-start.4 = (f32[16,2048]{1,0:T(8,128)S(1)}, f32[16,2048]{1,0:T(8,128)S(1)}, u32[]{:S(2)}, u32[]{:S(2)}) collective-permute-start(f32[16,2048]{1,0:T(8,128)S(1)} %pad_maximum_fusion.1), channel_id=1, source_target_pairs={{0,96},{32,64},{64,32},{96,0},{128,224},{160,192},{192,160},{224,1... | collective-permute-start | bytes 393224 | tf_op jit(solution)/shard_map/ppermute | solution.py:77
  85.0 1.0 copy-start.3
  86.1 30.6 %collective-permute-start.5 = (f32[128,2048]{1,0:T(8,128)S(1)}, f32[128,2048]{1,0:T(8,128)}, u32[]{:S(2)}, u32[]{:S(2)}) collective-permute-start(f32[128,2048]{1,0:T(8,128)S(1)} %constant_dynamic-update-slice_fusion.2), channel_id=1, source_target_pairs={{0,96},{32,64},{64,32},{96,0},{128,224},{160,192},{192,160},{224,1... | collective-permute-start | bytes 3145736 | tf_op jit(solution)/shard_map/ppermute | solution.py:77
  90.4 0.7 copy-start.6
  92.3 12.4 %all-to-all-start.3 = ((f32[8,16,128]{2,1,0:T(8,128)}), f32[8,16,128]{2,1,0:T(8,128)S(1)}, u32[]{:S(2)}, u32[]{:S(2)}) async-start(f32[8,16,128]{2,1,0:T(8,128)} %broadcast_in_dim.79), calls=%async_computation.3 | async-start | bytes 131072 | tf_op jit(solution)/shard_map/all_to_all | solution.py:16
  117.1 6.2 %collective-permute-start.6 = (f32[8,2048]{1,0:T(8,128)S(1)}, f32[8,2048]{1,0:T(8,128)S(1)}, u32[]{:S(2)}, u32[]{:S(2)}) collective-permute-start(f32[8,2048]{1,0:T(8,128)S(1)} %slice.123), channel_id=1, source_target_pairs={{0,96},{32,64},{64,32},{96,0},{128,224},{160,192},{192,160},{224,1... | collective-permute-start | bytes 196616 | tf_op jit(solution)/shard_map/ppermute | solution.py:77
  123.4 11.9 %collective-permute-start.8 = (f32[8,2048]{1,0:T(8,128)S(1)}, f32[8,2048]{1,0:T(8,128)S(1)}, u32[]{:S(2)}, u32[]{:S(2)}) collective-permute-start(f32[8,2048]{1,0:T(8,128)S(1)} %fusion.12), channel_id=1, source_target_pairs={{0,1},{1,0},{2,3},{3,2},{4,5},{5,4},{6,7},{7,6},{8,9},{9,8},{10,11... | collective-permute-start | bytes 196616 | tf_op jit(solution)/shard_map/ppermute | solution.py:49
  129.2 11.6 %collective-permute-start.7 = (f32[8,2048]{1,0:T(8,128)S(1)}, f32[8,2048]{1,0:T(8,128)S(1)}, u32[]{:S(2)}, u32[]{:S(2)}) collective-permute-start(f32[8,2048]{1,0:T(8,128)S(1)} %fusion.12), channel_id=1, source_target_pairs={{1,2},{3,4},{5,6},{7,8},{9,10},{11,12},{13,14},{15,16},{17,18},{19... | collective-permute-start | bytes 196616 | tf_op jit(solution)/shard_map/ppermute | solution.py:48
  140.9 0.8 copy-start.4
  141.0 0.8 copy-start.7
  188.7 10.8 %collective-permute-start.10 = (f32[8,2048]{1,0:T(8,128)S(1)}, f32[8,2048]{1,0:T(8,128)S(1)}, u32[]{:S(2)}, u32[]{:S(2)}) collective-permute-start(f32[8,2048]{1,0:T(8,128)S(1)} %convolution_subtract_fusion), channel_id=1, source_target_pairs={{0,1},{1,0},{2,3},{3,2},{4,5},{5,4},{6,7},{7,6},{8,9},{9,8},{10,11... | collective-permute-start | bytes 196616 | tf_op jit(solution)/shard_map/ppermute | solution.py:49
  193.4 11.6 %collective-permute-start.9 = (f32[8,2048]{1,0:T(8,128)S(1)}, f32[8,2048]{1,0:T(8,128)S(1)}, u32[]{:S(2)}, u32[]{:S(2)}) collective-permute-start(f32[8,2048]{1,0:T(8,128)S(1)} %convolution_subtract_fusion), channel_id=1, source_target_pairs={{1,2},{3,4},{5,6},{7,8},{9,10},{11,12},{13,14},{15,16},{17,18},{19... | collective-permute-start | bytes 196616 | tf_op jit(solution)/shard_map/ppermute | solution.py:48

commit v13 on v12

--- a/solution.py
+++ b/solution.py
@@ -45,8 +45,8 @@
     count = lax.axis_size("space")
     outer = [(i, i + 1) for i in range(1, count - 1, 2)]
     outer = outer + [(j, i) for i, j in outer]
+    inside = lax.ppermute(vectors, "space", [(i, i ^ 1) for i in range(count)])
     across = lax.ppermute(vectors, "space", outer)
-    inside = lax.ppermute(vectors, "space", [(i, i ^ 1) for i in range(count)])
     first = lax.axis_index("space") % 2 == 0
     return jnp.where(first, across, inside), jnp.where(first, inside, across)
 
@@ -95,11 +95,12 @@
     own = [states.reshape(-1, cells) for states in occupied]
     diagonal = 3.75 + potential[None, :, :] - energies[:, None, None]
     vectors = initial.reshape(count, cells)
-    run, other = tie((copies(own[0], "band", BAND_Z).reshape(-1, cells), own[1]))
+    pair = jnp.concatenate([vectors, swapped(vectors, 3)], axis=0)
+    run = copies(own[0], "band", BAND_Z).reshape(-1, cells)
+    run, other, pair = tie((run, own[1], pair))
     across = swapped(run, 1)
     second = copies(other, "band", BAND_Z).reshape(-1, cells)
-    pair = jnp.concatenate([vectors, swapped(vectors, 3)], axis=0)
-    across, second, pair = tie((across, second, pair))
+    across, second = tie((across, second))
     near = [jnp.concatenate([run, across], axis=0)]
     margin = space_sum(products(pair, near[0])) * weight
     margin, across, far = tie((margin, swapped(second, 1), swapped(near[0], 3)))
@@ -108,10 +109,10 @@
     pair, second, across = tie((pair - partial - other, second, across))
     near.append(jnp.concatenate([second, across], axis=0))
     margin = space_sum(products(pair, near[1])) * weight
-    margin, far_second = tie((margin, swapped(near[1], 3)))
     partial = combination(margin, near[1])
     vectors = pair[:count] - partial[:count] - swapped(partial[count:], 3)
-    blocks = [(near[0], far), (near[1], far_second)]
+    vectors, sent = tie((vectors, near[1]))
+    blocks = [(near[0], far), (near[1], swapped(sent, 3))]
     for iteration in range(ITERS):
         if iteration > 0:
             for block in blocks:

time: 210 us -> 212 us (level)
  starting transfers between devices: 61.4 us -> 74.8 us
  blocking collectives: 80 us -> 67.3 us
    all_to_all x3 -> x1, blocking collectives: 27.6 us -> 8.57 us  [copies(): return lax.all_to_all(sent, axis, 0, 0, axis_index_groups=groups)]
    all_to_all x3 -> x5, starting transfers between devices: 18.5 us -> 29.6 us  [copies(): return lax.all_to_all(sent, axis, 0, 0, axis_index_groups=groups)]
    ppermute x7, waiting for transfers between devices: 18.2 us -> 28.7 us  [swapped(): lax.ppermute(x, 'band', [(i, i ^ bits) for i in range(lax.axis_size('band...]
    ppermute x2, waiting for transfers between devices: 11.1 us -> 4.42 us  [neighbours(): across = lax.ppermute(vectors, 'space', outer)]
    psum x4, blocking collectives: 52.4 us -> 58.7 us  [space_sum(): return lax.psum(near, 'space', axis_index_groups=SPACE_Z)]
    ppermute x2, starting transfers between devices: 10.9 us -> 16 us  [neighbours(): across = lax.ppermute(vectors, 'space', outer)]
    ppermute x2, starting transfers between devices: 10.6 us -> 6.61 us  [neighbours(): inside = lax.ppermute(vectors, 'space', [(i, i ^ 1) for i in range(count)])]
    all_to_all x3 -> x5, waiting for transfers between devices: 17.1 us -> 14.2 us  [copies(): return lax.all_to_all(sent, axis, 0, 0, axis_index_groups=groups)]
  transfers between devices with their start and end apart: 14 -> 16, of which waited for: 7 -> 12; matrix products, arithmetic and copies ran while one was open for 1% -> 2% of each run, Pallas kernels for 0% -> 0%
where the time goes in v13:
time: 212 us; the launch traced here: 210 us
  starting transfers between devices  74.8 us (35%)
  blocking collectives  67.3 us (32%)
  waiting for transfers between devices  47.8 us (23%)
  local copies, waits for them, and re-layouts  8.46 us (4%)
  matrix products  7.66 us (4%)
  other arithmetic  2.46 us (1%)
    psum x4, blocking collectives, space_sum(): return lax.psum(near, 'space', axis_index_groups=SPACE_Z)  58.7 us
    all_to_all x5, starting transfers between devices, copies(): return lax.all_to_all(sent, axis, 0, 0, axis_index_groups=groups)  29.6 us
    ppermute x7, waiting for transfers between devices, swapped(): lax.ppermute(x, 'band', [(i, i ^ bits) for i in range(lax.axis_size('band...  28.7 us
    ppermute x7, starting transfers between devices, swapped(): lax.ppermute(x, 'band', [(i, i ^ bits) for i in range(lax.axis_size('band...  22.6 us
    ppermute x2, starting transfers between devices, neighbours(): across = lax.ppermute(vectors, 'space', outer)  16 us
    all_to_all x5, waiting for transfers between devices, copies(): return lax.all_to_all(sent, axis, 0, 0, axis_index_groups=groups)  14.2 us
    all_to_all x1, blocking collectives, copies(): return lax.all_to_all(sent, axis, 0, 0, axis_index_groups=groups)  8.57 us
    ppermute x2, starting transfers between devices, neighbours(): inside = lax.ppermute(vectors, 'space', [(i, i ^ 1) for i in range(count)])  6.61 us
  transfers between devices with their start and end apart: 16, of which 12 were waited for; matrix products, arithmetic and copies ran while one was open for 2% of the time, Pallas kernels for 0%

profile of v13, /device:TPU:7, one launch (start us, length us, event | category | flops | bytes accessed | tf_op | source)
XLA Modules:
  0.0 209.6 jit_solution(12664521926842787137)
XLA Ops:
  0.6 1.0 fusion.29
  1.7 0.8 broadcast_in_dim.76
  2.5 5.7 %all-to-all-start = ((f32[4,16,2048]{2,1,0:T(8,128)}), f32[4,16,2048]{2,1,0:T(8,128)S(1)}, u32[]{:S(2)}, u32[]{:S(2)}) async-start(f32[4,16,2048]{2,1,0:T(8,128)} %broadcast_in_dim.76), calls=%async_computation | async-start | bytes 1048576 | tf_op jit(solution)/shard_map/all_to_all | solution.py:16
  8.3 4.6 %collective-permute-start = (f32[8,2048]{1,0:T(8,128)S(1)}, f32[8,2048]{1,0:T(8,128)S(1)}, u32[]{:S(2)}, u32[]{:S(2)}) collective-permute-start(f32[8,2048]{1,0:T(8,128)S(1)} %bitcast.52), channel_id=1, source_target_pairs={{0,96},{32,64},{64,32},{96,0},{128,224},{160,192},{192,160},{224,1... | collective-permute-start | bytes 196616 | tf_op jit(solution)/shard_map/ppermute | solution.py:77
  13.0 1.9 collective-permute-done
  14.9 7.4 %all-to-all-done = f32[4,16,2048]{2,1,0:T(8,128)S(1)} async-done(((f32[4,16,2048]{2,1,0:T(8,128)}), f32[4,16,2048]{2,1,0:T(8,128)S(1)}, u32[]{:S(2)}, u32[]{:S(2)}) %all-to-all-start) | async-done | bytes 524320 | tf_op jit(solution)/shard_map/all_to_all | solution.py:16
  22.2 0.8 broadcast_in_dim.77
  23.1 3.5 %all-to-all-start.1 = ((f32[4,16,2048]{2,1,0:T(8,128)}), f32[4,16,2048]{2,1,0:T(8,128)S(1)}, u32[]{:S(2)}, u32[]{:S(2)}) async-start(f32[4,16,2048]{2,1,0:T(8,128)} %broadcast_in_dim.77), calls=%async_computation.1 | async-start | bytes 1048576 | tf_op jit(solution)/shard_map/all_to_all | solution.py:16
  26.5 3.2 %collective-permute-start.1 = (f32[64,2048]{1,0:T(8,128)S(1)}, f32[64,2048]{1,0:T(8,128)S(1)}, u32[]{:S(2)}, u32[]{:S(2)}) collective-permute-start(f32[64,2048]{1,0:T(8,128)S(1)} %bitcast.40), channel_id=1, source_target_pairs={{0,32},{32,0},{64,96},{96,64},{128,160},{160,128},{192,224},{224,1... | collective-permute-start | bytes 1572872 | tf_op jit(solution)/shard_map/ppermute | solution.py:77
  29.8 10.6 %collective-permute-done.1 = f32[64,2048]{1,0:T(8,128)S(1)} collective-permute-done((f32[64,2048]{1,0:T(8,128)S(1)}, f32[64,2048]{1,0:T(8,128)S(1)}, u32[]{:S(2)}, u32[]{:S(2)}) %collective-permute-start.1) | collective-permute-done | bytes 524320 | tf_op jit(solution)/shard_map/ppermute | solution.py:77
  40.5 4.6 %collective-permute-start.3 = (f32[128,2048]{1,0:T(8,128)S(1)}, f32[128,2048]{1,0:T(8,128)S(1)}, u32[]{:S(2)}, u32[]{:S(2)}) collective-permute-start(f32[128,2048]{1,0:T(8,128)S(1)} %constant_dynamic-update-slice_fusion), channel_id=1, source_target_pairs={{0,96},{32,64},{64,32},{96,0},{128,224},{160,192},{192,160},{224,1... | collective-permute-start | bytes 3145736 | tf_op jit(solution)/shard_map/ppermute | solution.py:77
  45.2 1.9 collective-permute-start.2
  47.1 0.5 fusion.39
  47.6 0.7 broadcast_in_dim.78
  48.3 7.1 %all-to-all-start.2 = ((f32[8,16,128]{2,1,0:T(8,128)}), f32[8,16,128]{2,1,0:T(8,128)S(1)}, u32[]{:S(2)}, u32[]{:S(2)}) async-start(f32[8,16,128]{2,1,0:T(8,128)} %broadcast_in_dim.78), calls=%async_computation.2 | async-start | bytes 131072 | tf_op jit(solution)/shard_map/all_to_all | solution.py:16
  55.4 3.1 %all-to-all-done.2 = f32[8,16,128]{2,1,0:T(8,128)S(1)} async-done(((f32[8,16,128]{2,1,0:T(8,128)}), f32[8,16,128]{2,1,0:T(8,128)S(1)}, u32[]{:S(2)}, u32[]{:S(2)}) %all-to-all-start.2) | async-done | bytes 65568 | tf_op jit(solution)/shard_map/all_to_all | solution.py:16
  58.6 17.2 %psum.28 = f32[16,128]{1,0:T(8,128)S(1)} all-reduce(f32[16,128]{1,0:T(8,128)S(1)} %reduce_sum.36), channel_id=1, replica_groups={{0,8,16,24},{1,9,17,25},{2,10,18,26},{3,11,19,27},{4,12,20,28},{5,13,21..., use_global_device_ids=true, to_apply=%region_1.0 | all-reduce | flops 2048 | bytes 16384 | tf_op jit(solution)/shard_map/psum | solution.py:21
  75.8 0.4 fusion.40
  76.2 0.4 copy-done.2
  76.6 2.8 %collective-permute-start.4 = (f32[16,2048]{1,0:T(8,128)S(1)}, f32[16,2048]{1,0:T(8,128)S(1)}, u32[]{:S(2)}, u32[]{:S(2)}) collective-permute-start(f32[16,2048]{1,0:T(8,128)S(1)} %pad_maximum_fusion.1), channel_id=1, source_target_pairs={{0,96},{32,64},{64,32},{96,0},{128,224},{160,192},{192,160},{224,1... | collective-permute-start | bytes 393224 | tf_op jit(solution)/shard_map/ppermute | solution.py:77
  79.5 4.2 %collective-permute-done.4 = f32[16,2048]{1,0:T(8,128)S(1)} collective-permute-done((f32[16,2048]{1,0:T(8,128)S(1)}, f32[16,2048]{1,0:T(8,128)S(1)}, u32[]{:S(2)}, u32[]{:S(2)}) %collective-permute-start.4) | collective-permute-done | bytes 131104 | tf_op jit(solution)/shard_map/ppermute | solution.py:77
  83.8 1.0 copy-done.3
  84.8 0.5 fusion.41
  85.3 0.7 broadcast_in_dim.79
  86.0 9.0 %all-to-all-start.3 = ((f32[8,16,128]{2,1,0:T(8,128)}), f32[8,16,128]{2,1,0:T(8,128)S(1)}, u32[]{:S(2)}, u32[]{:S(2)}) async-start(f32[8,16,128]{2,1,0:T(8,128)} %broadcast_in_dim.79), calls=%async_computation.3 | async-start | bytes 131072 | tf_op jit(solution)/shard_map/all_to_all | solution.py:16
  95.0 3.1 %all-to-all-done.3 = f32[8,16,128]{2,1,0:T(8,128)S(1)} async-done(((f32[8,16,128]{2,1,0:T(8,128)}), f32[8,16,128]{2,1,0:T(8,128)S(1)}, u32[]{:S(2)}, u32[]{:S(2)}) %all-to-all-start.3) | async-done | bytes 65568 | tf_op jit(solution)/shard_map/all_to_all | solution.py:16
  98.1 12.0 %psum.29 = f32[16,128]{1,0:T(8,128)S(1)} all-reduce(f32[16,128]{1,0:T(8,128)S(1)} %reduce_sum.37), channel_id=1, replica_groups={{0,8,16,24},{1,9,17,25},{2,10,18,26},{3,11,19,27},{4,12,20,28},{5,13,21..., use_global_device_ids=true, to_apply=%region_3.0 | all-reduce | flops 2048 | bytes 16384 | tf_op jit(solution)/shard_map/psum | solution.py:21
  110.1 0.4 fusion.13
  110.5 2.7 %collective-permute-start.5 = (f32[8,2048]{1,0:T(8,128)S(1)}, f32[8,2048]{1,0:T(8,128)S(1)}, u32[]{:S(2)}, u32[]{:S(2)}) collective-permute-start(f32[8,2048]{1,0:T(8,128)S(1)} %slice.123), channel_id=1, source_target_pairs={{0,96},{32,64},{64,32},{96,0},{128,224},{160,192},{192,160},{224,1... | collective-permute-start | bytes 196616 | tf_op jit(solution)/shard_map/ppermute | solution.py:77
  113.2 3.5 %collective-permute-done.5 = f32[8,2048]{1,0:T(8,128)S(1)} collective-permute-done((f32[8,2048]{1,0:T(8,128)S(1)}, f32[8,2048]{1,0:T(8,128)S(1)}, u32[]{:S(2)}, u32[]{:S(2)}) %collective-permute-start.5) | collective-permute-done | bytes 65568 | tf_op jit(solution)/shard_map/ppermute | solution.py:77
  116.8 9.4 %collective-permute-start.6 = (f32[8,2048]{1,0:T(8,128)S(1)}, f32[8,2048]{1,0:T(8,128)S(1)}, u32[]{:S(2)}, u32[]{:S(2)}) collective-permute-start(f32[8,2048]{1,0:T(8,128)S(1)} %fusion.12), channel_id=1, source_target_pairs={{1,2},{3,4},{5,6},{7,8},{9,10},{11,12},{13,14},{15,16},{17,18},{19... | collective-permute-start | bytes 196616 | tf_op jit(solution)/shard_map/ppermute | solution.py:49
  126.2 1.9 collective-permute-start.7
  128.1 0.1 fusion.35
  128.3 0.1 fusion.36
  128.4 0.1 fusion.37
  128.6 0.1 fusion.38
  128.7 0.6 collective-permute-done.7
  129.5 0.8 copy-done.4
  130.2 0.4 fusion
  130.7 0.5 fusion.42
  131.2 0.5 fusion.43
  131.7 0.7 broadcast_in_dim.85
  132.4 4.3 %all-to-all-start.4 = ((f32[8,8,256]{2,1,0:T(8,128)}), f32[8,8,256]{2,1,0:T(8,128)S(1)}, u32[]{:S(2)}, u32[]{:S(2)}) async-start(f32[8,8,256]{2,1,0:T(8,128)} %broadcast_in_dim.85), calls=%async_computation.4 | async-start | bytes 131072 | tf_op jit(solution)/shard_map/all_to_all | solution.py:16
  136.7 2.7 %collective-permute-start.8 = (f32[128,2048]{1,0:T(8,128)S(1)}, f32[128,2048]{1,0:T(8,128)}, u32[]{:S(2)}, u32[]{:S(2)}) collective-permute-start(f32[128,2048]{1,0:T(8,128)S(1)} %constant_dynamic-update-slice_fusion.2), channel_id=1, source_target_pairs={{0,96},{32,64},{64,32},{96,0},{128,224},{160,192},{192,160},{224,1... | collective-permute-start | bytes 3145736 | tf_op jit(solution)/shard_map/ppermute | solution.py:77
  139.4 0.5 all-to-all-done.4
  139.9 14.7 %psum.30 = f32[8,256]{1,0:T(8,128)S(1)} all-reduce(f32[8,256]{1,0:T(8,128)S(1)} %reduce_sum.38), channel_id=1, replica_groups={{0,8,16,24},{1,9,17,25},{2,10,18,26},{3,11,19,27},{4,12,20,28},{5,13,21..., use_global_device_ids=true, to_apply=%region_5.6 | all-reduce | flops 2048 | bytes 16384 | tf_op jit(solution)/shard_map/psum | solution.py:21
  154.6 0.4 convolution_subtract_fusion.3
  155.0 0.4 convolution_subtract_fusion.2
  155.3 0.5 fusion.44
  155.8 8.4 %collective-permute-done.8 = f32[128,2048]{1,0:T(8,128)} collective-permute-done((f32[128,2048]{1,0:T(8,128)S(1)}, f32[128,2048]{1,0:T(8,128)}, u32[]{:S(2)}, u32[]{:S(2)}) %collective-permute-start.8) | collective-permute-done | bytes 1048608 | tf_op jit(solution)/shard_map/ppermute | solution.py:77
  164.3 1.7 fusion.45
  166.1 8.6 %all_to_all.30 = f32[8,8,256]{2,1,0:T(8,128)S(1)} all-to-all(f32[8,8,256]{2,1,0:T(8,128)S(1)} %broadcast_in_dim.86), channel_id=1, replica_groups={{0,1,2,3,4,5,6,7},{8,9,10,11,12,13,14,15},{16,17,18,19,20,21,22,23},{24..., dimensions={0} | all-to-all | bytes 131072 | tf_op jit(solution)/shard_map/all_to_all | solution.py:16
  174.6 14.7 %psum.31 = f32[8,256]{1,0:T(8,128)S(1)} all-reduce(f32[8,256]{1,0:T(8,128)S(1)} %reduce_sum.39), channel_id=1, replica_groups={{0,8,16,24},{1,9,17,25},{2,10,18,26},{3,11,19,27},{4,12,20,28},{5,13,21..., use_global_device_ids=true, to_apply=%region_7.8 | all-reduce | flops 2048 | bytes 16384 | tf_op jit(solution)/shard_map/psum | solution.py:21
  189.4 0.4 convolution_subtract_fusion.1
  189.8 1.6 convolution_subtract_fusion
  191.3 4.7 %collective-permute-start.10 = (f32[8,2048]{1,0:T(8,128)S(1)}, f32[8,2048]{1,0:T(8,128)S(1)}, u32[]{:S(2)}, u32[]{:S(2)}) collective-permute-start(f32[8,2048]{1,0:T(8,128)S(1)} %convolution_subtract_fusion), channel_id=1, source_target_pairs={{0,1},{1,0},{2,3},{3,2},{4,5},{5,4},{6,7},{7,6},{8,9},{9,8},{10,11... | collective-permute-start | bytes 196616 | tf_op jit(solution)/shard_map/ppermute | solution.py:48
  196.0 6.6 %collective-permute-start.9 = (f32[8,2048]{1,0:T(8,128)S(1)}, f32[8,2048]{1,0:T(8,128)S(1)}, u32[]{:S(2)}, u32[]{:S(2)}) collective-permute-start(f32[8,2048]{1,0:T(8,128)S(1)} %convolution_subtract_fusion), channel_id=1, source_target_pairs={{1,2},{3,4},{5,6},{7,8},{9,10},{11,12},{13,14},{15,16},{17,18},{19... | collective-permute-start | bytes 196616 | tf_op jit(solution)/shard_map/ppermute | solution.py:49
  202.7 0.1 fusion.31
  202.8 0.1 fusion.32
  202.9 0.1 fusion.33
  203.1 0.1 fusion.34
  203.2 4.4 %collective-permute-done.9 = f32[8,2048]{1,0:T(8,128)S(1)} collective-permute-done((f32[8,2048]{1,0:T(8,128)S(1)}, f32[8,2048]{1,0:T(8,128)S(1)}, u32[]{:S(2)}, u32[]{:S(2)}) %collective-permute-start.9) | collective-permute-done | bytes 65568 | tf_op jit(solution)/shard_map/ppermute | solution.py:49
  207.8 1.1 fusion.1
  208.9 0.7 subtract_divide_fusion
  (53 shorter events, 0.9 us)
Async XLA Ops:
  2.5 5.8 %copy-start.5 = (f32[8,2,1024]{2,1,0:T(2,128)S(1)}, f32[8,2,1024]{2,1,0:T(2,128)}, u32[]{:S(2)}) copy-start(f32[8,2,1024]{2,1,0:T(2,128)} %param.6) | copy-start | bytes 196612
  2.5 19.7 %all-to-all-start = ((f32[4,16,2048]{2,1,0:T(8,128)}), f32[4,16,2048]{2,1,0:T(8,128)S(1)}, u32[]{:S(2)}, u32[]{:S(2)}) async-start(f32[4,16,2048]{2,1,0:T(8,128)} %broadcast_in_dim.76), calls=%async_computation | async-start | bytes 1048576 | tf_op jit(solution)/shard_map/all_to_all | solution.py:16
  8.3 6.6 %collective-permute-start = (f32[8,2048]{1,0:T(8,128)S(1)}, f32[8,2048]{1,0:T(8,128)S(1)}, u32[]{:S(2)}, u32[]{:S(2)}) collective-permute-start(f32[8,2048]{1,0:T(8,128)S(1)} %bitcast.52), channel_id=1, source_target_pairs={{0,96},{32,64},{64,32},{96,0},{128,224},{160,192},{192,160},{224,1... | collective-permute-start | bytes 196616 | tf_op jit(solution)/shard_map/ppermute | solution.py:77
  23.1 17.4 %all-to-all-start.1 = ((f32[4,16,2048]{2,1,0:T(8,128)}), f32[4,16,2048]{2,1,0:T(8,128)S(1)}, u32[]{:S(2)}, u32[]{:S(2)}) async-start(f32[4,16,2048]{2,1,0:T(8,128)} %broadcast_in_dim.77), calls=%async_computation.1 | async-start | bytes 1048576 | tf_op jit(solution)/shard_map/all_to_all | solution.py:16
  26.5 13.9 %collective-permute-start.1 = (f32[64,2048]{1,0:T(8,128)S(1)}, f32[64,2048]{1,0:T(8,128)S(1)}, u32[]{:S(2)}, u32[]{:S(2)}) collective-permute-start(f32[64,2048]{1,0:T(8,128)S(1)} %bitcast.40), channel_id=1, source_target_pairs={{0,32},{32,0},{64,96},{96,64},{128,160},{160,128},{192,224},{224,1... | collective-permute-start | bytes 1572872 | tf_op jit(solution)/shard_map/ppermute | solution.py:77
  40.5 4.7 %copy-start = (f32[4,16,2048]{2,1,0:T(8,128)}, f32[4,16,2048]{2,1,0:T(8,128)S(1)}, u32[]{:S(2)}) copy-start(f32[4,16,2048]{2,1,0:T(8,128)S(1)} %all-to-all-done.1) | copy-start | bytes 1572868
  40.5 35.3 %collective-permute-start.3 = (f32[128,2048]{1,0:T(8,128)S(1)}, f32[128,2048]{1,0:T(8,128)S(1)}, u32[]{:S(2)}, u32[]{:S(2)}) collective-permute-start(f32[128,2048]{1,0:T(8,128)S(1)} %constant_dynamic-update-slice_fusion), channel_id=1, source_target_pairs={{0,96},{32,64},{64,32},{96,0},{128,224},{160,192},{192,160},{224,1... | collective-permute-start | bytes 3145736 | tf_op jit(solution)/shard_map/ppermute | solution.py:77
  45.2 30.6 %collective-permute-start.2 = (f32[64,2048]{1,0:T(8,128)S(1)}, f32[64,2048]{1,0:T(8,128)S(1)}, u32[]{:S(2)}, u32[]{:S(2)}) collective-permute-start(f32[64,2048]{1,0:T(8,128)S(1)} %bitcast.38), channel_id=1, source_target_pairs={{0,32},{32,0},{64,96},{96,64},{128,160},{160,128},{192,224},{224,1... | collective-permute-start | bytes 1572872 | tf_op jit(solution)/shard_map/ppermute | solution.py:77
  48.3 10.3 %all-to-all-start.2 = ((f32[8,16,128]{2,1,0:T(8,128)}), f32[8,16,128]{2,1,0:T(8,128)S(1)}, u32[]{:S(2)}, u32[]{:S(2)}) async-start(f32[8,16,128]{2,1,0:T(8,128)} %broadcast_in_dim.78), calls=%async_computation.2 | async-start | bytes 131072 | tf_op jit(solution)/shard_map/all_to_all | solution.py:16
  75.8 0.8 copy-start.2
  75.8 3.6 %copy-start.6 = (f32[2,1024]{1,0:T(2,128)S(1)}, f32[2,1024]{1,0:T(2,128)}, u32[]{:S(2)}) copy-start(f32[2,1024]{1,0:T(2,128)} %param.8) | copy-start | bytes 24580
  76.6 7.1 %copy-start.1 = (f32[4,16,2048]{2,1,0:T(8,128)S(1)}, f32[4,16,2048]{2,1,0:T(8,128)}, u32[]{:S(2)}) copy-start(f32[4,16,2048]{2,1,0:T(8,128)} %copy-done) | copy-start | bytes 1572868
  76.6 7.1 %collective-permute-start.4 = (f32[16,2048]{1,0:T(8,128)S(1)}, f32[16,2048]{1,0:T(8,128)S(1)}, u32[]{:S(2)}, u32[]{:S(2)}) collective-permute-start(f32[16,2048]{1,0:T(8,128)S(1)} %pad_maximum_fusion.1), channel_id=1, source_target_pairs={{0,96},{32,64},{64,32},{96,0},{128,224},{160,192},{192,160},{224,1... | collective-permute-start | bytes 393224 | tf_op jit(solution)/shard_map/ppermute | solution.py:77
  83.7 1.0 copy-start.3
  86.0 12.1 %all-to-all-start.3 = ((f32[8,16,128]{2,1,0:T(8,128)}), f32[8,16,128]{2,1,0:T(8,128)S(1)}, u32[]{:S(2)}, u32[]{:S(2)}) async-start(f32[8,16,128]{2,1,0:T(8,128)} %broadcast_in_dim.79), calls=%async_computation.3 | async-start | bytes 131072 | tf_op jit(solution)/shard_map/all_to_all | solution.py:16
  110.5 6.2 %collective-permute-start.5 = (f32[8,2048]{1,0:T(8,128)S(1)}, f32[8,2048]{1,0:T(8,128)S(1)}, u32[]{:S(2)}, u32[]{:S(2)}) collective-permute-start(f32[8,2048]{1,0:T(8,128)S(1)} %slice.123), channel_id=1, source_target_pairs={{0,96},{32,64},{64,32},{96,0},{128,224},{160,192},{192,160},{224,1... | collective-permute-start | bytes 196616 | tf_op jit(solution)/shard_map/ppermute | solution.py:77
  116.8 11.9 %collective-permute-start.6 = (f32[8,2048]{1,0:T(8,128)S(1)}, f32[8,2048]{1,0:T(8,128)S(1)}, u32[]{:S(2)}, u32[]{:S(2)}) collective-permute-start(f32[8,2048]{1,0:T(8,128)S(1)} %fusion.12), channel_id=1, source_target_pairs={{1,2},{3,4},{5,6},{7,8},{9,10},{11,12},{13,14},{15,16},{17,18},{19... | collective-permute-start | bytes 196616 | tf_op jit(solution)/shard_map/ppermute | solution.py:49
  126.2 3.1 %collective-permute-start.7 = (f32[8,2048]{1,0:T(8,128)S(1)}, f32[8,2048]{1,0:T(8,128)S(1)}, u32[]{:S(2)}, u32[]{:S(2)}) collective-permute-start(f32[8,2048]{1,0:T(8,128)S(1)} %fusion.12), channel_id=1, source_target_pairs={{0,1},{1,0},{2,3},{3,2},{4,5},{5,4},{6,7},{7,6},{8,9},{9,8},{10,11... | collective-permute-start | bytes 196616 | tf_op jit(solution)/shard_map/ppermute | solution.py:48
  129.4 0.8 copy-start.4
  129.5 0.8 copy-start.7
  132.4 7.4 %all-to-all-start.4 = ((f32[8,8,256]{2,1,0:T(8,128)}), f32[8,8,256]{2,1,0:T(8,128)S(1)}, u32[]{:S(2)}, u32[]{:S(2)}) async-start(f32[8,8,256]{2,1,0:T(8,128)} %broadcast_in_dim.85), calls=%async_computation.4 | async-start | bytes 131072 | tf_op jit(solution)/shard_map/all_to_all | solution.py:16
  136.7 27.6 %collective-permute-start.8 = (f32[128,2048]{1,0:T(8,128)S(1)}, f32[128,2048]{1,0:T(8,128)}, u32[]{:S(2)}, u32[]{:S(2)}) collective-permute-start(f32[128,2048]{1,0:T(8,128)S(1)} %constant_dynamic-update-slice_fusion.2), channel_id=1, source_target_pairs={{0,96},{32,64},{64,32},{96,0},{128,224},{160,192},{192,160},{224,1... | collective-permute-start | bytes 3145736 | tf_op jit(solution)/shard_map/ppermute | solution.py:77
  191.3 11.9 %collective-permute-start.10 = (f32[8,2048]{1,0:T(8,128)S(1)}, f32[8,2048]{1,0:T(8,128)S(1)}, u32[]{:S(2)}, u32[]{:S(2)}) collective-permute-start(f32[8,2048]{1,0:T(8,128)S(1)} %convolution_subtract_fusion), channel_id=1, source_target_pairs={{0,1},{1,0},{2,3},{3,2},{4,5},{5,4},{6,7},{7,6},{8,9},{9,8},{10,11... | collective-permute-start | bytes 196616 | tf_op jit(solution)/shard_map/ppermute | solution.py:48
  196.0 11.6 %collective-permute-start.9 = (f32[8,2048]{1,0:T(8,128)S(1)}, f32[8,2048]{1,0:T(8,128)S(1)}, u32[]{:S(2)}, u32[]{:S(2)}) collective-permute-start(f32[8,2048]{1,0:T(8,128)S(1)} %convolution_subtract_fusion), channel_id=1, source_target_pairs={{1,2},{3,4},{5,6},{7,8},{9,10},{11,12},{13,14},{15,16},{17,18},{19... | collective-permute-start | bytes 196616 | tf_op jit(solution)/shard_map/ppermute | solution.py:49

commit v14 on v1

--- a/solution.py
+++ b/solution.py
@@ -15,11 +15,6 @@
     count = len(groups[0])
     sent = jnp.broadcast_to(x[None], (count,) + x.shape)
     return lax.all_to_all(sent, axis, 0, 0, axis_index_groups=groups)
-
-
-def gathered(states):
-    columns = copies(states, "band", BAND_Z)
-    return copies(columns, "band", BAND_Y).reshape(-1, states.shape[-1])
 
 
 def space_sum(x):
@@ -47,12 +42,25 @@
     )
 
 
+def summed_margin(parts, vectors, weight):
+    product = jnp.concatenate([products(vectors, part) for part in parts], axis=1)
+    return space_sum(product) * weight
+
+
+def corrected(parts, vectors, margin):
+    at = 0
+    for part in parts:
+        vectors = vectors - combination(margin[:, at : at + part.shape[0]], part)
+        at += part.shape[0]
+    return vectors
+
+
 def neighbours(vectors):
     count = lax.axis_size("space")
     outer = [(i, i + 1) for i in range(1, count - 1, 2)]
     outer = outer + [(j, i) for i, j in outer]
+    inside = lax.ppermute(vectors, "space", [(i, i ^ 1) for i in range(count)])
     across = lax.ppermute(vectors, "space", outer)
-    inside = lax.ppermute(vectors, "space", [(i, i ^ 1) for i in range(count)])
     first = lax.axis_index("space") % 2 == 0
     return jnp.where(first, across, inside), jnp.where(first, inside, across)
 
@@ -79,24 +87,35 @@
     return second / 24.0 - 2.0 / 3.0 * nearest
 
 
+def swapped(x, bits):
+    return lax.ppermute(x, "band", [(i, i ^ bits) for i in range(lax.axis_size("band"))])
+
+
 def on_device(occupied, initial, right_side, potential, energies):
     count, planes, line = initial.shape
-    weight = 1.0 / (planes * lax.axis_size("space") * line)
-    states = [occupied[0].reshape(-1, planes * line), occupied[1].reshape(-1, planes * line)]
-    later = lax.all_gather(states[1], "band", axis=0, tiled=True)
-    blocks = [gathered(states[0]), later]
+    cells = planes * line
+    weight = 1.0 / (lax.axis_size("space") * cells)
+    tie = lax.optimization_barrier
+    own = [states.reshape(-1, cells) for states in occupied]
     diagonal = 3.75 + potential[None, :, :] - energies[:, None, None]
-    vectors = initial.reshape(count, planes * line)
+    vectors = initial.reshape(count, cells)
+    run = copies(jnp.stack(own), "band", BAND_Z)
+    first, run = tie((copies(run[:, 0].reshape(-1, cells), "band", BAND_Y).reshape(-1, cells), run[:, 1]))
+    run = run.reshape(-1, cells)
+    second = (run,) + tuple(swapped(run, bits) for bits in (1, 3, 2))
+    blocks = [(first,), second]
     for iteration in range(ITERS):
-        for block in blocks:
-            margin = space_sum(products(vectors, block)) * weight
-            vectors = vectors - combination(margin, block)
+        for index in range(2):
+            margin = summed_margin(blocks[index], vectors, weight)
+            if iteration == 0 and index == 0:
+                margin, blocks[1] = tie((margin, blocks[1]))
+            vectors = corrected(blocks[index], vectors, margin)
         low, high = neighbours(vectors)
         shape = (count, planes, line)
         vectors = vectors.reshape(shape)
         rest = right_side - coupling(vectors, low.reshape(shape), high.reshape(shape))
         residual = rest - diagonal * vectors
-        vectors = (rest / diagonal).reshape(count, planes * line)
+        vectors = (rest / diagonal).reshape(count, cells)
     return (vectors.reshape(shape), residual)
 
 

time: 215 us -> 218 us (1.014)
  between operations: 14.3 us -> 1.05 us
  blocking collectives: 93 us -> 101 us
  matrix products: 9.32 us -> 16.1 us
  starting transfers between devices: 45.2 us -> 47.8 us
    ppermute x2, waiting for transfers between devices: 0.01 us -> 12.7 us  [neighbours(): across = lax.ppermute(vectors, 'space', outer)]
    all_to_all x3, blocking collectives: 36.3 us -> 47.6 us  [copies(): return lax.all_to_all(sent, axis, 0, 0, axis_index_groups=groups)]
    ppermute x2, starting transfers between devices: 21 us -> 9.82 us  [neighbours(): across = lax.ppermute(vectors, 'space', outer)]
    all_to_all x3, waiting for transfers between devices: 41.5 us -> 30.5 us  [copies(): return lax.all_to_all(sent, axis, 0, 0, axis_index_groups=groups)]
    ppermute x0 -> x3, starting transfers between devices: none -> 8.41 us  [swapped(): lax.ppermute(x, 'band', [(i, i ^ bits) for i in range(lax.axis_size('band...]
    ppermute x2, starting transfers between devices: 3.84 us -> 9.2 us  [neighbours(): inside = lax.ppermute(vectors, 'space', [(i, i ^ 1) for i in range(count)])]
    dot_general x4 -> x10, matrix products: 4.04 us -> 7.52 us  [combination(): jnp.einsum('vj,jc->vc', margin, states, precision=lax.Precision.HIGH, pre...]
    psum x4, blocking collectives: 56.7 us -> 53.2 us  [space_sum(): return lax.psum(near, 'space', axis_index_groups=SPACE_Z)]
  transfers between devices with their start and end apart: 8 -> 10, of which waited for: 5 -> 5; matrix products, arithmetic and copies ran while one was open for 2% -> 1% of each run, Pallas kernels for 0% -> 0%
where the time goes in v14:
time: 218 us; the launch traced here: 217 us
  blocking collectives  101 us (46%)
  starting transfers between devices  47.8 us (22%)
  waiting for transfers between devices  43.2 us (20%)
  matrix products  16.1 us (7%)
  local copies, waits for them, and re-layouts  5.76 us (3%)
  other arithmetic  2.56 us (1%)
    psum x4, blocking collectives, space_sum(): return lax.psum(near, 'space', axis_index_groups=SPACE_Z)  53.2 us
    all_to_all x3, blocking collectives, copies(): return lax.all_to_all(sent, axis, 0, 0, axis_index_groups=groups)  47.6 us
    all_to_all x3, waiting for transfers between devices, copies(): return lax.all_to_all(sent, axis, 0, 0, axis_index_groups=groups)  30.5 us
    all_to_all x3, starting transfers between devices, copies(): return lax.all_to_all(sent, axis, 0, 0, axis_index_groups=groups)  20.3 us
    ppermute x2, waiting for transfers between devices, neighbours(): across = lax.ppermute(vectors, 'space', outer)  12.7 us
    ppermute x2, starting transfers between devices, neighbours(): across = lax.ppermute(vectors, 'space', outer)  9.82 us
    ppermute x2, starting transfers between devices, neighbours(): inside = lax.ppermute(vectors, 'space', [(i, i ^ 1) for i in range(count)])  9.2 us
    dot_general x10, matrix products, products(): jnp.einsum('vc,jc->vj', vectors, states, precision=lax.Precision.HIGH, pr...  8.55 us
  transfers between devices with their start and end apart: 10, of which 5 were waited for; matrix products, arithmetic and copies ran while one was open for 1% of the time, Pallas kernels for 0%

profile of v14, /device:TPU:7, one launch (start us, length us, event | category | flops | bytes accessed | tf_op | source)
XLA Modules:
  0.0 217.1 jit_solution(14944763258481980444)
XLA Ops:
  0.6 1.0 fusion.43
  1.6 0.1 stack_reshape_unstack.6
  1.7 0.1 stack_reshape_unstack.7
  1.9 0.1 broadcast_in_dim.75
  2.0 30.3 %all_to_all.30 = f32[4,2,16,2048]{3,2,1,0:T(8,128)S(1)} all-to-all(f32[4,2,16,2048]{3,2,1,0:T(8,128)S(1)} %broadcast_in_dim.75), channel_id=1, replica_groups={{0,128,256,384},{32,160,288,416},{64,192,320,448},{96,224,352,480},{1,1..., dimensions={0} | all-to-all | bytes 2097152 | tf_op jit(solution)/shard_map/all_to_all | solution.py:17
  32.3 0.1 slice_bitcast_fusion
  32.4 1.6 broadcast_in_dim.77
  34.0 4.3 %all-to-all-start.1 = ((f32[4,64,2048]{2,1,0:T(8,128)}), f32[4,64,2048]{2,1,0:T(8,128)S(1)}, u32[]{:S(2)}, u32[]{:S(2)}) async-start(f32[4,64,2048]{2,1,0:T(8,128)} %broadcast_in_dim.77), calls=%async_computation.1 | async-start | bytes 4194304 | tf_op jit(solution)/shard_map/all_to_all | solution.py:17
  38.4 24.2 %all-to-all-done.1 = f32[4,64,2048]{2,1,0:T(8,128)S(1)} async-done(((f32[4,64,2048]{2,1,0:T(8,128)}), f32[4,64,2048]{2,1,0:T(8,128)S(1)}, u32[]{:S(2)}, u32[]{:S(2)}) %all-to-all-start.1) | async-done | bytes 2097184 | tf_op jit(solution)/shard_map/all_to_all | solution.py:17
  62.6 2.2 %collective-permute-start.2 = (f32[64,2048]{1,0:T(8,128)S(1)}, f32[64,2048]{1,0:T(8,128)S(1)}, u32[]{:S(2)}, u32[]{:S(2)}) collective-permute-start(f32[64,2048]{1,0:T(8,128)S(1)} %bitcast.53), channel_id=1, source_target_pairs={{0,64},{32,96},{64,0},{96,32},{128,192},{160,224},{192,128},{224,1... | collective-permute-start | bytes 1572872 | tf_op jit(solution)/shard_map/ppermute | solution.py:91
  64.8 4.3 %collective-permute-start.1 = (f32[64,2048]{1,0:T(8,128)S(1)}, f32[64,2048]{1,0:T(8,128)}, u32[]{:S(2)}, u32[]{:S(2)}) collective-permute-start(f32[64,2048]{1,0:T(8,128)S(1)} %bitcast.54), channel_id=1, source_target_pairs={{0,96},{32,64},{64,32},{96,0},{128,224},{160,192},{192,160},{224,1... | collective-permute-start | bytes 1572872 | tf_op jit(solution)/shard_map/ppermute | solution.py:91
  69.1 1.9 collective-permute-start
  71.0 0.9 convolution_bitcast_fusion
  71.9 0.7 broadcast_in_dim.78
  72.6 8.2 %all-to-all-start.2 = ((f32[8,8,256]{2,1,0:T(8,128)}), f32[8,8,256]{2,1,0:T(8,128)S(1)}, u32[]{:S(2)}, u32[]{:S(2)}) async-start(f32[8,8,256]{2,1,0:T(8,128)} %broadcast_in_dim.78), calls=%async_computation.2 | async-start | bytes 131072 | tf_op jit(solution)/shard_map/all_to_all | solution.py:17
  80.8 3.1 %all-to-all-done.2 = f32[8,8,256]{2,1,0:T(8,128)S(1)} async-done(((f32[8,8,256]{2,1,0:T(8,128)}), f32[8,8,256]{2,1,0:T(8,128)S(1)}, u32[]{:S(2)}, u32[]{:S(2)}) %all-to-all-start.2) | async-done | bytes 65568 | tf_op jit(solution)/shard_map/all_to_all | solution.py:17
  84.0 16.7 %psum.28 = f32[8,256]{1,0:T(8,128)S(1)} all-reduce(f32[8,256]{1,0:T(8,128)S(1)} %reduce_sum.36), channel_id=1, replica_groups={{0,8,16,24},{1,9,17,25},{2,10,18,26},{3,11,19,27},{4,12,20,28},{5,13,21..., use_global_device_ids=true, to_apply=%region_1.0 | all-reduce | flops 2048 | bytes 16384 | tf_op jit(solution)/shard_map/psum | solution.py:22
  100.7 0.6 convolution_subtract_fusion.3
  101.3 0.3 fusion.55
  101.6 1.4 fusion.54
  103.0 1.4 fusion.53
  104.4 0.3 fusion.52
  104.7 0.1 pad_maximum_fusion.5
  104.8 0.6 broadcast_in_dim.79
  105.4 7.8 %all-to-all-start.3 = ((f32[8,8,256]{2,1,0:T(8,128)}), f32[8,8,256]{2,1,0:T(8,128)S(1)}, u32[]{:S(2)}, u32[]{:S(2)}) async-start(f32[8,8,256]{2,1,0:T(8,128)} %broadcast_in_dim.79), calls=%async_computation.3 | async-start | bytes 131072 | tf_op jit(solution)/shard_map/all_to_all | solution.py:17
  113.2 3.1 %all-to-all-done.3 = f32[8,8,256]{2,1,0:T(8,128)S(1)} async-done(((f32[8,8,256]{2,1,0:T(8,128)}), f32[8,8,256]{2,1,0:T(8,128)S(1)}, u32[]{:S(2)}, u32[]{:S(2)}) %all-to-all-start.3) | async-done | bytes 65568 | tf_op jit(solution)/shard_map/all_to_all | solution.py:17
  116.3 12.3 %psum.29 = f32[8,256]{1,0:T(8,128)S(1)} all-reduce(f32[8,256]{1,0:T(8,128)S(1)} %reduce_sum.37), channel_id=1, replica_groups={{0,8,16,24},{1,9,17,25},{2,10,18,26},{3,11,19,27},{4,12,20,28},{5,13,21..., use_global_device_ids=true, to_apply=%region_3.0 | all-reduce | flops 2048 | bytes 16384 | tf_op jit(solution)/shard_map/psum | solution.py:22
  128.7 0.3 fusion.26
  128.9 1.3 fusion.28
  130.2 1.3 fusion.30
  131.5 0.3 fusion.2
  131.8 4.6 %collective-permute-start.4 = (f32[8,2048]{1,0:T(8,128)S(1)}, f32[8,2048]{1,0:T(8,128)S(1)}, u32[]{:S(2)}, u32[]{:S(2)}) collective-permute-start(f32[8,2048]{1,0:T(8,128)S(1)} %fusion.2), channel_id=1, source_target_pairs={{0,1},{1,0},{2,3},{3,2},{4,5},{5,4},{6,7},{7,6},{8,9},{9,8},{10,11... | collective-permute-start | bytes 196616 | tf_op jit(solution)/shard_map/ppermute | solution.py:62
  136.5 5.3 %collective-permute-start.3 = (f32[8,2048]{1,0:T(8,128)S(1)}, f32[8,2048]{1,0:T(8,128)S(1)}, u32[]{:S(2)}, u32[]{:S(2)}) collective-permute-start(f32[8,2048]{1,0:T(8,128)S(1)} %fusion.2), channel_id=1, source_target_pairs={{1,2},{3,4},{5,6},{7,8},{9,10},{11,12},{13,14},{15,16},{17,18},{19... | collective-permute-start | bytes 196616 | tf_op jit(solution)/shard_map/ppermute | solution.py:63
  141.8 0.1 copy.36
  141.8 0.1 fusion.50
  142.0 0.1 fusion.51
  142.1 0.1 fusion.49
  142.2 0.1 fusion.48
  142.4 6.2 %collective-permute-done.3 = f32[8,2048]{1,0:T(8,128)S(1)} collective-permute-done((f32[8,2048]{1,0:T(8,128)S(1)}, f32[8,2048]{1,0:T(8,128)S(1)}, u32[]{:S(2)}, u32[]{:S(2)}) %collective-permute-start.3) | collective-permute-done | bytes 65568 | tf_op jit(solution)/shard_map/ppermute | solution.py:63
  148.8 0.4 fusion.6
  149.2 0.9 fusion.56
  150.2 7.2 %all_to_all.31 = f32[8,8,256]{2,1,0:T(8,128)S(1)} all-to-all(f32[8,8,256]{2,1,0:T(8,128)S(1)} %broadcast_in_dim.85), channel_id=1, replica_groups={{0,1,2,3,4,5,6,7},{8,9,10,11,12,13,14,15},{16,17,18,19,20,21,22,23},{24..., dimensions={0} | all-to-all | bytes 131072 | tf_op jit(solution)/shard_map/all_to_all | solution.py:17
  157.4 11.0 %psum.30 = f32[8,256]{1,0:T(8,128)S(1)} all-reduce(f32[8,256]{1,0:T(8,128)S(1)} %reduce_sum.38), channel_id=1, replica_groups={{0,8,16,24},{1,9,17,25},{2,10,18,26},{3,11,19,27},{4,12,20,28},{5,13,21..., use_global_device_ids=true, to_apply=%region_5.6 | all-reduce | flops 2048 | bytes 16384 | tf_op jit(solution)/shard_map/psum | solution.py:22
  168.4 0.6 convolution_subtract_fusion.1
  169.1 0.3 fusion.60
  169.4 1.4 fusion.59
  170.7 1.4 fusion.58
  172.1 0.3 fusion.57
  172.4 0.1 pad_maximum_fusion.6
  172.5 10.1 %all_to_all.32 = f32[8,8,256]{2,1,0:T(8,128)S(1)} all-to-all(f32[8,8,256]{2,1,0:T(8,128)S(1)} %broadcast_in_dim.86), channel_id=1, replica_groups={{0,1,2,3,4,5,6,7},{8,9,10,11,12,13,14,15},{16,17,18,19,20,21,22,23},{24..., dimensions={0} | all-to-all | bytes 131072 | tf_op jit(solution)/shard_map/all_to_all | solution.py:17
  182.6 13.2 %psum.31 = f32[8,256]{1,0:T(8,128)S(1)} all-reduce(f32[8,256]{1,0:T(8,128)S(1)} %reduce_sum.39), channel_id=1, replica_groups={{0,8,16,24},{1,9,17,25},{2,10,18,26},{3,11,19,27},{4,12,20,28},{5,13,21..., use_global_device_ids=true, to_apply=%region_7.8 | all-reduce | flops 2048 | bytes 16384 | tf_op jit(solution)/shard_map/psum | solution.py:22
  195.8 0.3 fusion.19
  196.1 1.3 fusion.21
  197.4 1.3 fusion.23
  198.7 0.3 fusion.5
  199.0 4.6 %collective-permute-start.6 = (f32[8,2048]{1,0:T(8,128)S(1)}, f32[8,2048]{1,0:T(8,128)S(1)}, u32[]{:S(2)}, u32[]{:S(2)}) collective-permute-start(f32[8,2048]{1,0:T(8,128)S(1)} %fusion.5), channel_id=1, source_target_pairs={{0,1},{1,0},{2,3},{3,2},{4,5},{5,4},{6,7},{7,6},{8,9},{9,8},{10,11... | collective-permute-start | bytes 196616 | tf_op jit(solution)/shard_map/ppermute | solution.py:62
  203.6 4.5 %collective-permute-start.5 = (f32[8,2048]{1,0:T(8,128)S(1)}, f32[8,2048]{1,0:T(8,128)S(1)}, u32[]{:S(2)}, u32[]{:S(2)}) collective-permute-start(f32[8,2048]{1,0:T(8,128)S(1)} %fusion.5), channel_id=1, source_target_pairs={{1,2},{3,4},{5,6},{7,8},{9,10},{11,12},{13,14},{15,16},{17,18},{19... | collective-permute-start | bytes 196616 | tf_op jit(solution)/shard_map/ppermute | solution.py:63
  208.2 0.1 fusion.46
  208.3 0.1 fusion.47
  208.4 0.1 fusion.45
  208.6 0.1 fusion.44
  208.7 6.5 %collective-permute-done.5 = f32[8,2048]{1,0:T(8,128)S(1)} collective-permute-done((f32[8,2048]{1,0:T(8,128)S(1)}, f32[8,2048]{1,0:T(8,128)S(1)}, u32[]{:S(2)}, u32[]{:S(2)}) %collective-permute-start.5) | collective-permute-done | bytes 65568 | tf_op jit(solution)/shard_map/ppermute | solution.py:63
  215.3 1.1 fusion.7
  216.4 0.7 subtract_divide_fusion
  (35 shorter events, 0.5 us)
Async XLA Ops:
  34.0 4.3 %copy-start.1 = (f32[8,2,1024]{2,1,0:T(2,128)S(1)}, f32[8,2,1024]{2,1,0:T(2,128)}, u32[]{:S(2)}) copy-start(f32[8,2,1024]{2,1,0:T(2,128)} %param.6) | copy-start | bytes 196612
  34.0 4.3 %copy-start.2 = (f32[2,1024]{1,0:T(2,128)S(1)}, f32[2,1024]{1,0:T(2,128)}, u32[]{:S(2)}) copy-start(f32[2,1024]{1,0:T(2,128)} %param.8) | copy-start | bytes 24580
  34.0 28.6 %all-to-all-start.1 = ((f32[4,64,2048]{2,1,0:T(8,128)}), f32[4,64,2048]{2,1,0:T(8,128)S(1)}, u32[]{:S(2)}, u32[]{:S(2)}) async-start(f32[4,64,2048]{2,1,0:T(8,128)} %broadcast_in_dim.77), calls=%async_computation.1 | async-start | bytes 4194304 | tf_op jit(solution)/shard_map/all_to_all | solution.py:17
  62.6 38.1 %collective-permute-start.2 = (f32[64,2048]{1,0:T(8,128)S(1)}, f32[64,2048]{1,0:T(8,128)S(1)}, u32[]{:S(2)}, u32[]{:S(2)}) collective-permute-start(f32[64,2048]{1,0:T(8,128)S(1)} %bitcast.53), channel_id=1, source_target_pairs={{0,64},{32,96},{64,0},{96,32},{128,192},{160,224},{192,128},{224,1... | collective-permute-start | bytes 1572872 | tf_op jit(solution)/shard_map/ppermute | solution.py:91
  64.8 35.9 %collective-permute-start.1 = (f32[64,2048]{1,0:T(8,128)S(1)}, f32[64,2048]{1,0:T(8,128)}, u32[]{:S(2)}, u32[]{:S(2)}) collective-permute-start(f32[64,2048]{1,0:T(8,128)S(1)} %bitcast.54), channel_id=1, source_target_pairs={{0,96},{32,64},{64,32},{96,0},{128,224},{160,192},{192,160},{224,1... | collective-permute-start | bytes 1572872 | tf_op jit(solution)/shard_map/ppermute | solution.py:91
  69.1 31.6 %collective-permute-start = (f32[64,2048]{1,0:T(8,128)S(1)}, f32[64,2048]{1,0:T(8,128)}, u32[]{:S(2)}, u32[]{:S(2)}) collective-permute-start(f32[64,2048]{1,0:T(8,128)S(1)} %bitcast.55), channel_id=1, source_target_pairs={{0,32},{32,0},{64,96},{96,64},{128,160},{160,128},{192,224},{224,1... | collective-permute-start | bytes 1572872 | tf_op jit(solution)/shard_map/ppermute | solution.py:91
  72.6 11.4 %all-to-all-start.2 = ((f32[8,8,256]{2,1,0:T(8,128)}), f32[8,8,256]{2,1,0:T(8,128)S(1)}, u32[]{:S(2)}, u32[]{:S(2)}) async-start(f32[8,8,256]{2,1,0:T(8,128)} %broadcast_in_dim.78), calls=%async_computation.2 | async-start | bytes 131072 | tf_op jit(solution)/shard_map/all_to_all | solution.py:17
  105.4 10.9 %all-to-all-start.3 = ((f32[8,8,256]{2,1,0:T(8,128)}), f32[8,8,256]{2,1,0:T(8,128)S(1)}, u32[]{:S(2)}, u32[]{:S(2)}) async-start(f32[8,8,256]{2,1,0:T(8,128)} %broadcast_in_dim.79), calls=%async_computation.3 | async-start | bytes 131072 | tf_op jit(solution)/shard_map/all_to_all | solution.py:17
  128.6 20.1 %copy-start = (f32[8,2,1024]{2,1,0:T(2,128)S(1)}, f32[8,2,1024]{2,1,0:T(2,128)}, u32[]{:S(2)}) copy-start(f32[8,2,1024]{2,1,0:T(2,128)} %param.7) | copy-start | bytes 196612
  128.6 20.1 %copy-start.3 = (f32[8]{0:T(128)S(1)}, f32[8]{0:T(128)}, u32[]{:S(2)}) copy-start(f32[8]{0:T(128)} %param.9) | copy-start | bytes 100
  131.8 10.6 %collective-permute-start.4 = (f32[8,2048]{1,0:T(8,128)S(1)}, f32[8,2048]{1,0:T(8,128)S(1)}, u32[]{:S(2)}, u32[]{:S(2)}) collective-permute-start(f32[8,2048]{1,0:T(8,128)S(1)} %fusion.2), channel_id=1, source_target_pairs={{0,1},{1,0},{2,3},{3,2},{4,5},{5,4},{6,7},{7,6},{8,9},{9,8},{10,11... | collective-permute-start | bytes 196616 | tf_op jit(solution)/shard_map/ppermute | solution.py:62
  136.5 12.2 %collective-permute-start.3 = (f32[8,2048]{1,0:T(8,128)S(1)}, f32[8,2048]{1,0:T(8,128)S(1)}, u32[]{:S(2)}, u32[]{:S(2)}) collective-permute-start(f32[8,2048]{1,0:T(8,128)S(1)} %fusion.2), channel_id=1, source_target_pairs={{1,2},{3,4},{5,6},{7,8},{9,10},{11,12},{13,14},{15,16},{17,18},{19... | collective-permute-start | bytes 196616 | tf_op jit(solution)/shard_map/ppermute | solution.py:63
  199.0 9.7 %collective-permute-start.6 = (f32[8,2048]{1,0:T(8,128)S(1)}, f32[8,2048]{1,0:T(8,128)S(1)}, u32[]{:S(2)}, u32[]{:S(2)}) collective-permute-start(f32[8,2048]{1,0:T(8,128)S(1)} %fusion.5), channel_id=1, source_target_pairs={{0,1},{1,0},{2,3},{3,2},{4,5},{5,4},{6,7},{7,6},{8,9},{9,8},{10,11... | collective-permute-start | bytes 196616 | tf_op jit(solution)/shard_map/ppermute | solution.py:62
  203.6 11.6 %collective-permute-start.5 = (f32[8,2048]{1,0:T(8,128)S(1)}, f32[8,2048]{1,0:T(8,128)S(1)}, u32[]{:S(2)}, u32[]{:S(2)}) collective-permute-start(f32[8,2048]{1,0:T(8,128)S(1)} %fusion.5), channel_id=1, source_target_pairs={{1,2},{3,4},{5,6},{7,8},{9,10},{11,12},{13,14},{15,16},{17,18},{19... | collective-permute-start | bytes 196616 | tf_op jit(solution)/shard_map/ppermute | solution.py:63

commit v15 on v13

--- a/solution.py
+++ b/solution.py
@@ -6,6 +6,12 @@
 NZ = 32
 ITERS = 2
 BAND_Z = [[z * 4 + y for z in range(4)] for y in range(4)]
+PAIR_PLANE = [
+    [(z * 4 + y) * 32 + far * 8 + r for y in pair for r in range(8)]
+    for z in range(4)
+    for pair in ((0, 3), (1, 2))
+    for far in range(4)
+]
 SPACE_PLANE = [[z * 8 + r for r in range(8)] for z in range(4)]
 SPACE_Z = [[z * 8 + r for z in range(4)] for r in range(8)]
 
@@ -77,6 +83,13 @@
     return lax.ppermute(x, "band", [(i, i ^ bits) for i in range(lax.axis_size("band"))])
 
 
+def pair_margins(product, lower, weight):
+    total = lax.psum(product, "space", axis_index_groups=SPACE_Z)
+    every = weight * copies(total, ("band", "space"), PAIR_PLANE)
+    ahead, behind = jnp.sum(every[:8], axis=0), jnp.sum(every[8:], axis=0)
+    return jnp.where(lower, ahead, behind), jnp.where(lower, behind, ahead)
+
+
 def project_whole(parts, vectors, weight):
     product = jnp.concatenate([products(vectors, part) for part in parts], axis=1)
     margin = space_sum(product) * weight
@@ -95,24 +108,29 @@
     own = [states.reshape(-1, cells) for states in occupied]
     diagonal = 3.75 + potential[None, :, :] - energies[:, None, None]
     vectors = initial.reshape(count, cells)
-    pair = jnp.concatenate([vectors, swapped(vectors, 3)], axis=0)
+    lower = lax.axis_index("band") % 4 < 2
+    partner = swapped(vectors, 3)
+    pair = jnp.concatenate(
+        [jnp.where(lower, vectors, partner), jnp.where(lower, partner, vectors)], axis=0
+    )
     run = copies(own[0], "band", BAND_Z).reshape(-1, cells)
     run, other, pair = tie((run, own[1], pair))
     across = swapped(run, 1)
     second = copies(other, "band", BAND_Z).reshape(-1, cells)
     across, second = tie((across, second))
-    near = [jnp.concatenate([run, across], axis=0)]
-    margin = space_sum(products(pair, near[0])) * weight
-    margin, across, far = tie((margin, swapped(second, 1), swapped(near[0], 3)))
-    partial = combination(margin, near[0])
-    other = swapped(jnp.concatenate([partial[count:], partial[:count]], axis=0), 3)
-    pair, second, across = tie((pair - partial - other, second, across))
-    near.append(jnp.concatenate([second, across], axis=0))
-    margin = space_sum(products(pair, near[1])) * weight
-    partial = combination(margin, near[1])
-    vectors = pair[:count] - partial[:count] - swapped(partial[count:], 3)
-    vectors, sent = tie((vectors, near[1]))
-    blocks = [(near[0], far), (near[1], swapped(sent, 3))]
+    near = jnp.concatenate([run, across], axis=0)
+    margins = pair_margins(products(pair, near), lower, weight)
+    margins, across, far = tie((margins, swapped(second, 1), swapped(near, 3)))
+    first = (near, far)
+    for margin, part in zip(margins, first):
+        pair = pair - combination(margin, part)
+    near = jnp.concatenate([second, across], axis=0)
+    margins = pair_margins(products(pair, near), lower, weight)
+    margins, far = tie((margins, swapped(near, 3)))
+    blocks = [first, (near, far)]
+    vectors = jnp.where(lower, pair[:count], pair[count:])
+    for margin, part in zip(margins, blocks[1]):
+        vectors = vectors - combination(jnp.where(lower, margin[:count], margin[count:]), part)
     for iteration in range(ITERS):
         if iteration > 0:
             for block in blocks:

time: 212 us -> 199 us (0.939)
  starting transfers between devices: 74.8 us -> 62.8 us
  waiting for transfers between devices: 47.8 us -> 41.6 us
  blocking collectives: 67.3 us -> 70.2 us
    psum x4 -> x2, blocking collectives: 58.7 us -> 23.2 us  [space_sum(): return lax.psum(near, 'space', axis_index_groups=SPACE_Z)]
    psum x0 -> x2, blocking collectives: none -> 29.8 us  [pair_margins(): total = lax.psum(product, 'space', axis_index_groups=SPACE_Z)]
    ppermute x7 -> x5, waiting for transfers between devices: 28.7 us -> 12.6 us  [swapped(): lax.ppermute(x, 'band', [(i, i ^ bits) for i in range(lax.axis_size('band...]
    all_to_all x1 -> x2, blocking collectives: 8.57 us -> 17.2 us  [copies(): return lax.all_to_all(sent, axis, 0, 0, axis_index_groups=groups)]
    ppermute x2, waiting for transfers between devices: 4.42 us -> 11.2 us  [neighbours(): across = lax.ppermute(vectors, 'space', outer)]
    ppermute x7 -> x5, starting transfers between devices: 22.6 us -> 17 us  [swapped(): lax.ppermute(x, 'band', [(i, i ^ bits) for i in range(lax.axis_size('band...]
    ppermute x2, starting transfers between devices: 16 us -> 10.7 us  [neighbours(): across = lax.ppermute(vectors, 'space', outer)]
    all_to_all x5 -> x4, waiting for transfers between devices: 14.2 us -> 17.8 us  [copies(): return lax.all_to_all(sent, axis, 0, 0, axis_index_groups=groups)]
  transfers between devices with their start and end apart: 16 -> 13, of which waited for: 12 -> 8; matrix products, arithmetic and copies ran while one was open for 2% -> 3% of each run, Pallas kernels for 0% -> 0%
where the time goes in v15:
time: 199 us; the launch traced here: 196 us
  blocking collectives  70.2 us (35%)
  starting transfers between devices  62.8 us (32%)
  waiting for transfers between devices  41.6 us (21%)
  matrix products  9.63 us (5%)
  local copies, waits for them, and re-layouts  8.49 us (4%)
  other arithmetic  2.46 us (1%)
    psum x2, blocking collectives, pair_margins(): total = lax.psum(product, 'space', axis_index_groups=SPACE_Z)  29.8 us
    all_to_all x4, starting transfers between devices, copies(): return lax.all_to_all(sent, axis, 0, 0, axis_index_groups=groups)  28.1 us
    psum x2, blocking collectives, space_sum(): return lax.psum(near, 'space', axis_index_groups=SPACE_Z)  23.2 us
    all_to_all x4, waiting for transfers between devices, copies(): return lax.all_to_all(sent, axis, 0, 0, axis_index_groups=groups)  17.8 us
    all_to_all x2, blocking collectives, copies(): return lax.all_to_all(sent, axis, 0, 0, axis_index_groups=groups)  17.2 us
    ppermute x5, starting transfers between devices, swapped(): lax.ppermute(x, 'band', [(i, i ^ bits) for i in range(lax.axis_size('band...  17 us
    ppermute x5, waiting for transfers between devices, swapped(): lax.ppermute(x, 'band', [(i, i ^ bits) for i in range(lax.axis_size('band...  12.6 us
    ppermute x2, waiting for transfers between devices, neighbours(): across = lax.ppermute(vectors, 'space', outer)  11.2 us
  transfers between devices with their start and end apart: 13, of which 8 were waited for; matrix products, arithmetic and copies ran while one was open for 3% of the time, Pallas kernels for 0%

profile of v15, /device:TPU:7, one launch (start us, length us, event | category | flops | bytes accessed | tf_op | source)
XLA Modules:
  0.0 196.4 jit_solution(5980857218185376)
XLA Ops:
  0.6 1.0 fusion.33
  1.7 0.8 broadcast_in_dim.76
  2.5 5.7 %all-to-all-start = ((f32[4,16,2048]{2,1,0:T(8,128)}), f32[4,16,2048]{2,1,0:T(8,128)S(1)}, u32[]{:S(2)}, u32[]{:S(2)}) async-start(f32[4,16,2048]{2,1,0:T(8,128)} %broadcast_in_dim.76), calls=%async_computation | async-start | bytes 1048576 | tf_op jit(solution)/shard_map/all_to_all | solution.py:22
  8.3 4.6 %collective-permute-start = (f32[8,2048]{1,0:T(8,128)S(1)}, f32[8,2048]{1,0:T(8,128)S(1)}, u32[]{:S(2)}, u32[]{:S(2)}) collective-permute-start(f32[8,2048]{1,0:T(8,128)S(1)} %bitcast.53), channel_id=1, source_target_pairs={{0,96},{32,64},{64,32},{96,0},{128,224},{160,192},{192,160},{224,1... | collective-permute-start | bytes 196616 | tf_op jit(solution)/shard_map/ppermute | solution.py:83
  13.0 1.9 collective-permute-done
  14.9 7.3 %all-to-all-done = f32[4,16,2048]{2,1,0:T(8,128)S(1)} async-done(((f32[4,16,2048]{2,1,0:T(8,128)}), f32[4,16,2048]{2,1,0:T(8,128)S(1)}, u32[]{:S(2)}, u32[]{:S(2)}) %all-to-all-start) | async-done | bytes 524320 | tf_op jit(solution)/shard_map/all_to_all | solution.py:22
  22.2 0.8 broadcast_in_dim.77
  23.1 4.3 %all-to-all-start.1 = ((f32[4,16,2048]{2,1,0:T(8,128)}), f32[4,16,2048]{2,1,0:T(8,128)}, u32[]{:S(2)}, u32[]{:S(2)}) async-start(f32[4,16,2048]{2,1,0:T(8,128)} %broadcast_in_dim.77), calls=%async_computation.1 | async-start | bytes 1048576 | tf_op jit(solution)/shard_map/all_to_all | solution.py:22
  27.3 3.2 %collective-permute-start.1 = (f32[64,2048]{1,0:T(8,128)S(1)}, f32[64,2048]{1,0:T(8,128)S(1)}, u32[]{:S(2)}, u32[]{:S(2)}) collective-permute-start(f32[64,2048]{1,0:T(8,128)S(1)} %bitcast.41), channel_id=1, source_target_pairs={{0,32},{32,0},{64,96},{96,64},{128,160},{160,128},{192,224},{224,1... | collective-permute-start | bytes 1572872 | tf_op jit(solution)/shard_map/ppermute | solution.py:83
  30.6 10.7 %collective-permute-done.1 = f32[64,2048]{1,0:T(8,128)S(1)} collective-permute-done((f32[64,2048]{1,0:T(8,128)S(1)}, f32[64,2048]{1,0:T(8,128)S(1)}, u32[]{:S(2)}, u32[]{:S(2)}) %collective-permute-start.1) | collective-permute-done | bytes 524320 | tf_op jit(solution)/shard_map/ppermute | solution.py:83
  41.3 0.1 all-to-all-done.1
  41.4 3.2 %collective-permute-start.2 = (f32[64,2048]{1,0:T(8,128)}, f32[64,2048]{1,0:T(8,128)}, u32[]{:S(2)}, u32[]{:S(2)}) collective-permute-start(f32[64,2048]{1,0:T(8,128)} %bitcast.1), channel_id=1, source_target_pairs={{0,32},{32,0},{64,96},{96,64},{128,160},{160,128},{192,224},{224,1... | collective-permute-start | bytes 1572872 | tf_op jit(solution)/shard_map/ppermute | solution.py:83
  44.6 3.8 %collective-permute-start.3 = (f32[128,2048]{1,0:T(8,128)S(1)}, f32[128,2048]{1,0:T(8,128)S(1)}, u32[]{:S(2)}, u32[]{:S(2)}) collective-permute-start(f32[128,2048]{1,0:T(8,128)S(1)} %constant_dynamic-update-slice_fusion), channel_id=1, source_target_pairs={{0,96},{32,64},{64,32},{96,0},{128,224},{160,192},{192,160},{224,1... | collective-permute-start | bytes 3145736 | tf_op jit(solution)/shard_map/ppermute | solution.py:83
  48.4 0.5 fusion.42
  48.9 17.5 %psum.28 = f32[16,128]{1,0:T(8,128)S(1)} all-reduce(f32[16,128]{1,0:T(8,128)S(1)} %fusion.42), channel_id=1, replica_groups={{0,8,16,24},{1,9,17,25},{2,10,18,26},{3,11,19,27},{4,12,20,28},{5,13,21..., use_global_device_ids=true, to_apply=%region_0.1 | all-reduce | flops 2048 | bytes 16384 | tf_op jit(solution)/shard_map/psum | solution.py:87
  66.5 0.7 broadcast_in_dim.78
  67.1 9.4 %all-to-all-start.2 = ((f32[16,16,128]{2,1,0:T(8,128)}), f32[16,16,128]{2,1,0:T(8,128)S(1)}, u32[]{:S(2)}, u32[]{:S(2)}) async-start(f32[16,16,128]{2,1,0:T(8,128)} %broadcast_in_dim.78), calls=%async_computation.2 | async-start | bytes 262144 | tf_op jit(solution)/shard_map/all_to_all | solution.py:22
  76.5 1.1 constant_dynamic-update-slice_fusion.3
  77.6 4.7 %all-to-all-done.2 = f32[16,16,128]{2,1,0:T(8,128)S(1)} async-done(((f32[16,16,128]{2,1,0:T(8,128)}), f32[16,16,128]{2,1,0:T(8,128)S(1)}, u32[]{:S(2)}, u32[]{:S(2)}) %all-to-all-start.2) | async-done | bytes 131104 | tf_op jit(solution)/shard_map/all_to_all | solution.py:22
  82.4 1.1 constant_dynamic-update-slice_fusion.2
  83.4 2.2 %collective-permute-start.4 = (f32[128,2048]{1,0:T(8,128)S(1)}, f32[128,2048]{1,0:T(8,128)}, u32[]{:S(2)}, u32[]{:S(2)}) collective-permute-start(f32[128,2048]{1,0:T(8,128)S(1)} %constant_dynamic-update-slice_fusion.2), channel_id=1, source_target_pairs={{0,96},{32,64},{64,32},{96,0},{128,224},{160,192},{192,160},{224,1... | collective-permute-start | bytes 3145736 | tf_op jit(solution)/shard_map/ppermute | solution.py:83
  85.6 0.4 fusion.43
  86.0 0.4 fusion
  86.4 0.5 fusion.44
  86.9 12.3 %psum.29 = f32[16,128]{1,0:T(8,128)S(1)} all-reduce(f32[16,128]{1,0:T(8,128)S(1)} %fusion.44), channel_id=1, replica_groups={{0,8,16,24},{1,9,17,25},{2,10,18,26},{3,11,19,27},{4,12,20,28},{5,13,21..., use_global_device_ids=true, to_apply=%region_3.4 | all-reduce | flops 2048 | bytes 16384 | tf_op jit(solution)/shard_map/psum | solution.py:87
  99.2 0.7 broadcast_in_dim.79
  99.9 8.7 %all-to-all-start.3 = ((f32[16,16,128]{2,1,0:T(8,128)}), f32[16,16,128]{2,1,0:T(8,128)S(1)}, u32[]{:S(2)}, u32[]{:S(2)}) async-start(f32[16,16,128]{2,1,0:T(8,128)} %broadcast_in_dim.79), calls=%async_computation.3 | async-start | bytes 262144 | tf_op jit(solution)/shard_map/all_to_all | solution.py:22
  108.6 5.7 %all-to-all-done.3 = f32[16,16,128]{2,1,0:T(8,128)S(1)} async-done(((f32[16,16,128]{2,1,0:T(8,128)}), f32[16,16,128]{2,1,0:T(8,128)S(1)}, u32[]{:S(2)}, u32[]{:S(2)}) %all-to-all-start.3) | async-done | bytes 131104 | tf_op jit(solution)/shard_map/all_to_all | solution.py:22
  114.4 0.4 convolution_subtract_fusion.6
  114.8 1.6 convolution_subtract_fusion.5
  116.4 2.2 %collective-permute-start.6 = (f32[8,2048]{1,0:T(8,128)S(1)}, f32[8,2048]{1,0:T(8,128)S(1)}, u32[]{:S(2)}, u32[]{:S(2)}) collective-permute-start(f32[8,2048]{1,0:T(8,128)S(1)} %convolution_subtract_fusion.5), channel_id=1, source_target_pairs={{0,1},{1,0},{2,3},{3,2},{4,5},{5,4},{6,7},{7,6},{8,9},{9,8},{10,11... | collective-permute-start | bytes 196616 | tf_op jit(solution)/shard_map/ppermute | solution.py:54
  118.6 5.3 %collective-permute-start.5 = (f32[8,2048]{1,0:T(8,128)S(1)}, f32[8,2048]{1,0:T(8,128)S(1)}, u32[]{:S(2)}, u32[]{:S(2)}) collective-permute-start(f32[8,2048]{1,0:T(8,128)S(1)} %convolution_subtract_fusion.5), channel_id=1, source_target_pairs={{1,2},{3,4},{5,6},{7,8},{9,10},{11,12},{13,14},{15,16},{17,18},{19... | collective-permute-start | bytes 196616 | tf_op jit(solution)/shard_map/ppermute | solution.py:55
  124.0 0.1 copy.36
  124.0 0.1 fusion.40
  124.1 0.1 fusion.41
  124.3 0.1 fusion.39
  124.4 0.1 fusion.38
  124.6 5.6 %collective-permute-done.5 = f32[8,2048]{1,0:T(8,128)S(1)} collective-permute-done((f32[8,2048]{1,0:T(8,128)S(1)}, f32[8,2048]{1,0:T(8,128)S(1)}, u32[]{:S(2)}, u32[]{:S(2)}) %collective-permute-start.5) | collective-permute-done | bytes 65568 | tf_op jit(solution)/shard_map/ppermute | solution.py:55
  130.2 0.1 copy.40
  130.3 0.1 copy.41
  130.4 0.8 copy-done
  131.1 0.4 fusion.1
  131.6 0.5 fusion.46
  132.1 0.5 fusion.45
  132.7 7.2 %all_to_all.30 = f32[8,8,256]{2,1,0:T(8,128)S(1)} all-to-all(f32[8,8,256]{2,1,0:T(8,128)S(1)} %broadcast_in_dim.85), channel_id=1, replica_groups={{0,1,2,3,4,5,6,7},{8,9,10,11,12,13,14,15},{16,17,18,19,20,21,22,23},{24..., dimensions={0} | all-to-all | bytes 131072 | tf_op jit(solution)/shard_map/all_to_all | solution.py:22
  139.9 11.0 %psum.30 = f32[8,256]{1,0:T(8,128)S(1)} all-reduce(f32[8,256]{1,0:T(8,128)S(1)} %reduce_sum.58), channel_id=1, replica_groups={{0,8,16,24},{1,9,17,25},{2,10,18,26},{3,11,19,27},{4,12,20,28},{5,13,21..., use_global_device_ids=true, to_apply=%region_7.8 | all-reduce | flops 2048 | bytes 16384 | tf_op jit(solution)/shard_map/psum | solution.py:27
  150.9 0.4 convolution_subtract_fusion.4
  151.2 0.4 convolution_subtract_fusion.3
  151.6 1.7 fusion.48
  153.3 0.5 fusion.47
  153.9 10.0 %all_to_all.31 = f32[8,8,256]{2,1,0:T(8,128)S(1)} all-to-all(f32[8,8,256]{2,1,0:T(8,128)S(1)} %broadcast_in_dim.86), channel_id=1, replica_groups={{0,1,2,3,4,5,6,7},{8,9,10,11,12,13,14,15},{16,17,18,19,20,21,22,23},{24..., dimensions={0} | all-to-all | bytes 131072 | tf_op jit(solution)/shard_map/all_to_all | solution.py:22
  163.9 12.2 %psum.31 = f32[8,256]{1,0:T(8,128)S(1)} all-reduce(f32[8,256]{1,0:T(8,128)S(1)} %reduce_sum.59), channel_id=1, replica_groups={{0,8,16,24},{1,9,17,25},{2,10,18,26},{3,11,19,27},{4,12,20,28},{5,13,21..., use_global_device_ids=true, to_apply=%region_9.10 | all-reduce | flops 2048 | bytes 16384 | tf_op jit(solution)/shard_map/psum | solution.py:27
  176.1 0.4 convolution_subtract_fusion.2
  176.5 1.6 convolution_subtract_fusion.1
  178.1 4.7 %collective-permute-start.8 = (f32[8,2048]{1,0:T(8,128)S(1)}, f32[8,2048]{1,0:T(8,128)S(1)}, u32[]{:S(2)}, u32[]{:S(2)}) collective-permute-start(f32[8,2048]{1,0:T(8,128)S(1)} %convolution_subtract_fusion.1), channel_id=1, source_target_pairs={{0,1},{1,0},{2,3},{3,2},{4,5},{5,4},{6,7},{7,6},{8,9},{9,8},{10,11... | collective-permute-start | bytes 196616 | tf_op jit(solution)/shard_map/ppermute | solution.py:54
  182.8 5.4 %collective-permute-start.7 = (f32[8,2048]{1,0:T(8,128)S(1)}, f32[8,2048]{1,0:T(8,128)S(1)}, u32[]{:S(2)}, u32[]{:S(2)}) collective-permute-start(f32[8,2048]{1,0:T(8,128)S(1)} %convolution_subtract_fusion.1), channel_id=1, source_target_pairs={{1,2},{3,4},{5,6},{7,8},{9,10},{11,12},{13,14},{15,16},{17,18},{19... | collective-permute-start | bytes 196616 | tf_op jit(solution)/shard_map/ppermute | solution.py:55
  188.2 0.1 copy.50
  188.2 0.1 fusion.36
  188.3 0.1 fusion.37
  188.5 0.1 fusion.35
  188.6 0.1 fusion.34
  188.8 5.6 %collective-permute-done.7 = f32[8,2048]{1,0:T(8,128)S(1)} collective-permute-done((f32[8,2048]{1,0:T(8,128)S(1)}, f32[8,2048]{1,0:T(8,128)S(1)}, u32[]{:S(2)}, u32[]{:S(2)}) %collective-permute-start.7) | collective-permute-done | bytes 65568 | tf_op jit(solution)/shard_map/ppermute | solution.py:55
  194.5 1.1 fusion.2
  195.6 0.7 subtract_divide_fusion
  (41 shorter events, 0.5 us)
Async XLA Ops:
  2.5 5.8 %copy-start.1 = (f32[8,2,1024]{2,1,0:T(2,128)S(1)}, f32[8,2,1024]{2,1,0:T(2,128)}, u32[]{:S(2)}) copy-start(f32[8,2,1024]{2,1,0:T(2,128)} %param.6) | copy-start | bytes 196612
  2.5 19.7 %all-to-all-start = ((f32[4,16,2048]{2,1,0:T(8,128)}), f32[4,16,2048]{2,1,0:T(8,128)S(1)}, u32[]{:S(2)}, u32[]{:S(2)}) async-start(f32[4,16,2048]{2,1,0:T(8,128)} %broadcast_in_dim.76), calls=%async_computation | async-start | bytes 1048576 | tf_op jit(solution)/shard_map/all_to_all | solution.py:22
  8.3 6.6 %collective-permute-start = (f32[8,2048]{1,0:T(8,128)S(1)}, f32[8,2048]{1,0:T(8,128)S(1)}, u32[]{:S(2)}, u32[]{:S(2)}) collective-permute-start(f32[8,2048]{1,0:T(8,128)S(1)} %bitcast.53), channel_id=1, source_target_pairs={{0,96},{32,64},{64,32},{96,0},{128,224},{160,192},{192,160},{224,1... | collective-permute-start | bytes 196616 | tf_op jit(solution)/shard_map/ppermute | solution.py:83
  23.1 7.5 %copy-start.2 = (f32[2,1024]{1,0:T(2,128)S(1)}, f32[2,1024]{1,0:T(2,128)}, u32[]{:S(2)}) copy-start(f32[2,1024]{1,0:T(2,128)} %param.8) | copy-start | bytes 24580
  23.1 18.3 %all-to-all-start.1 = ((f32[4,16,2048]{2,1,0:T(8,128)}), f32[4,16,2048]{2,1,0:T(8,128)}, u32[]{:S(2)}, u32[]{:S(2)}) async-start(f32[4,16,2048]{2,1,0:T(8,128)} %broadcast_in_dim.77), calls=%async_computation.1 | async-start | bytes 1048576 | tf_op jit(solution)/shard_map/all_to_all | solution.py:22
  27.3 14.0 %collective-permute-start.1 = (f32[64,2048]{1,0:T(8,128)S(1)}, f32[64,2048]{1,0:T(8,128)S(1)}, u32[]{:S(2)}, u32[]{:S(2)}) collective-permute-start(f32[64,2048]{1,0:T(8,128)S(1)} %bitcast.41), channel_id=1, source_target_pairs={{0,32},{32,0},{64,96},{96,64},{128,160},{160,128},{192,224},{224,1... | collective-permute-start | bytes 1572872 | tf_op jit(solution)/shard_map/ppermute | solution.py:83
  41.4 41.0 %collective-permute-start.2 = (f32[64,2048]{1,0:T(8,128)}, f32[64,2048]{1,0:T(8,128)}, u32[]{:S(2)}, u32[]{:S(2)}) collective-permute-start(f32[64,2048]{1,0:T(8,128)} %bitcast.1), channel_id=1, source_target_pairs={{0,32},{32,0},{64,96},{96,64},{128,160},{160,128},{192,224},{224,1... | collective-permute-start | bytes 1572872 | tf_op jit(solution)/shard_map/ppermute | solution.py:83
  44.6 37.7 %collective-permute-start.3 = (f32[128,2048]{1,0:T(8,128)S(1)}, f32[128,2048]{1,0:T(8,128)S(1)}, u32[]{:S(2)}, u32[]{:S(2)}) collective-permute-start(f32[128,2048]{1,0:T(8,128)S(1)} %constant_dynamic-update-slice_fusion), channel_id=1, source_target_pairs={{0,96},{32,64},{64,32},{96,0},{128,224},{160,192},{192,160},{224,1... | collective-permute-start | bytes 3145736 | tf_op jit(solution)/shard_map/ppermute | solution.py:83
  67.1 15.1 %all-to-all-start.2 = ((f32[16,16,128]{2,1,0:T(8,128)}), f32[16,16,128]{2,1,0:T(8,128)S(1)}, u32[]{:S(2)}, u32[]{:S(2)}) async-start(f32[16,16,128]{2,1,0:T(8,128)} %broadcast_in_dim.78), calls=%async_computation.2 | async-start | bytes 262144 | tf_op jit(solution)/shard_map/all_to_all | solution.py:22
  83.4 31.0 %collective-permute-start.4 = (f32[128,2048]{1,0:T(8,128)S(1)}, f32[128,2048]{1,0:T(8,128)}, u32[]{:S(2)}, u32[]{:S(2)}) collective-permute-start(f32[128,2048]{1,0:T(8,128)S(1)} %constant_dynamic-update-slice_fusion.2), channel_id=1, source_target_pairs={{0,96},{32,64},{64,32},{96,0},{128,224},{160,192},{192,160},{224,1... | collective-permute-start | bytes 3145736 | tf_op jit(solution)/shard_map/ppermute | solution.py:83
  99.9 14.5 %all-to-all-start.3 = ((f32[16,16,128]{2,1,0:T(8,128)}), f32[16,16,128]{2,1,0:T(8,128)S(1)}, u32[]{:S(2)}, u32[]{:S(2)}) async-start(f32[16,16,128]{2,1,0:T(8,128)} %broadcast_in_dim.79), calls=%async_computation.3 | async-start | bytes 262144 | tf_op jit(solution)/shard_map/all_to_all | solution.py:22
  116.4 8.2 %collective-permute-start.6 = (f32[8,2048]{1,0:T(8,128)S(1)}, f32[8,2048]{1,0:T(8,128)S(1)}, u32[]{:S(2)}, u32[]{:S(2)}) collective-permute-start(f32[8,2048]{1,0:T(8,128)S(1)} %convolution_subtract_fusion.5), channel_id=1, source_target_pairs={{0,1},{1,0},{2,3},{3,2},{4,5},{5,4},{6,7},{7,6},{8,9},{9,8},{10,11... | collective-permute-start | bytes 196616 | tf_op jit(solution)/shard_map/ppermute | solution.py:54
  118.6 11.6 %collective-permute-start.5 = (f32[8,2048]{1,0:T(8,128)S(1)}, f32[8,2048]{1,0:T(8,128)S(1)}, u32[]{:S(2)}, u32[]{:S(2)}) collective-permute-start(f32[8,2048]{1,0:T(8,128)S(1)} %convolution_subtract_fusion.5), channel_id=1, source_target_pairs={{1,2},{3,4},{5,6},{7,8},{9,10},{11,12},{13,14},{15,16},{17,18},{19... | collective-permute-start | bytes 196616 | tf_op jit(solution)/shard_map/ppermute | solution.py:55
  130.3 0.8 copy-start
  130.4 0.8 copy-start.3
  178.1 10.7 %collective-permute-start.8 = (f32[8,2048]{1,0:T(8,128)S(1)}, f32[8,2048]{1,0:T(8,128)S(1)}, u32[]{:S(2)}, u32[]{:S(2)}) collective-permute-start(f32[8,2048]{1,0:T(8,128)S(1)} %convolution_subtract_fusion.1), channel_id=1, source_target_pairs={{0,1},{1,0},{2,3},{3,2},{4,5},{5,4},{6,7},{7,6},{8,9},{9,8},{10,11... | collective-permute-start | bytes 196616 | tf_op jit(solution)/shard_map/ppermute | solution.py:54
  182.8 11.6 %collective-permute-start.7 = (f32[8,2048]{1,0:T(8,128)S(1)}, f32[8,2048]{1,0:T(8,128)S(1)}, u32[]{:S(2)}, u32[]{:S(2)}) collective-permute-start(f32[8,2048]{1,0:T(8,128)S(1)} %convolution_subtract_fusion.1), channel_id=1, source_target_pairs={{1,2},{3,4},{5,6},{7,8},{9,10},{11,12},{13,14},{15,16},{17,18},{19... | collective-permute-start | bytes 196616 | tf_op jit(solution)/shard_map/ppermute | solution.py:55

commit v16 on v15

--- a/solution.py
+++ b/solution.py
@@ -83,11 +83,12 @@
     return lax.ppermute(x, "band", [(i, i ^ bits) for i in range(lax.axis_size("band"))])
 
 
-def pair_margins(product, lower, weight):
+def pair_margins(product, lower, weight, beside=None):
     total = lax.psum(product, "space", axis_index_groups=SPACE_Z)
+    total, beside = lax.optimization_barrier((total, beside))
     every = weight * copies(total, ("band", "space"), PAIR_PLANE)
     ahead, behind = jnp.sum(every[:8], axis=0), jnp.sum(every[8:], axis=0)
-    return jnp.where(lower, ahead, behind), jnp.where(lower, behind, ahead)
+    return (jnp.where(lower, ahead, behind), jnp.where(lower, behind, ahead)), beside
 
 
 def project_whole(parts, vectors, weight):
@@ -117,15 +118,14 @@
     run, other, pair = tie((run, own[1], pair))
     across = swapped(run, 1)
     second = copies(other, "band", BAND_Z).reshape(-1, cells)
-    across, second = tie((across, second))
     near = jnp.concatenate([run, across], axis=0)
-    margins = pair_margins(products(pair, near), lower, weight)
-    margins, across, far = tie((margins, swapped(second, 1), swapped(near, 3)))
+    margins, across = pair_margins(products(pair, near), lower, weight, swapped(second, 1))
+    margins, far = tie((margins, swapped(near, 3)))
     first = (near, far)
     for margin, part in zip(margins, first):
         pair = pair - combination(margin, part)
     near = jnp.concatenate([second, across], axis=0)
-    margins = pair_margins(products(pair, near), lower, weight)
+    margins, _ = pair_margins(products(pair, near), lower, weight)
     margins, far = tie((margins, swapped(near, 3)))
     blocks = [first, (near, far)]
     vectors = jnp.where(lower, pair[:count], pair[count:])
@@ -140,7 +140,7 @@
         vectors = vectors.reshape(shape)
         rest = right_side - coupling(vectors, low.reshape(shape), high.reshape(shape))
         residual = rest - diagonal * vectors
-        vectors = (rest / diagonal).reshape(count, cells)
+        vectors = (vectors + residual / diagonal).reshape(count, cells)
     return (vectors.reshape(shape), residual)
 
 

time: 199 us -> 192 us (0.965)
  waiting for transfers between devices: 41.6 us -> 38.6 us
  local copies, waits for them, and re-layouts: 8.49 us -> 6.35 us
    ppermute x5, waiting for transfers between devices: 12.6 us -> 1.87 us  [swapped(): lax.ppermute(x, 'band', [(i, i ^ bits) for i in range(lax.axis_size('band...]
    all_to_all x4, waiting for transfers between devices: 17.8 us -> 24.2 us  [copies(): return lax.all_to_all(sent, axis, 0, 0, axis_index_groups=groups)]
    all_to_all x4, starting transfers between devices: 28.1 us -> 25.8 us  [copies(): return lax.all_to_all(sent, axis, 0, 0, axis_index_groups=groups)]
    ppermute x5, starting transfers between devices: 17 us -> 19.1 us  [swapped(): lax.ppermute(x, 'band', [(i, i ^ bits) for i in range(lax.axis_size('band...]
  transfers between devices with their start and end apart: 13 -> 13, of which waited for: 8 -> 7; matrix products, arithmetic and copies ran while one was open for 3% -> 4% of each run, Pallas kernels for 0% -> 0%
where the time goes in v16:
time: 192 us; the launch traced here: 191 us
  blocking collectives  70.7 us (37%)
  starting transfers between devices  61.9 us (32%)
  waiting for transfers between devices  38.6 us (20%)
  matrix products  9.63 us (5%)
  local copies, waits for them, and re-layouts  6.35 us (3%)
  other arithmetic  2.88 us (2%)
    psum x2, blocking collectives, pair_margins(): total = lax.psum(product, 'space', axis_index_groups=SPACE_Z)  29.6 us
    all_to_all x4, starting transfers between devices, copies(): return lax.all_to_all(sent, axis, 0, 0, axis_index_groups=groups)  25.8 us
    all_to_all x4, waiting for transfers between devices, copies(): return lax.all_to_all(sent, axis, 0, 0, axis_index_groups=groups)  24.2 us
    psum x2, blocking collectives, space_sum(): return lax.psum(near, 'space', axis_index_groups=SPACE_Z)  23.9 us
    ppermute x5, starting transfers between devices, swapped(): lax.ppermute(x, 'band', [(i, i ^ bits) for i in range(lax.axis_size('band...  19.1 us
    all_to_all x2, blocking collectives, copies(): return lax.all_to_all(sent, axis, 0, 0, axis_index_groups=groups)  17.2 us
    ppermute x2, waiting for transfers between devices, neighbours(): across = lax.ppermute(vectors, 'space', outer)  12.6 us
    ppermute x2, starting transfers between devices, neighbours(): across = lax.ppermute(vectors, 'space', outer)  10 us
  transfers between devices with their start and end apart: 13, of which 7 were waited for; matrix products, arithmetic and copies ran while one was open for 4% of the time, Pallas kernels for 0%

profile of v16, /device:TPU:7, one launch (start us, length us, event | category | flops | bytes accessed | tf_op | source)
XLA Modules:
  0.0 191.2 jit_solution(6728319295912485024)
XLA Ops:
  0.6 1.0 fusion.42
  1.7 0.8 broadcast_in_dim.76
  2.5 5.7 %all-to-all-start = ((f32[4,16,2048]{2,1,0:T(8,128)}), f32[4,16,2048]{2,1,0:T(8,128)S(1)}, u32[]{:S(2)}, u32[]{:S(2)}) async-start(f32[4,16,2048]{2,1,0:T(8,128)} %broadcast_in_dim.76), calls=%async_computation | async-start | bytes 1048576 | tf_op jit(solution)/shard_map/all_to_all | solution.py:22
  8.3 4.6 %collective-permute-start = (f32[8,2048]{1,0:T(8,128)S(1)}, f32[8,2048]{1,0:T(8,128)S(1)}, u32[]{:S(2)}, u32[]{:S(2)}) collective-permute-start(f32[8,2048]{1,0:T(8,128)S(1)} %bitcast.55), channel_id=1, source_target_pairs={{0,96},{32,64},{64,32},{96,0},{128,224},{160,192},{192,160},{224,1... | collective-permute-start | bytes 196616 | tf_op jit(solution)/shard_map/ppermute | solution.py:83
  13.0 1.9 collective-permute-done
  14.9 7.3 %all-to-all-done = f32[4,16,2048]{2,1,0:T(8,128)S(1)} async-done(((f32[4,16,2048]{2,1,0:T(8,128)}), f32[4,16,2048]{2,1,0:T(8,128)S(1)}, u32[]{:S(2)}, u32[]{:S(2)}) %all-to-all-start) | async-done | bytes 524320 | tf_op jit(solution)/shard_map/all_to_all | solution.py:22
  22.2 0.8 broadcast_in_dim.77
  23.1 3.6 %all-to-all-start.1 = ((f32[4,16,2048]{2,1,0:T(8,128)}), f32[4,16,2048]{2,1,0:T(8,128)S(1)}, u32[]{:S(2)}, u32[]{:S(2)}) async-start(f32[4,16,2048]{2,1,0:T(8,128)} %broadcast_in_dim.77), calls=%async_computation.1 | async-start | bytes 1048576 | tf_op jit(solution)/shard_map/all_to_all | solution.py:22
  26.7 3.2 %collective-permute-start.1 = (f32[64,2048]{1,0:T(8,128)S(1)}, f32[64,2048]{1,0:T(8,128)S(1)}, u32[]{:S(2)}, u32[]{:S(2)}) collective-permute-start(f32[64,2048]{1,0:T(8,128)S(1)} %bitcast.43), channel_id=1, source_target_pairs={{0,32},{32,0},{64,96},{96,64},{128,160},{160,128},{192,224},{224,1... | collective-permute-start | bytes 1572872 | tf_op jit(solution)/shard_map/ppermute | solution.py:83
  29.9 10.7 %all-to-all-done.1 = f32[4,16,2048]{2,1,0:T(8,128)S(1)} async-done(((f32[4,16,2048]{2,1,0:T(8,128)}), f32[4,16,2048]{2,1,0:T(8,128)S(1)}, u32[]{:S(2)}, u32[]{:S(2)}) %all-to-all-start.1) | async-done | bytes 524320 | tf_op jit(solution)/shard_map/all_to_all | solution.py:22
  40.6 3.2 %collective-permute-start.2 = (f32[64,2048]{1,0:T(8,128)S(1)}, f32[64,2048]{1,0:T(8,128)S(1)}, u32[]{:S(2)}, u32[]{:S(2)}) collective-permute-start(f32[64,2048]{1,0:T(8,128)S(1)} %bitcast.37), channel_id=1, source_target_pairs={{0,32},{32,0},{64,96},{96,64},{128,160},{160,128},{192,224},{224,1... | collective-permute-start | bytes 1572872 | tf_op jit(solution)/shard_map/ppermute | solution.py:83
  43.9 3.8 %collective-permute-start.3 = (f32[128,2048]{1,0:T(8,128)S(1)}, f32[128,2048]{1,0:T(8,128)}, u32[]{:S(2)}, u32[]{:S(2)}) collective-permute-start(f32[128,2048]{1,0:T(8,128)S(1)} %constant_dynamic-update-slice_fusion), channel_id=1, source_target_pairs={{0,96},{32,64},{64,32},{96,0},{128,224},{160,192},{192,160},{224,1... | collective-permute-start | bytes 3145736 | tf_op jit(solution)/shard_map/ppermute | solution.py:83
  47.8 0.5 fusion.51
  48.3 17.2 %psum.28 = f32[16,128]{1,0:T(8,128)S(1)} all-reduce(f32[16,128]{1,0:T(8,128)S(1)} %fusion.51), channel_id=1, replica_groups={{0,8,16,24},{1,9,17,25},{2,10,18,26},{3,11,19,27},{4,12,20,28},{5,13,21..., use_global_device_ids=true, to_apply=%region_0.1 | all-reduce | flops 2048 | bytes 16384 | tf_op jit(solution)/shard_map/psum | solution.py:87
  65.5 0.7 broadcast_in_dim.78
  66.2 9.0 %all-to-all-start.2 = ((f32[16,16,128]{2,1,0:T(8,128)}), f32[16,16,128]{2,1,0:T(8,128)S(1)}, u32[]{:S(2)}, u32[]{:S(2)}) async-start(f32[16,16,128]{2,1,0:T(8,128)} %broadcast_in_dim.78), calls=%async_computation.2 | async-start | bytes 262144 | tf_op jit(solution)/shard_map/all_to_all | solution.py:22
  75.1 1.1 pad_maximum_fusion
  76.2 4.3 %collective-permute-start.4 = (f32[128,2048]{1,0:T(8,128)}, f32[128,2048]{1,0:T(8,128)S(1)}, u32[]{:S(2)}, u32[]{:S(2)}) collective-permute-start(f32[128,2048]{1,0:T(8,128)} %pad_maximum_fusion), channel_id=1, source_target_pairs={{0,96},{32,64},{64,32},{96,0},{128,224},{160,192},{192,160},{224,1... | collective-permute-start | bytes 3145736 | tf_op jit(solution)/shard_map/ppermute | solution.py:83
  80.5 0.4 all-to-all-done.2
  80.9 1.6 fusion.52
  82.5 0.4 fusion
  82.9 0.5 fusion.40
  83.4 12.4 %psum.29 = f32[16,128]{1,0:T(8,128)S(1)} all-reduce(f32[16,128]{1,0:T(8,128)S(1)} %fusion.40), channel_id=1, replica_groups={{0,8,16,24},{1,9,17,25},{2,10,18,26},{3,11,19,27},{4,12,20,28},{5,13,21..., use_global_device_ids=true, to_apply=%region_3.4 | all-reduce | flops 2048 | bytes 16384 | tf_op jit(solution)/shard_map/psum | solution.py:87
  95.8 0.7 broadcast_in_dim.79
  96.5 7.5 %all-to-all-start.3 = ((f32[16,16,128]{2,1,0:T(8,128)}), f32[16,16,128]{2,1,0:T(8,128)S(1)}, u32[]{:S(2)}, u32[]{:S(2)}) async-start(f32[16,16,128]{2,1,0:T(8,128)} %broadcast_in_dim.79), calls=%async_computation.3 | async-start | bytes 262144 | tf_op jit(solution)/shard_map/all_to_all | solution.py:22
  104.0 5.8 %all-to-all-done.3 = f32[16,16,128]{2,1,0:T(8,128)S(1)} async-done(((f32[16,16,128]{2,1,0:T(8,128)}), f32[16,16,128]{2,1,0:T(8,128)S(1)}, u32[]{:S(2)}, u32[]{:S(2)}) %all-to-all-start.3) | async-done | bytes 131104 | tf_op jit(solution)/shard_map/all_to_all | solution.py:22
  109.8 0.4 fusion.32
  110.1 0.4 convolution_subtract_fusion.4
  110.5 2.2 %collective-permute-start.6 = (f32[8,2048]{1,0:T(8,128)S(1)}, f32[8,2048]{1,0:T(8,128)S(1)}, u32[]{:S(2)}, u32[]{:S(2)}) collective-permute-start(f32[8,2048]{1,0:T(8,128)S(1)} %convolution_subtract_fusion.4), channel_id=1, source_target_pairs={{0,1},{1,0},{2,3},{3,2},{4,5},{5,4},{6,7},{7,6},{8,9},{9,8},{10,11... | collective-permute-start | bytes 196616 | tf_op jit(solution)/shard_map/ppermute | solution.py:54
  112.8 5.1 %collective-permute-start.5 = (f32[8,2048]{1,0:T(8,128)S(1)}, f32[8,2048]{1,0:T(8,128)S(1)}, u32[]{:S(2)}, u32[]{:S(2)}) collective-permute-start(f32[8,2048]{1,0:T(8,128)S(1)} %convolution_subtract_fusion.4), channel_id=1, source_target_pairs={{1,2},{3,4},{5,6},{7,8},{9,10},{11,12},{13,14},{15,16},{17,18},{19... | collective-permute-start | bytes 196616 | tf_op jit(solution)/shard_map/ppermute | solution.py:55
  117.9 0.1 copy.54
  117.9 0.1 fusion.50
  118.1 0.1 fusion.48
  118.2 0.1 fusion.49
  118.4 0.1 fusion.47
  118.5 6.5 %collective-permute-done.5 = f32[8,2048]{1,0:T(8,128)S(1)} collective-permute-done((f32[8,2048]{1,0:T(8,128)S(1)}, f32[8,2048]{1,0:T(8,128)S(1)}, u32[]{:S(2)}, u32[]{:S(2)}) %collective-permute-start.5) | collective-permute-done | bytes 65568 | tf_op jit(solution)/shard_map/ppermute | solution.py:55
  125.1 0.1 copy.43
  125.1 0.1 copy.44
  125.2 0.0 copy-start.3
  125.2 0.8 copy-done
  126.0 0.5 fusion.17
  126.5 1.7 fusion.54
  128.2 0.5 fusion.53
  128.7 7.2 %all_to_all.30 = f32[8,8,256]{2,1,0:T(8,128)S(1)} all-to-all(f32[8,8,256]{2,1,0:T(8,128)S(1)} %broadcast_in_dim.85), channel_id=1, replica_groups={{0,1,2,3,4,5,6,7},{8,9,10,11,12,13,14,15},{16,17,18,19,20,21,22,23},{24..., dimensions={0} | all-to-all | bytes 131072 | tf_op jit(solution)/shard_map/all_to_all | solution.py:22
  136.0 11.3 %psum.30 = f32[8,256]{1,0:T(8,128)S(1)} all-reduce(f32[8,256]{1,0:T(8,128)S(1)} %reduce_sum.58), channel_id=1, replica_groups={{0,8,16,24},{1,9,17,25},{2,10,18,26},{3,11,19,27},{4,12,20,28},{5,13,21..., use_global_device_ids=true, to_apply=%region_7.8 | all-reduce | flops 2048 | bytes 16384 | tf_op jit(solution)/shard_map/psum | solution.py:27
  147.3 1.6 fusion.20
  148.9 0.4 fusion.1
  149.2 0.5 fusion.55
  149.7 0.5 fusion.39
  150.3 10.0 %all_to_all.31 = f32[8,8,256]{2,1,0:T(8,128)S(1)} all-to-all(f32[8,8,256]{2,1,0:T(8,128)S(1)} %broadcast_in_dim.86), channel_id=1, replica_groups={{0,1,2,3,4,5,6,7},{8,9,10,11,12,13,14,15},{16,17,18,19,20,21,22,23},{24..., dimensions={0} | all-to-all | bytes 131072 | tf_op jit(solution)/shard_map/all_to_all | solution.py:22
  160.3 12.6 %psum.31 = f32[8,256]{1,0:T(8,128)S(1)} all-reduce(f32[8,256]{1,0:T(8,128)S(1)} %reduce_sum.59), channel_id=1, replica_groups={{0,8,16,24},{1,9,17,25},{2,10,18,26},{3,11,19,27},{4,12,20,28},{5,13,21..., use_global_device_ids=true, to_apply=%region_9.10 | all-reduce | flops 2048 | bytes 16384 | tf_op jit(solution)/shard_map/psum | solution.py:27
  172.9 0.4 convolution_subtract_fusion.2
  173.3 0.4 convolution_subtract_fusion.1
  173.6 4.7 %collective-permute-start.8 = (f32[8,2048]{1,0:T(8,128)S(1)}, f32[8,2048]{1,0:T(8,128)S(1)}, u32[]{:S(2)}, u32[]{:S(2)}) collective-permute-start(f32[8,2048]{1,0:T(8,128)S(1)} %convolution_subtract_fusion.1), channel_id=1, source_target_pairs={{0,1},{1,0},{2,3},{3,2},{4,5},{5,4},{6,7},{7,6},{8,9},{9,8},{10,11... | collective-permute-start | bytes 196616 | tf_op jit(solution)/shard_map/ppermute | solution.py:54
  178.3 4.9 %collective-permute-start.7 = (f32[8,2048]{1,0:T(8,128)S(1)}, f32[8,2048]{1,0:T(8,128)S(1)}, u32[]{:S(2)}, u32[]{:S(2)}) collective-permute-start(f32[8,2048]{1,0:T(8,128)S(1)} %convolution_subtract_fusion.1), channel_id=1, source_target_pairs={{1,2},{3,4},{5,6},{7,8},{9,10},{11,12},{13,14},{15,16},{17,18},{19... | collective-permute-start | bytes 196616 | tf_op jit(solution)/shard_map/ppermute | solution.py:55
  183.2 0.1 copy.70
  183.3 0.1 fusion.46
  183.4 0.1 fusion.44
  183.6 0.1 fusion.45
  183.7 0.1 fusion.43
  183.9 6.0 %collective-permute-done.7 = f32[8,2048]{1,0:T(8,128)S(1)} collective-permute-done((f32[8,2048]{1,0:T(8,128)S(1)}, f32[8,2048]{1,0:T(8,128)S(1)}, u32[]{:S(2)}, u32[]{:S(2)}) %collective-permute-start.7) | collective-permute-done | bytes 65568 | tf_op jit(solution)/shard_map/ppermute | solution.py:55
  189.9 0.1 copy.59
  190.0 0.1 copy.60
  190.0 1.1 fusion.3
  (39 shorter events, 0.4 us)
Async XLA Ops:
  2.5 5.8 %copy-start.1 = (f32[8,2,1024]{2,1,0:T(2,128)S(1)}, f32[8,2,1024]{2,1,0:T(2,128)}, u32[]{:S(2)}) copy-start(f32[8,2,1024]{2,1,0:T(2,128)} %param.6) | copy-start | bytes 196612
  2.5 19.7 %all-to-all-start = ((f32[4,16,2048]{2,1,0:T(8,128)}), f32[4,16,2048]{2,1,0:T(8,128)S(1)}, u32[]{:S(2)}, u32[]{:S(2)}) async-start(f32[4,16,2048]{2,1,0:T(8,128)} %broadcast_in_dim.76), calls=%async_computation | async-start | bytes 1048576 | tf_op jit(solution)/shard_map/all_to_all | solution.py:22
  8.3 6.6 %collective-permute-start = (f32[8,2048]{1,0:T(8,128)S(1)}, f32[8,2048]{1,0:T(8,128)S(1)}, u32[]{:S(2)}, u32[]{:S(2)}) collective-permute-start(f32[8,2048]{1,0:T(8,128)S(1)} %bitcast.55), channel_id=1, source_target_pairs={{0,96},{32,64},{64,32},{96,0},{128,224},{160,192},{192,160},{224,1... | collective-permute-start | bytes 196616 | tf_op jit(solution)/shard_map/ppermute | solution.py:83
  23.1 6.8 %copy-start.2 = (f32[2,1024]{1,0:T(2,128)S(1)}, f32[2,1024]{1,0:T(2,128)}, u32[]{:S(2)}) copy-start(f32[2,1024]{1,0:T(2,128)} %param.8) | copy-start | bytes 24580
  23.1 17.6 %all-to-all-start.1 = ((f32[4,16,2048]{2,1,0:T(8,128)}), f32[4,16,2048]{2,1,0:T(8,128)S(1)}, u32[]{:S(2)}, u32[]{:S(2)}) async-start(f32[4,16,2048]{2,1,0:T(8,128)} %broadcast_in_dim.77), calls=%async_computation.1 | async-start | bytes 1048576 | tf_op jit(solution)/shard_map/all_to_all | solution.py:22
  26.7 17.2 %collective-permute-start.1 = (f32[64,2048]{1,0:T(8,128)S(1)}, f32[64,2048]{1,0:T(8,128)S(1)}, u32[]{:S(2)}, u32[]{:S(2)}) collective-permute-start(f32[64,2048]{1,0:T(8,128)S(1)} %bitcast.43), channel_id=1, source_target_pairs={{0,32},{32,0},{64,96},{96,64},{128,160},{160,128},{192,224},{224,1... | collective-permute-start | bytes 1572872 | tf_op jit(solution)/shard_map/ppermute | solution.py:83
  40.6 24.9 %collective-permute-start.2 = (f32[64,2048]{1,0:T(8,128)S(1)}, f32[64,2048]{1,0:T(8,128)S(1)}, u32[]{:S(2)}, u32[]{:S(2)}) collective-permute-start(f32[64,2048]{1,0:T(8,128)S(1)} %bitcast.37), channel_id=1, source_target_pairs={{0,32},{32,0},{64,96},{96,64},{128,160},{160,128},{192,224},{224,1... | collective-permute-start | bytes 1572872 | tf_op jit(solution)/shard_map/ppermute | solution.py:83
  43.9 37.0 %collective-permute-start.3 = (f32[128,2048]{1,0:T(8,128)S(1)}, f32[128,2048]{1,0:T(8,128)}, u32[]{:S(2)}, u32[]{:S(2)}) collective-permute-start(f32[128,2048]{1,0:T(8,128)S(1)} %constant_dynamic-update-slice_fusion), channel_id=1, source_target_pairs={{0,96},{32,64},{64,32},{96,0},{128,224},{160,192},{192,160},{224,1... | collective-permute-start | bytes 3145736 | tf_op jit(solution)/shard_map/ppermute | solution.py:83
  66.2 14.7 %all-to-all-start.2 = ((f32[16,16,128]{2,1,0:T(8,128)}), f32[16,16,128]{2,1,0:T(8,128)S(1)}, u32[]{:S(2)}, u32[]{:S(2)}) async-start(f32[16,16,128]{2,1,0:T(8,128)} %broadcast_in_dim.78), calls=%async_computation.2 | async-start | bytes 262144 | tf_op jit(solution)/shard_map/all_to_all | solution.py:22
  76.2 33.6 %collective-permute-start.4 = (f32[128,2048]{1,0:T(8,128)}, f32[128,2048]{1,0:T(8,128)S(1)}, u32[]{:S(2)}, u32[]{:S(2)}) collective-permute-start(f32[128,2048]{1,0:T(8,128)} %pad_maximum_fusion), channel_id=1, source_target_pairs={{0,96},{32,64},{64,32},{96,0},{128,224},{160,192},{192,160},{224,1... | collective-permute-start | bytes 3145736 | tf_op jit(solution)/shard_map/ppermute | solution.py:83
  96.5 13.2 %all-to-all-start.3 = ((f32[16,16,128]{2,1,0:T(8,128)}), f32[16,16,128]{2,1,0:T(8,128)S(1)}, u32[]{:S(2)}, u32[]{:S(2)}) async-start(f32[16,16,128]{2,1,0:T(8,128)} %broadcast_in_dim.79), calls=%async_computation.3 | async-start | bytes 262144 | tf_op jit(solution)/shard_map/all_to_all | solution.py:22
  110.5 8.0 %collective-permute-start.6 = (f32[8,2048]{1,0:T(8,128)S(1)}, f32[8,2048]{1,0:T(8,128)S(1)}, u32[]{:S(2)}, u32[]{:S(2)}) collective-permute-start(f32[8,2048]{1,0:T(8,128)S(1)} %convolution_subtract_fusion.4), channel_id=1, source_target_pairs={{0,1},{1,0},{2,3},{3,2},{4,5},{5,4},{6,7},{7,6},{8,9},{9,8},{10,11... | collective-permute-start | bytes 196616 | tf_op jit(solution)/shard_map/ppermute | solution.py:54
  112.8 12.3 %collective-permute-start.5 = (f32[8,2048]{1,0:T(8,128)S(1)}, f32[8,2048]{1,0:T(8,128)S(1)}, u32[]{:S(2)}, u32[]{:S(2)}) collective-permute-start(f32[8,2048]{1,0:T(8,128)S(1)} %convolution_subtract_fusion.4), channel_id=1, source_target_pairs={{1,2},{3,4},{5,6},{7,8},{9,10},{11,12},{13,14},{15,16},{17,18},{19... | collective-permute-start | bytes 196616 | tf_op jit(solution)/shard_map/ppermute | solution.py:55
  125.1 0.8 copy-start
  125.2 0.8 copy-start.3
  173.6 10.2 %collective-permute-start.8 = (f32[8,2048]{1,0:T(8,128)S(1)}, f32[8,2048]{1,0:T(8,128)S(1)}, u32[]{:S(2)}, u32[]{:S(2)}) collective-permute-start(f32[8,2048]{1,0:T(8,128)S(1)} %convolution_subtract_fusion.1), channel_id=1, source_target_pairs={{0,1},{1,0},{2,3},{3,2},{4,5},{5,4},{6,7},{7,6},{8,9},{9,8},{10,11... | collective-permute-start | bytes 196616 | tf_op jit(solution)/shard_map/ppermute | solution.py:54
  178.3 11.6 %collective-permute-start.7 = (f32[8,2048]{1,0:T(8,128)S(1)}, f32[8,2048]{1,0:T(8,128)S(1)}, u32[]{:S(2)}, u32[]{:S(2)}) collective-permute-start(f32[8,2048]{1,0:T(8,128)S(1)} %convolution_subtract_fusion.1), channel_id=1, source_target_pairs={{1,2},{3,4},{5,6},{7,8},{9,10},{11,12},{13,14},{15,16},{17,18},{19... | collective-permute-start | bytes 196616 | tf_op jit(solution)/shard_map/ppermute | solution.py:55

commit v17 on v16

--- a/solution.py
+++ b/solution.py
@@ -51,8 +51,9 @@
     count = lax.axis_size("space")
     outer = [(i, i + 1) for i in range(1, count - 1, 2)]
     outer = outer + [(j, i) for i, j in outer]
-    inside = lax.ppermute(vectors, "space", [(i, i ^ 1) for i in range(count)])
     across = lax.ppermute(vectors, "space", outer)
+    both = lax.psum(vectors, "space", axis_index_groups=[[i, i + 1] for i in range(0, count, 2)])
+    inside = both - vectors
     first = lax.axis_index("space") % 2 == 0
     return jnp.where(first, across, inside), jnp.where(first, inside, across)
 
@@ -83,10 +84,17 @@
     return lax.ppermute(x, "band", [(i, i ^ bits) for i in range(lax.axis_size("band"))])
 
 
-def pair_margins(product, lower, weight, beside=None):
+def pair_margins(product, lower, weight, beside=None, own_only=False):
     total = lax.psum(product, "space", axis_index_groups=SPACE_Z)
     total, beside = lax.optimization_barrier((total, beside))
-    every = weight * copies(total, ("band", "space"), PAIR_PLANE)
+    if own_only:
+        count = product.shape[0] // 2
+        rows = jnp.broadcast_to(total.reshape(2, 1, count, -1), (2, 8, count, total.shape[1]))
+        every = weight * lax.all_to_all(
+            rows.reshape(16, count, -1), ("band", "space"), 0, 0, axis_index_groups=PAIR_PLANE
+        )
+    else:
+        every = weight * copies(total, ("band", "space"), PAIR_PLANE)
     ahead, behind = jnp.sum(every[:8], axis=0), jnp.sum(every[8:], axis=0)
     return (jnp.where(lower, ahead, behind), jnp.where(lower, behind, ahead)), beside
 
@@ -125,12 +133,12 @@
     for margin, part in zip(margins, first):
         pair = pair - combination(margin, part)
     near = jnp.concatenate([second, across], axis=0)
-    margins, _ = pair_margins(products(pair, near), lower, weight)
+    margins, _ = pair_margins(products(pair, near), lower, weight, own_only=True)
     margins, far = tie((margins, swapped(near, 3)))
     blocks = [first, (near, far)]
     vectors = jnp.where(lower, pair[:count], pair[count:])
     for margin, part in zip(margins, blocks[1]):
-        vectors = vectors - combination(jnp.where(lower, margin[:count], margin[count:]), part)
+        vectors = vectors - combination(margin, part)
     for iteration in range(ITERS):
         if iteration > 0:
             for block in blocks:

time: 192 us -> 268 us (1.40)
  waiting for transfers between devices: 38.6 us -> 90.6 us
  between operations: 1.13 us -> 14.6 us
  blocking collectives: 70.7 us -> 76.2 us
  starting transfers between devices: 61.9 us -> 56.5 us
  local copies, waits for them, and re-layouts: 6.35 us -> 10.6 us
  other arithmetic: 2.88 us -> 6.03 us
    psum x0 -> x2, waiting for transfers between devices: none -> 65.5 us  [neighbours(): lax.psum(vectors, 'space', axis_index_groups=[[i, i + 1] for i in range(0...]
    ppermute x2, waiting for transfers between devices: 12.6 us -> 0.01 us  [neighbours(): across = lax.ppermute(vectors, 'space', outer)]
    all_to_all x4 -> x3, starting transfers between devices: 25.8 us -> 18.2 us  [copies(): return lax.all_to_all(sent, axis, 0, 0, axis_index_groups=groups)]
    all_to_all x0 -> x1, starting transfers between devices: none -> 7.33 us  [pair_margins(): lax.all_to_all(rows.reshape(16, count, -1), ('band', 'space'), 0, 0, axis...]
    ppermute x2 -> x0, starting transfers between devices: 6.91 us -> none  [neighbours(): inside = lax.ppermute(vectors, 'space', [(i, i ^ 1) for i in range(count)])]
    all_to_all x4 -> x3, waiting for transfers between devices: 24.2 us -> 18.4 us  [copies(): return lax.all_to_all(sent, axis, 0, 0, axis_index_groups=groups)]
    psum x2, blocking collectives: 23.9 us -> 28.9 us  [space_sum(): return lax.psum(near, 'space', axis_index_groups=SPACE_Z)]
    all_to_all x0 -> x1, waiting for transfers between devices: none -> 4.8 us  [pair_margins(): lax.all_to_all(rows.reshape(16, count, -1), ('band', 'space'), 0, 0, axis...]
where the time goes in v17:
time: 268 us; the launch traced here: 265 us
  waiting for transfers between devices  90.6 us (34%)
  blocking collectives  76.2 us (28%)
  starting transfers between devices  56.5 us (21%)
  between operations  14.6 us (5%)
  matrix products  10.9 us (4%)
  local copies, waits for them, and re-layouts  10.6 us (4%)
  other arithmetic  6.03 us (2%)
    psum x2, waiting for transfers between devices, neighbours(): lax.psum(vectors, 'space', axis_index_groups=[[i, i + 1] for i in range(0...  65.5 us
    psum x2, blocking collectives, pair_margins(): total = lax.psum(product, 'space', axis_index_groups=SPACE_Z)  29.7 us
    psum x2, blocking collectives, space_sum(): return lax.psum(near, 'space', axis_index_groups=SPACE_Z)  28.9 us
    ppermute x5, starting transfers between devices, swapped(): lax.ppermute(x, 'band', [(i, i ^ bits) for i in range(lax.axis_size('band...  19.1 us
    all_to_all x3, waiting for transfers between devices, copies(): return lax.all_to_all(sent, axis, 0, 0, axis_index_groups=groups)  18.4 us
    all_to_all x3, starting transfers between devices, copies(): return lax.all_to_all(sent, axis, 0, 0, axis_index_groups=groups)  18.2 us
    all_to_all x2, blocking collectives, copies(): return lax.all_to_all(sent, axis, 0, 0, axis_index_groups=groups)  17.6 us
    ppermute x2, starting transfers between devices, neighbours(): across = lax.ppermute(vectors, 'space', outer)  11.8 us
  transfers between devices with their start and end apart: 13, of which 7 were waited for; matrix products, arithmetic and copies ran while one was open for 4% of the time, Pallas kernels for 0%

profile of v17, /device:TPU:7, one launch (start us, length us, event | category | flops | bytes accessed | tf_op | source)
XLA Modules:
  0.0 265.4 jit_solution(2094956275923694412)
XLA Ops:
  7.2 1.0 fusion.35
  8.2 0.8 broadcast_in_dim.77
  9.0 5.7 %all-to-all-start = ((f32[4,16,2048]{2,1,0:T(8,128)}), f32[4,16,2048]{2,1,0:T(8,128)S(1)}, u32[]{:S(2)}, u32[]{:S(2)}) async-start(f32[4,16,2048]{2,1,0:T(8,128)} %broadcast_in_dim.77), calls=%async_computation | async-start | bytes 1048576 | tf_op jit(solution)/shard_map/all_to_all | solution.py:22
  14.8 4.6 %collective-permute-start = (f32[8,2048]{1,0:T(8,128)S(1)}, f32[8,2048]{1,0:T(8,128)S(1)}, u32[]{:S(2)}, u32[]{:S(2)}) collective-permute-start(f32[8,2048]{1,0:T(8,128)S(1)} %bitcast.60), channel_id=1, source_target_pairs={{0,96},{32,64},{64,32},{96,0},{128,224},{160,192},{192,160},{224,1... | collective-permute-start | bytes 196616 | tf_op jit(solution)/shard_map/ppermute | solution.py:84
  19.5 1.9 collective-permute-done
  21.4 7.3 %all-to-all-done = f32[4,16,2048]{2,1,0:T(8,128)S(1)} async-done(((f32[4,16,2048]{2,1,0:T(8,128)}), f32[4,16,2048]{2,1,0:T(8,128)S(1)}, u32[]{:S(2)}, u32[]{:S(2)}) %all-to-all-start) | async-done | bytes 524320 | tf_op jit(solution)/shard_map/all_to_all | solution.py:22
  28.8 0.8 broadcast_in_dim.78
  29.6 3.5 %all-to-all-start.1 = ((f32[4,16,2048]{2,1,0:T(8,128)}), f32[4,16,2048]{2,1,0:T(8,128)S(1)}, u32[]{:S(2)}, u32[]{:S(2)}) async-start(f32[4,16,2048]{2,1,0:T(8,128)} %broadcast_in_dim.78), calls=%async_computation.1 | async-start | bytes 1048576 | tf_op jit(solution)/shard_map/all_to_all | solution.py:22
  33.1 3.2 %collective-permute-start.1 = (f32[64,2048]{1,0:T(8,128)S(1)}, f32[64,2048]{1,0:T(8,128)S(1)}, u32[]{:S(2)}, u32[]{:S(2)}) collective-permute-start(f32[64,2048]{1,0:T(8,128)S(1)} %bitcast.47), channel_id=1, source_target_pairs={{0,32},{32,0},{64,96},{96,64},{128,160},{160,128},{192,224},{224,1... | collective-permute-start | bytes 1572872 | tf_op jit(solution)/shard_map/ppermute | solution.py:84
  36.4 10.7 %all-to-all-done.1 = f32[4,16,2048]{2,1,0:T(8,128)S(1)} async-done(((f32[4,16,2048]{2,1,0:T(8,128)}), f32[4,16,2048]{2,1,0:T(8,128)S(1)}, u32[]{:S(2)}, u32[]{:S(2)}) %all-to-all-start.1) | async-done | bytes 524320 | tf_op jit(solution)/shard_map/all_to_all | solution.py:22
  47.0 3.2 %collective-permute-start.2 = (f32[64,2048]{1,0:T(8,128)S(1)}, f32[64,2048]{1,0:T(8,128)S(1)}, u32[]{:S(2)}, u32[]{:S(2)}) collective-permute-start(f32[64,2048]{1,0:T(8,128)S(1)} %bitcast.41), channel_id=1, source_target_pairs={{0,32},{32,0},{64,96},{96,64},{128,160},{160,128},{192,224},{224,1... | collective-permute-start | bytes 1572872 | tf_op jit(solution)/shard_map/ppermute | solution.py:84
  50.3 3.8 %collective-permute-start.3 = (f32[128,2048]{1,0:T(8,128)S(1)}, f32[128,2048]{1,0:T(8,128)}, u32[]{:S(2)}, u32[]{:S(2)}) collective-permute-start(f32[128,2048]{1,0:T(8,128)S(1)} %constant_dynamic-update-slice_fusion), channel_id=1, source_target_pairs={{0,96},{32,64},{64,32},{96,0},{128,224},{160,192},{192,160},{224,1... | collective-permute-start | bytes 3145736 | tf_op jit(solution)/shard_map/ppermute | solution.py:84
  54.1 0.5 fusion.44
  54.7 17.2 %psum.42 = f32[16,128]{1,0:T(8,128)S(1)} all-reduce(f32[16,128]{1,0:T(8,128)S(1)} %fusion.44), channel_id=1, replica_groups={{0,8,16,24},{1,9,17,25},{2,10,18,26},{3,11,19,27},{4,12,20,28},{5,13,21..., use_global_device_ids=true, to_apply=%region_0.1 | all-reduce | flops 2048 | bytes 16384 | tf_op jit(solution)/shard_map/psum | solution.py:88
  71.9 0.7 broadcast_in_dim.79
  72.5 9.0 %all-to-all-start.2 = ((f32[16,16,128]{2,1,0:T(8,128)}), f32[16,16,128]{2,1,0:T(8,128)S(1)}, u32[]{:S(2)}, u32[]{:S(2)}) async-start(f32[16,16,128]{2,1,0:T(8,128)} %broadcast_in_dim.79), calls=%async_computation.2 | async-start | bytes 262144 | tf_op jit(solution)/shard_map/all_to_all | solution.py:22
  81.5 1.1 pad_maximum_fusion
  82.6 4.3 %collective-permute-start.4 = (f32[128,2048]{1,0:T(8,128)}, f32[128,2048]{1,0:T(8,128)S(1)}, u32[]{:S(2)}, u32[]{:S(2)}) collective-permute-start(f32[128,2048]{1,0:T(8,128)} %pad_maximum_fusion), channel_id=1, source_target_pairs={{0,96},{32,64},{64,32},{96,0},{128,224},{160,192},{192,160},{224,1... | collective-permute-start | bytes 3145736 | tf_op jit(solution)/shard_map/ppermute | solution.py:84
  86.9 0.4 all-to-all-done.2
  87.3 1.6 fusion.45
  88.9 0.4 fusion
  89.3 0.5 fusion.33
  89.8 12.5 %psum.43 = f32[16,128]{1,0:T(8,128)S(1)} all-reduce(f32[16,128]{1,0:T(8,128)S(1)} %fusion.33), channel_id=1, replica_groups={{0,8,16,24},{1,9,17,25},{2,10,18,26},{3,11,19,27},{4,12,20,28},{5,13,21..., use_global_device_ids=true, to_apply=%region_3.4 | all-reduce | flops 2048 | bytes 16384 | tf_op jit(solution)/shard_map/psum | solution.py:88
  102.3 0.6 broadcast_in_dim.81
  102.9 7.3 %all-to-all-start.3 = ((f32[16,8,128]{2,1,0:T(8,128)}), f32[16,8,128]{2,1,0:T(8,128)S(1)}, u32[]{:S(2)}, u32[]{:S(2)}) async-start(f32[16,8,128]{2,1,0:T(8,128)} %bitcast.3), calls=%async_computation.3 | async-start | bytes 131072 | tf_op jit(solution)/shard_map/all_to_all | solution.py:93
  110.3 0.6 fusion.26
  110.9 4.8 %all-to-all-done.3 = f32[16,8,128]{2,1,0:T(8,128)S(1)} async-done(((f32[16,8,128]{2,1,0:T(8,128)}), f32[16,8,128]{2,1,0:T(8,128)S(1)}, u32[]{:S(2)}, u32[]{:S(2)}) %all-to-all-start.3) | async-done | bytes 65568 | tf_op jit(solution)/shard_map/all_to_all | solution.py:93
  115.7 0.4 fusion.32
  116.1 1.0 fusion.17
  117.1 5.4 %collective-permute-start.5 = (f32[8,2048]{1,0:T(8,128)}, f32[8,2048]{1,0:T(8,128)S(1)}, u32[]{:S(2)}, u32[]{:S(2)}) collective-permute-start(f32[8,2048]{1,0:T(8,128)} %fusion.17), channel_id=1, source_target_pairs={{1,2},{3,4},{5,6},{7,8},{9,10},{11,12},{13,14},{15,16},{17,18},{19... | collective-permute-start | bytes 196616 | tf_op jit(solution)/shard_map/ppermute | solution.py:54
  122.5 0.9 copy.54
  123.4 0.1 fusion.43
  123.5 0.8 fusion.41
  124.3 0.8 fusion.42
  125.1 0.8 fusion.40
  125.9 31.2 %all-reduce.19.cloned.1.call-done = f32[8,2048]{1,0:T(8,128)} async-done(((f32[8,2048]{1,0:T(8,128)}), f32[8,2048]{1,0:T(8,128)}) %all-reduce.19.cloned.1.call-update) | async-done | bytes 65552 | tf_op jit(solution)/shard_map/psum | solution.py:55
  157.1 0.9 broadcast_select_fusion.3
  158.1 0.1 copy.43
  158.3 0.6 copy-done.2
  158.9 0.1 copy-done
  159.0 0.5 fusion.18
  159.5 1.7 fusion.47
  161.2 0.5 fusion.46
  161.8 7.6 %all_to_all.30 = f32[8,8,256]{2,1,0:T(8,128)S(1)} all-to-all(f32[8,8,256]{2,1,0:T(8,128)S(1)} %broadcast_in_dim.87), channel_id=1, replica_groups={{0,1,2,3,4,5,6,7},{8,9,10,11,12,13,14,15},{16,17,18,19,20,21,22,23},{24..., dimensions={0} | all-to-all | bytes 131072 | tf_op jit(solution)/shard_map/all_to_all | solution.py:22
  169.4 15.0 %psum.45 = f32[8,256]{1,0:T(8,128)S(1)} all-reduce(f32[8,256]{1,0:T(8,128)S(1)} %reduce_sum.58), channel_id=1, replica_groups={{0,8,16,24},{1,9,17,25},{2,10,18,26},{3,11,19,27},{4,12,20,28},{5,13,21..., use_global_device_ids=true, to_apply=%region_8.9 | all-reduce | flops 2048 | bytes 16384 | tf_op jit(solution)/shard_map/psum | solution.py:27
  184.4 1.6 fusion.21
  186.0 0.4 fusion.1
  186.4 0.5 fusion.48
  186.9 0.5 fusion.31
  187.4 10.0 %all_to_all.31 = f32[8,8,256]{2,1,0:T(8,128)S(1)} all-to-all(f32[8,8,256]{2,1,0:T(8,128)S(1)} %broadcast_in_dim.88), channel_id=1, replica_groups={{0,1,2,3,4,5,6,7},{8,9,10,11,12,13,14,15},{16,17,18,19,20,21,22,23},{24..., dimensions={0} | all-to-all | bytes 131072 | tf_op jit(solution)/shard_map/all_to_all | solution.py:22
  197.5 13.9 %psum.46 = f32[8,256]{1,0:T(8,128)S(1)} all-reduce(f32[8,256]{1,0:T(8,128)S(1)} %reduce_sum.59), channel_id=1, replica_groups={{0,8,16,24},{1,9,17,25},{2,10,18,26},{3,11,19,27},{4,12,20,28},{5,13,21..., use_global_device_ids=true, to_apply=%region_10.11 | all-reduce | flops 2048 | bytes 16384 | tf_op jit(solution)/shard_map/psum | solution.py:27
  211.4 0.4 convolution_subtract_fusion.2
  211.7 1.0 convolution_subtract_fusion.1
  212.7 6.4 %collective-permute-start.6 = (f32[8,2048]{1,0:T(8,128)}, f32[8,2048]{1,0:T(8,128)S(1)}, u32[]{:S(2)}, u32[]{:S(2)}) collective-permute-start(f32[8,2048]{1,0:T(8,128)} %convolution_subtract_fusion.1), channel_id=1, source_target_pairs={{1,2},{3,4},{5,6},{7,8},{9,10},{11,12},{13,14},{15,16},{17,18},{19... | collective-permute-start | bytes 196616 | tf_op jit(solution)/shard_map/ppermute | solution.py:54
  219.1 0.9 copy.70
  220.0 0.1 fusion.39
  220.2 0.1 fusion.37
  220.3 0.1 fusion.38
  220.5 0.1 fusion.36
  220.6 34.3 %all-reduce.21.cloned.1.call-done = f32[8,2048]{1,0:T(8,128)} async-done(((f32[8,2048]{1,0:T(8,128)}), f32[8,2048]{1,0:T(8,128)}) %all-reduce.21.cloned.1.call-update) | async-done | bytes 65552 | tf_op jit(solution)/shard_map/psum | solution.py:55
  254.9 0.9 broadcast_select_fusion.1
  255.9 0.5 copy-done.10
  256.4 0.2 copy-done.8
  256.6 2.0 fusion.3
  (61 shorter events, 0.8 us)
Async XLA Ops:
  9.0 5.8 %copy-start.6 = (f32[8,2,1024]{2,1,0:T(2,128)S(1)}, f32[8,2,1024]{2,1,0:T(2,128)}, u32[]{:S(2)}) copy-start(f32[8,2,1024]{2,1,0:T(2,128)} %param.6) | copy-start | bytes 196612
  9.0 19.7 %all-to-all-start = ((f32[4,16,2048]{2,1,0:T(8,128)}), f32[4,16,2048]{2,1,0:T(8,128)S(1)}, u32[]{:S(2)}, u32[]{:S(2)}) async-start(f32[4,16,2048]{2,1,0:T(8,128)} %broadcast_in_dim.77), calls=%async_computation | async-start | bytes 1048576 | tf_op jit(solution)/shard_map/all_to_all | solution.py:22
  14.8 6.6 %collective-permute-start = (f32[8,2048]{1,0:T(8,128)S(1)}, f32[8,2048]{1,0:T(8,128)S(1)}, u32[]{:S(2)}, u32[]{:S(2)}) collective-permute-start(f32[8,2048]{1,0:T(8,128)S(1)} %bitcast.60), channel_id=1, source_target_pairs={{0,96},{32,64},{64,32},{96,0},{128,224},{160,192},{192,160},{224,1... | collective-permute-start | bytes 196616 | tf_op jit(solution)/shard_map/ppermute | solution.py:84
  29.6 17.4 %all-to-all-start.1 = ((f32[4,16,2048]{2,1,0:T(8,128)}), f32[4,16,2048]{2,1,0:T(8,128)S(1)}, u32[]{:S(2)}, u32[]{:S(2)}) async-start(f32[4,16,2048]{2,1,0:T(8,128)} %broadcast_in_dim.78), calls=%async_computation.1 | async-start | bytes 1048576 | tf_op jit(solution)/shard_map/all_to_all | solution.py:22
  33.1 3.2 %copy-start.11 = (f32[2,1024]{1,0:T(2,128)S(1)}, f32[2,1024]{1,0:T(2,128)}, u32[]{:S(2)}) copy-start(f32[2,1024]{1,0:T(2,128)} %param.8) | copy-start | bytes 24580
  33.1 17.2 %collective-permute-start.1 = (f32[64,2048]{1,0:T(8,128)S(1)}, f32[64,2048]{1,0:T(8,128)S(1)}, u32[]{:S(2)}, u32[]{:S(2)}) collective-permute-start(f32[64,2048]{1,0:T(8,128)S(1)} %bitcast.47), channel_id=1, source_target_pairs={{0,32},{32,0},{64,96},{96,64},{128,160},{160,128},{192,224},{224,1... | collective-permute-start | bytes 1572872 | tf_op jit(solution)/shard_map/ppermute | solution.py:84
  47.0 24.8 %collective-permute-start.2 = (f32[64,2048]{1,0:T(8,128)S(1)}, f32[64,2048]{1,0:T(8,128)S(1)}, u32[]{:S(2)}, u32[]{:S(2)}) collective-permute-start(f32[64,2048]{1,0:T(8,128)S(1)} %bitcast.41), channel_id=1, source_target_pairs={{0,32},{32,0},{64,96},{96,64},{128,160},{160,128},{192,224},{224,1... | collective-permute-start | bytes 1572872 | tf_op jit(solution)/shard_map/ppermute | solution.py:84
  50.3 37.0 %collective-permute-start.3 = (f32[128,2048]{1,0:T(8,128)S(1)}, f32[128,2048]{1,0:T(8,128)}, u32[]{:S(2)}, u32[]{:S(2)}) collective-permute-start(f32[128,2048]{1,0:T(8,128)S(1)} %constant_dynamic-update-slice_fusion), channel_id=1, source_target_pairs={{0,96},{32,64},{64,32},{96,0},{128,224},{160,192},{192,160},{224,1... | collective-permute-start | bytes 3145736 | tf_op jit(solution)/shard_map/ppermute | solution.py:84
  72.5 14.7 %all-to-all-start.2 = ((f32[16,16,128]{2,1,0:T(8,128)}), f32[16,16,128]{2,1,0:T(8,128)S(1)}, u32[]{:S(2)}, u32[]{:S(2)}) async-start(f32[16,16,128]{2,1,0:T(8,128)} %broadcast_in_dim.79), calls=%async_computation.2 | async-start | bytes 262144 | tf_op jit(solution)/shard_map/all_to_all | solution.py:22
  82.6 33.2 %collective-permute-start.4 = (f32[128,2048]{1,0:T(8,128)}, f32[128,2048]{1,0:T(8,128)S(1)}, u32[]{:S(2)}, u32[]{:S(2)}) collective-permute-start(f32[128,2048]{1,0:T(8,128)} %pad_maximum_fusion), channel_id=1, source_target_pairs={{0,96},{32,64},{64,32},{96,0},{128,224},{160,192},{192,160},{224,1... | collective-permute-start | bytes 3145736 | tf_op jit(solution)/shard_map/ppermute | solution.py:84
  102.9 12.8 %all-to-all-start.3 = ((f32[16,8,128]{2,1,0:T(8,128)}), f32[16,8,128]{2,1,0:T(8,128)S(1)}, u32[]{:S(2)}, u32[]{:S(2)}) async-start(f32[16,8,128]{2,1,0:T(8,128)} %bitcast.3), calls=%async_computation.3 | async-start | bytes 131072 | tf_op jit(solution)/shard_map/all_to_all | solution.py:93
  110.3 46.8 %all-reduce.19.cloned.1.call-start = ((), (), s32[]{:S(2)}) async-start(), calls=%async_computation.6 | async-start | bytes 131072 | tf_op jit(solution)/shard_map/psum | solution.py:55
  117.1 40.0 %collective-permute-start.5 = (f32[8,2048]{1,0:T(8,128)}, f32[8,2048]{1,0:T(8,128)S(1)}, u32[]{:S(2)}, u32[]{:S(2)}) collective-permute-start(f32[8,2048]{1,0:T(8,128)} %fusion.17), channel_id=1, source_target_pairs={{1,2},{3,4},{5,6},{7,8},{9,10},{11,12},{13,14},{15,16},{17,18},{19... | collective-permute-start | bytes 196616 | tf_op jit(solution)/shard_map/ppermute | solution.py:54
  125.1 129.8 %all-reduce.21.cloned.1.call-start = ((), (), s32[]{:S(2)}) async-start(), calls=%async_computation.7 | async-start | bytes 131072 | tf_op jit(solution)/shard_map/psum | solution.py:55
  157.1 1.1 copy-start.4
  157.1 1.1 copy-start.5
  158.0 0.8 copy-start.2
  158.0 0.9 copy-start.3
  158.1 0.9 copy-start
  158.1 0.9 copy-start.1
  158.1 0.9 copy-start.9
  158.2 0.8 copy-start.7
  158.2 0.8 copy-start.12
  212.7 42.2 %collective-permute-start.6 = (f32[8,2048]{1,0:T(8,128)}, f32[8,2048]{1,0:T(8,128)S(1)}, u32[]{:S(2)}, u32[]{:S(2)}) collective-permute-start(f32[8,2048]{1,0:T(8,128)} %convolution_subtract_fusion.1), channel_id=1, source_target_pairs={{1,2},{3,4},{5,6},{7,8},{9,10},{11,12},{13,14},{15,16},{17,18},{19... | collective-permute-start | bytes 196616 | tf_op jit(solution)/shard_map/ppermute | solution.py:54
  255.8 0.7 copy-start.10
  255.9 0.7 copy-start.8
  255.9 0.7 copy-start.13
Sparse Core Ops, SparseCore 0:
  125.2 31.8 all-reduce.18
  220.6 34.2 all-reduce.20

commit v18 on v17

--- a/solution.py
+++ b/solution.py
@@ -51,9 +51,8 @@
     count = lax.axis_size("space")
     outer = [(i, i + 1) for i in range(1, count - 1, 2)]
     outer = outer + [(j, i) for i, j in outer]
+    inside = lax.ppermute(vectors, "space", [(i, i ^ 1) for i in range(count)])
     across = lax.ppermute(vectors, "space", outer)
-    both = lax.psum(vectors, "space", axis_index_groups=[[i, i + 1] for i in range(0, count, 2)])
-    inside = both - vectors
     first = lax.axis_index("space") % 2 == 0
     return jnp.where(first, across, inside), jnp.where(first, inside, across)
 
@@ -128,9 +127,11 @@
     second = copies(other, "band", BAND_Z).reshape(-1, cells)
     near = jnp.concatenate([run, across], axis=0)
     margins, across = pair_margins(products(pair, near), lower, weight, swapped(second, 1))
-    margins, far = tie((margins, swapped(near, 3)))
-    first = (near, far)
-    for margin, part in zip(margins, first):
+    margins, far = tie((margins, (swapped(run, 3), swapped(run, 2))))
+    first = (near,) + far
+    width = run.shape[0]
+    columns = (margins[0], margins[1][:, :width], margins[1][:, width:])
+    for margin, part in zip(columns, first):
         pair = pair - combination(margin, part)
     near = jnp.concatenate([second, across], axis=0)
     margins, _ = pair_margins(products(pair, near), lower, weight, own_only=True)

time: 268 us -> 194 us (0.72)
  waiting for transfers between devices: 90.6 us -> 29.8 us
  between operations: 14.6 us -> 1.13 us
  starting transfers between devices: 56.5 us -> 67.2 us
  blocking collectives: 76.2 us -> 72.2 us
  local copies, waits for them, and re-layouts: 10.6 us -> 7.35 us
  other arithmetic: 6.03 us -> 2.9 us
    psum x2 -> x0, waiting for transfers between devices: 65.5 us -> none  [neighbours(): lax.psum(vectors, 'space', axis_index_groups=[[i, i + 1] for i in range(0...]
    psum x2, blocking collectives: 28.9 us -> 24.9 us  [space_sum(): return lax.psum(near, 'space', axis_index_groups=SPACE_Z)]
    ppermute x0 -> x2, starting transfers between devices: none -> 3.84 us  [neighbours(): inside = lax.ppermute(vectors, 'space', [(i, i ^ 1) for i in range(count)])]
    ppermute x2, waiting for transfers between devices: 0.01 us -> 3.58 us  [neighbours(): across = lax.ppermute(vectors, 'space', outer)]
    ppermute x2, starting transfers between devices: 11.8 us -> 14.6 us  [neighbours(): across = lax.ppermute(vectors, 'space', outer)]
    ppermute x5 -> x6, starting transfers between devices: 19.1 us -> 21.8 us  [swapped(): lax.ppermute(x, 'band', [(i, i ^ bits) for i in range(lax.axis_size('band...]
    dot_general x8 -> x10, matrix products: 6.58 us -> 7.37 us  [combination(): jnp.einsum('vj,jc->vc', margin, states, precision=lax.Precision.HIGH, pre...]
  transfers between devices with their start and end apart: 13 -> 14, of which waited for: 7 -> 8; matrix products, arithmetic and copies ran while one was open for 4% -> 5% of each run, Pallas kernels for 0% -> 0%
where the time goes in v18:
time: 194 us; the launch traced here: 193 us
  blocking collectives  72.2 us (37%)
  starting transfers between devices  67.2 us (35%)
  waiting for transfers between devices  29.8 us (15%)
  matrix products  12.7 us (7%)
  local copies, waits for them, and re-layouts  7.35 us (4%)
  other arithmetic  2.9 us (1%)
    psum x2, blocking collectives, pair_margins(): total = lax.psum(product, 'space', axis_index_groups=SPACE_Z)  30.2 us
    psum x2, blocking collectives, space_sum(): return lax.psum(near, 'space', axis_index_groups=SPACE_Z)  24.9 us
    ppermute x6, starting transfers between devices, swapped(): lax.ppermute(x, 'band', [(i, i ^ bits) for i in range(lax.axis_size('band...  21.8 us
    all_to_all x3, starting transfers between devices, copies(): return lax.all_to_all(sent, axis, 0, 0, axis_index_groups=groups)  19.7 us
    all_to_all x3, waiting for transfers between devices, copies(): return lax.all_to_all(sent, axis, 0, 0, axis_index_groups=groups)  18.4 us
    all_to_all x2, blocking collectives, copies(): return lax.all_to_all(sent, axis, 0, 0, axis_index_groups=groups)  17.1 us
    ppermute x2, starting transfers between devices, neighbours(): across = lax.ppermute(vectors, 'space', outer)  14.6 us
    dot_general x10, matrix products, combination(): jnp.einsum('vj,jc->vc', margin, states, precision=lax.Precision.HIGH, pre...  7.37 us
  transfers between devices with their start and end apart: 14, of which 8 were waited for; matrix products, arithmetic and copies ran while one was open for 5% of the time, Pallas kernels for 0%

profile of v18, /device:TPU:7, one launch (start us, length us, event | category | flops | bytes accessed | tf_op | source)
XLA Modules:
  0.0 193.2 jit_solution(5385112883674540877)
XLA Ops:
  0.6 1.0 fusion.43
  1.7 0.8 broadcast_in_dim.77
  2.5 5.7 %all-to-all-start = ((f32[4,16,2048]{2,1,0:T(8,128)}), f32[4,16,2048]{2,1,0:T(8,128)}, u32[]{:S(2)}, u32[]{:S(2)}) async-start(f32[4,16,2048]{2,1,0:T(8,128)} %broadcast_in_dim.77), calls=%async_computation | async-start | bytes 1048576 | tf_op jit(solution)/shard_map/all_to_all | solution.py:22
  8.3 4.6 %collective-permute-start = (f32[8,2048]{1,0:T(8,128)S(1)}, f32[8,2048]{1,0:T(8,128)S(1)}, u32[]{:S(2)}, u32[]{:S(2)}) collective-permute-start(f32[8,2048]{1,0:T(8,128)S(1)} %bitcast.61), channel_id=1, source_target_pairs={{0,96},{32,64},{64,32},{96,0},{128,224},{160,192},{192,160},{224,1... | collective-permute-start | bytes 196616 | tf_op jit(solution)/shard_map/ppermute | solution.py:83
  13.0 2.0 %collective-permute-done = f32[8,2048]{1,0:T(8,128)S(1)} collective-permute-done((f32[8,2048]{1,0:T(8,128)S(1)}, f32[8,2048]{1,0:T(8,128)S(1)}, u32[]{:S(2)}, u32[]{:S(2)}) %collective-permute-start) | collective-permute-done | bytes 65568 | tf_op jit(solution)/shard_map/ppermute | solution.py:83
  15.0 7.3 %all-to-all-done = f32[4,16,2048]{2,1,0:T(8,128)} async-done(((f32[4,16,2048]{2,1,0:T(8,128)}), f32[4,16,2048]{2,1,0:T(8,128)}, u32[]{:S(2)}, u32[]{:S(2)}) %all-to-all-start) | async-done | bytes 524320 | tf_op jit(solution)/shard_map/all_to_all | solution.py:22
  22.3 0.8 broadcast_in_dim.78
  23.2 3.5 %all-to-all-start.1 = ((f32[4,16,2048]{2,1,0:T(8,128)}), f32[4,16,2048]{2,1,0:T(8,128)S(1)}, u32[]{:S(2)}, u32[]{:S(2)}) async-start(f32[4,16,2048]{2,1,0:T(8,128)} %broadcast_in_dim.78), calls=%async_computation.1 | async-start | bytes 1048576 | tf_op jit(solution)/shard_map/all_to_all | solution.py:22
  26.7 3.2 %collective-permute-start.1 = (f32[64,2048]{1,0:T(8,128)}, f32[64,2048]{1,0:T(8,128)S(1)}, u32[]{:S(2)}, u32[]{:S(2)}) collective-permute-start(f32[64,2048]{1,0:T(8,128)} %bitcast), channel_id=1, source_target_pairs={{0,32},{32,0},{64,96},{96,64},{128,160},{160,128},{192,224},{224,1... | collective-permute-start | bytes 1572872 | tf_op jit(solution)/shard_map/ppermute | solution.py:83
  29.9 10.7 %all-to-all-done.1 = f32[4,16,2048]{2,1,0:T(8,128)S(1)} async-done(((f32[4,16,2048]{2,1,0:T(8,128)}), f32[4,16,2048]{2,1,0:T(8,128)S(1)}, u32[]{:S(2)}, u32[]{:S(2)}) %all-to-all-start.1) | async-done | bytes 524320 | tf_op jit(solution)/shard_map/all_to_all | solution.py:22
  40.6 3.2 %collective-permute-start.2 = (f32[64,2048]{1,0:T(8,128)S(1)}, f32[64,2048]{1,0:T(8,128)S(1)}, u32[]{:S(2)}, u32[]{:S(2)}) collective-permute-start(f32[64,2048]{1,0:T(8,128)S(1)} %bitcast.44), channel_id=1, source_target_pairs={{0,32},{32,0},{64,96},{96,64},{128,160},{160,128},{192,224},{224,1... | collective-permute-start | bytes 1572872 | tf_op jit(solution)/shard_map/ppermute | solution.py:83
  43.8 1.1 constant_dynamic-update-slice_fusion.1
  44.9 3.8 %collective-permute-start.3 = (f32[64,2048]{1,0:T(8,128)}, f32[64,2048]{1,0:T(8,128)}, u32[]{:S(2)}, u32[]{:S(2)}) collective-permute-start(f32[64,2048]{1,0:T(8,128)} %bitcast), channel_id=1, source_target_pairs={{0,96},{32,64},{64,32},{96,0},{128,224},{160,192},{192,160},{224,1... | collective-permute-start | bytes 1572872 | tf_op jit(solution)/shard_map/ppermute | solution.py:83
  48.7 2.6 %collective-permute-start.4 = (f32[64,2048]{1,0:T(8,128)}, f32[64,2048]{1,0:T(8,128)}, u32[]{:S(2)}, u32[]{:S(2)}) collective-permute-start(f32[64,2048]{1,0:T(8,128)} %bitcast), channel_id=1, source_target_pairs={{0,64},{32,96},{64,0},{96,32},{128,192},{160,224},{192,128},{224,1... | collective-permute-start | bytes 1572872 | tf_op jit(solution)/shard_map/ppermute | solution.py:83
  51.4 0.5 fusion.52
  51.9 17.9 %psum.28 = f32[16,128]{1,0:T(8,128)S(1)} all-reduce(f32[16,128]{1,0:T(8,128)S(1)} %fusion.52), channel_id=1, replica_groups={{0,8,16,24},{1,9,17,25},{2,10,18,26},{3,11,19,27},{4,12,20,28},{5,13,21..., use_global_device_ids=true, to_apply=%region_0.1 | all-reduce | flops 2048 | bytes 16384 | tf_op jit(solution)/shard_map/psum | solution.py:87
  69.8 0.7 broadcast_in_dim.79
  70.5 10.5 %all-to-all-start.2 = ((f32[16,16,128]{2,1,0:T(8,128)}), f32[16,16,128]{2,1,0:T(8,128)S(1)}, u32[]{:S(2)}, u32[]{:S(2)}) async-start(f32[16,16,128]{2,1,0:T(8,128)} %broadcast_in_dim.79), calls=%async_computation.2 | async-start | bytes 262144 | tf_op jit(solution)/shard_map/all_to_all | solution.py:22
  81.0 1.0 pad_maximum_fusion
  82.0 4.3 %collective-permute-start.5 = (f32[128,2048]{1,0:T(8,128)}, f32[128,2048]{1,0:T(8,128)S(1)}, u32[]{:S(2)}, u32[]{:S(2)}) collective-permute-start(f32[128,2048]{1,0:T(8,128)} %pad_maximum_fusion), channel_id=1, source_target_pairs={{0,96},{32,64},{64,32},{96,0},{128,224},{160,192},{192,160},{224,1... | collective-permute-start | bytes 3145736 | tf_op jit(solution)/shard_map/ppermute | solution.py:83
  86.3 0.4 all-to-all-done.2
  86.8 1.3 fusion.23
  88.1 1.3 fusion.21
  89.5 0.4 fusion.1
  89.8 0.5 fusion.41
  90.3 12.3 %psum.29 = f32[16,128]{1,0:T(8,128)S(1)} all-reduce(f32[16,128]{1,0:T(8,128)S(1)} %fusion.41), channel_id=1, replica_groups={{0,8,16,24},{1,9,17,25},{2,10,18,26},{3,11,19,27},{4,12,20,28},{5,13,21..., use_global_device_ids=true, to_apply=%region_3.4 | all-reduce | flops 2048 | bytes 16384 | tf_op jit(solution)/shard_map/psum | solution.py:87
  102.7 0.6 broadcast_in_dim.81
  103.3 7.2 %all-to-all-start.3 = ((f32[16,8,128]{2,1,0:T(8,128)}), f32[16,8,128]{2,1,0:T(8,128)S(1)}, u32[]{:S(2)}, u32[]{:S(2)}) async-start(f32[16,8,128]{2,1,0:T(8,128)} %bitcast.3), calls=%async_computation.3 | async-start | bytes 131072 | tf_op jit(solution)/shard_map/all_to_all | solution.py:92
  110.5 5.4 %all-to-all-done.3 = f32[16,8,128]{2,1,0:T(8,128)S(1)} async-done(((f32[16,8,128]{2,1,0:T(8,128)}), f32[16,8,128]{2,1,0:T(8,128)S(1)}, u32[]{:S(2)}, u32[]{:S(2)}) %all-to-all-start.3) | async-done | bytes 65568 | tf_op jit(solution)/shard_map/all_to_all | solution.py:92
  116.0 0.4 fusion.40
  116.3 0.4 fusion.19
  116.7 5.8 %collective-permute-start.6 = (f32[8,2048]{1,0:T(8,128)S(1)}, f32[8,2048]{1,0:T(8,128)S(1)}, u32[]{:S(2)}, u32[]{:S(2)}) collective-permute-start(f32[8,2048]{1,0:T(8,128)S(1)} %fusion.19), channel_id=1, source_target_pairs={{1,2},{3,4},{5,6},{7,8},{9,10},{11,12},{13,14},{15,16},{17,18},{19... | collective-permute-start | bytes 196616 | tf_op jit(solution)/shard_map/ppermute | solution.py:55
  122.4 1.9 collective-permute-start.7
  124.4 0.1 fusion.48
  124.6 0.1 fusion.49
  124.7 0.1 fusion.50
  124.8 0.1 fusion.51
  125.0 3.3 %collective-permute-done.6 = f32[8,2048]{1,0:T(8,128)S(1)} collective-permute-done((f32[8,2048]{1,0:T(8,128)S(1)}, f32[8,2048]{1,0:T(8,128)S(1)}, u32[]{:S(2)}, u32[]{:S(2)}) %collective-permute-start.6) | collective-permute-done | bytes 65568 | tf_op jit(solution)/shard_map/ppermute | solution.py:55
  128.5 0.8 copy-done
  129.2 0.5 fusion.20
  129.7 0.5 fusion.53
  130.2 1.4 fusion.54
  131.6 1.4 fusion.55
  133.0 0.1 pad_maximum_fusion.6
  133.1 7.2 %all_to_all.30 = f32[8,8,256]{2,1,0:T(8,128)S(1)} all-to-all(f32[8,8,256]{2,1,0:T(8,128)S(1)} %broadcast_in_dim.87), channel_id=1, replica_groups={{0,1,2,3,4,5,6,7},{8,9,10,11,12,13,14,15},{16,17,18,19,20,21,22,23},{24..., dimensions={0} | all-to-all | bytes 131072 | tf_op jit(solution)/shard_map/all_to_all | solution.py:22
  140.3 13.4 %psum.30 = f32[8,256]{1,0:T(8,128)S(1)} all-reduce(f32[8,256]{1,0:T(8,128)S(1)} %reduce_sum.58), channel_id=1, replica_groups={{0,8,16,24},{1,9,17,25},{2,10,18,26},{3,11,19,27},{4,12,20,28},{5,13,21..., use_global_device_ids=true, to_apply=%region_7.8 | all-reduce | flops 2048 | bytes 16384 | tf_op jit(solution)/shard_map/psum | solution.py:27
  153.7 1.3 fusion.29
  155.0 1.3 fusion.27
  156.3 0.4 fusion.3
  156.7 0.5 fusion.39
  157.2 0.5 fusion.56
  157.8 9.9 %all_to_all.31 = f32[8,8,256]{2,1,0:T(8,128)S(1)} all-to-all(f32[8,8,256]{2,1,0:T(8,128)S(1)} %broadcast_in_dim.88), channel_id=1, replica_groups={{0,1,2,3,4,5,6,7},{8,9,10,11,12,13,14,15},{16,17,18,19,20,21,22,23},{24..., dimensions={0} | all-to-all | bytes 131072 | tf_op jit(solution)/shard_map/all_to_all | solution.py:22
  167.7 11.4 %psum.31 = f32[8,256]{1,0:T(8,128)S(1)} all-reduce(f32[8,256]{1,0:T(8,128)S(1)} %reduce_sum.59), channel_id=1, replica_groups={{0,8,16,24},{1,9,17,25},{2,10,18,26},{3,11,19,27},{4,12,20,28},{5,13,21..., use_global_device_ids=true, to_apply=%region_9.10 | all-reduce | flops 2048 | bytes 16384 | tf_op jit(solution)/shard_map/psum | solution.py:27
  179.2 0.4 convolution_subtract_fusion.2
  179.5 0.4 convolution_subtract_fusion.1
  179.9 8.9 %collective-permute-start.8 = (f32[8,2048]{1,0:T(8,128)S(1)}, f32[8,2048]{1,0:T(8,128)S(1)}, u32[]{:S(2)}, u32[]{:S(2)}) collective-permute-start(f32[8,2048]{1,0:T(8,128)S(1)} %convolution_subtract_fusion.1), channel_id=1, source_target_pairs={{1,2},{3,4},{5,6},{7,8},{9,10},{11,12},{13,14},{15,16},{17,18},{19... | collective-permute-start | bytes 196616 | tf_op jit(solution)/shard_map/ppermute | solution.py:55
  188.7 1.9 collective-permute-start.9
  190.7 0.1 fusion.44
  190.9 0.1 fusion.45
  191.0 0.1 fusion.46
  191.1 0.1 fusion.47
  191.3 0.3 collective-permute-done.8
  191.5 0.3 collective-permute-done.9
  192.0 1.1 fusion.5
  (44 shorter events, 0.7 us)
Async XLA Ops:
  2.5 5.8 %copy-start.1 = (f32[8,2,1024]{2,1,0:T(2,128)S(1)}, f32[8,2,1024]{2,1,0:T(2,128)}, u32[]{:S(2)}) copy-start(f32[8,2,1024]{2,1,0:T(2,128)} %param.6) | copy-start | bytes 196612
  2.5 19.8 %all-to-all-start = ((f32[4,16,2048]{2,1,0:T(8,128)}), f32[4,16,2048]{2,1,0:T(8,128)}, u32[]{:S(2)}, u32[]{:S(2)}) async-start(f32[4,16,2048]{2,1,0:T(8,128)} %broadcast_in_dim.77), calls=%async_computation | async-start | bytes 1048576 | tf_op jit(solution)/shard_map/all_to_all | solution.py:22
  8.3 6.7 %collective-permute-start = (f32[8,2048]{1,0:T(8,128)S(1)}, f32[8,2048]{1,0:T(8,128)S(1)}, u32[]{:S(2)}, u32[]{:S(2)}) collective-permute-start(f32[8,2048]{1,0:T(8,128)S(1)} %bitcast.61), channel_id=1, source_target_pairs={{0,96},{32,64},{64,32},{96,0},{128,224},{160,192},{192,160},{224,1... | collective-permute-start | bytes 196616 | tf_op jit(solution)/shard_map/ppermute | solution.py:83
  23.2 17.4 %all-to-all-start.1 = ((f32[4,16,2048]{2,1,0:T(8,128)}), f32[4,16,2048]{2,1,0:T(8,128)S(1)}, u32[]{:S(2)}, u32[]{:S(2)}) async-start(f32[4,16,2048]{2,1,0:T(8,128)} %broadcast_in_dim.78), calls=%async_computation.1 | async-start | bytes 1048576 | tf_op jit(solution)/shard_map/all_to_all | solution.py:22
  26.7 3.2 %copy-start.2 = (f32[2,1024]{1,0:T(2,128)S(1)}, f32[2,1024]{1,0:T(2,128)}, u32[]{:S(2)}) copy-start(f32[2,1024]{1,0:T(2,128)} %param.8) | copy-start | bytes 24580
  26.7 24.7 %collective-permute-start.1 = (f32[64,2048]{1,0:T(8,128)}, f32[64,2048]{1,0:T(8,128)S(1)}, u32[]{:S(2)}, u32[]{:S(2)}) collective-permute-start(f32[64,2048]{1,0:T(8,128)} %bitcast), channel_id=1, source_target_pairs={{0,32},{32,0},{64,96},{96,64},{128,160},{160,128},{192,224},{224,1... | collective-permute-start | bytes 1572872 | tf_op jit(solution)/shard_map/ppermute | solution.py:83
  40.6 29.2 %collective-permute-start.2 = (f32[64,2048]{1,0:T(8,128)S(1)}, f32[64,2048]{1,0:T(8,128)S(1)}, u32[]{:S(2)}, u32[]{:S(2)}) collective-permute-start(f32[64,2048]{1,0:T(8,128)S(1)} %bitcast.44), channel_id=1, source_target_pairs={{0,32},{32,0},{64,96},{96,64},{128,160},{160,128},{192,224},{224,1... | collective-permute-start | bytes 1572872 | tf_op jit(solution)/shard_map/ppermute | solution.py:83
  44.9 41.9 %collective-permute-start.3 = (f32[64,2048]{1,0:T(8,128)}, f32[64,2048]{1,0:T(8,128)}, u32[]{:S(2)}, u32[]{:S(2)}) collective-permute-start(f32[64,2048]{1,0:T(8,128)} %bitcast), channel_id=1, source_target_pairs={{0,96},{32,64},{64,32},{96,0},{128,224},{160,192},{192,160},{224,1... | collective-permute-start | bytes 1572872 | tf_op jit(solution)/shard_map/ppermute | solution.py:83
  48.7 38.1 %collective-permute-start.4 = (f32[64,2048]{1,0:T(8,128)}, f32[64,2048]{1,0:T(8,128)}, u32[]{:S(2)}, u32[]{:S(2)}) collective-permute-start(f32[64,2048]{1,0:T(8,128)} %bitcast), channel_id=1, source_target_pairs={{0,64},{32,96},{64,0},{96,32},{128,192},{160,224},{192,128},{224,1... | collective-permute-start | bytes 1572872 | tf_op jit(solution)/shard_map/ppermute | solution.py:83
  70.5 16.3 %all-to-all-start.2 = ((f32[16,16,128]{2,1,0:T(8,128)}), f32[16,16,128]{2,1,0:T(8,128)S(1)}, u32[]{:S(2)}, u32[]{:S(2)}) async-start(f32[16,16,128]{2,1,0:T(8,128)} %broadcast_in_dim.79), calls=%async_computation.2 | async-start | bytes 262144 | tf_op jit(solution)/shard_map/all_to_all | solution.py:22
  82.0 33.9 %collective-permute-start.5 = (f32[128,2048]{1,0:T(8,128)}, f32[128,2048]{1,0:T(8,128)S(1)}, u32[]{:S(2)}, u32[]{:S(2)}) collective-permute-start(f32[128,2048]{1,0:T(8,128)} %pad_maximum_fusion), channel_id=1, source_target_pairs={{0,96},{32,64},{64,32},{96,0},{128,224},{160,192},{192,160},{224,1... | collective-permute-start | bytes 3145736 | tf_op jit(solution)/shard_map/ppermute | solution.py:83
  103.3 12.6 %all-to-all-start.3 = ((f32[16,8,128]{2,1,0:T(8,128)}), f32[16,8,128]{2,1,0:T(8,128)S(1)}, u32[]{:S(2)}, u32[]{:S(2)}) async-start(f32[16,8,128]{2,1,0:T(8,128)} %bitcast.3), calls=%async_computation.3 | async-start | bytes 131072 | tf_op jit(solution)/shard_map/all_to_all | solution.py:92
  116.7 11.6 %collective-permute-start.6 = (f32[8,2048]{1,0:T(8,128)S(1)}, f32[8,2048]{1,0:T(8,128)S(1)}, u32[]{:S(2)}, u32[]{:S(2)}) collective-permute-start(f32[8,2048]{1,0:T(8,128)S(1)} %fusion.19), channel_id=1, source_target_pairs={{1,2},{3,4},{5,6},{7,8},{9,10},{11,12},{13,14},{15,16},{17,18},{19... | collective-permute-start | bytes 196616 | tf_op jit(solution)/shard_map/ppermute | solution.py:55
  122.4 5.9 %collective-permute-start.7 = (f32[8,2048]{1,0:T(8,128)S(1)}, f32[8,2048]{1,0:T(8,128)S(1)}, u32[]{:S(2)}, u32[]{:S(2)}) collective-permute-start(f32[8,2048]{1,0:T(8,128)S(1)} %fusion.19), channel_id=1, source_target_pairs={{0,1},{1,0},{2,3},{3,2},{4,5},{5,4},{6,7},{7,6},{8,9},{9,8},{10,11... | collective-permute-start | bytes 196616 | tf_op jit(solution)/shard_map/ppermute | solution.py:54
  128.4 0.8 copy-start
  128.5 0.8 copy-start.3
  179.9 11.7 %collective-permute-start.8 = (f32[8,2048]{1,0:T(8,128)S(1)}, f32[8,2048]{1,0:T(8,128)S(1)}, u32[]{:S(2)}, u32[]{:S(2)}) collective-permute-start(f32[8,2048]{1,0:T(8,128)S(1)} %convolution_subtract_fusion.1), channel_id=1, source_target_pairs={{1,2},{3,4},{5,6},{7,8},{9,10},{11,12},{13,14},{15,16},{17,18},{19... | collective-permute-start | bytes 196616 | tf_op jit(solution)/shard_map/ppermute | solution.py:55
  188.7 3.1 %collective-permute-start.9 = (f32[8,2048]{1,0:T(8,128)S(1)}, f32[8,2048]{1,0:T(8,128)S(1)}, u32[]{:S(2)}, u32[]{:S(2)}) collective-permute-start(f32[8,2048]{1,0:T(8,128)S(1)} %convolution_subtract_fusion.1), channel_id=1, source_target_pairs={{0,1},{1,0},{2,3},{3,2},{4,5},{5,4},{6,7},{7,6},{8,9},{9,8},{10,11... | collective-permute-start | bytes 196616 | tf_op jit(solution)/shard_map/ppermute | solution.py:54

commit v19 on v17

--- a/solution.py
+++ b/solution.py
@@ -52,8 +52,8 @@
     outer = [(i, i + 1) for i in range(1, count - 1, 2)]
     outer = outer + [(j, i) for i, j in outer]
     across = lax.ppermute(vectors, "space", outer)
-    both = lax.psum(vectors, "space", axis_index_groups=[[i, i + 1] for i in range(0, count, 2)])
-    inside = both - vectors
+    across, vectors = lax.optimization_barrier((across, vectors))
+    inside = lax.ppermute(vectors, "space", [(i, i ^ 1) for i in range(count)])
     first = lax.axis_index("space") % 2 == 0
     return jnp.where(first, across, inside), jnp.where(first, inside, across)
 

time: 268 us -> 191 us (0.71)
  waiting for transfers between devices: 90.6 us -> 37.7 us
  between operations: 14.6 us -> 1.11 us
  blocking collectives: 76.2 us -> 70.9 us
  starting transfers between devices: 56.5 us -> 61.6 us
  local copies, waits for them, and re-layouts: 10.6 us -> 6.32 us
  other arithmetic: 6.03 us -> 2.87 us
    psum x2 -> x0, waiting for transfers between devices: 65.5 us -> none  [neighbours(): lax.psum(vectors, 'space', axis_index_groups=[[i, i + 1] for i in range(0...]
    ppermute x2, waiting for transfers between devices: 0.01 us -> 9.86 us  [neighbours(): across = lax.ppermute(vectors, 'space', outer)]
    psum x2, blocking collectives: 28.9 us -> 24 us  [space_sum(): return lax.psum(near, 'space', axis_index_groups=SPACE_Z)]
    ppermute x0 -> x2, starting transfers between devices: none -> 3.82 us  [neighbours(): inside = lax.ppermute(vectors, 'space', [(i, i ^ 1) for i in range(count)])]
  transfers between devices with their start and end apart: 13 -> 13, of which waited for: 7 -> 9; matrix products, arithmetic and copies ran while one was open for 4% -> 4% of each run, Pallas kernels for 0% -> 0%
where the time goes in v19:
time: 191 us; the launch traced here: 190 us
  blocking collectives  70.9 us (37%)
  starting transfers between devices  61.6 us (32%)
  waiting for transfers between devices  37.7 us (20%)
  matrix products  9.63 us (5%)
  local copies, waits for them, and re-layouts  6.32 us (3%)
  other arithmetic  2.87 us (2%)
    psum x2, blocking collectives, pair_margins(): total = lax.psum(product, 'space', axis_index_groups=SPACE_Z)  29.7 us
    psum x2, blocking collectives, space_sum(): return lax.psum(near, 'space', axis_index_groups=SPACE_Z)  24 us
    ppermute x5, starting transfers between devices, swapped(): lax.ppermute(x, 'band', [(i, i ^ bits) for i in range(lax.axis_size('band...  19.1 us
    all_to_all x3, waiting for transfers between devices, copies(): return lax.all_to_all(sent, axis, 0, 0, axis_index_groups=groups)  18.4 us
    all_to_all x3, starting transfers between devices, copies(): return lax.all_to_all(sent, axis, 0, 0, axis_index_groups=groups)  18.2 us
    all_to_all x2, blocking collectives, copies(): return lax.all_to_all(sent, axis, 0, 0, axis_index_groups=groups)  17.3 us
    ppermute x2, starting transfers between devices, neighbours(): across = lax.ppermute(vectors, 'space', outer)  13.1 us
    ppermute x2, waiting for transfers between devices, neighbours(): across = lax.ppermute(vectors, 'space', outer)  9.86 us
  transfers between devices with their start and end apart: 13, of which 9 were waited for; matrix products, arithmetic and copies ran while one was open for 4% of the time, Pallas kernels for 0%

profile of v19, /device:TPU:7, one launch (start us, length us, event | category | flops | bytes accessed | tf_op | source)
XLA Modules:
  0.0 190.2 jit_solution(13699390949529220536)
XLA Ops:
  0.6 1.0 fusion.35
  1.7 0.8 broadcast_in_dim.77
  2.5 5.7 %all-to-all-start = ((f32[4,16,2048]{2,1,0:T(8,128)}), f32[4,16,2048]{2,1,0:T(8,128)S(1)}, u32[]{:S(2)}, u32[]{:S(2)}) async-start(f32[4,16,2048]{2,1,0:T(8,128)} %broadcast_in_dim.77), calls=%async_computation | async-start | bytes 1048576 | tf_op jit(solution)/shard_map/all_to_all | solution.py:22
  8.3 4.6 %collective-permute-start = (f32[8,2048]{1,0:T(8,128)S(1)}, f32[8,2048]{1,0:T(8,128)S(1)}, u32[]{:S(2)}, u32[]{:S(2)}) collective-permute-start(f32[8,2048]{1,0:T(8,128)S(1)} %bitcast.59), channel_id=1, source_target_pairs={{0,96},{32,64},{64,32},{96,0},{128,224},{160,192},{192,160},{224,1... | collective-permute-start | bytes 196616 | tf_op jit(solution)/shard_map/ppermute | solution.py:84
  13.0 1.9 collective-permute-done
  14.9 7.3 %all-to-all-done = f32[4,16,2048]{2,1,0:T(8,128)S(1)} async-done(((f32[4,16,2048]{2,1,0:T(8,128)}), f32[4,16,2048]{2,1,0:T(8,128)S(1)}, u32[]{:S(2)}, u32[]{:S(2)}) %all-to-all-start) | async-done | bytes 524320 | tf_op jit(solution)/shard_map/all_to_all | solution.py:22
  22.2 0.8 broadcast_in_dim.78
  23.1 3.5 %all-to-all-start.1 = ((f32[4,16,2048]{2,1,0:T(8,128)}), f32[4,16,2048]{2,1,0:T(8,128)S(1)}, u32[]{:S(2)}, u32[]{:S(2)}) async-start(f32[4,16,2048]{2,1,0:T(8,128)} %broadcast_in_dim.78), calls=%async_computation.1 | async-start | bytes 1048576 | tf_op jit(solution)/shard_map/all_to_all | solution.py:22
  26.6 3.2 %collective-permute-start.1 = (f32[64,2048]{1,0:T(8,128)S(1)}, f32[64,2048]{1,0:T(8,128)S(1)}, u32[]{:S(2)}, u32[]{:S(2)}) collective-permute-start(f32[64,2048]{1,0:T(8,128)S(1)} %bitcast.47), channel_id=1, source_target_pairs={{0,32},{32,0},{64,96},{96,64},{128,160},{160,128},{192,224},{224,1... | collective-permute-start | bytes 1572872 | tf_op jit(solution)/shard_map/ppermute | solution.py:84
  29.8 10.7 %all-to-all-done.1 = f32[4,16,2048]{2,1,0:T(8,128)S(1)} async-done(((f32[4,16,2048]{2,1,0:T(8,128)}), f32[4,16,2048]{2,1,0:T(8,128)S(1)}, u32[]{:S(2)}, u32[]{:S(2)}) %all-to-all-start.1) | async-done | bytes 524320 | tf_op jit(solution)/shard_map/all_to_all | solution.py:22
  40.5 3.2 %collective-permute-start.2 = (f32[64,2048]{1,0:T(8,128)S(1)}, f32[64,2048]{1,0:T(8,128)S(1)}, u32[]{:S(2)}, u32[]{:S(2)}) collective-permute-start(f32[64,2048]{1,0:T(8,128)S(1)} %bitcast.41), channel_id=1, source_target_pairs={{0,32},{32,0},{64,96},{96,64},{128,160},{160,128},{192,224},{224,1... | collective-permute-start | bytes 1572872 | tf_op jit(solution)/shard_map/ppermute | solution.py:84
  43.8 3.8 %collective-permute-start.3 = (f32[128,2048]{1,0:T(8,128)S(1)}, f32[128,2048]{1,0:T(8,128)}, u32[]{:S(2)}, u32[]{:S(2)}) collective-permute-start(f32[128,2048]{1,0:T(8,128)S(1)} %constant_dynamic-update-slice_fusion), channel_id=1, source_target_pairs={{0,96},{32,64},{64,32},{96,0},{128,224},{160,192},{192,160},{224,1... | collective-permute-start | bytes 3145736 | tf_op jit(solution)/shard_map/ppermute | solution.py:84
  47.6 0.5 fusion.44
  48.1 17.2 %psum.28 = f32[16,128]{1,0:T(8,128)S(1)} all-reduce(f32[16,128]{1,0:T(8,128)S(1)} %fusion.44), channel_id=1, replica_groups={{0,8,16,24},{1,9,17,25},{2,10,18,26},{3,11,19,27},{4,12,20,28},{5,13,21..., use_global_device_ids=true, to_apply=%region_0.1 | all-reduce | flops 2048 | bytes 16384 | tf_op jit(solution)/shard_map/psum | solution.py:88
  65.4 0.7 broadcast_in_dim.79
  66.0 9.0 %all-to-all-start.2 = ((f32[16,16,128]{2,1,0:T(8,128)}), f32[16,16,128]{2,1,0:T(8,128)S(1)}, u32[]{:S(2)}, u32[]{:S(2)}) async-start(f32[16,16,128]{2,1,0:T(8,128)} %broadcast_in_dim.79), calls=%async_computation.2 | async-start | bytes 262144 | tf_op jit(solution)/shard_map/all_to_all | solution.py:22
  75.0 1.1 pad_maximum_fusion
  76.1 4.3 %collective-permute-start.4 = (f32[128,2048]{1,0:T(8,128)}, f32[128,2048]{1,0:T(8,128)S(1)}, u32[]{:S(2)}, u32[]{:S(2)}) collective-permute-start(f32[128,2048]{1,0:T(8,128)} %pad_maximum_fusion), channel_id=1, source_target_pairs={{0,96},{32,64},{64,32},{96,0},{128,224},{160,192},{192,160},{224,1... | collective-permute-start | bytes 3145736 | tf_op jit(solution)/shard_map/ppermute | solution.py:84
  80.4 0.4 all-to-all-done.2
  80.8 1.6 fusion.45
  82.4 0.4 fusion
  82.8 0.5 fusion.33
  83.3 12.5 %psum.29 = f32[16,128]{1,0:T(8,128)S(1)} all-reduce(f32[16,128]{1,0:T(8,128)S(1)} %fusion.33), channel_id=1, replica_groups={{0,8,16,24},{1,9,17,25},{2,10,18,26},{3,11,19,27},{4,12,20,28},{5,13,21..., use_global_device_ids=true, to_apply=%region_3.4 | all-reduce | flops 2048 | bytes 16384 | tf_op jit(solution)/shard_map/psum | solution.py:88
  95.8 0.6 broadcast_in_dim.81
  96.4 7.3 %all-to-all-start.3 = ((f32[16,8,128]{2,1,0:T(8,128)}), f32[16,8,128]{2,1,0:T(8,128)S(1)}, u32[]{:S(2)}, u32[]{:S(2)}) async-start(f32[16,8,128]{2,1,0:T(8,128)} %bitcast.3), calls=%async_computation.3 | async-start | bytes 131072 | tf_op jit(solution)/shard_map/all_to_all | solution.py:93
  103.8 5.4 %all-to-all-done.3 = f32[16,8,128]{2,1,0:T(8,128)S(1)} async-done(((f32[16,8,128]{2,1,0:T(8,128)}), f32[16,8,128]{2,1,0:T(8,128)S(1)}, u32[]{:S(2)}, u32[]{:S(2)}) %all-to-all-start.3) | async-done | bytes 65568 | tf_op jit(solution)/shard_map/all_to_all | solution.py:93
  109.2 0.4 fusion.32
  109.6 0.4 fusion.17
  109.9 5.4 %collective-permute-start.5 = (f32[8,2048]{1,0:T(8,128)S(1)}, f32[8,2048]{1,0:T(8,128)S(1)}, u32[]{:S(2)}, u32[]{:S(2)}) collective-permute-start(f32[8,2048]{1,0:T(8,128)S(1)} %fusion.17), channel_id=1, source_target_pairs={{1,2},{3,4},{5,6},{7,8},{9,10},{11,12},{13,14},{15,16},{17,18},{19... | collective-permute-start | bytes 196616 | tf_op jit(solution)/shard_map/ppermute | solution.py:54
  115.3 0.1 copy.54
  115.4 0.1 fusion.43
  115.5 0.1 fusion.41
  115.6 0.1 fusion.42
  115.8 6.5 %collective-permute-done.5 = f32[8,2048]{1,0:T(8,128)S(1)} collective-permute-done((f32[8,2048]{1,0:T(8,128)S(1)}, f32[8,2048]{1,0:T(8,128)S(1)}, u32[]{:S(2)}, u32[]{:S(2)}) %collective-permute-start.5) | collective-permute-done | bytes 65568 | tf_op jit(solution)/shard_map/ppermute | solution.py:54
  122.3 1.9 %collective-permute-start.6 = (f32[8,2048]{1,0:T(8,128)S(1)}, f32[8,2048]{1,0:T(8,128)S(1)}, u32[]{:S(2)}, u32[]{:S(2)}) collective-permute-start(f32[8,2048]{1,0:T(8,128)S(1)} %fusion.17), channel_id=1, source_target_pairs={{0,1},{1,0},{2,3},{3,2},{4,5},{5,4},{6,7},{7,6},{8,9},{9,8},{10,11... | collective-permute-start | bytes 196616 | tf_op jit(solution)/shard_map/ppermute | solution.py:56
  124.2 0.1 fusion.40
  124.3 1.1 collective-permute-done.6
  125.4 0.1 copy.43
  125.5 0.1 copy.44
  125.6 0.8 copy-done
  126.4 0.5 fusion.18
  126.9 1.7 fusion.47
  128.6 0.5 fusion.46
  129.1 7.2 %all_to_all.30 = f32[8,8,256]{2,1,0:T(8,128)S(1)} all-to-all(f32[8,8,256]{2,1,0:T(8,128)S(1)} %broadcast_in_dim.87), channel_id=1, replica_groups={{0,1,2,3,4,5,6,7},{8,9,10,11,12,13,14,15},{16,17,18,19,20,21,22,23},{24..., dimensions={0} | all-to-all | bytes 131072 | tf_op jit(solution)/shard_map/all_to_all | solution.py:22
  136.4 11.5 %psum.30 = f32[8,256]{1,0:T(8,128)S(1)} all-reduce(f32[8,256]{1,0:T(8,128)S(1)} %reduce_sum.58), channel_id=1, replica_groups={{0,8,16,24},{1,9,17,25},{2,10,18,26},{3,11,19,27},{4,12,20,28},{5,13,21..., use_global_device_ids=true, to_apply=%region_7.8 | all-reduce | flops 2048 | bytes 16384 | tf_op jit(solution)/shard_map/psum | solution.py:27
  147.9 1.6 fusion.21
  149.5 0.4 fusion.1
  149.9 0.5 fusion.48
  150.4 0.5 fusion.31
  150.9 10.0 %all_to_all.31 = f32[8,8,256]{2,1,0:T(8,128)S(1)} all-to-all(f32[8,8,256]{2,1,0:T(8,128)S(1)} %broadcast_in_dim.88), channel_id=1, replica_groups={{0,1,2,3,4,5,6,7},{8,9,10,11,12,13,14,15},{16,17,18,19,20,21,22,23},{24..., dimensions={0} | all-to-all | bytes 131072 | tf_op jit(solution)/shard_map/all_to_all | solution.py:22
  160.9 12.5 %psum.31 = f32[8,256]{1,0:T(8,128)S(1)} all-reduce(f32[8,256]{1,0:T(8,128)S(1)} %reduce_sum.59), channel_id=1, replica_groups={{0,8,16,24},{1,9,17,25},{2,10,18,26},{3,11,19,27},{4,12,20,28},{5,13,21..., use_global_device_ids=true, to_apply=%region_9.10 | all-reduce | flops 2048 | bytes 16384 | tf_op jit(solution)/shard_map/psum | solution.py:27
  173.5 0.4 convolution_subtract_fusion.2
  173.8 0.4 convolution_subtract_fusion.1
  174.2 7.8 %collective-permute-start.7 = (f32[8,2048]{1,0:T(8,128)S(1)}, f32[8,2048]{1,0:T(8,128)S(1)}, u32[]{:S(2)}, u32[]{:S(2)}) collective-permute-start(f32[8,2048]{1,0:T(8,128)S(1)} %convolution_subtract_fusion.1), channel_id=1, source_target_pairs={{1,2},{3,4},{5,6},{7,8},{9,10},{11,12},{13,14},{15,16},{17,18},{19... | collective-permute-start | bytes 196616 | tf_op jit(solution)/shard_map/ppermute | solution.py:54
  182.0 0.1 copy.70
  182.0 0.1 fusion.39
  182.2 0.1 fusion.37
  182.3 0.1 fusion.38
  182.4 3.4 %collective-permute-done.7 = f32[8,2048]{1,0:T(8,128)S(1)} collective-permute-done((f32[8,2048]{1,0:T(8,128)S(1)}, f32[8,2048]{1,0:T(8,128)S(1)}, u32[]{:S(2)}, u32[]{:S(2)}) %collective-permute-start.7) | collective-permute-done | bytes 65568 | tf_op jit(solution)/shard_map/ppermute | solution.py:54
  185.8 1.9 %collective-permute-start.8 = (f32[8,2048]{1,0:T(8,128)S(1)}, f32[8,2048]{1,0:T(8,128)S(1)}, u32[]{:S(2)}, u32[]{:S(2)}) collective-permute-start(f32[8,2048]{1,0:T(8,128)S(1)} %convolution_subtract_fusion.1), channel_id=1, source_target_pairs={{0,1},{1,0},{2,3},{3,2},{4,5},{5,4},{6,7},{7,6},{8,9},{9,8},{10,11... | collective-permute-start | bytes 196616 | tf_op jit(solution)/shard_map/ppermute | solution.py:56
  187.7 0.1 fusion.36
  187.8 1.1 collective-permute-done.8
  188.9 0.1 copy.59
  189.1 1.1 fusion.3
  (39 shorter events, 0.5 us)
Async XLA Ops:
  2.5 5.8 %copy-start.1 = (f32[8,2,1024]{2,1,0:T(2,128)S(1)}, f32[8,2,1024]{2,1,0:T(2,128)}, u32[]{:S(2)}) copy-start(f32[8,2,1024]{2,1,0:T(2,128)} %param.6) | copy-start | bytes 196612
  2.5 19.7 %all-to-all-start = ((f32[4,16,2048]{2,1,0:T(8,128)}), f32[4,16,2048]{2,1,0:T(8,128)S(1)}, u32[]{:S(2)}, u32[]{:S(2)}) async-start(f32[4,16,2048]{2,1,0:T(8,128)} %broadcast_in_dim.77), calls=%async_computation | async-start | bytes 1048576 | tf_op jit(solution)/shard_map/all_to_all | solution.py:22
  8.3 6.6 %collective-permute-start = (f32[8,2048]{1,0:T(8,128)S(1)}, f32[8,2048]{1,0:T(8,128)S(1)}, u32[]{:S(2)}, u32[]{:S(2)}) collective-permute-start(f32[8,2048]{1,0:T(8,128)S(1)} %bitcast.59), channel_id=1, source_target_pairs={{0,96},{32,64},{64,32},{96,0},{128,224},{160,192},{192,160},{224,1... | collective-permute-start | bytes 196616 | tf_op jit(solution)/shard_map/ppermute | solution.py:84
  23.1 17.4 %all-to-all-start.1 = ((f32[4,16,2048]{2,1,0:T(8,128)}), f32[4,16,2048]{2,1,0:T(8,128)S(1)}, u32[]{:S(2)}, u32[]{:S(2)}) async-start(f32[4,16,2048]{2,1,0:T(8,128)} %broadcast_in_dim.78), calls=%async_computation.1 | async-start | bytes 1048576 | tf_op jit(solution)/shard_map/all_to_all | solution.py:22
  26.6 3.2 %copy-start.2 = (f32[2,1024]{1,0:T(2,128)S(1)}, f32[2,1024]{1,0:T(2,128)}, u32[]{:S(2)}) copy-start(f32[2,1024]{1,0:T(2,128)} %param.8) | copy-start | bytes 24580
  26.6 17.2 %collective-permute-start.1 = (f32[64,2048]{1,0:T(8,128)S(1)}, f32[64,2048]{1,0:T(8,128)S(1)}, u32[]{:S(2)}, u32[]{:S(2)}) collective-permute-start(f32[64,2048]{1,0:T(8,128)S(1)} %bitcast.47), channel_id=1, source_target_pairs={{0,32},{32,0},{64,96},{96,64},{128,160},{160,128},{192,224},{224,1... | collective-permute-start | bytes 1572872 | tf_op jit(solution)/shard_map/ppermute | solution.py:84
  40.5 24.8 %collective-permute-start.2 = (f32[64,2048]{1,0:T(8,128)S(1)}, f32[64,2048]{1,0:T(8,128)S(1)}, u32[]{:S(2)}, u32[]{:S(2)}) collective-permute-start(f32[64,2048]{1,0:T(8,128)S(1)} %bitcast.41), channel_id=1, source_target_pairs={{0,32},{32,0},{64,96},{96,64},{128,160},{160,128},{192,224},{224,1... | collective-permute-start | bytes 1572872 | tf_op jit(solution)/shard_map/ppermute | solution.py:84
  43.8 37.0 %collective-permute-start.3 = (f32[128,2048]{1,0:T(8,128)S(1)}, f32[128,2048]{1,0:T(8,128)}, u32[]{:S(2)}, u32[]{:S(2)}) collective-permute-start(f32[128,2048]{1,0:T(8,128)S(1)} %constant_dynamic-update-slice_fusion), channel_id=1, source_target_pairs={{0,96},{32,64},{64,32},{96,0},{128,224},{160,192},{192,160},{224,1... | collective-permute-start | bytes 3145736 | tf_op jit(solution)/shard_map/ppermute | solution.py:84
  66.0 14.7 %all-to-all-start.2 = ((f32[16,16,128]{2,1,0:T(8,128)}), f32[16,16,128]{2,1,0:T(8,128)S(1)}, u32[]{:S(2)}, u32[]{:S(2)}) async-start(f32[16,16,128]{2,1,0:T(8,128)} %broadcast_in_dim.79), calls=%async_computation.2 | async-start | bytes 262144 | tf_op jit(solution)/shard_map/all_to_all | solution.py:22
  76.1 33.1 %collective-permute-start.4 = (f32[128,2048]{1,0:T(8,128)}, f32[128,2048]{1,0:T(8,128)S(1)}, u32[]{:S(2)}, u32[]{:S(2)}) collective-permute-start(f32[128,2048]{1,0:T(8,128)} %pad_maximum_fusion), channel_id=1, source_target_pairs={{0,96},{32,64},{64,32},{96,0},{128,224},{160,192},{192,160},{224,1... | collective-permute-start | bytes 3145736 | tf_op jit(solution)/shard_map/ppermute | solution.py:84
  96.4 12.8 %all-to-all-start.3 = ((f32[16,8,128]{2,1,0:T(8,128)}), f32[16,8,128]{2,1,0:T(8,128)S(1)}, u32[]{:S(2)}, u32[]{:S(2)}) async-start(f32[16,8,128]{2,1,0:T(8,128)} %bitcast.3), calls=%async_computation.3 | async-start | bytes 131072 | tf_op jit(solution)/shard_map/all_to_all | solution.py:93
  109.9 12.3 %collective-permute-start.5 = (f32[8,2048]{1,0:T(8,128)S(1)}, f32[8,2048]{1,0:T(8,128)S(1)}, u32[]{:S(2)}, u32[]{:S(2)}) collective-permute-start(f32[8,2048]{1,0:T(8,128)S(1)} %fusion.17), channel_id=1, source_target_pairs={{1,2},{3,4},{5,6},{7,8},{9,10},{11,12},{13,14},{15,16},{17,18},{19... | collective-permute-start | bytes 196616 | tf_op jit(solution)/shard_map/ppermute | solution.py:54
  122.3 3.1 %collective-permute-start.6 = (f32[8,2048]{1,0:T(8,128)S(1)}, f32[8,2048]{1,0:T(8,128)S(1)}, u32[]{:S(2)}, u32[]{:S(2)}) collective-permute-start(f32[8,2048]{1,0:T(8,128)S(1)} %fusion.17), channel_id=1, source_target_pairs={{0,1},{1,0},{2,3},{3,2},{4,5},{5,4},{6,7},{7,6},{8,9},{9,8},{10,11... | collective-permute-start | bytes 196616 | tf_op jit(solution)/shard_map/ppermute | solution.py:56
  125.5 0.8 copy-start
  125.6 0.8 copy-start.3
  174.2 11.6 %collective-permute-start.7 = (f32[8,2048]{1,0:T(8,128)S(1)}, f32[8,2048]{1,0:T(8,128)S(1)}, u32[]{:S(2)}, u32[]{:S(2)}) collective-permute-start(f32[8,2048]{1,0:T(8,128)S(1)} %convolution_subtract_fusion.1), channel_id=1, source_target_pairs={{1,2},{3,4},{5,6},{7,8},{9,10},{11,12},{13,14},{15,16},{17,18},{19... | collective-permute-start | bytes 196616 | tf_op jit(solution)/shard_map/ppermute | solution.py:54
  185.8 3.1 %collective-permute-start.8 = (f32[8,2048]{1,0:T(8,128)S(1)}, f32[8,2048]{1,0:T(8,128)S(1)}, u32[]{:S(2)}, u32[]{:S(2)}) collective-permute-start(f32[8,2048]{1,0:T(8,128)S(1)} %convolution_subtract_fusion.1), channel_id=1, source_target_pairs={{0,1},{1,0},{2,3},{3,2},{4,5},{5,4},{6,7},{7,6},{8,9},{9,8},{10,11... | collective-permute-start | bytes 196616 | tf_op jit(solution)/shard_map/ppermute | solution.py:56

commit v20 on v19

--- a/solution.py
+++ b/solution.py
@@ -114,7 +114,6 @@
     cells = planes * line
     weight = 1.0 / (lax.axis_size("space") * cells)
     tie = lax.optimization_barrier
-    own = [states.reshape(-1, cells) for states in occupied]
     diagonal = 3.75 + potential[None, :, :] - energies[:, None, None]
     vectors = initial.reshape(count, cells)
     lower = lax.axis_index("band") % 4 < 2
@@ -122,10 +121,10 @@
     pair = jnp.concatenate(
         [jnp.where(lower, vectors, partner), jnp.where(lower, partner, vectors)], axis=0
     )
-    run = copies(own[0], "band", BAND_Z).reshape(-1, cells)
-    run, other, pair = tie((run, own[1], pair))
+    run = copies(occupied[0].reshape(-1, cells), "band", BAND_Z).reshape(-1, cells)
+    run, other, pair = tie((run, occupied[1], pair))
     across = swapped(run, 1)
-    second = copies(other, "band", BAND_Z).reshape(-1, cells)
+    second = copies(other.reshape(-1, cells), "band", BAND_Z).reshape(-1, cells)
     near = jnp.concatenate([run, across], axis=0)
     margins, across = pair_margins(products(pair, near), lower, weight, swapped(second, 1))
     margins, far = tie((margins, swapped(near, 3)))

time: 191 us -> 191 us (level)
  no operation moved by 1% of the time
where the time goes in v20:
time: 191 us; the launch traced here: 190 us
  blocking collectives  70.9 us (37%)
  starting transfers between devices  61.6 us (32%)
  waiting for transfers between devices  37.8 us (20%)
  matrix products  9.63 us (5%)
  local copies, waits for them, and re-layouts  6.32 us (3%)
  other arithmetic  2.87 us (2%)
    psum x2, blocking collectives, pair_margins(): total = lax.psum(product, 'space', axis_index_groups=SPACE_Z)  29.7 us
    psum x2, blocking collectives, space_sum(): return lax.psum(near, 'space', axis_index_groups=SPACE_Z)  24 us
    ppermute x5, starting transfers between devices, swapped(): lax.ppermute(x, 'band', [(i, i ^ bits) for i in range(lax.axis_size('band...  19.1 us
    all_to_all x3, waiting for transfers between devices, copies(): return lax.all_to_all(sent, axis, 0, 0, axis_index_groups=groups)  18.4 us
    all_to_all x3, starting transfers between devices, copies(): return lax.all_to_all(sent, axis, 0, 0, axis_index_groups=groups)  18.2 us
    all_to_all x2, blocking collectives, copies(): return lax.all_to_all(sent, axis, 0, 0, axis_index_groups=groups)  17.3 us
    ppermute x2, starting transfers between devices, neighbours(): across = lax.ppermute(vectors, 'space', outer)  13.1 us
    ppermute x2, waiting for transfers between devices, neighbours(): across = lax.ppermute(vectors, 'space', outer)  9.86 us
  transfers between devices with their start and end apart: 13, of which 9 were waited for; matrix products, arithmetic and copies ran while one was open for 4% of the time, Pallas kernels for 0%

profile of v20, /device:TPU:7, one launch (start us, length us, event | category | flops | bytes accessed | tf_op | source)
XLA Modules:
  0.0 190.3 jit_solution(6286613606695650298)
XLA Ops:
  0.6 1.0 slice_bitcast_fusion
  1.7 0.8 broadcast_in_dim.78
  2.5 5.7 %all-to-all-start = ((f32[4,16,2048]{2,1,0:T(8,128)}), f32[4,16,2048]{2,1,0:T(8,128)S(1)}, u32[]{:S(2)}, u32[]{:S(2)}) async-start(f32[4,16,2048]{2,1,0:T(8,128)} %broadcast_in_dim.78), calls=%async_computation | async-start | bytes 1048576 | tf_op jit(solution)/shard_map/all_to_all | solution.py:22
  8.3 4.6 %collective-permute-start = (f32[8,2048]{1,0:T(8,128)S(1)}, f32[8,2048]{1,0:T(8,128)S(1)}, u32[]{:S(2)}, u32[]{:S(2)}) collective-permute-start(f32[8,2048]{1,0:T(8,128)S(1)} %bitcast.60), channel_id=1, source_target_pairs={{0,96},{32,64},{64,32},{96,0},{128,224},{160,192},{192,160},{224,1... | collective-permute-start | bytes 196616 | tf_op jit(solution)/shard_map/ppermute | solution.py:84
  12.9 1.9 %collective-permute-done = f32[8,2048]{1,0:T(8,128)S(1)} collective-permute-done((f32[8,2048]{1,0:T(8,128)S(1)}, f32[8,2048]{1,0:T(8,128)S(1)}, u32[]{:S(2)}, u32[]{:S(2)}) %collective-permute-start) | collective-permute-done | bytes 65568 | tf_op jit(solution)/shard_map/ppermute | solution.py:84
  14.9 7.3 %all-to-all-done = f32[4,16,2048]{2,1,0:T(8,128)S(1)} async-done(((f32[4,16,2048]{2,1,0:T(8,128)}), f32[4,16,2048]{2,1,0:T(8,128)S(1)}, u32[]{:S(2)}, u32[]{:S(2)}) %all-to-all-start) | async-done | bytes 524320 | tf_op jit(solution)/shard_map/all_to_all | solution.py:22
  22.3 0.8 broadcast_in_dim.80
  23.1 3.5 %all-to-all-start.1 = ((f32[4,16,2048]{2,1,0:T(8,128)}), f32[4,16,2048]{2,1,0:T(8,128)S(1)}, u32[]{:S(2)}, u32[]{:S(2)}) async-start(f32[4,16,2048]{2,1,0:T(8,128)} %broadcast_in_dim.80), calls=%async_computation.1 | async-start | bytes 1048576 | tf_op jit(solution)/shard_map/all_to_all | solution.py:22
  26.6 3.2 %collective-permute-start.1 = (f32[64,2048]{1,0:T(8,128)S(1)}, f32[64,2048]{1,0:T(8,128)S(1)}, u32[]{:S(2)}, u32[]{:S(2)}) collective-permute-start(f32[64,2048]{1,0:T(8,128)S(1)} %bitcast.48), channel_id=1, source_target_pairs={{0,32},{32,0},{64,96},{96,64},{128,160},{160,128},{192,224},{224,1... | collective-permute-start | bytes 1572872 | tf_op jit(solution)/shard_map/ppermute | solution.py:84
  29.9 10.7 %all-to-all-done.1 = f32[4,16,2048]{2,1,0:T(8,128)S(1)} async-done(((f32[4,16,2048]{2,1,0:T(8,128)}), f32[4,16,2048]{2,1,0:T(8,128)S(1)}, u32[]{:S(2)}, u32[]{:S(2)}) %all-to-all-start.1) | async-done | bytes 524320 | tf_op jit(solution)/shard_map/all_to_all | solution.py:22
  40.5 3.2 %collective-permute-start.2 = (f32[64,2048]{1,0:T(8,128)S(1)}, f32[64,2048]{1,0:T(8,128)S(1)}, u32[]{:S(2)}, u32[]{:S(2)}) collective-permute-start(f32[64,2048]{1,0:T(8,128)S(1)} %bitcast.42), channel_id=1, source_target_pairs={{0,32},{32,0},{64,96},{96,64},{128,160},{160,128},{192,224},{224,1... | collective-permute-start | bytes 1572872 | tf_op jit(solution)/shard_map/ppermute | solution.py:84
  43.8 3.8 %collective-permute-start.3 = (f32[128,2048]{1,0:T(8,128)S(1)}, f32[128,2048]{1,0:T(8,128)}, u32[]{:S(2)}, u32[]{:S(2)}) collective-permute-start(f32[128,2048]{1,0:T(8,128)S(1)} %constant_dynamic-update-slice_fusion), channel_id=1, source_target_pairs={{0,96},{32,64},{64,32},{96,0},{128,224},{160,192},{192,160},{224,1... | collective-permute-start | bytes 3145736 | tf_op jit(solution)/shard_map/ppermute | solution.py:84
  47.7 0.5 fusion.43
  48.2 17.2 %psum.28 = f32[16,128]{1,0:T(8,128)S(1)} all-reduce(f32[16,128]{1,0:T(8,128)S(1)} %fusion.43), channel_id=1, replica_groups={{0,8,16,24},{1,9,17,25},{2,10,18,26},{3,11,19,27},{4,12,20,28},{5,13,21..., use_global_device_ids=true, to_apply=%region_0.1 | all-reduce | flops 2048 | bytes 16384 | tf_op jit(solution)/shard_map/psum | solution.py:88
  65.4 0.7 broadcast_in_dim.81
  66.1 9.0 %all-to-all-start.2 = ((f32[16,16,128]{2,1,0:T(8,128)}), f32[16,16,128]{2,1,0:T(8,128)S(1)}, u32[]{:S(2)}, u32[]{:S(2)}) async-start(f32[16,16,128]{2,1,0:T(8,128)} %broadcast_in_dim.81), calls=%async_computation.2 | async-start | bytes 262144 | tf_op jit(solution)/shard_map/all_to_all | solution.py:22
  75.0 1.1 pad_maximum_fusion
  76.1 4.3 %collective-permute-start.4 = (f32[128,2048]{1,0:T(8,128)}, f32[128,2048]{1,0:T(8,128)S(1)}, u32[]{:S(2)}, u32[]{:S(2)}) collective-permute-start(f32[128,2048]{1,0:T(8,128)} %pad_maximum_fusion), channel_id=1, source_target_pairs={{0,96},{32,64},{64,32},{96,0},{128,224},{160,192},{192,160},{224,1... | collective-permute-start | bytes 3145736 | tf_op jit(solution)/shard_map/ppermute | solution.py:84
  80.4 0.4 all-to-all-done.2
  80.9 1.6 fusion.44
  82.4 0.4 fusion
  82.8 0.5 fusion.33
  83.3 12.5 %psum.29 = f32[16,128]{1,0:T(8,128)S(1)} all-reduce(f32[16,128]{1,0:T(8,128)S(1)} %fusion.33), channel_id=1, replica_groups={{0,8,16,24},{1,9,17,25},{2,10,18,26},{3,11,19,27},{4,12,20,28},{5,13,21..., use_global_device_ids=true, to_apply=%region_3.4 | all-reduce | flops 2048 | bytes 16384 | tf_op jit(solution)/shard_map/psum | solution.py:88
  95.8 0.6 broadcast_in_dim.83
  96.5 7.3 %all-to-all-start.3 = ((f32[16,8,128]{2,1,0:T(8,128)}), f32[16,8,128]{2,1,0:T(8,128)S(1)}, u32[]{:S(2)}, u32[]{:S(2)}) async-start(f32[16,8,128]{2,1,0:T(8,128)} %bitcast.4), calls=%async_computation.3 | async-start | bytes 131072 | tf_op jit(solution)/shard_map/all_to_all | solution.py:93
  103.8 5.4 %all-to-all-done.3 = f32[16,8,128]{2,1,0:T(8,128)S(1)} async-done(((f32[16,8,128]{2,1,0:T(8,128)}), f32[16,8,128]{2,1,0:T(8,128)S(1)}, u32[]{:S(2)}, u32[]{:S(2)}) %all-to-all-start.3) | async-done | bytes 65568 | tf_op jit(solution)/shard_map/all_to_all | solution.py:93
  109.3 0.4 fusion.32
  109.6 0.4 fusion.17
  110.0 5.4 %collective-permute-start.5 = (f32[8,2048]{1,0:T(8,128)S(1)}, f32[8,2048]{1,0:T(8,128)S(1)}, u32[]{:S(2)}, u32[]{:S(2)}) collective-permute-start(f32[8,2048]{1,0:T(8,128)S(1)} %fusion.17), channel_id=1, source_target_pairs={{1,2},{3,4},{5,6},{7,8},{9,10},{11,12},{13,14},{15,16},{17,18},{19... | collective-permute-start | bytes 196616 | tf_op jit(solution)/shard_map/ppermute | solution.py:54
  115.4 0.1 copy.54
  115.4 0.1 fusion.42
  115.6 0.1 fusion.40
  115.7 0.1 fusion.41
  115.8 6.5 %collective-permute-done.5 = f32[8,2048]{1,0:T(8,128)S(1)} collective-permute-done((f32[8,2048]{1,0:T(8,128)S(1)}, f32[8,2048]{1,0:T(8,128)S(1)}, u32[]{:S(2)}, u32[]{:S(2)}) %collective-permute-start.5) | collective-permute-done | bytes 65568 | tf_op jit(solution)/shard_map/ppermute | solution.py:54
  122.3 1.9 %collective-permute-start.6 = (f32[8,2048]{1,0:T(8,128)S(1)}, f32[8,2048]{1,0:T(8,128)S(1)}, u32[]{:S(2)}, u32[]{:S(2)}) collective-permute-start(f32[8,2048]{1,0:T(8,128)S(1)} %fusion.17), channel_id=1, source_target_pairs={{0,1},{1,0},{2,3},{3,2},{4,5},{5,4},{6,7},{7,6},{8,9},{9,8},{10,11... | collective-permute-start | bytes 196616 | tf_op jit(solution)/shard_map/ppermute | solution.py:56
  124.3 0.1 fusion.39
  124.4 1.1 collective-permute-done.6
  125.5 0.1 copy.43
  125.6 0.1 copy.44
  125.6 0.8 copy-done
  126.4 0.5 fusion.18
  126.9 1.7 fusion.46
  128.6 0.5 fusion.45
  129.2 7.2 %all_to_all.30 = f32[8,8,256]{2,1,0:T(8,128)S(1)} all-to-all(f32[8,8,256]{2,1,0:T(8,128)S(1)} %broadcast_in_dim.89), channel_id=1, replica_groups={{0,1,2,3,4,5,6,7},{8,9,10,11,12,13,14,15},{16,17,18,19,20,21,22,23},{24..., dimensions={0} | all-to-all | bytes 131072 | tf_op jit(solution)/shard_map/all_to_all | solution.py:22
  136.4 11.5 %psum.30 = f32[8,256]{1,0:T(8,128)S(1)} all-reduce(f32[8,256]{1,0:T(8,128)S(1)} %reduce_sum.58), channel_id=1, replica_groups={{0,8,16,24},{1,9,17,25},{2,10,18,26},{3,11,19,27},{4,12,20,28},{5,13,21..., use_global_device_ids=true, to_apply=%region_7.8 | all-reduce | flops 2048 | bytes 16384 | tf_op jit(solution)/shard_map/psum | solution.py:27
  148.0 1.6 fusion.21
  149.5 0.4 fusion.1
  149.9 0.5 fusion.47
  150.4 0.5 fusion.31
  151.0 10.0 %all_to_all.31 = f32[8,8,256]{2,1,0:T(8,128)S(1)} all-to-all(f32[8,8,256]{2,1,0:T(8,128)S(1)} %broadcast_in_dim.90), channel_id=1, replica_groups={{0,1,2,3,4,5,6,7},{8,9,10,11,12,13,14,15},{16,17,18,19,20,21,22,23},{24..., dimensions={0} | all-to-all | bytes 131072 | tf_op jit(solution)/shard_map/all_to_all | solution.py:22
  161.0 12.5 %psum.31 = f32[8,256]{1,0:T(8,128)S(1)} all-reduce(f32[8,256]{1,0:T(8,128)S(1)} %reduce_sum.59), channel_id=1, replica_groups={{0,8,16,24},{1,9,17,25},{2,10,18,26},{3,11,19,27},{4,12,20,28},{5,13,21..., use_global_device_ids=true, to_apply=%region_9.10 | all-reduce | flops 2048 | bytes 16384 | tf_op jit(solution)/shard_map/psum | solution.py:27
  173.5 0.4 convolution_subtract_fusion.2
  173.9 0.4 convolution_subtract_fusion.1
  174.2 7.8 %collective-permute-start.7 = (f32[8,2048]{1,0:T(8,128)S(1)}, f32[8,2048]{1,0:T(8,128)S(1)}, u32[]{:S(2)}, u32[]{:S(2)}) collective-permute-start(f32[8,2048]{1,0:T(8,128)S(1)} %convolution_subtract_fusion.1), channel_id=1, source_target_pairs={{1,2},{3,4},{5,6},{7,8},{9,10},{11,12},{13,14},{15,16},{17,18},{19... | collective-permute-start | bytes 196616 | tf_op jit(solution)/shard_map/ppermute | solution.py:54
  182.0 0.1 copy.70
  182.1 0.1 fusion.38
  182.2 0.1 fusion.36
  182.3 0.1 fusion.37
  182.5 3.4 %collective-permute-done.7 = f32[8,2048]{1,0:T(8,128)S(1)} collective-permute-done((f32[8,2048]{1,0:T(8,128)S(1)}, f32[8,2048]{1,0:T(8,128)S(1)}, u32[]{:S(2)}, u32[]{:S(2)}) %collective-permute-start.7) | collective-permute-done | bytes 65568 | tf_op jit(solution)/shard_map/ppermute | solution.py:54
  185.8 1.9 %collective-permute-start.8 = (f32[8,2048]{1,0:T(8,128)S(1)}, f32[8,2048]{1,0:T(8,128)S(1)}, u32[]{:S(2)}, u32[]{:S(2)}) collective-permute-start(f32[8,2048]{1,0:T(8,128)S(1)} %convolution_subtract_fusion.1), channel_id=1, source_target_pairs={{0,1},{1,0},{2,3},{3,2},{4,5},{5,4},{6,7},{7,6},{8,9},{9,8},{10,11... | collective-permute-start | bytes 196616 | tf_op jit(solution)/shard_map/ppermute | solution.py:56
  187.7 0.1 fusion.35
  187.9 1.1 collective-permute-done.8
  189.0 0.1 copy.59
  189.1 1.1 fusion.3
  (39 shorter events, 0.5 us)
Async XLA Ops:
  2.5 5.8 %copy-start.1 = (f32[8,2,1024]{2,1,0:T(2,128)S(1)}, f32[8,2,1024]{2,1,0:T(2,128)}, u32[]{:S(2)}) copy-start(f32[8,2,1024]{2,1,0:T(2,128)} %param.6) | copy-start | bytes 196612
  2.5 19.7 %all-to-all-start = ((f32[4,16,2048]{2,1,0:T(8,128)}), f32[4,16,2048]{2,1,0:T(8,128)S(1)}, u32[]{:S(2)}, u32[]{:S(2)}) async-start(f32[4,16,2048]{2,1,0:T(8,128)} %broadcast_in_dim.78), calls=%async_computation | async-start | bytes 1048576 | tf_op jit(solution)/shard_map/all_to_all | solution.py:22
  8.3 6.6 %collective-permute-start = (f32[8,2048]{1,0:T(8,128)S(1)}, f32[8,2048]{1,0:T(8,128)S(1)}, u32[]{:S(2)}, u32[]{:S(2)}) collective-permute-start(f32[8,2048]{1,0:T(8,128)S(1)} %bitcast.60), channel_id=1, source_target_pairs={{0,96},{32,64},{64,32},{96,0},{128,224},{160,192},{192,160},{224,1... | collective-permute-start | bytes 196616 | tf_op jit(solution)/shard_map/ppermute | solution.py:84
  23.1 17.4 %all-to-all-start.1 = ((f32[4,16,2048]{2,1,0:T(8,128)}), f32[4,16,2048]{2,1,0:T(8,128)S(1)}, u32[]{:S(2)}, u32[]{:S(2)}) async-start(f32[4,16,2048]{2,1,0:T(8,128)} %broadcast_in_dim.80), calls=%async_computation.1 | async-start | bytes 1048576 | tf_op jit(solution)/shard_map/all_to_all | solution.py:22
  26.6 3.2 %copy-start.2 = (f32[2,1024]{1,0:T(2,128)S(1)}, f32[2,1024]{1,0:T(2,128)}, u32[]{:S(2)}) copy-start(f32[2,1024]{1,0:T(2,128)} %param.8) | copy-start | bytes 24580
  26.6 17.2 %collective-permute-start.1 = (f32[64,2048]{1,0:T(8,128)S(1)}, f32[64,2048]{1,0:T(8,128)S(1)}, u32[]{:S(2)}, u32[]{:S(2)}) collective-permute-start(f32[64,2048]{1,0:T(8,128)S(1)} %bitcast.48), channel_id=1, source_target_pairs={{0,32},{32,0},{64,96},{96,64},{128,160},{160,128},{192,224},{224,1... | collective-permute-start | bytes 1572872 | tf_op jit(solution)/shard_map/ppermute | solution.py:84
  40.5 24.8 %collective-permute-start.2 = (f32[64,2048]{1,0:T(8,128)S(1)}, f32[64,2048]{1,0:T(8,128)S(1)}, u32[]{:S(2)}, u32[]{:S(2)}) collective-permute-start(f32[64,2048]{1,0:T(8,128)S(1)} %bitcast.42), channel_id=1, source_target_pairs={{0,32},{32,0},{64,96},{96,64},{128,160},{160,128},{192,224},{224,1... | collective-permute-start | bytes 1572872 | tf_op jit(solution)/shard_map/ppermute | solution.py:84
  43.8 37.0 %collective-permute-start.3 = (f32[128,2048]{1,0:T(8,128)S(1)}, f32[128,2048]{1,0:T(8,128)}, u32[]{:S(2)}, u32[]{:S(2)}) collective-permute-start(f32[128,2048]{1,0:T(8,128)S(1)} %constant_dynamic-update-slice_fusion), channel_id=1, source_target_pairs={{0,96},{32,64},{64,32},{96,0},{128,224},{160,192},{192,160},{224,1... | collective-permute-start | bytes 3145736 | tf_op jit(solution)/shard_map/ppermute | solution.py:84
  66.1 14.7 %all-to-all-start.2 = ((f32[16,16,128]{2,1,0:T(8,128)}), f32[16,16,128]{2,1,0:T(8,128)S(1)}, u32[]{:S(2)}, u32[]{:S(2)}) async-start(f32[16,16,128]{2,1,0:T(8,128)} %broadcast_in_dim.81), calls=%async_computation.2 | async-start | bytes 262144 | tf_op jit(solution)/shard_map/all_to_all | solution.py:22
  76.1 33.1 %collective-permute-start.4 = (f32[128,2048]{1,0:T(8,128)}, f32[128,2048]{1,0:T(8,128)S(1)}, u32[]{:S(2)}, u32[]{:S(2)}) collective-permute-start(f32[128,2048]{1,0:T(8,128)} %pad_maximum_fusion), channel_id=1, source_target_pairs={{0,96},{32,64},{64,32},{96,0},{128,224},{160,192},{192,160},{224,1... | collective-permute-start | bytes 3145736 | tf_op jit(solution)/shard_map/ppermute | solution.py:84
  96.5 12.8 %all-to-all-start.3 = ((f32[16,8,128]{2,1,0:T(8,128)}), f32[16,8,128]{2,1,0:T(8,128)S(1)}, u32[]{:S(2)}, u32[]{:S(2)}) async-start(f32[16,8,128]{2,1,0:T(8,128)} %bitcast.4), calls=%async_computation.3 | async-start | bytes 131072 | tf_op jit(solution)/shard_map/all_to_all | solution.py:93
  110.0 12.3 %collective-permute-start.5 = (f32[8,2048]{1,0:T(8,128)S(1)}, f32[8,2048]{1,0:T(8,128)S(1)}, u32[]{:S(2)}, u32[]{:S(2)}) collective-permute-start(f32[8,2048]{1,0:T(8,128)S(1)} %fusion.17), channel_id=1, source_target_pairs={{1,2},{3,4},{5,6},{7,8},{9,10},{11,12},{13,14},{15,16},{17,18},{19... | collective-permute-start | bytes 196616 | tf_op jit(solution)/shard_map/ppermute | solution.py:54
  122.3 3.1 %collective-permute-start.6 = (f32[8,2048]{1,0:T(8,128)S(1)}, f32[8,2048]{1,0:T(8,128)S(1)}, u32[]{:S(2)}, u32[]{:S(2)}) collective-permute-start(f32[8,2048]{1,0:T(8,128)S(1)} %fusion.17), channel_id=1, source_target_pairs={{0,1},{1,0},{2,3},{3,2},{4,5},{5,4},{6,7},{7,6},{8,9},{9,8},{10,11... | collective-permute-start | bytes 196616 | tf_op jit(solution)/shard_map/ppermute | solution.py:56
  125.6 0.8 copy-start
  125.6 0.8 copy-start.3
  174.2 11.6 %collective-permute-start.7 = (f32[8,2048]{1,0:T(8,128)S(1)}, f32[8,2048]{1,0:T(8,128)S(1)}, u32[]{:S(2)}, u32[]{:S(2)}) collective-permute-start(f32[8,2048]{1,0:T(8,128)S(1)} %convolution_subtract_fusion.1), channel_id=1, source_target_pairs={{1,2},{3,4},{5,6},{7,8},{9,10},{11,12},{13,14},{15,16},{17,18},{19... | collective-permute-start | bytes 196616 | tf_op jit(solution)/shard_map/ppermute | solution.py:54
  185.8 3.1 %collective-permute-start.8 = (f32[8,2048]{1,0:T(8,128)S(1)}, f32[8,2048]{1,0:T(8,128)S(1)}, u32[]{:S(2)}, u32[]{:S(2)}) collective-permute-start(f32[8,2048]{1,0:T(8,128)S(1)} %convolution_subtract_fusion.1), channel_id=1, source_target_pairs={{0,1},{1,0},{2,3},{3,2},{4,5},{5,4},{6,7},{7,6},{8,9},{9,8},{10,11... | collective-permute-start | bytes 196616 | tf_op jit(solution)/shard_map/ppermute | solution.py:56
